TPU v7x, 32 devices: a whole 2x2x4 slice. The times are simulated.
32 devices in a mesh: groups: 2 (over y), rec: 4 (over z), attr: 4 (over x, core).
Axes of the slice: x: 2, y: 2, z: 4, core: 2. Of those that a mesh axis runs over, the one named last changes fastest.
Arguments:
- cells: bfloat16 [64, 49152], P(('groups', 'rec'), 'attr'), parts along dimension 0, may hold values from -1000 to 1000
- cotangent: bfloat16 [64, 49152], P(('groups', 'rec'), 'attr'), parts along dimension 0, may hold values from -6 to 6
- qkv_attr: bfloat16 [192, 576], replicated, may hold values from -8 to 8
- out_attr: bfloat16 [192, 192], replicated, may hold values from -0.4375 to 0.4375
- qkv_samp: bfloat16 [192, 576], replicated, may hold values from -8 to 8
- out_samp: bfloat16 [192, 192], replicated, may hold values from -0.4375 to 0.4375
- up_weight: bfloat16 [192, 768], replicated, may hold values from -0.4375 to 0.4375
- down_weight: bfloat16 [768, 192], replicated, may hold values from -0.21875 to 0.21875
- train_split: int32 [64], P('groups'), parts along dimension 0, may hold values from 0 to 1, as said below
Outputs:
- grad_cells: bfloat16 [64, 49152], P(('groups', 'rec'), 'attr'), parts along dimension 0
- grad_qkv_attr: float32 [384, 576], P('groups'), parts along dimension 0
- grad_out_attr: float32 [384, 192], P('groups'), parts along dimension 0
- grad_qkv_samp: float32 [384, 576], P('groups'), parts along dimension 0
- grad_out_samp: float32 [384, 192], P('groups'), parts along dimension 0
- grad_up: float32 [384, 768], P('groups'), parts along dimension 0
- grad_down: float32 [1536, 192], P('groups'), parts along dimension 0
There are 2 independent parts, one for each index of `groups`. A program takes and returns all parts, laid end to end along the dimension named above; an argument that names none is the same for every part. Nothing has to cross between parts.
Inputs may be any that keep to these rules, and one draw needn't show every extreme that they name: `train_split`: every table window has at least one training record.
All inputs are finite; a program needn't handle non-finite values.
Results may differ from a plain program's by a relative error of at most 0.018.
The roundings to bfloat16 on the way count: a program that leaves them out, or rounds other values in their place, can miss the bound.
Values may be sent and summed in bfloat16 or wider, within the bound.
No kernel may reach another device: no remote copies, remote signals or barrier semaphores. Data moves between devices by JAX's collectives and lax.ppermute only.
A program may use at most 64 MiB of HBM per device.

v0:
```python
import functools
import math

import jax
import jax.numpy as jnp
from jax import lax
from jax.experimental import pallas as pl
from jax.experimental.pallas import tpu as pltpu
from jax.sharding import PartitionSpec as P

E = 192
HEADS = 6
FF = 768
HEAD = E // HEADS
LANES = 128
BF = jnp.bfloat16
F32 = jnp.float32
EXP2 = math.log2(math.e) / math.sqrt(HEAD)
SCALE = 1.0 / math.sqrt(HEAD)
HALF_ROOT = math.sqrt(0.5)
BELL = 1.0 / math.sqrt(2.0 * math.pi)


def nn(left, right):
    return lax.dot_general(left, right, (((1,), (0,)), ((), ())), preferred_element_type=F32)


def nt(left, right):
    return lax.dot_general(left, right, (((1,), (1,)), ((), ())), preferred_element_type=F32)


def tn(left, right):
    return lax.dot_general(left, right, (((0,), (0,)), ((), ())), preferred_element_type=F32)


def digits(index, sizes):
    out = []
    for size in reversed(sizes):
        if size & (size - 1) == 0:
            out.append(index & (size - 1))
            index = index >> (size.bit_length() - 1)
        else:
            out.append(lax.rem(index, size))
            index = lax.div(index, size)
    return out[::-1]


def wrap(index, size):
    return digits(index + size, (size,))[0]


def one_hot(rows, source):
    own = lax.broadcasted_iota(jnp.int32, (rows, source.shape[1]), 0)
    return jnp.where(own == source, 1.0, 0.0).astype(BF)


def lane_index(size):
    return lax.broadcasted_iota(jnp.int32, (1, size), 1)


def eye(size):
    return one_hot(size, lane_index(size))


def side_by_side(refs):
    return jnp.concatenate([ref[...] for ref in refs], axis=1)


def put_tiles(refs, table):
    width = refs[0].shape[1]
    for position, ref in enumerate(refs):
        ref[...] = table[:, position * width : (position + 1) * width].astype(ref.dtype)


class Plan:
    def __init__(self, cells, ranks_rec, ranks_attr):
        self.ranks_rec, self.ranks_attr = ranks_rec, ranks_attr
        self.rec, self.attr = cells.shape[0], cells.shape[1] // E
        self.cells = self.rec * self.attr
        self.own_rec = self.rec // ranks_attr
        self.own_attr = self.attr // ranks_rec
        self.all_rec = self.rec * ranks_rec
        self.all_attr = self.attr * ranks_attr
        self.row_tile = self.own_rec * self.attr
        self.col_tile = self.rec * self.own_attr

    def row_digits(self, index):
        return digits(index, (self.ranks_attr, self.own_rec, self.attr))

    def col_digits(self, index):
        return digits(index, (self.ranks_rec, self.ranks_attr, self.own_rec, self.own_attr))

    def record_of(self, step, own):
        return self.own_rec * wrap(step + lax.axis_index("attr"), self.ranks_attr) + own

    def attr_of(self, step, own):
        return self.own_attr * wrap(step + lax.axis_index("rec"), self.ranks_rec) + own

    def rows_from_owned(self):
        step, own, attr = self.row_digits(lane_index(self.cells))
        return attr * self.rec + self.record_of(step, own)

    def cols_from_owned(self):
        far, near, own, attr = self.col_digits(lane_index(self.cells))
        return self.attr_of(far, attr) * self.rec + self.record_of(near, own)

    def cols_from_rows(self):
        far, near, own, attr = self.col_digits(lane_index(self.cells))
        return (near * self.own_rec + own) * self.attr + self.attr_of(far, attr)

    def grouped_from_rows(self):
        own, step, attr = digits(lane_index(self.cells), (self.own_rec, self.ranks_attr, self.attr))
        return (step * self.own_rec + own) * self.attr + attr

    def grouped_from_cols(self):
        attr, place = digits(lane_index(self.cells), (self.own_attr, self.all_rec))
        return place * self.own_attr + attr


def split_kernel(plan, to_rows, table_ref, *refs):
    outs, rows = refs[:-1], refs[-1]
    for pair in range(plan.attr // 2):
        both = table_ref[:, 2 * E * pair : 2 * E * (pair + 1)].astype(F32)
        for side in range(2):
            start = (2 * pair + side) * plan.rec
            rows[start : start + plan.rec, :] = both[:, side * E : (side + 1) * E]
    turned = nt(eye(E), rows[...].astype(BF)).astype(BF)
    source = plan.rows_from_owned() if to_rows else plan.cols_from_owned()
    put_tiles(outs, nn(turned, one_hot(plan.cells, source)))


def join_kernel(plan, *refs):
    tiles, out_ref, rows = refs[:-2], refs[-2], refs[-1]
    rows[...] = nt(one_hot(plan.cells, plan.rows_from_owned()), side_by_side(tiles))
    for pair in range(plan.attr // 2):
        start = 2 * pair * plan.rec
        both = [rows[start + side * plan.rec : start + (side + 1) * plan.rec, :] for side in range(2)]
        out_ref[:, 2 * E * pair : 2 * E * (pair + 1)] = jnp.concatenate(both, axis=1).astype(BF)


def to_cols_kernel(plan, *refs):
    tiles, outs = refs[: plan.ranks_attr], refs[plan.ranks_attr :]
    put_tiles(outs, nn(side_by_side(tiles), one_hot(plan.cells, plan.cols_from_rows())))


def to_rows_kernel(plan, *refs):
    tiles, outs = refs[: plan.ranks_rec], refs[plan.ranks_rec :]
    put_tiles(outs, nt(side_by_side(tiles), one_hot(plan.cells, plan.cols_from_rows())))


def turn_kernel(count, *refs):
    for source, target in zip(refs[:count], refs[count:]):
        target[...] = source[...].astype(F32).T.astype(BF)


def norm(table):
    center = table - jnp.mean(table, axis=0, keepdims=True)
    spread = jnp.mean(center * center, axis=0, keepdims=True)
    root = lax.rsqrt(spread + 1e-05)
    return center * root, root


def norm_back(grad, normed, root):
    along = jnp.mean(grad * normed, axis=0, keepdims=True)
    return root * (grad - jnp.mean(grad, axis=0, keepdims=True) - normed * along)


def blocks_of(width, total):
    return [slice(start, start + width) for start in range(0, total, width)]


def heads_of(ref, part, head, cols):
    start = part * E + head * HEAD
    return ref[start : start + HEAD, cols]


def attend(x_ref, normed_ref, proj_ref, probs_ref, mixed_ref, qkv_t, out_t, width, mask):
    results = []
    for place, cols in enumerate(blocks_of(width, x_ref.shape[1])):
        table = x_ref[:, cols].astype(F32)
        normed_ref[:, cols] = norm(table)[0].astype(BF)
        proj_ref[:, cols] = nn(qkv_t[...], normed_ref[:, cols]).astype(BF)
        for head in range(HEADS):
            query, key, value = (heads_of(proj_ref, part, head, cols) for part in range(3))
            scores = tn(key, query)
            if mask is not None:
                scores = scores + mask
            expo = jnp.exp2((scores - jnp.max(scores, axis=0, keepdims=True)) * EXP2)
            probs = (expo * (1.0 / jnp.sum(expo, axis=0, keepdims=True))).astype(BF)
            probs_ref[place * HEADS + head] = probs
            mixed_ref[head * HEAD : (head + 1) * HEAD, cols] = nn(value, probs).astype(BF)
        results.append(x_ref[:, cols].astype(F32) + nn(out_t[...], mixed_ref[:, cols]))
    return results


def attend_back(grad_ref, x_ref, proj_ref, probs_ref, grad_proj_ref, qkv, out, width):
    results = []
    for place, cols in enumerate(blocks_of(width, x_ref.shape[1])):
        grad_mixed = nn(out[...], grad_ref[:, cols]).astype(BF)
        for head in range(HEADS):
            query, key, value = (heads_of(proj_ref, part, head, cols) for part in range(3))
            grad_head = grad_mixed[head * HEAD : (head + 1) * HEAD]
            probs = probs_ref[place * HEADS + head]
            grad_probs = tn(value, grad_head).astype(BF).astype(F32)
            wide = probs.astype(F32)
            moved = grad_probs * wide
            grad_scores = (moved - wide * jnp.sum(moved, axis=0, keepdims=True)) * SCALE
            grad_scores = grad_scores.astype(BF)
            for part, value_of in enumerate(
                (nn(key, grad_scores), nt(query, grad_scores), nt(grad_head, probs))
            ):
                start = part * E + head * HEAD
                grad_proj_ref[start : start + HEAD, cols] = value_of.astype(BF)
        grad_normed = nn(qkv[...], grad_proj_ref[:, cols]).astype(BF).astype(F32)
        normed, root = norm(x_ref[:, cols].astype(F32))
        results.append(norm_back(grad_normed, normed, root) + grad_ref[:, cols].astype(F32))
    return results


def put_attend_grads(out_ref, normed_ref, grad_proj_ref, mixed_ref, grad_ref):
    qkv = nt(normed_ref[...], grad_proj_ref[...])
    out = nt(mixed_ref[...], grad_ref[...])
    whole = 3 * E // LANES
    for tile in range(whole):
        out_ref[tile * E : (tile + 1) * E, :] = qkv[:, tile * LANES : (tile + 1) * LANES].astype(BF)
    mixed = jnp.concatenate([qkv[:, whole * LANES :], out[:, LANES:]], axis=1)
    out_ref[whole * E : (whole + 1) * E, :] = mixed.astype(BF)
    out_ref[(whole + 1) * E : (whole + 2) * E, :] = out[:, :LANES].astype(BF)


def take_attend_grads(in_ref, first, qkv_ref, out_ref, factor):
    whole = 3 * E // LANES

    def tile(number):
        return in_ref[first + number * E : first + (number + 1) * E, :].astype(F32) * factor

    for number in range(whole):
        qkv_ref[:, number * LANES : (number + 1) * LANES] = tile(number)
    mixed = tile(whole)
    qkv_ref[:, whole * LANES :] = mixed[:, : LANES // 2]
    out_ref[:, :LANES] = tile(whole + 1)
    out_ref[:, LANES:] = mixed[:, LANES // 2 :]


def rows_forward_kernel(plan, *refs):
    tiles, refs = refs[: plan.ranks_attr], refs[plan.ranks_attr :]
    (qkv_t, out_t), refs = refs[:2], refs[2:]
    outs, (x_ref, normed_ref, proj_ref, probs_ref, mixed_ref) = refs[: plan.ranks_attr], refs[plan.ranks_attr :]
    order = one_hot(plan.cells, plan.grouped_from_rows())
    x_ref[...] = nn(side_by_side(tiles), order).astype(BF)
    first = attend(x_ref, normed_ref, proj_ref, probs_ref, mixed_ref, qkv_t, out_t, plan.all_attr, None)
    put_tiles(outs, nt(jnp.concatenate(first, axis=1).astype(BF), order))


def rows_back_kernel(plan, *refs):
    tiles, refs = refs[: plan.ranks_attr], refs[plan.ranks_attr :]
    (qkv, out, x_ref, normed_ref, proj_ref, probs_ref, mixed_ref), refs = refs[:7], refs[7:]
    outs, (sums_ref, grad_ref, grad_proj_ref) = refs[: plan.ranks_attr], refs[plan.ranks_attr :]
    order = one_hot(plan.cells, plan.grouped_from_rows())
    grad_ref[...] = nn(side_by_side(tiles), order).astype(BF)
    grads = attend_back(grad_ref, x_ref, proj_ref, probs_ref, grad_proj_ref, qkv, out, plan.all_attr)
    put_tiles(outs, nt(jnp.concatenate(grads, axis=1).astype(BF), order))
    put_attend_grads(sums_ref, normed_ref, grad_proj_ref, mixed_ref, grad_ref)


def cols_kernel(plan, *refs):
    count = plan.ranks_rec
    tiles, cot_tiles, refs = refs[:count], refs[count : 2 * count], refs[2 * count :]
    (train_ref, qkv, out, up, down, qkv_t, out_t, up_t), refs = refs[:8], refs[8:]
    outs, (sums_ref,), refs = refs[:count], refs[count : count + 1], refs[count + 1 :]
    x_ref, cot_ref, normed_ref, proj_ref, probs_ref, mixed_ref, second_ref = refs[:7]
    pre_ref, hidden_ref, grad_pre_ref, grad_ref, grad_proj_ref = refs[7:]
    width = max(LANES, plan.all_rec)
    order = one_hot(plan.cells, plan.grouped_from_cols())
    x_ref[...] = nn(side_by_side(tiles), order).astype(BF)
    cot_ref[...] = nn(side_by_side(cot_tiles), order).astype(BF)

    row = lax.broadcasted_iota(jnp.int32, (width, 1), 0)
    sequence, far, near, own = digits(row, (width // plan.all_rec, plan.ranks_rec, plan.ranks_attr, plan.own_rec))
    record = plan.rec * wrap(lax.axis_index("rec") - far, plan.ranks_rec) + plan.record_of(near, own)
    chosen = (record == lane_index(plan.all_rec)) & (train_ref[...] > 0)
    allowed = jnp.max(jnp.where(chosen, 1.0, 0.0), axis=1, keepdims=True) > 0.5
    asker = digits(lane_index(width), (width // plan.all_rec, plan.all_rec))[0]
    mask = jnp.where(allowed & (sequence == asker), 0.0, -1e30)

    second = attend(x_ref, normed_ref, proj_ref, probs_ref, mixed_ref, qkv_t, out_t, width, mask)
    for cols, value in zip(blocks_of(width, plan.cells), second):
        second_ref[:, cols] = value.astype(BF)

    table, root = norm(second_ref[...].astype(F32))
    normed_second = table.astype(BF)
    pre_ref[...] = nn(up_t[...], normed_second)
    grad_pre_ref[...] = nn(down[...], cot_ref[...])
    step = 32
    for start in range(0, FF, step):
        rows = slice(start, start + step)
        pre = pre_ref[rows, :]
        gate = 0.5 + 0.5 * lax.erf(pre * HALF_ROOT)
        hidden_ref[rows, :] = (pre * gate).astype(BF)
        slope = gate + pre * (jnp.exp(-0.5 * pre * pre) * BELL)
        grad_pre_ref[rows, :] = grad_pre_ref[rows, :].astype(BF).astype(F32) * slope
    grad_pre = grad_pre_ref[...].astype(BF)

    base = 6 * E
    grad_up = nt(normed_second, grad_pre)
    for tile in range(FF // LANES):
        rows = slice(base + tile * E, base + (tile + 1) * E)
        sums_ref[rows, :] = grad_up[:, tile * LANES : (tile + 1) * LANES].astype(BF)
    base = 12 * E
    grad_down = nt(hidden_ref[...], cot_ref[...])
    sums_ref[base : base + FF, :] = grad_down[:, :LANES].astype(BF)
    rest = jnp.concatenate([grad_down[: FF // 2, LANES:], grad_down[FF // 2 :, LANES:]], axis=1)
    sums_ref[base + FF : base + FF + FF // 2, :] = rest.astype(BF)

    grad_normed = nn(up[...], grad_pre).astype(BF).astype(F32)
    grad = norm_back(grad_normed, table, root) + cot_ref[...].astype(F32)
    grad_ref[...] = grad.astype(BF)
    grads = attend_back(grad_ref, x_ref, proj_ref, probs_ref, grad_proj_ref, qkv, out, width)
    put_tiles(outs, nt(jnp.concatenate(grads, axis=1).astype(BF), order))
    put_attend_grads(sums_ref, normed_ref, grad_proj_ref, mixed_ref, grad_ref)


def finish_cols_kernel(factor, sums_ref, qkv_ref, out_ref, up_ref, down_ref):
    take_attend_grads(sums_ref, 0, qkv_ref, out_ref, factor)
    base = 6 * E
    for tile in range(FF // LANES):
        rows = slice(base + tile * E, base + (tile + 1) * E)
        up_ref[:, tile * LANES : (tile + 1) * LANES] = sums_ref[rows, :].astype(F32) * factor
    base = 12 * E
    down_ref[:, :LANES] = sums_ref[base : base + FF, :].astype(F32) * factor
    rest = sums_ref[base + FF : base + FF + FF // 2, :].astype(F32) * factor
    down_ref[: FF // 2, LANES:] = rest[:, : LANES // 2]
    down_ref[FF // 2 :, LANES:] = rest[:, LANES // 2 :]


def finish_rows_kernel(factor, sums_ref, qkv_ref, out_ref):
    take_attend_grads(sums_ref, 0, qkv_ref, out_ref, factor)


def call(body, outs, scratch, *args):
    whole = pl.BlockSpec(memory_space=pltpu.VMEM)
    return pl.pallas_call(
        body,
        out_shape=[jax.ShapeDtypeStruct(shape, dtype) for shape, dtype in outs],
        in_specs=[whole] * len(args),
        out_specs=[whole] * len(outs),
        scratch_shapes=[pltpu.VMEM(shape, dtype) for shape, dtype in scratch],
        compiler_params=pltpu.CompilerParams(vmem_limit_bytes=48 * 1024 * 1024),
    )(*args)


def exchange(tiles, axis, sign):
    size = len(tiles)
    return [tiles[0]] + [
        lax.ppermute(tiles[k], axis, [(i, (i + sign * k) % size) for i in range(size)])
        for k in range(1, size)
    ]


def scatter_sum(parts, axis):
    size, own = parts.shape[0], lax.axis_index(axis)
    tiles = [
        lax.dynamic_index_in_dim(parts, (own + k) % size, 0, keepdims=False) for k in range(size)
    ]
    return sum(tile.astype(F32) for tile in exchange(tiles, axis, 1)).astype(BF)


def gather(part, axis, size):
    got = exchange([part] * size, axis, 1)
    ordered = [got[0]] + got[:0:-1]
    both = jnp.concatenate(ordered + ordered[:-1], axis=0)
    rows = part.shape[0]
    start = (size - lax.axis_index(axis)) % size * rows
    return lax.dynamic_slice_in_dim(both, start, size * rows, 0)


def total(sums, ranks_rec, ranks_attr):
    rows = sums.shape[0]
    part = scatter_sum(sums.reshape(ranks_attr, rows // ranks_attr, LANES), "attr")
    part = scatter_sum(part.reshape(ranks_rec, rows // ranks_attr // ranks_rec, LANES), "rec")
    return gather(gather(part, "rec", ranks_rec), "attr", ranks_attr)


def local(
    cells, cotangent, qkv_attr, out_attr, qkv_samp, out_samp, up_weight, down_weight, train_split
):
    ranks_rec, ranks_attr = lax.axis_size("rec"), lax.axis_size("attr")
    plan = Plan(cells, ranks_rec, ranks_attr)
    count = plan.cells
    factor = 1.0 / math.sqrt(plan.all_rec * plan.all_attr)
    row_tiles = [((E, plan.row_tile), BF)] * ranks_attr
    col_tiles = [((E, plan.col_tile), BF)] * ranks_rec
    table, wide = ((E, count), BF), ((3 * E, count), BF)

    def probs(width):
        return ((count // width * HEADS, width, width), BF)

    def kernel(body, *static):
        return functools.partial(body, plan, *static)

    rows = call(kernel(split_kernel, True), row_tiles, [((count, E), F32)], cells)
    rows = exchange(rows, "attr", 1)
    weights = (qkv_attr, out_attr, qkv_samp, out_samp, up_weight)
    qkv_attr_t, out_attr_t, qkv_samp_t, out_samp_t, up_t = call(
        functools.partial(turn_kernel, len(weights)), [(w.shape[::-1], BF) for w in weights], [], *weights
    )
    cot = call(kernel(split_kernel, False), col_tiles, [((count, E), F32)], cotangent)
    cot = exchange(cot, "rec", 1)

    got = call(
        kernel(rows_forward_kernel),
        row_tiles + [table, table, wide, probs(plan.all_attr), table],
        [],
        *rows,
        qkv_attr_t,
        out_attr_t,
    )
    first, saved = got[:ranks_attr], got[ranks_attr:]
    first = exchange(first, "attr", -1)
    cols = exchange(call(kernel(to_cols_kernel), col_tiles, [], *first), "rec", 1)

    width = max(LANES, plan.all_rec)
    sums_rows = 6 * E
    got = call(
        kernel(cols_kernel),
        col_tiles + [((3 * sums_rows, LANES), BF)],
        [table, table, table, wide, probs(width), table, table]
        + [((FF, count), F32), ((FF, count), BF), ((FF, count), F32), table, wide],
        *cols,
        *cot,
        train_split.reshape(1, -1),
        qkv_samp,
        out_samp,
        up_weight,
        down_weight,
        qkv_samp_t,
        out_samp_t,
        up_t,
    )
    grads, sums = exchange(got[:ranks_rec], "rec", -1), got[ranks_rec]
    grads = exchange(call(kernel(to_rows_kernel), row_tiles, [], *grads), "attr", 1)

    got = call(
        kernel(rows_back_kernel),
        row_tiles + [((sums_rows, LANES), BF)],
        [table, wide],
        *grads,
        qkv_attr,
        out_attr,
        *saved,
    )
    grads, row_sums = exchange(got[:ranks_attr], "attr", -1), got[ranks_attr]
    (grad_cells,) = call(kernel(join_kernel), [(cells.shape, BF)], [((count, E), F32)], *grads)

    sums = total(sums, ranks_rec, ranks_attr)
    grad_qkv_samp, grad_out_samp, grad_up, grad_down = call(
        functools.partial(finish_cols_kernel, factor),
        [((E, 3 * E), F32), ((E, E), F32), ((E, FF), F32), ((FF, E), F32)],
        [],
        sums,
    )
    row_sums = total(row_sums, ranks_rec, ranks_attr)
    grad_qkv_attr, grad_out_attr = call(
        functools.partial(finish_rows_kernel, factor), [((E, 3 * E), F32), ((E, E), F32)], [], row_sums
    )
    return (grad_cells, grad_qkv_attr, grad_out_attr, grad_qkv_samp, grad_out_samp, grad_up, grad_down)


def solution(mesh):
    own = P(("groups", "rec"), "attr")
    in_specs = (own, own) + (P(),) * 6 + (P("groups"),)
    out_specs = (own,) + (P("groups", None),) * 6
    return jax.shard_map(local, mesh=mesh, in_specs=in_specs, out_specs=out_specs, check_vma=False)
```

profile of v0, /device:TPU:0, one launch (start us, length us, event | category | flops | bytes accessed | tf_op | source)
XLA Modules:
  0.0 142.8 jit_solution(17621071279600452734)
XLA Ops:
  0.7 1.0 copy-done.22
  2.6 2.6 %collective-permute-start.1 = (bf16[192,128]{1,0:T(8,128)(2,1)S(1)}, bf16[192,128]{1,0:T(8,128)(2,1)S(1)}, u32[]{:S(2)}, u32[]{:S(2)}) collective-permute-start(bf16[192,128]{1,0:T(8,128)(2,1)S(1)} %get-tuple-element.55), channel_id=1, source_target_pairs={{0,2},{1,3},{2,0},{3,1},{4,6},{5,7},{6,4},{7,5},{8,10},{9,11},{10,... | collective-permute-start | bytes 147464 | tf_op jit(solution)/shard_map/ppermute | solution.py:355
  5.2 1.4 collective-permute-start.2
  6.6 1.0 copy-done
  7.6 0.9 copy-done.2
  8.5 0.9 copy-done.4
  9.4 0.9 copy-done.10
  10.3 0.9 copy-done.12
  12.3 5.0 %shard_map.146 = (bf16[192,128]{1,0:T(8,128)(2,1)S(1)}, bf16[192,128]{1,0:T(8,128)(2,1)S(1)}, bf16[192,128]{1,0:T(8,128)(2,1)S(1)}, bf16[192,128]{1,0:T(8,128)(2...) custom-call(bf16[192,128]{1,0:T(8,128)(2,1)S(1)} %get-tuple-element., ...), custom_call_target="tpu_custom_call" | custom-call | tf_op jit(solution)/shard_map/pallas_call | solution.py:342
  19.4 1.2 shard_map.148
  20.6 1.6 %collective-permute-start.9 = (bf16[192,128]{1,0:T(8,128)(2,1)S(1)}, bf16[192,128]{1,0:T(8,128)(2,1)S(1)}, u32[]{:S(2)}, u32[]{:S(2)}) collective-permute-start(bf16[192,128]{1,0:T(8,128)(2,1)S(1)} %get-tuple-element.68), channel_id=1, source_target_pairs={{0,4},{4,8},{8,12},{12,0},{1,5},{5,9},{9,13},{13,1},{2,6},{6,10},{... | collective-permute-start | bytes 147464 | tf_op jit(solution)/shard_map/ppermute | solution.py:355
  22.2 2.6 %collective-permute-start.10 = (bf16[192,128]{1,0:T(8,128)(2,1)}, bf16[192,128]{1,0:T(8,128)(2,1)}, u32[]{:S(2)}, u32[]{:S(2)}) collective-permute-start(bf16[192,128]{1,0:T(8,128)(2,1)} %get-tuple-element.69), channel_id=1, source_target_pairs={{0,8},{4,12},{8,0},{12,4},{1,9},{5,13},{9,1},{13,5},{2,10},{6,14},... | collective-permute-start | bytes 147464 | tf_op jit(solution)/shard_map/ppermute | solution.py:355
  24.8 1.3 collective-permute-start.11
  26.2 0.9 shard_map.147
  29.7 2.7 %collective-permute-start.8 = (bf16[192,128]{1,0:T(8,128)(2,1)}, bf16[192,128]{1,0:T(8,128)(2,1)}, u32[]{:S(2)}, u32[]{:S(2)}) collective-permute-start(bf16[192,128]{1,0:T(8,128)(2,1)} %get-tuple-element.66), channel_id=1, source_target_pairs={{0,12},{4,0},{8,4},{12,8},{1,13},{5,1},{9,5},{13,9},{2,14},{6,2},{... | collective-permute-start | bytes 147464 | tf_op jit(solution)/shard_map/ppermute | solution.py:355
  32.4 1.1 copy.16.refs_12_
  33.6 0.9 collective-permute-done.6.refs_1_
  34.4 1.4 collective-permute-done.7.refs_2_
  35.9 1.0 copy-done.9
  36.9 1.0 copy-done.15
  37.8 0.9 copy-done.25
  38.7 0.8 copy-done.31
  39.5 0.8 copy-done.33
  40.3 0.8 copy-done.35
  41.1 14.8 %shard_map.149 = (bf16[192,128]{1,0:T(8,128)(2,1)S(1)}, bf16[192,128]{1,0:T(8,128)(2,1)S(1)}, bf16[192,128]{1,0:T(8,128)(2,1)S(1)}, bf16[192,128]{1,0:T(8,128)(2,1)S(1)}, bf16[3456,128]{1,0:T(8,128)(2,1)S(1)}) custom-call(bf16[192,128]{1,0:T(8,128)(2,1)S(1)} %copy-done.35, bf16[192,128]{1,0:T(8,128)(2,1)} %collective-permute-done.6.refs_1_, ...), custom_call_target="tpu_custom_call" | custom-call | tf_op jit(solution)/shard_map/pallas_call | solution.py:342
  56.0 0.9 copy-done.6
  56.9 2.8 %collective-permute-start.12 = (bf16[192,128]{1,0:T(8,128)(2,1)S(1)}, bf16[192,128]{1,0:T(8,128)(2,1)S(1)}, u32[]{:S(2)}, u32[]{:S(2)}) collective-permute-start(bf16[192,128]{1,0:T(8,128)(2,1)S(1)} %get-tuple-element.75), channel_id=1, source_target_pairs={{0,12},{4,0},{8,4},{12,8},{1,13},{5,1},{9,5},{13,9},{2,14},{6,2},{... | collective-permute-start | bytes 147464 | tf_op jit(solution)/shard_map/ppermute | solution.py:355
  60.2 1.2 collective-permute-done.12.refs_1_
  61.4 3.2 %collective-permute-done.13.refs_2_ = bf16[192,128]{1,0:T(8,128)(2,1)S(1)} collective-permute-done((bf16[192,128]{1,0:T(8,128)(2,1)S(1)}, bf16[192,128]{1,0:T(8,128)(2,1)S(1)}, u32[]{:S(2)}, u32[]{:S(2)}) %collective-permute-start.13) | collective-permute-done | bytes 49184 | tf_op jit(solution)/shard_map/ppermute | solution.py:355
  64.6 1.1 collective-permute-done.14.refs_3_
  66.2 1.6 %collective-permute-start.16 = (bf16[192,128]{1,0:T(8,128)(2,1)S(1)}, bf16[192,128]{1,0:T(8,128)(2,1)S(1)}, u32[]{:S(2)}, u32[]{:S(2)}) collective-permute-start(bf16[192,128]{1,0:T(8,128)(2,1)S(1)} %get-tuple-element.80), channel_id=1, source_target_pairs={{0,2},{1,3},{2,0},{3,1},{4,6},{5,7},{6,4},{7,5},{8,10},{9,11},{10,... | collective-permute-start | bytes 147464 | tf_op jit(solution)/shard_map/ppermute | solution.py:355
  67.8 1.4 collective-permute-start.17
  71.6 0.9 copy-done.17
  72.5 0.9 copy-done.19
  73.5 0.9 copy-done.21
  75.2 0.8 copy-done.29
  76.0 5.8 %shard_map.151 = (bf16[192,128]{1,0:T(8,128)(2,1)S(1)}, bf16[192,128]{1,0:T(8,128)(2,1)S(1)}, bf16[192,128]{1,0:T(8,128)(2,1)S(1)}, bf16[192,128]{1,0:T(8,128)(2,1)S(1)}, bf16[1152,128]{1,0:T(8,128)(2,1)}) custom-call(bf16[192,128]{1,0:T(8,128)(2,1)S(1)} %get-tuple-element.78.refs_0_, bf16[192,128]{1,0:T(8,128)(2,1)S(1)} %collective-permute-done.15.refs_1_, ...), custom_call_target="tpu_custom_call" | custom-call | tf_op jit(solution)/shard_map/pallas_call | solution.py:342
  83.7 1.0 dynamic-slice_bitcast_fusion.5
  84.7 1.7 %collective-permute-start.23 = (bf16[288,128]{1,0:T(8,128)(2,1)S(1)}, bf16[288,128]{1,0:T(8,128)(2,1)S(1)}, u32[]{:S(2)}, u32[]{:S(2)}) collective-permute-start(bf16[288,128]{1,0:T(8,128)(2,1)S(1)} %get-tuple-element.118), channel_id=1, source_target_pairs={{0,3},{1,0},{2,1},{3,2},{4,7},{5,4},{6,5},{7,6},{8,11},{9,8},{10,9... | collective-permute-start | bytes 221192 | tf_op jit(solution)/shard_map/ppermute | solution.py:355
  86.9 1.9 %collective-permute-done.23 = bf16[288,128]{1,0:T(8,128)(2,1)S(1)} collective-permute-done((bf16[288,128]{1,0:T(8,128)(2,1)S(1)}, bf16[288,128]{1,0:T(8,128)(2,1)S(1)}, u32[]{:S(2)}, u32[]{:S(2)}) %collective-permute-start.23) | collective-permute-done | bytes 73760 | tf_op jit(solution)/shard_map/ppermute | solution.py:355
  88.8 2.7 %collective-permute-done.22 = bf16[288,128]{1,0:T(8,128)(2,1)S(1)} collective-permute-done((bf16[288,128]{1,0:T(8,128)(2,1)S(1)}, bf16[288,128]{1,0:T(8,128)(2,1)S(1)}, u32[]{:S(2)}, u32[]{:S(2)}) %collective-permute-start.22) | collective-permute-done | bytes 73760 | tf_op jit(solution)/shard_map/ppermute | solution.py:355
  91.5 0.9 fusion.5
  93.5 1.9 %collective-permute-start.24 = (bf16[72,128]{1,0:T(8,128)(2,1)S(1)}, bf16[72,128]{1,0:T(8,128)(2,1)S(1)}, u32[]{:S(2)}, u32[]{:S(2)}) collective-permute-start(bf16[72,128]{1,0:T(8,128)(2,1)S(1)} %get-tuple-element.123), channel_id=1, source_target_pairs={{0,4},{4,8},{8,12},{12,0},{1,5},{5,9},{9,13},{13,1},{2,6},{6,10},{... | collective-permute-start | bytes 55304 | tf_op jit(solution)/shard_map/ppermute | solution.py:355
  95.5 1.4 collective-permute-start.19
  97.6 1.5 %collective-permute-done.24 = bf16[72,128]{1,0:T(8,128)(2,1)S(1)} collective-permute-done((bf16[72,128]{1,0:T(8,128)(2,1)S(1)}, bf16[72,128]{1,0:T(8,128)(2,1)S(1)}, u32[]{:S(2)}, u32[]{:S(2)}) %collective-permute-start.24) | collective-permute-done | bytes 18464 | tf_op jit(solution)/shard_map/ppermute | solution.py:355
  99.1 1.7 %collective-permute-start.27 = (bf16[72,128]{1,0:T(8,128)(2,1)S(1)}, bf16[72,128]{1,0:T(8,128)(2,1)S(1)}, u32[]{:S(2)}, u32[]{:S(2)}) collective-permute-start(bf16[72,128]{1,0:T(8,128)(2,1)S(1)} %get-tuple-element.113), channel_id=1, source_target_pairs={{0,12},{4,0},{8,4},{12,8},{1,13},{5,1},{9,5},{13,9},{2,14},{6,2},{... | collective-permute-start | bytes 55304 | tf_op jit(solution)/shard_map/ppermute | solution.py:355
  100.9 1.4 %collective-permute-start.34 = (bf16[864,128]{1,0:T(8,128)(2,1)S(1)}, bf16[864,128]{1,0:T(8,128)(2,1)S(1)}, u32[]{:S(2)}, u32[]{:S(2)}) collective-permute-start(bf16[864,128]{1,0:T(8,128)(2,1)S(1)} %get-tuple-element.116), channel_id=1, source_target_pairs={{0,2},{1,3},{2,0},{3,1},{4,6},{5,7},{6,4},{7,5},{8,10},{9,11},{10,... | collective-permute-start | bytes 663560 | tf_op jit(solution)/shard_map/ppermute | solution.py:355
  102.5 1.1 shard_map.152
  104.5 3.8 %collective-permute-done.28 = bf16[72,128]{1,0:T(8,128)(2,1)S(1)} collective-permute-done((bf16[72,128]{1,0:T(8,128)(2,1)S(1)}, bf16[72,128]{1,0:T(8,128)(2,1)S(1)}, u32[]{:S(2)}, u32[]{:S(2)}) %collective-permute-start.28) | collective-permute-done | bytes 18464 | tf_op jit(solution)/shard_map/ppermute | solution.py:355
  108.3 1.0 collective-permute-done.29
  109.4 3.6 %collective-permute-done.34 = bf16[864,128]{1,0:T(8,128)(2,1)S(1)} collective-permute-done((bf16[864,128]{1,0:T(8,128)(2,1)S(1)}, bf16[864,128]{1,0:T(8,128)(2,1)S(1)}, u32[]{:S(2)}, u32[]{:S(2)}) %collective-permute-start.34) | collective-permute-done | bytes 221216 | tf_op jit(solution)/shard_map/ppermute | solution.py:355
  113.8 1.5 %collective-permute-start.37 = (bf16[216,128]{1,0:T(8,128)(2,1)S(1)}, bf16[216,128]{1,0:T(8,128)(2,1)S(1)}, u32[]{:S(2)}, u32[]{:S(2)}) collective-permute-start(bf16[216,128]{1,0:T(8,128)(2,1)S(1)} %get-tuple-element.122), channel_id=1, source_target_pairs={{0,8},{4,12},{8,0},{12,4},{1,9},{5,13},{9,1},{13,5},{2,10},{6,14},... | collective-permute-start | bytes 165896 | tf_op jit(solution)/shard_map/ppermute | solution.py:355
  116.3 1.4 %collective-permute-done.38 = bf16[216,128]{1,0:T(8,128)(2,1)S(1)} collective-permute-done((bf16[216,128]{1,0:T(8,128)(2,1)S(1)}, bf16[216,128]{1,0:T(8,128)(2,1)S(1)}, u32[]{:S(2)}, u32[]{:S(2)}) %collective-permute-start.38) | collective-permute-done | bytes 55328 | tf_op jit(solution)/shard_map/ppermute | solution.py:355
  117.7 1.3 collective-permute-done.37
  119.1 2.2 %collective-permute-done.36 = bf16[216,128]{1,0:T(8,128)(2,1)S(1)} collective-permute-done((bf16[216,128]{1,0:T(8,128)(2,1)S(1)}, bf16[216,128]{1,0:T(8,128)(2,1)S(1)}, u32[]{:S(2)}, u32[]{:S(2)}) %collective-permute-start.36) | collective-permute-done | bytes 55328 | tf_op jit(solution)/shard_map/ppermute | solution.py:355
  122.1 1.3 collective-permute-start.41
  123.6 3.0 %collective-permute-done.39 = bf16[216,128]{1,0:T(8,128)(2,1)S(1)} collective-permute-done((bf16[216,128]{1,0:T(8,128)(2,1)S(1)}, bf16[216,128]{1,0:T(8,128)(2,1)S(1)}, u32[]{:S(2)}, u32[]{:S(2)}) %collective-permute-start.39) | collective-permute-done | bytes 55328 | tf_op jit(solution)/shard_map/ppermute | solution.py:355
  127.1 1.4 collective-permute-done.41
  129.4 0.9 shard_map.153
  130.5 3.9 %collective-permute-done.42 = bf16[864,128]{1,0:T(8,128)(2,1)S(1)} collective-permute-done((bf16[864,128]{1,0:T(8,128)(2,1)S(1)}, bf16[864,128]{1,0:T(8,128)(2,1)S(1)}, u32[]{:S(2)}, u32[]{:S(2)}) %collective-permute-start.42) | collective-permute-done | bytes 221216 | tf_op jit(solution)/shard_map/ppermute | solution.py:355
  134.3 5.1 %collective-permute-done.43 = bf16[864,128]{1,0:T(8,128)(2,1)S(1)} collective-permute-done((bf16[864,128]{1,0:T(8,128)(2,1)S(1)}, bf16[864,128]{1,0:T(8,128)(2,1)S(1)}, u32[]{:S(2)}, u32[]{:S(2)}) %collective-permute-start.43) | collective-permute-done | bytes 221216 | tf_op jit(solution)/shard_map/ppermute | solution.py:355
  139.4 0.9 collective-permute-done.44
  140.6 1.1 shard_map.154
  141.7 1.1 copy.17
  (155 shorter events, 21.1 us)
Async XLA Ops:
  0.6 35.2 %copy-start.11 = (bf16[192,192]{1,0:T(8,128)(2,1)S(1)}, bf16[192,192]{1,0:T(8,128)(2,1)}, u32[]{:S(2)}) copy-start(bf16[192,192]{1,0:T(8,128)(2,1)} %refs_10_.1) | copy-start | bytes 221188
  0.6 1.0 copy-start.22
  1.6 34.2 %copy-start.36 = (s32[32]{0:T(128)S(1)}, s32[32]{0:T(128)}, u32[]{:S(2)}) copy-start(s32[32]{0:T(128)} %param.17) | copy-start | bytes 388
  2.1 10.2 %collective-permute-start = (bf16[192,128]{1,0:T(8,128)(2,1)S(1)}, bf16[192,128]{1,0:T(8,128)(2,1)S(1)}, u32[]{:S(2)}, u32[]{:S(2)}) collective-permute-start(bf16[192,128]{1,0:T(8,128)(2,1)S(1)} %get-tuple-element.54), channel_id=1, source_target_pairs={{0,1},{1,2},{2,3},{3,0},{4,5},{5,6},{6,7},{7,4},{8,9},{9,10},{10,1... | collective-permute-start | bytes 147464 | tf_op jit(solution)/shard_map/ppermute | solution.py:355
  2.6 9.7 %collective-permute-start.1 = (bf16[192,128]{1,0:T(8,128)(2,1)S(1)}, bf16[192,128]{1,0:T(8,128)(2,1)S(1)}, u32[]{:S(2)}, u32[]{:S(2)}) collective-permute-start(bf16[192,128]{1,0:T(8,128)(2,1)S(1)} %get-tuple-element.55), channel_id=1, source_target_pairs={{0,2},{1,3},{2,0},{3,1},{4,6},{5,7},{6,4},{7,5},{8,10},{9,11},{10,... | collective-permute-start | bytes 147464 | tf_op jit(solution)/shard_map/ppermute | solution.py:355
  5.2 7.1 %collective-permute-start.2 = (bf16[192,128]{1,0:T(8,128)(2,1)S(1)}, bf16[192,128]{1,0:T(8,128)(2,1)S(1)}, u32[]{:S(2)}, u32[]{:S(2)}) collective-permute-start(bf16[192,128]{1,0:T(8,128)(2,1)S(1)} %get-tuple-element.56), channel_id=1, source_target_pairs={{0,3},{1,0},{2,1},{3,2},{4,7},{5,4},{6,5},{7,6},{8,11},{9,8},{10,9... | collective-permute-start | bytes 147464 | tf_op jit(solution)/shard_map/ppermute | solution.py:355
  6.6 1.0 copy-start
  7.6 0.9 copy-start.2
  8.5 0.9 copy-start.4
  11.2 8.2 %copy-start.23 = (bf16[8,12288]{1,0:T(8,128)(2,1)S(1)}, bf16[8,12288]{1,0:T(8,128)(2,1)}, u32[]{:S(2)}) copy-start(bf16[8,12288]{1,0:T(8,128)(2,1)} %table_ref.3) | copy-start | bytes 589828
  11.2 24.6 %copy-start.1 = (bf16[192,768]{1,0:T(8,128)(2,1)S(1)}, bf16[192,768]{1,0:T(8,128)(2,1)}, u32[]{:S(2)}) copy-start(bf16[192,768]{1,0:T(8,128)(2,1)} %refs_11_.1) | copy-start | bytes 884740
  11.2 24.6 %copy-start.3 = (bf16[192,576]{1,0:T(8,128)(2,1)S(1)}, bf16[192,576]{1,0:T(8,128)(2,1)}, u32[]{:S(2)}) copy-start(bf16[192,576]{1,0:T(8,128)(2,1)} %refs_9_.1) | copy-start | bytes 663556
  12.3 17.4 %copy-start.8 = (bf16[768,192]{1,0:T(8,128)(2,1)}, bf16[768,192]{1,0:T(8,128)(2,1)S(1)}, u32[]{:S(2)}) copy-start(bf16[768,192]{1,0:T(8,128)(2,1)S(1)} %get-tuple-element.73.refs_15_) | copy-start | bytes 884740
  12.3 17.4 %copy-start.14 = (bf16[576,192]{1,0:T(8,128)(2,1)}, bf16[576,192]{1,0:T(8,128)(2,1)S(1)}, u32[]{:S(2)}) copy-start(bf16[576,192]{1,0:T(8,128)(2,1)S(1)} %get-tuple-element.71.refs_13_) | copy-start | bytes 663556
  18.7 11.0 %copy-start.16 = (bf16[192,512]{1,0:T(8,128)(2,1)}, bf16[192,512]{1,0:T(8,128)(2,1)S(1)}, u32[]{:S(2)}) copy-start(bf16[192,512]{1,0:T(8,128)(2,1)S(1)} %get-tuple-element.82.refs_6_) | copy-start | bytes 589828
  18.7 6.1 %collective-permute-start.3 = (bf16[192,128]{1,0:T(8,128)(2,1)S(1)}, bf16[192,128]{1,0:T(8,128)(2,1)S(1)}, u32[]{:S(2)}, u32[]{:S(2)}) collective-permute-start(bf16[192,128]{1,0:T(8,128)(2,1)S(1)} %get-tuple-element.60), channel_id=1, source_target_pairs={{0,3},{1,0},{2,1},{3,2},{4,7},{5,4},{6,5},{7,6},{8,11},{9,8},{10,9... | collective-permute-start | bytes 147464 | tf_op jit(solution)/shard_map/ppermute | solution.py:355
  18.7 7.5 %collective-permute-start.4 = (bf16[192,128]{1,0:T(8,128)(2,1)S(1)}, bf16[192,128]{1,0:T(8,128)(2,1)S(1)}, u32[]{:S(2)}, u32[]{:S(2)}) collective-permute-start(bf16[192,128]{1,0:T(8,128)(2,1)S(1)} %get-tuple-element.61), channel_id=1, source_target_pairs={{0,2},{1,3},{2,0},{3,1},{4,6},{5,7},{6,4},{7,5},{8,10},{9,11},{10,... | collective-permute-start | bytes 147464 | tf_op jit(solution)/shard_map/ppermute | solution.py:355
  19.4 6.7 %collective-permute-start.5 = (bf16[192,128]{1,0:T(8,128)(2,1)S(1)}, bf16[192,128]{1,0:T(8,128)(2,1)S(1)}, u32[]{:S(2)}, u32[]{:S(2)}) collective-permute-start(bf16[192,128]{1,0:T(8,128)(2,1)S(1)} %get-tuple-element.62), channel_id=1, source_target_pairs={{0,1},{1,2},{2,3},{3,0},{4,5},{5,6},{6,7},{7,4},{8,9},{9,10},{10,1... | collective-permute-start | bytes 147464 | tf_op jit(solution)/shard_map/ppermute | solution.py:355
  20.6 9.1 %copy-start.30 = (bf16[192,128]{1,0:T(8,128)(2,1)}, bf16[192,128]{1,0:T(8,128)(2,1)S(1)}, u32[]{:S(2)}) copy-start(bf16[192,128]{1,0:T(8,128)(2,1)S(1)} %get-tuple-element.67.refs_4_) | copy-start | bytes 147460
  20.6 8.5 %collective-permute-start.9 = (bf16[192,128]{1,0:T(8,128)(2,1)S(1)}, bf16[192,128]{1,0:T(8,128)(2,1)S(1)}, u32[]{:S(2)}, u32[]{:S(2)}) collective-permute-start(bf16[192,128]{1,0:T(8,128)(2,1)S(1)} %get-tuple-element.68), channel_id=1, source_target_pairs={{0,4},{4,8},{8,12},{12,0},{1,5},{5,9},{9,13},{13,1},{2,6},{6,10},{... | collective-permute-start | bytes 147464 | tf_op jit(solution)/shard_map/ppermute | solution.py:355
  22.2 11.3 %collective-permute-start.10 = (bf16[192,128]{1,0:T(8,128)(2,1)}, bf16[192,128]{1,0:T(8,128)(2,1)}, u32[]{:S(2)}, u32[]{:S(2)}) collective-permute-start(bf16[192,128]{1,0:T(8,128)(2,1)} %get-tuple-element.69), channel_id=1, source_target_pairs={{0,8},{4,12},{8,0},{12,4},{1,9},{5,13},{9,1},{13,5},{2,10},{6,14},... | collective-permute-start | bytes 147464 | tf_op jit(solution)/shard_map/ppermute | solution.py:355
  24.8 8.8 %collective-permute-start.11 = (bf16[192,128]{1,0:T(8,128)(2,1)}, bf16[192,128]{1,0:T(8,128)(2,1)}, u32[]{:S(2)}, u32[]{:S(2)}) collective-permute-start(bf16[192,128]{1,0:T(8,128)(2,1)} %get-tuple-element.70), channel_id=1, source_target_pairs={{0,12},{4,0},{8,4},{12,8},{1,13},{5,1},{9,5},{13,9},{2,14},{6,2},{... | collective-permute-start | bytes 147464 | tf_op jit(solution)/shard_map/ppermute | solution.py:355
  27.7 6.7 %collective-permute-start.6 = (bf16[192,128]{1,0:T(8,128)(2,1)}, bf16[192,128]{1,0:T(8,128)(2,1)}, u32[]{:S(2)}, u32[]{:S(2)}) collective-permute-start(bf16[192,128]{1,0:T(8,128)(2,1)} %get-tuple-element.64), channel_id=1, source_target_pairs={{0,4},{4,8},{8,12},{12,0},{1,5},{5,9},{9,13},{13,1},{2,6},{6,10},{... | collective-permute-start | bytes 147464 | tf_op jit(solution)/shard_map/ppermute | solution.py:355
  28.4 7.5 %collective-permute-start.7 = (bf16[192,128]{1,0:T(8,128)(2,1)}, bf16[192,128]{1,0:T(8,128)(2,1)}, u32[]{:S(2)}, u32[]{:S(2)}) collective-permute-start(bf16[192,128]{1,0:T(8,128)(2,1)} %get-tuple-element.65), channel_id=1, source_target_pairs={{0,8},{4,12},{8,0},{12,4},{1,9},{5,13},{9,1},{13,5},{2,10},{6,14},... | collective-permute-start | bytes 147464 | tf_op jit(solution)/shard_map/ppermute | solution.py:355
  29.7 41.9 %copy-start.5 = (bf16[192,576]{1,0:T(8,128)(2,1)S(1)}, bf16[192,576]{1,0:T(8,128)(2,1)}, u32[]{:S(2)}) copy-start(bf16[192,576]{1,0:T(8,128)(2,1)} %refs_4_.3) | copy-start | bytes 663556
  29.7 41.9 %copy-start.13 = (bf16[192,192]{1,0:T(8,128)(2,1)S(1)}, bf16[192,192]{1,0:T(8,128)(2,1)}, u32[]{:S(2)}) copy-start(bf16[192,192]{1,0:T(8,128)(2,1)} %refs_5_.1) | copy-start | bytes 221188
  29.7 6.1 %collective-permute-start.8 = (bf16[192,128]{1,0:T(8,128)(2,1)}, bf16[192,128]{1,0:T(8,128)(2,1)}, u32[]{:S(2)}, u32[]{:S(2)}) collective-permute-start(bf16[192,128]{1,0:T(8,128)(2,1)} %get-tuple-element.66), channel_id=1, source_target_pairs={{0,12},{4,0},{8,4},{12,8},{1,13},{5,1},{9,5},{13,9},{2,14},{6,2},{... | collective-permute-start | bytes 147464 | tf_op jit(solution)/shard_map/ppermute | solution.py:355
  35.9 1.0 copy-start.9
  36.9 1.0 copy-start.15
  56.9 4.5 %collective-permute-start.12 = (bf16[192,128]{1,0:T(8,128)(2,1)S(1)}, bf16[192,128]{1,0:T(8,128)(2,1)S(1)}, u32[]{:S(2)}, u32[]{:S(2)}) collective-permute-start(bf16[192,128]{1,0:T(8,128)(2,1)S(1)} %get-tuple-element.75), channel_id=1, source_target_pairs={{0,12},{4,0},{8,4},{12,8},{1,13},{5,1},{9,5},{13,9},{2,14},{6,2},{... | collective-permute-start | bytes 147464 | tf_op jit(solution)/shard_map/ppermute | solution.py:355
  59.6 5.0 %collective-permute-start.13 = (bf16[192,128]{1,0:T(8,128)(2,1)S(1)}, bf16[192,128]{1,0:T(8,128)(2,1)S(1)}, u32[]{:S(2)}, u32[]{:S(2)}) collective-permute-start(bf16[192,128]{1,0:T(8,128)(2,1)S(1)} %get-tuple-element.76), channel_id=1, source_target_pairs={{0,8},{4,12},{8,0},{12,4},{1,9},{5,13},{9,1},{13,5},{2,10},{6,14},... | collective-permute-start | bytes 147464 | tf_op jit(solution)/shard_map/ppermute | solution.py:355
  59.9 5.9 %collective-permute-start.14 = (bf16[192,128]{1,0:T(8,128)(2,1)S(1)}, bf16[192,128]{1,0:T(8,128)(2,1)S(1)}, u32[]{:S(2)}, u32[]{:S(2)}) collective-permute-start(bf16[192,128]{1,0:T(8,128)(2,1)S(1)} %get-tuple-element.77), channel_id=1, source_target_pairs={{0,4},{4,8},{8,12},{12,0},{1,5},{5,9},{9,13},{13,1},{2,6},{6,10},{... | collective-permute-start | bytes 147464 | tf_op jit(solution)/shard_map/ppermute | solution.py:355
  66.1 3.6 %collective-permute-start.15 = (bf16[192,128]{1,0:T(8,128)(2,1)S(1)}, bf16[192,128]{1,0:T(8,128)(2,1)S(1)}, u32[]{:S(2)}, u32[]{:S(2)}) collective-permute-start(bf16[192,128]{1,0:T(8,128)(2,1)S(1)} %get-tuple-element.79), channel_id=1, source_target_pairs={{0,1},{1,2},{2,3},{3,0},{4,5},{5,6},{6,7},{7,4},{8,9},{9,10},{10,1... | collective-permute-start | bytes 147464 | tf_op jit(solution)/shard_map/ppermute | solution.py:355
  66.2 4.2 %collective-permute-start.16 = (bf16[192,128]{1,0:T(8,128)(2,1)S(1)}, bf16[192,128]{1,0:T(8,128)(2,1)S(1)}, u32[]{:S(2)}, u32[]{:S(2)}) collective-permute-start(bf16[192,128]{1,0:T(8,128)(2,1)S(1)} %get-tuple-element.80), channel_id=1, source_target_pairs={{0,2},{1,3},{2,0},{3,1},{4,6},{5,7},{6,4},{7,5},{8,10},{9,11},{10,... | collective-permute-start | bytes 147464 | tf_op jit(solution)/shard_map/ppermute | solution.py:355
  67.8 3.2 %collective-permute-start.17 = (bf16[192,128]{1,0:T(8,128)(2,1)S(1)}, bf16[192,128]{1,0:T(8,128)(2,1)S(1)}, u32[]{:S(2)}, u32[]{:S(2)}) collective-permute-start(bf16[192,128]{1,0:T(8,128)(2,1)S(1)} %get-tuple-element.81), channel_id=1, source_target_pairs={{0,3},{1,0},{2,1},{3,2},{4,7},{5,4},{6,5},{7,6},{8,11},{9,8},{10,9... | collective-permute-start | bytes 147464 | tf_op jit(solution)/shard_map/ppermute | solution.py:355
  71.6 0.9 copy-start.17
  76.0 24.7 %copy-start.7 = (bf16[3456,128]{1,0:T(8,128)(2,1)S(1)}, bf16[3456,128]{1,0:T(8,128)(2,1)}, u32[]{:S(2)}) copy-start(bf16[3456,128]{1,0:T(8,128)(2,1)} %copy-done.6) | copy-start | bytes 2654212
  84.7 4.2 %collective-permute-start.23 = (bf16[288,128]{1,0:T(8,128)(2,1)S(1)}, bf16[288,128]{1,0:T(8,128)(2,1)S(1)}, u32[]{:S(2)}, u32[]{:S(2)}) collective-permute-start(bf16[288,128]{1,0:T(8,128)(2,1)S(1)} %get-tuple-element.118), channel_id=1, source_target_pairs={{0,3},{1,0},{2,1},{3,2},{4,7},{5,4},{6,5},{7,6},{8,11},{9,8},{10,9... | collective-permute-start | bytes 221192 | tf_op jit(solution)/shard_map/ppermute | solution.py:355
  86.4 5.1 %collective-permute-start.22 = (bf16[288,128]{1,0:T(8,128)(2,1)S(1)}, bf16[288,128]{1,0:T(8,128)(2,1)S(1)}, u32[]{:S(2)}, u32[]{:S(2)}) collective-permute-start(bf16[288,128]{1,0:T(8,128)(2,1)S(1)} %get-tuple-element.119), channel_id=1, source_target_pairs={{0,2},{1,3},{2,0},{3,1},{4,6},{5,7},{6,4},{7,5},{8,10},{9,11},{10,... | collective-permute-start | bytes 221192 | tf_op jit(solution)/shard_map/ppermute | solution.py:355
  86.9 4.6 %collective-permute-start.21 = (bf16[288,128]{1,0:T(8,128)(2,1)S(1)}, bf16[288,128]{1,0:T(8,128)(2,1)S(1)}, u32[]{:S(2)}, u32[]{:S(2)}) collective-permute-start(bf16[288,128]{1,0:T(8,128)(2,1)S(1)} %get-tuple-element.117), channel_id=1, source_target_pairs={{0,1},{1,2},{2,3},{3,0},{4,5},{5,6},{6,7},{7,4},{8,9},{9,10},{10,1... | collective-permute-start | bytes 221192 | tf_op jit(solution)/shard_map/ppermute | solution.py:355
  92.5 4.4 %collective-permute-start.26 = (bf16[72,128]{1,0:T(8,128)(2,1)S(1)}, bf16[72,128]{1,0:T(8,128)(2,1)S(1)}, u32[]{:S(2)}, u32[]{:S(2)}) collective-permute-start(bf16[72,128]{1,0:T(8,128)(2,1)S(1)} %get-tuple-element.124), channel_id=1, source_target_pairs={{0,12},{4,0},{8,4},{12,8},{1,13},{5,1},{9,5},{13,9},{2,14},{6,2},{... | collective-permute-start | bytes 55304 | tf_op jit(solution)/shard_map/ppermute | solution.py:355
  92.9 4.7 %collective-permute-start.25 = (bf16[72,128]{1,0:T(8,128)(2,1)S(1)}, bf16[72,128]{1,0:T(8,128)(2,1)S(1)}, u32[]{:S(2)}, u32[]{:S(2)}) collective-permute-start(bf16[72,128]{1,0:T(8,128)(2,1)S(1)} %get-tuple-element.125), channel_id=1, source_target_pairs={{0,8},{4,12},{8,0},{12,4},{1,9},{5,13},{9,1},{13,5},{2,10},{6,14},... | collective-permute-start | bytes 55304 | tf_op jit(solution)/shard_map/ppermute | solution.py:355
  93.5 5.6 %collective-permute-start.24 = (bf16[72,128]{1,0:T(8,128)(2,1)S(1)}, bf16[72,128]{1,0:T(8,128)(2,1)S(1)}, u32[]{:S(2)}, u32[]{:S(2)}) collective-permute-start(bf16[72,128]{1,0:T(8,128)(2,1)S(1)} %get-tuple-element.123), channel_id=1, source_target_pairs={{0,4},{4,8},{8,12},{12,0},{1,5},{5,9},{9,13},{13,1},{2,6},{6,10},{... | collective-permute-start | bytes 55304 | tf_op jit(solution)/shard_map/ppermute | solution.py:355
  95.5 5.4 %collective-permute-start.18 = (bf16[192,128]{1,0:T(8,128)(2,1)}, bf16[192,128]{1,0:T(8,128)(2,1)S(1)}, u32[]{:S(2)}, u32[]{:S(2)}) collective-permute-start(bf16[192,128]{1,0:T(8,128)(2,1)} %copy-done.39), channel_id=1, source_target_pairs={{0,3},{1,0},{2,1},{3,2},{4,7},{5,4},{6,5},{7,6},{8,11},{9,8},{10,9... | collective-permute-start | bytes 147464 | tf_op jit(solution)/shard_map/ppermute | solution.py:355
  95.5 6.9 %collective-permute-start.19 = (bf16[192,128]{1,0:T(8,128)(2,1)}, bf16[192,128]{1,0:T(8,128)(2,1)S(1)}, u32[]{:S(2)}, u32[]{:S(2)}) collective-permute-start(bf16[192,128]{1,0:T(8,128)(2,1)} %copy-done.38), channel_id=1, source_target_pairs={{0,2},{1,3},{2,0},{3,1},{4,6},{5,7},{6,4},{7,5},{8,10},{9,11},{10,... | collective-permute-start | bytes 147464 | tf_op jit(solution)/shard_map/ppermute | solution.py:355
  96.8 5.6 %collective-permute-start.20 = (bf16[192,128]{1,0:T(8,128)(2,1)}, bf16[192,128]{1,0:T(8,128)(2,1)S(1)}, u32[]{:S(2)}, u32[]{:S(2)}) collective-permute-start(bf16[192,128]{1,0:T(8,128)(2,1)} %copy-done.37), channel_id=1, source_target_pairs={{0,1},{1,2},{2,3},{3,0},{4,5},{5,6},{6,7},{7,4},{8,9},{9,10},{10,1... | collective-permute-start | bytes 147464 | tf_op jit(solution)/shard_map/ppermute | solution.py:355
  99.1 4.7 %collective-permute-start.27 = (bf16[72,128]{1,0:T(8,128)(2,1)S(1)}, bf16[72,128]{1,0:T(8,128)(2,1)S(1)}, u32[]{:S(2)}, u32[]{:S(2)}) collective-permute-start(bf16[72,128]{1,0:T(8,128)(2,1)S(1)} %get-tuple-element.113), channel_id=1, source_target_pairs={{0,12},{4,0},{8,4},{12,8},{1,13},{5,1},{9,5},{13,9},{2,14},{6,2},{... | collective-permute-start | bytes 55304 | tf_op jit(solution)/shard_map/ppermute | solution.py:355
  100.8 8.6 %collective-permute-start.35 = (bf16[864,128]{1,0:T(8,128)(2,1)S(1)}, bf16[864,128]{1,0:T(8,128)(2,1)S(1)}, u32[]{:S(2)}, u32[]{:S(2)}) collective-permute-start(bf16[864,128]{1,0:T(8,128)(2,1)S(1)} %get-tuple-element.115), channel_id=1, source_target_pairs={{0,3},{1,0},{2,1},{3,2},{4,7},{5,4},{6,5},{7,6},{8,11},{9,8},{10,9... | collective-permute-start | bytes 663560 | tf_op jit(solution)/shard_map/ppermute | solution.py:355
  100.9 12.2 %collective-permute-start.34 = (bf16[864,128]{1,0:T(8,128)(2,1)S(1)}, bf16[864,128]{1,0:T(8,128)(2,1)S(1)}, u32[]{:S(2)}, u32[]{:S(2)}) collective-permute-start(bf16[864,128]{1,0:T(8,128)(2,1)S(1)} %get-tuple-element.116), channel_id=1, source_target_pairs={{0,2},{1,3},{2,0},{3,1},{4,6},{5,7},{6,4},{7,5},{8,10},{9,11},{10,... | collective-permute-start | bytes 663560 | tf_op jit(solution)/shard_map/ppermute | solution.py:355
  102.3 10.9 %collective-permute-start.33 = (bf16[864,128]{1,0:T(8,128)(2,1)S(1)}, bf16[864,128]{1,0:T(8,128)(2,1)S(1)}, u32[]{:S(2)}, u32[]{:S(2)}) collective-permute-start(bf16[864,128]{1,0:T(8,128)(2,1)S(1)} %get-tuple-element.114), channel_id=1, source_target_pairs={{0,1},{1,2},{2,3},{3,0},{4,5},{5,6},{6,7},{7,4},{8,9},{9,10},{10,1... | collective-permute-start | bytes 663560 | tf_op jit(solution)/shard_map/ppermute | solution.py:355
  103.6 4.7 %collective-permute-start.28 = (bf16[72,128]{1,0:T(8,128)(2,1)S(1)}, bf16[72,128]{1,0:T(8,128)(2,1)S(1)}, u32[]{:S(2)}, u32[]{:S(2)}) collective-permute-start(bf16[72,128]{1,0:T(8,128)(2,1)S(1)} %get-tuple-element.113), channel_id=1, source_target_pairs={{0,8},{4,12},{8,0},{12,4},{1,9},{5,13},{9,1},{13,5},{2,10},{6,14},... | collective-permute-start | bytes 55304 | tf_op jit(solution)/shard_map/ppermute | solution.py:355
  103.8 5.6 %collective-permute-start.29 = (bf16[72,128]{1,0:T(8,128)(2,1)S(1)}, bf16[72,128]{1,0:T(8,128)(2,1)S(1)}, u32[]{:S(2)}, u32[]{:S(2)}) collective-permute-start(bf16[72,128]{1,0:T(8,128)(2,1)S(1)} %get-tuple-element.113), channel_id=1, source_target_pairs={{0,4},{4,8},{8,12},{12,0},{1,5},{5,9},{9,13},{13,1},{2,6},{6,10},{... | collective-permute-start | bytes 55304 | tf_op jit(solution)/shard_map/ppermute | solution.py:355
  113.4 4.3 %collective-permute-start.38 = (bf16[216,128]{1,0:T(8,128)(2,1)S(1)}, bf16[216,128]{1,0:T(8,128)(2,1)S(1)}, u32[]{:S(2)}, u32[]{:S(2)}) collective-permute-start(bf16[216,128]{1,0:T(8,128)(2,1)S(1)} %get-tuple-element.121), channel_id=1, source_target_pairs={{0,12},{4,0},{8,4},{12,8},{1,13},{5,1},{9,5},{13,9},{2,14},{6,2},{... | collective-permute-start | bytes 165896 | tf_op jit(solution)/shard_map/ppermute | solution.py:355
  113.8 5.2 %collective-permute-start.37 = (bf16[216,128]{1,0:T(8,128)(2,1)S(1)}, bf16[216,128]{1,0:T(8,128)(2,1)S(1)}, u32[]{:S(2)}, u32[]{:S(2)}) collective-permute-start(bf16[216,128]{1,0:T(8,128)(2,1)S(1)} %get-tuple-element.122), channel_id=1, source_target_pairs={{0,8},{4,12},{8,0},{12,4},{1,9},{5,13},{9,1},{13,5},{2,10},{6,14},... | collective-permute-start | bytes 165896 | tf_op jit(solution)/shard_map/ppermute | solution.py:355
  115.3 6.0 %collective-permute-start.36 = (bf16[216,128]{1,0:T(8,128)(2,1)S(1)}, bf16[216,128]{1,0:T(8,128)(2,1)S(1)}, u32[]{:S(2)}, u32[]{:S(2)}) collective-permute-start(bf16[216,128]{1,0:T(8,128)(2,1)S(1)} %get-tuple-element.120), channel_id=1, source_target_pairs={{0,4},{4,8},{8,12},{12,0},{1,5},{5,9},{9,13},{13,1},{2,6},{6,10},{... | collective-permute-start | bytes 165896 | tf_op jit(solution)/shard_map/ppermute | solution.py:355
  115.5 6.6 %collective-permute-start.30 = (bf16[288,128]{1,0:T(8,128)(2,1)S(1)}, bf16[288,128]{1,0:T(8,128)(2,1)S(1)}, u32[]{:S(2)}, u32[]{:S(2)}) collective-permute-start(bf16[288,128]{1,0:T(8,128)(2,1)S(1)} %get-tuple-element.111), channel_id=1, source_target_pairs={{0,3},{1,0},{2,1},{3,2},{4,7},{5,4},{6,5},{7,6},{8,11},{9,8},{10,9... | collective-permute-start | bytes 221192 | tf_op jit(solution)/shard_map/ppermute | solution.py:355
  115.6 7.9 %collective-permute-start.31 = (bf16[288,128]{1,0:T(8,128)(2,1)S(1)}, bf16[288,128]{1,0:T(8,128)(2,1)S(1)}, u32[]{:S(2)}, u32[]{:S(2)}) collective-permute-start(bf16[288,128]{1,0:T(8,128)(2,1)S(1)} %get-tuple-element.111), channel_id=1, source_target_pairs={{0,2},{1,3},{2,0},{3,1},{4,6},{5,7},{6,4},{7,5},{8,10},{9,11},{10,... | collective-permute-start | bytes 221192 | tf_op jit(solution)/shard_map/ppermute | solution.py:355
  117.7 5.8 %collective-permute-start.32 = (bf16[288,128]{1,0:T(8,128)(2,1)S(1)}, bf16[288,128]{1,0:T(8,128)(2,1)S(1)}, u32[]{:S(2)}, u32[]{:S(2)}) collective-permute-start(bf16[288,128]{1,0:T(8,128)(2,1)S(1)} %get-tuple-element.111), channel_id=1, source_target_pairs={{0,1},{1,2},{2,3},{3,0},{4,5},{5,6},{6,7},{7,4},{8,9},{9,10},{10,1... | collective-permute-start | bytes 221192 | tf_op jit(solution)/shard_map/ppermute | solution.py:355
  121.3 5.2 %collective-permute-start.39 = (bf16[216,128]{1,0:T(8,128)(2,1)S(1)}, bf16[216,128]{1,0:T(8,128)(2,1)S(1)}, u32[]{:S(2)}, u32[]{:S(2)}) collective-permute-start(bf16[216,128]{1,0:T(8,128)(2,1)S(1)} %get-tuple-element.109), channel_id=1, source_target_pairs={{0,12},{4,0},{8,4},{12,8},{1,13},{5,1},{9,5},{13,9},{2,14},{6,2},{... | collective-permute-start | bytes 165896 | tf_op jit(solution)/shard_map/ppermute | solution.py:355
  122.1 5.1 %collective-permute-start.40 = (bf16[216,128]{1,0:T(8,128)(2,1)S(1)}, bf16[216,128]{1,0:T(8,128)(2,1)S(1)}, u32[]{:S(2)}, u32[]{:S(2)}) collective-permute-start(bf16[216,128]{1,0:T(8,128)(2,1)S(1)} %get-tuple-element.109), channel_id=1, source_target_pairs={{0,8},{4,12},{8,0},{12,4},{1,9},{5,13},{9,1},{13,5},{2,10},{6,14},... | collective-permute-start | bytes 165896 | tf_op jit(solution)/shard_map/ppermute | solution.py:355
  122.1 6.4 %collective-permute-start.41 = (bf16[216,128]{1,0:T(8,128)(2,1)S(1)}, bf16[216,128]{1,0:T(8,128)(2,1)S(1)}, u32[]{:S(2)}, u32[]{:S(2)}) collective-permute-start(bf16[216,128]{1,0:T(8,128)(2,1)S(1)} %get-tuple-element.109), channel_id=1, source_target_pairs={{0,4},{4,8},{8,12},{12,0},{1,5},{5,9},{9,13},{13,1},{2,6},{6,10},{... | collective-permute-start | bytes 165896 | tf_op jit(solution)/shard_map/ppermute | solution.py:355
  128.6 5.7 %collective-permute-start.42 = (bf16[864,128]{1,0:T(8,128)(2,1)S(1)}, bf16[864,128]{1,0:T(8,128)(2,1)S(1)}, u32[]{:S(2)}, u32[]{:S(2)}) collective-permute-start(bf16[864,128]{1,0:T(8,128)(2,1)S(1)} %get-tuple-element.107), channel_id=1, source_target_pairs={{0,3},{1,0},{2,1},{3,2},{4,7},{5,4},{6,5},{7,6},{8,11},{9,8},{10,9... | collective-permute-start | bytes 663560 | tf_op jit(solution)/shard_map/ppermute | solution.py:355
  128.7 10.7 %collective-permute-start.43 = (bf16[864,128]{1,0:T(8,128)(2,1)S(1)}, bf16[864,128]{1,0:T(8,128)(2,1)S(1)}, u32[]{:S(2)}, u32[]{:S(2)}) collective-permute-start(bf16[864,128]{1,0:T(8,128)(2,1)S(1)} %get-tuple-element.107), channel_id=1, source_target_pairs={{0,2},{1,3},{2,0},{3,1},{4,6},{5,7},{6,4},{7,5},{8,10},{9,11},{10,... | collective-permute-start | bytes 663560 | tf_op jit(solution)/shard_map/ppermute | solution.py:355
  130.3 10.0 %collective-permute-start.44 = (bf16[864,128]{1,0:T(8,128)(2,1)S(1)}, bf16[864,128]{1,0:T(8,128)(2,1)S(1)}, u32[]{:S(2)}, u32[]{:S(2)}) collective-permute-start(bf16[864,128]{1,0:T(8,128)(2,1)S(1)} %get-tuple-element.107), channel_id=1, source_target_pairs={{0,1},{1,2},{2,3},{3,0},{4,5},{5,6},{6,7},{7,4},{8,9},{9,10},{10,1... | collective-permute-start | bytes 663560 | tf_op jit(solution)/shard_map/ppermute | solution.py:355
  (21 other events, 15.8 us)
where the time goes:
time: 144 us; the launch traced here: 143 us
  waiting for transfers between devices  44 us (31%)
  starting transfers between devices  38.1 us (26%)
  Pallas kernels  32.2 us (22%)
  local copies, waits for them, and re-layouts  26.2 us (18%)
    ppermute x45, waiting for transfers between devices, exchange(): lax.ppermute(tiles[k], axis, [(i, (i + sign * k) % size) for i in range(s...  44 us
    ppermute x45, starting transfers between devices, exchange(): lax.ppermute(tiles[k], axis, [(i, (i + sign * k) % size) for i in range(s...  38.1 us
    pallas_call x11, Pallas kernels, call(): pl.pallas_call(body, out_shape=[jax.ShapeDtypeStruct(shape, dtype) for sh...  32.2 us
    unnamed x104, local copies, waits for them, and re-layouts  25 us
  transfers between devices with their start and end apart: 45, of which 24 were waited for; matrix products, arithmetic and copies ran while one was open for 1% of the time, Pallas kernels for 3%

commit v1 on v0

--- a/solution.py
+++ b/solution.py
@@ -1,5 +1,6 @@
 import functools
 import math
+from typing import NamedTuple
 
 import jax
 import jax.numpy as jnp
@@ -13,6 +14,7 @@
 FF = 768
 HEAD = E // HEADS
 LANES = 128
+VMEM = 24 * 1024 * 1024
 BF = jnp.bfloat16
 F32 = jnp.float32
 EXP2 = math.log2(math.e) / math.sqrt(HEAD)
@@ -117,7 +119,8 @@
         return place * self.own_attr + attr
 
 
-def split_kernel(plan, to_rows, table_ref, *refs):
+def split_kernel(plan, to_rows, wait, table_ref, *refs):
+    wait()
     outs, rows = refs[:-1], refs[-1]
     for pair in range(plan.attr // 2):
         both = table_ref[:, 2 * E * pair : 2 * E * (pair + 1)].astype(F32)
@@ -129,7 +132,7 @@
     put_tiles(outs, nn(turned, one_hot(plan.cells, source)))
 
 
-def join_kernel(plan, *refs):
+def join_kernel(plan, wait, *refs):
     tiles, out_ref, rows = refs[:-2], refs[-2], refs[-1]
     rows[...] = nt(one_hot(plan.cells, plan.rows_from_owned()), side_by_side(tiles))
     for pair in range(plan.attr // 2):
@@ -138,18 +141,20 @@
         out_ref[:, 2 * E * pair : 2 * E * (pair + 1)] = jnp.concatenate(both, axis=1).astype(BF)
 
 
-def to_cols_kernel(plan, *refs):
+def to_cols_kernel(plan, wait, *refs):
     tiles, outs = refs[: plan.ranks_attr], refs[plan.ranks_attr :]
     put_tiles(outs, nn(side_by_side(tiles), one_hot(plan.cells, plan.cols_from_rows())))
 
 
-def to_rows_kernel(plan, *refs):
+def to_rows_kernel(plan, wait, *refs):
     tiles, outs = refs[: plan.ranks_rec], refs[plan.ranks_rec :]
     put_tiles(outs, nt(side_by_side(tiles), one_hot(plan.cells, plan.cols_from_rows())))
 
 
-def turn_kernel(count, *refs):
-    for source, target in zip(refs[:count], refs[count:]):
+def split_turn_kernel(plan, count, wait, table_ref, *refs):
+    weights, refs = refs[:count], refs[count:]
+    split_kernel(plan, False, wait, table_ref, *refs[: plan.ranks_rec], refs[-1])
+    for source, target in zip(weights, refs[plan.ranks_rec : -1]):
         target[...] = source[...].astype(F32).T.astype(BF)
 
 
@@ -217,6 +222,12 @@
     return results
 
 
+def put_halves(bit, sums_ref, keep_ref, send_ref):
+    rows, mine = keep_ref.shape[0], has_bit("attr", bit)
+    for ref, half in ((keep_ref, mine), (send_ref, 1 - mine)):
+        ref[...] = sums_ref[pl.ds(pl.multiple_of(half * rows, rows), rows), :]
+
+
 def put_attend_grads(out_ref, normed_ref, grad_proj_ref, mixed_ref, grad_ref):
     qkv = nt(normed_ref[...], grad_proj_ref[...])
     out = nt(mixed_ref[...], grad_ref[...])
@@ -242,7 +253,7 @@
     out_ref[:, LANES:] = mixed[:, LANES // 2 :]
 
 
-def rows_forward_kernel(plan, *refs):
+def rows_forward_kernel(plan, wait, *refs):
     tiles, refs = refs[: plan.ranks_attr], refs[plan.ranks_attr :]
     (qkv_t, out_t), refs = refs[:2], refs[2:]
     outs, (x_ref, normed_ref, proj_ref, probs_ref, mixed_ref) = refs[: plan.ranks_attr], refs[plan.ranks_attr :]
@@ -252,18 +263,21 @@
     put_tiles(outs, nt(jnp.concatenate(first, axis=1).astype(BF), order))
 
 
-def rows_back_kernel(plan, *refs):
+def rows_back_kernel(plan, wait, *refs):
     tiles, refs = refs[: plan.ranks_attr], refs[plan.ranks_attr :]
     (qkv, out, x_ref, normed_ref, proj_ref, probs_ref, mixed_ref), refs = refs[:7], refs[7:]
-    outs, (sums_ref, grad_ref, grad_proj_ref) = refs[: plan.ranks_attr], refs[plan.ranks_attr :]
+    outs, refs = refs[: plan.ranks_attr], refs[plan.ranks_attr :]
+    keep_ref, send_ref, sums_ref, grad_ref, grad_proj_ref = refs
     order = one_hot(plan.cells, plan.grouped_from_rows())
     grad_ref[...] = nn(side_by_side(tiles), order).astype(BF)
+    wait()
     grads = attend_back(grad_ref, x_ref, proj_ref, probs_ref, grad_proj_ref, qkv, out, plan.all_attr)
     put_tiles(outs, nt(jnp.concatenate(grads, axis=1).astype(BF), order))
     put_attend_grads(sums_ref, normed_ref, grad_proj_ref, mixed_ref, grad_ref)
-
-
-def cols_kernel(plan, *refs):
+    put_halves(bits_of("attr")[0], sums_ref, keep_ref, send_ref)
+
+
+def cols_kernel(plan, wait, *refs):
     count = plan.ranks_rec
     tiles, cot_tiles, refs = refs[:count], refs[count : 2 * count], refs[2 * count :]
     (train_ref, qkv, out, up, down, qkv_t, out_t, up_t), refs = refs[:8], refs[8:]
@@ -273,6 +287,7 @@
     width = max(LANES, plan.all_rec)
     order = one_hot(plan.cells, plan.grouped_from_cols())
     x_ref[...] = nn(side_by_side(tiles), order).astype(BF)
+    wait()
     cot_ref[...] = nn(side_by_side(cot_tiles), order).astype(BF)
 
     row = lax.broadcasted_iota(jnp.int32, (width, 1), 0)
@@ -301,16 +316,13 @@
         grad_pre_ref[rows, :] = grad_pre_ref[rows, :].astype(BF).astype(F32) * slope
     grad_pre = grad_pre_ref[...].astype(BF)
 
-    base = 6 * E
-    grad_up = nt(normed_second, grad_pre)
-    for tile in range(FF // LANES):
-        rows = slice(base + tile * E, base + (tile + 1) * E)
-        sums_ref[rows, :] = grad_up[:, tile * LANES : (tile + 1) * LANES].astype(BF)
-    base = 12 * E
-    grad_down = nt(hidden_ref[...], cot_ref[...])
-    sums_ref[base : base + FF, :] = grad_down[:, :LANES].astype(BF)
-    rest = jnp.concatenate([grad_down[: FF // 2, LANES:], grad_down[FF // 2 :, LANES:]], axis=1)
-    sums_ref[base + FF : base + FF + FF // 2, :] = rest.astype(BF)
+    for base, grad_weight in (
+        (6 * E, nt(normed_second, grad_pre)),
+        (12 * E, nt(cot_ref[...], hidden_ref[...])),
+    ):
+        for tile in range(FF // LANES):
+            rows = slice(base + tile * E, base + (tile + 1) * E)
+            sums_ref[rows, :] = grad_weight[:, tile * LANES : (tile + 1) * LANES].astype(BF)
 
     grad_normed = nn(up[...], grad_pre).astype(BF).astype(F32)
     grad = norm_back(grad_normed, table, root) + cot_ref[...].astype(F32)
@@ -320,33 +332,70 @@
     put_attend_grads(sums_ref, normed_ref, grad_proj_ref, mixed_ref, grad_ref)
 
 
-def finish_cols_kernel(factor, sums_ref, qkv_ref, out_ref, up_ref, down_ref):
+def finish_cols_kernel(factor, bits, wait, *refs):
+    parts, (qkv_ref, out_ref, up_ref, down_ref, sums_ref) = refs[:-5], refs[-5:]
+    lay_out(bits, parts, sums_ref)
     take_attend_grads(sums_ref, 0, qkv_ref, out_ref, factor)
-    base = 6 * E
-    for tile in range(FF // LANES):
-        rows = slice(base + tile * E, base + (tile + 1) * E)
-        up_ref[:, tile * LANES : (tile + 1) * LANES] = sums_ref[rows, :].astype(F32) * factor
-    base = 12 * E
-    down_ref[:, :LANES] = sums_ref[base : base + FF, :].astype(F32) * factor
-    rest = sums_ref[base + FF : base + FF + FF // 2, :].astype(F32) * factor
-    down_ref[: FF // 2, LANES:] = rest[:, : LANES // 2]
-    down_ref[FF // 2 :, LANES:] = rest[:, LANES // 2 :]
-
-
-def finish_rows_kernel(factor, sums_ref, qkv_ref, out_ref):
+    for base, ref in ((6 * E, up_ref), (12 * E, down_ref)):
+        for tile in range(FF // LANES):
+            rows = slice(base + tile * E, base + (tile + 1) * E)
+            ref[:, tile * LANES : (tile + 1) * LANES] = sums_ref[rows, :].astype(F32) * factor
+
+
+def finish_rows_kernel(factor, bits, wait, *refs):
+    parts, (qkv_ref, out_ref, sums_ref) = refs[:-3], refs[-3:]
+    lay_out(bits, parts, sums_ref)
     take_attend_grads(sums_ref, 0, qkv_ref, out_ref, factor)
 
 
-def call(body, outs, scratch, *args):
-    whole = pl.BlockSpec(memory_space=pltpu.VMEM)
+class Far(NamedTuple):
+    array: jax.Array
+
+
+class Near(NamedTuple):
+    array: jax.Array
+
+
+def call(body, outs, scratch, *args, after=()):
+    far = [n for n, arg in enumerate(args) if isinstance(arg, Far)]
+    n_in, n_after, n_out, n_far = len(args), len(after), len(outs), len(far)
+    whole, anywhere = pl.BlockSpec(memory_space=pltpu.VMEM), pl.BlockSpec(memory_space=pl.ANY)
+    hbm = pl.BlockSpec(memory_space=pltpu.HBM)
+
+    def kernel(*refs):
+        given, refs = list(refs[:n_in]), refs[n_in + n_after :]
+        copies = []
+        if far:
+            held, sems, refs = refs[-1 - n_far : -1], refs[-1], refs[: -1 - n_far]
+            for order, (number, ref) in enumerate(zip(far, held)):
+                copies.append(pltpu.make_async_copy(given[number], ref, sems.at[order]))
+                given[number] = ref
+        for copy in copies:
+            copy.start()
+
+        def wait():
+            for copy in copies:
+                copy.wait()
+
+        body(wait, *given, *refs)
+
+    arrays = []
+    for arg in args:
+        space = {Far: pltpu.HBM, Near: pltpu.VMEM}.get(type(arg))
+        arrays.append(arg if space is None else pltpu.with_memory_space_constraint(arg.array, space))
+    held = [pltpu.VMEM(arrays[n].shape, arrays[n].dtype) for n in far]
     return pl.pallas_call(
-        body,
-        out_shape=[jax.ShapeDtypeStruct(shape, dtype) for shape, dtype in outs],
-        in_specs=[whole] * len(args),
-        out_specs=[whole] * len(outs),
-        scratch_shapes=[pltpu.VMEM(shape, dtype) for shape, dtype in scratch],
-        compiler_params=pltpu.CompilerParams(vmem_limit_bytes=48 * 1024 * 1024),
-    )(*args)
+        kernel,
+        out_shape=[
+            (pltpu.VMEM if out[2:] else jax.ShapeDtypeStruct)(out[0], out[1]) for out in outs
+        ],
+        in_specs=[hbm if isinstance(arg, Far) else whole for arg in args] + [anywhere] * n_after,
+        out_specs=[whole] * n_out,
+        scratch_shapes=[pltpu.VMEM(shape, dtype) for shape, dtype in scratch]
+        + held
+        + ([pltpu.SemaphoreType.DMA((n_far,))] if far else []),
+        compiler_params=pltpu.CompilerParams(vmem_limit_bytes=VMEM),
+    )(*arrays, *after)
 
 
 def exchange(tiles, axis, sign):
@@ -357,28 +406,68 @@
     ]
 
 
-def scatter_sum(parts, axis):
-    size, own = parts.shape[0], lax.axis_index(axis)
-    tiles = [
-        lax.dynamic_index_in_dim(parts, (own + k) % size, 0, keepdims=False) for k in range(size)
-    ]
-    return sum(tile.astype(F32) for tile in exchange(tiles, axis, 1)).astype(BF)
-
-
-def gather(part, axis, size):
-    got = exchange([part] * size, axis, 1)
-    ordered = [got[0]] + got[:0:-1]
-    both = jnp.concatenate(ordered + ordered[:-1], axis=0)
-    rows = part.shape[0]
-    start = (size - lax.axis_index(axis)) % size * rows
-    return lax.dynamic_slice_in_dim(both, start, size * rows, 0)
-
-
-def total(sums, ranks_rec, ranks_attr):
-    rows = sums.shape[0]
-    part = scatter_sum(sums.reshape(ranks_attr, rows // ranks_attr, LANES), "attr")
-    part = scatter_sum(part.reshape(ranks_rec, rows // ranks_attr // ranks_rec, LANES), "rec")
-    return gather(gather(part, "rec", ranks_rec), "attr", ranks_attr)
+def swap(part, axis, bit):
+    size = lax.axis_size(axis)
+    return lax.ppermute(part, axis, [(i, i ^ bit) for i in range(size)])
+
+
+def has_bit(axis, bit):
+    return digits(lax.axis_index(axis) // bit, (2,))[0]
+
+
+def halve_kernel(bit, wait, *refs):
+    parts, (keep, send) = refs[:-2], refs[-2:]
+    rows, mine = keep.shape[0], has_bit("attr", bit)
+    for ref, half in ((keep, mine), (send, 1 - mine)):
+        place = pl.ds(pl.multiple_of(half * rows, rows), rows)
+        ref[...] = sum(part[place, :].astype(F32) for part in parts).astype(BF)
+
+
+def add_kernel(wait, *refs):
+    refs[-1][...] = sum(part[...].astype(F32) for part in refs[:-1]).astype(BF)
+
+
+def lay_out(bits, parts, rows_ref):
+    rows = parts[0].shape[0]
+    for number, ref in enumerate(parts):
+        place = 0
+        for order, bit in enumerate(bits):
+            own = has_bit("attr", bit)
+            place = place * 2 + (1 - own if number >> order & 1 else own)
+        rows_ref[pl.ds(pl.multiple_of(place * rows, rows), rows), :] = ref[...]
+
+
+def bits_of(axis):
+    return [1 << n for n in range(lax.axis_size(axis).bit_length() - 1)]
+
+
+class Total:
+    def __init__(self, *parts):
+        self.parts, self.rows = list(parts), parts[0].shape[0]
+
+    def halve(self, bit, after=()):
+        self.rows //= 2
+        keep, send = call(
+            functools.partial(halve_kernel, bit), [((self.rows, LANES), BF)] * 2, [], *self.parts, after=after
+        )
+        self.parts = [keep, swap(send, "attr", bit)]
+        return [keep]
+
+    def add(self, bit=0, after=()):
+        (part,) = call(add_kernel, [((self.rows, LANES), BF)], [], *self.parts, after=after)
+        self.parts = [part] + ([swap(part, "rec", bit)] if bit else [])
+        return [part]
+
+    def spread(self, bits):
+        done = {0: self.parts[0]}
+        for order, bit in reversed(list(enumerate(bits))):
+            done.update({number | 1 << order: swap(part, "attr", bit) for number, part in sorted(done.items())})
+        return [done[number] for number in sorted(done)]
+
+
+def padded(rows):
+    devices = lax.axis_size("attr")
+    return -(-rows // (16 * devices)) * 16 * devices
 
 
 def local(
@@ -398,71 +487,96 @@
     def kernel(body, *static):
         return functools.partial(body, plan, *static)
 
-    rows = call(kernel(split_kernel, True), row_tiles, [((count, E), F32)], cells)
+    rows = call(kernel(split_kernel, True), row_tiles, [((count, E), F32)], Far(cells))
     rows = exchange(rows, "attr", 1)
-    weights = (qkv_attr, out_attr, qkv_samp, out_samp, up_weight)
-    qkv_attr_t, out_attr_t, qkv_samp_t, out_samp_t, up_t = call(
-        functools.partial(turn_kernel, len(weights)), [(w.shape[::-1], BF) for w in weights], [], *weights
+    weights = (qkv_attr, out_attr, qkv_samp, out_samp, up_weight, down_weight.T)
+    got = call(
+        kernel(split_turn_kernel, len(weights)),
+        col_tiles + [(w.shape[::-1], BF, "near") for w in weights],
+        [((count, E), F32)],
+        Far(cotangent),
+        *[Far(w) for w in weights],
+        after=[rows[0]],
     )
-    cot = call(kernel(split_kernel, False), col_tiles, [((count, E), F32)], cotangent)
-    cot = exchange(cot, "rec", 1)
+    cot = exchange(got[:ranks_rec], "rec", 1)
+    turned = [Near(w) for w in got[ranks_rec:]]
 
     got = call(
         kernel(rows_forward_kernel),
-        row_tiles + [table, table, wide, probs(plan.all_attr), table],
+        row_tiles + [out + ("near",) for out in (table, table, wide, probs(plan.all_attr), table)],
         [],
         *rows,
-        qkv_attr_t,
-        out_attr_t,
+        *turned[:2],
     )
-    first, saved = got[:ranks_attr], got[ranks_attr:]
+    first, saved = got[:ranks_attr], [Near(array) for array in got[ranks_attr:]]
     first = exchange(first, "attr", -1)
     cols = exchange(call(kernel(to_cols_kernel), col_tiles, [], *first), "rec", 1)
 
     width = max(LANES, plan.all_rec)
-    sums_rows = 6 * E
+    rows_sums, cols_sums = padded(6 * E), padded(18 * E)
     got = call(
         kernel(cols_kernel),
-        col_tiles + [((3 * sums_rows, LANES), BF)],
+        col_tiles + [((cols_sums, LANES), BF)],
         [table, table, table, wide, probs(width), table, table]
         + [((FF, count), F32), ((FF, count), BF), ((FF, count), F32), table, wide],
         *cols,
         *cot,
         train_split.reshape(1, -1),
-        qkv_samp,
-        out_samp,
-        up_weight,
-        down_weight,
-        qkv_samp_t,
-        out_samp_t,
-        up_t,
+        Far(qkv_samp),
+        Far(out_samp),
+        Far(up_weight),
+        turned[5],
+        turned[2],
+        turned[3],
+        turned[4],
     )
-    grads, sums = exchange(got[:ranks_rec], "rec", -1), got[ranks_rec]
-    grads = exchange(call(kernel(to_rows_kernel), row_tiles, [], *grads), "attr", 1)
+    near, far = bits_of("attr"), bits_of("rec")
+    grads, sums = exchange(got[:ranks_rec], "rec", -1), Total(got[ranks_rec])
+    mark = sums.halve(near[0])
+    for bit in near[1:]:
+        mark = sums.halve(bit, after=mark)
+    grads = exchange(call(kernel(to_rows_kernel), row_tiles, [], *grads, after=mark), "attr", 1)
+    mark = sums.add(far[0])
 
     got = call(
         kernel(rows_back_kernel),
-        row_tiles + [((sums_rows, LANES), BF)],
-        [table, wide],
+        row_tiles + [((rows_sums // 2, LANES), BF)] * 2,
+        [((rows_sums, LANES), BF), table, wide],
         *grads,
-        qkv_attr,
-        out_attr,
+        Far(qkv_attr),
+        Far(out_attr),
         *saved,
+        after=mark,
     )
-    grads, row_sums = exchange(got[:ranks_attr], "attr", -1), got[ranks_attr]
-    (grad_cells,) = call(kernel(join_kernel), [(cells.shape, BF)], [((count, E), F32)], *grads)
-
-    sums = total(sums, ranks_rec, ranks_attr)
+    grads, row_sums = exchange(got[:ranks_attr], "attr", -1), Total(*got[ranks_attr:])
+    row_sums.parts[1] = swap(row_sums.parts[1], "attr", near[0])
+    mark = []
+    for bit in near[1:]:
+        mark = row_sums.halve(bit, after=mark)
+    for bit in far[1:]:
+        mark = sums.add(bit, after=mark)
+    mark = row_sums.add(far[0], after=mark)
+    (grad_cells,) = call(kernel(join_kernel), [(cells.shape, BF)], [((count, E), F32)], *grads, after=mark)
+    mark = [grad_cells]
+    for bit in far[1:]:
+        mark = row_sums.add(bit, after=mark)
+    mark = sums.add(after=mark)
+    parts = sums.spread(near)
+    row_sums.add(after=mark)
+    row_parts = row_sums.spread(near)
     grad_qkv_samp, grad_out_samp, grad_up, grad_down = call(
-        functools.partial(finish_cols_kernel, factor),
-        [((E, 3 * E), F32), ((E, E), F32), ((E, FF), F32), ((FF, E), F32)],
-        [],
-        sums,
+        functools.partial(finish_cols_kernel, factor, near),
+        [((E, 3 * E), F32), ((E, E), F32), ((E, FF), F32), ((E, FF), F32)],
+        [((cols_sums, LANES), BF)],
+        *parts,
     )
-    row_sums = total(row_sums, ranks_rec, ranks_attr)
     grad_qkv_attr, grad_out_attr = call(
-        functools.partial(finish_rows_kernel, factor), [((E, 3 * E), F32), ((E, E), F32)], [], row_sums
+        functools.partial(finish_rows_kernel, factor, near),
+        [((E, 3 * E), F32), ((E, E), F32)],
+        [((rows_sums, LANES), BF)],
+        *row_parts,
     )
+    grad_down = grad_down.T
     return (grad_cells, grad_qkv_attr, grad_out_attr, grad_qkv_samp, grad_out_samp, grad_up, grad_down)
 
 

time: 144 us -> 98.9 us (0.69)
  local copies, waits for them, and re-layouts: 26.2 us -> 0.93 us
  waiting for transfers between devices: 44 us -> 31.6 us
  starting transfers between devices: 38.1 us -> 31.2 us
  Pallas kernels: 32.2 us -> 34.1 us
    ppermute x45 -> x21, waiting for transfers between devices: 44 us -> 9.69 us  [exchange(): lax.ppermute(tiles[k], axis, [(i, (i + sign * k) % size) for i in range(s...]
    unnamed x104 -> x4, local copies, waits for them, and re-layouts: 25 us -> 0.93 us
    ppermute x0 -> x14, waiting for transfers between devices: none -> 21.9 us  [swap(): return lax.ppermute(part, axis, [(i, i ^ bit) for i in range(size)])]
    ppermute x45 -> x21, starting transfers between devices: 38.1 us -> 23.6 us  [exchange(): lax.ppermute(tiles[k], axis, [(i, (i + sign * k) % size) for i in range(s...]
    ppermute x0 -> x14, starting transfers between devices: none -> 7.6 us  [swap(): return lax.ppermute(part, axis, [(i, i ^ bit) for i in range(size)])]
    pallas_call x11 -> x19, Pallas kernels: 32.2 us -> 34.1 us  [call(): pl.pallas_call(kernel, out_shape=[(pltpu.VMEM if out[2:] else jax.ShapeDt...]
  transfers between devices with their start and end apart: 45 -> 35, of which waited for: 24 -> 17; matrix products, arithmetic and copies ran while one was open for 1% -> 0% of each run, Pallas kernels for 3% -> 11%
where the time goes in v1:
time: 98.9 us; the launch traced here: 98.6 us
  Pallas kernels  34.1 us (34%)
  waiting for transfers between devices  31.6 us (32%)
  starting transfers between devices  31.2 us (32%)
    pallas_call x19, Pallas kernels, call(): pl.pallas_call(kernel, out_shape=[(pltpu.VMEM if out[2:] else jax.ShapeDt...  34.1 us
    ppermute x21, starting transfers between devices, exchange(): lax.ppermute(tiles[k], axis, [(i, (i + sign * k) % size) for i in range(s...  23.6 us
    ppermute x14, waiting for transfers between devices, swap(): return lax.ppermute(part, axis, [(i, i ^ bit) for i in range(size)])  21.9 us
    ppermute x21, waiting for transfers between devices, exchange(): lax.ppermute(tiles[k], axis, [(i, (i + sign * k) % size) for i in range(s...  9.69 us
    ppermute x14, starting transfers between devices, swap(): return lax.ppermute(part, axis, [(i, i ^ bit) for i in range(size)])  7.6 us
  transfers between devices with their start and end apart: 35, of which 17 were waited for; matrix products, arithmetic and copies ran while one was open for 0% of the time, Pallas kernels for 11%

profile of v1, /device:TPU:0, one launch (start us, length us, event | category | flops | bytes accessed | tf_op | source)
XLA Modules:
  0.0 98.6 jit_solution(3784833926522844444)
XLA Ops:
  0.6 1.5 %shard_map.144 = (bf16[192,128]{1,0:T(8,128)(2,1)S(1)}, bf16[192,128]{1,0:T(8,128)(2,1)S(1)}, bf16[192,128]{1,0:T(8,128)(2,1)S(1)}, bf16[192,128]{1,0:T(8,128)(2,1)S(1)}) custom-call(bf16[8,12288]{1,0:T(8,128)(2,1)} %refs_0_.2), custom_call_target="tpu_custom_call" | custom-call | tf_op jit(solution)/shard_map/pallas_call | solution.py:387
  2.1 0.5 collective-permute-start
  2.6 2.6 %collective-permute-start.1 = (bf16[192,128]{1,0:T(8,128)(2,1)S(1)}, bf16[192,128]{1,0:T(8,128)(2,1)S(1)}, u32[]{:S(2)}, u32[]{:S(2)}) collective-permute-start(bf16[192,128]{1,0:T(8,128)(2,1)S(1)} %get-tuple-element.63), channel_id=1, source_target_pairs={{0,2},{1,3},{2,0},{3,1},{4,6},{5,7},{6,4},{7,5},{8,10},{9,11},{10,... | collective-permute-start | bytes 147464 | tf_op jit(solution)/shard_map/ppermute | solution.py:404
  5.2 1.4 %collective-permute-start.2 = (bf16[192,128]{1,0:T(8,128)(2,1)S(1)}, bf16[192,128]{1,0:T(8,128)(2,1)S(1)}, u32[]{:S(2)}, u32[]{:S(2)}) collective-permute-start(bf16[192,128]{1,0:T(8,128)(2,1)S(1)} %get-tuple-element.64), channel_id=1, source_target_pairs={{0,3},{1,0},{2,1},{3,2},{4,7},{5,4},{6,5},{7,6},{8,11},{9,8},{10,9... | collective-permute-start | bytes 147464 | tf_op jit(solution)/shard_map/ppermute | solution.py:404
  6.6 2.1 %shard_map.145 = (bf16[192,128]{1,0:T(8,128)(2,1)S(1)}, bf16[192,128]{1,0:T(8,128)(2,1)S(1)}, bf16[192,128]{1,0:T(8,128)(2,1)S(1)}, bf16[192,128]{1,0:T(8,128)(2...) custom-call(bf16[8,12288]{1,0:T(8,128)(2,1)} %refs_0_.3, ...), custom_call_target="tpu_custom_call" | custom-call | tf_op jit(solution)/shard_map/pallas_call | solution.py:387
  8.7 0.0 collective-permute-done.1.refs_2_
  8.7 0.0 collective-permute-done.2.refs_3_
  8.7 5.0 %shard_map.146 = (bf16[192,128]{1,0:T(8,128)(2,1)S(1)}, bf16[192,128]{1,0:T(8,128)(2,1)S(1)}, bf16[192,128]{1,0:T(8,128)(2,1)S(1)}, bf16[192,128]{1,0:T(8,128)(2...) custom-call(bf16[192,128]{1,0:T(8,128)(2,1)S(1)} %get-tuple-element., ...), custom_call_target="tpu_custom_call" | custom-call | tf_op jit(solution)/shard_map/pallas_call | solution.py:387
  13.7 1.4 %collective-permute-start.3 = (bf16[192,128]{1,0:T(8,128)(2,1)S(1)}, bf16[192,128]{1,0:T(8,128)(2,1)S(1)}, u32[]{:S(2)}, u32[]{:S(2)}) collective-permute-start(bf16[192,128]{1,0:T(8,128)(2,1)S(1)} %get-tuple-element.68), channel_id=1, source_target_pairs={{0,3},{1,0},{2,1},{3,2},{4,7},{5,4},{6,5},{7,6},{8,11},{9,8},{10,9... | collective-permute-start | bytes 147464 | tf_op jit(solution)/shard_map/ppermute | solution.py:404
  15.1 0.3 collective-permute-start.4
  15.4 1.8 %collective-permute-start.9 = (bf16[192,128]{1,0:T(8,128)(2,1)S(1)}, bf16[192,128]{1,0:T(8,128)(2,1)S(1)}, u32[]{:S(2)}, u32[]{:S(2)}) collective-permute-start(bf16[192,128]{1,0:T(8,128)(2,1)S(1)} %get-tuple-element.76), channel_id=1, source_target_pairs={{0,4},{4,8},{8,12},{12,0},{1,5},{5,9},{9,13},{13,1},{2,6},{6,10},{... | collective-permute-start | bytes 147464 | tf_op jit(solution)/shard_map/ppermute | solution.py:404
  17.2 2.6 %collective-permute-start.10 = (bf16[192,128]{1,0:T(8,128)(2,1)S(1)}, bf16[192,128]{1,0:T(8,128)(2,1)S(1)}, u32[]{:S(2)}, u32[]{:S(2)}) collective-permute-start(bf16[192,128]{1,0:T(8,128)(2,1)S(1)} %get-tuple-element.77), channel_id=1, source_target_pairs={{0,8},{4,12},{8,0},{12,4},{1,9},{5,13},{9,1},{13,5},{2,10},{6,14},... | collective-permute-start | bytes 147464 | tf_op jit(solution)/shard_map/ppermute | solution.py:404
  19.8 1.3 %collective-permute-start.11 = (bf16[192,128]{1,0:T(8,128)(2,1)S(1)}, bf16[192,128]{1,0:T(8,128)(2,1)S(1)}, u32[]{:S(2)}, u32[]{:S(2)}) collective-permute-start(bf16[192,128]{1,0:T(8,128)(2,1)S(1)} %get-tuple-element.78), channel_id=1, source_target_pairs={{0,12},{4,0},{8,4},{12,8},{1,13},{5,1},{9,5},{13,9},{2,14},{6,2},{... | collective-permute-start | bytes 147464 | tf_op jit(solution)/shard_map/ppermute | solution.py:404
  21.2 0.3 shard_map.147
  21.5 0.7 collective-permute-start.6
  22.2 2.0 %collective-permute-start.7 = (bf16[192,128]{1,0:T(8,128)(2,1)S(1)}, bf16[192,128]{1,0:T(8,128)(2,1)S(1)}, u32[]{:S(2)}, u32[]{:S(2)}) collective-permute-start(bf16[192,128]{1,0:T(8,128)(2,1)S(1)} %get-tuple-element.73), channel_id=1, source_target_pairs={{0,8},{4,12},{8,0},{12,4},{1,9},{5,13},{9,1},{13,5},{2,10},{6,14},... | collective-permute-start | bytes 147464 | tf_op jit(solution)/shard_map/ppermute | solution.py:404
  24.2 1.3 %collective-permute-start.8 = (bf16[192,128]{1,0:T(8,128)(2,1)S(1)}, bf16[192,128]{1,0:T(8,128)(2,1)S(1)}, u32[]{:S(2)}, u32[]{:S(2)}) collective-permute-start(bf16[192,128]{1,0:T(8,128)(2,1)S(1)} %get-tuple-element.74), channel_id=1, source_target_pairs={{0,12},{4,0},{8,4},{12,8},{1,13},{5,1},{9,5},{13,9},{2,14},{6,2},{... | collective-permute-start | bytes 147464 | tf_op jit(solution)/shard_map/ppermute | solution.py:404
  25.6 2.5 %collective-permute-done.6.refs_1_ = bf16[192,128]{1,0:T(8,128)(2,1)S(1)} collective-permute-done((bf16[192,128]{1,0:T(8,128)(2,1)S(1)}, bf16[192,128]{1,0:T(8,128)(2,1)S(1)}, u32[]{:S(2)}, u32[]{:S(2)}) %collective-permute-start.6) | collective-permute-done | bytes 49184 | tf_op jit(solution)/shard_map/ppermute | solution.py:404
  28.0 1.7 %collective-permute-done.7.refs_2_ = bf16[192,128]{1,0:T(8,128)(2,1)S(1)} collective-permute-done((bf16[192,128]{1,0:T(8,128)(2,1)S(1)}, bf16[192,128]{1,0:T(8,128)(2,1)S(1)}, u32[]{:S(2)}, u32[]{:S(2)}) %collective-permute-start.7) | collective-permute-done | bytes 49184 | tf_op jit(solution)/shard_map/ppermute | solution.py:404
  29.8 15.0 %shard_map.148 = (bf16[192,128]{1,0:T(8,128)(2,1)S(1)}, bf16[192,128]{1,0:T(8,128)(2,1)S(1)}, bf16[192,128]{1,0:T(8,128)(2,1)S(1)}, bf16[192,128]{1,0:T(8,128)(2,1)S(1)}, bf16[3456,128]{1,0:T(8,128)(2,1)S(1)}) custom-call(bf16[192,128]{1,0:T(8,128)(2,1)S(1)} %get-tuple-element.71.refs_0_, bf16[192,128]{1,0:T(8,128)(2,1)S(1)} %collective-permute-done.6.refs_1_, ...), custom_call_target="tpu_custom_call" | custom-call | tf_op jit(solution)/shard_map/pallas_call | solution.py:387
  44.8 0.2 shard_map.149
  44.9 0.1 collective-permute-start.15
  45.0 1.8 %collective-permute-done.15.refs_1_ = bf16[1728,128]{1,0:T(8,128)(2,1)S(1)} collective-permute-done((bf16[1728,128]{1,0:T(8,128)(2,1)S(1)}, bf16[1728,128]{1,0:T(8,128)(2,1)S(1)}, u32[]{:S(2)}, u32[]{:S(2)}) %collective-permute-start.15) | collective-permute-done | bytes 442400 | tf_op jit(solution)/shard_map/ppermute | solution.py:411
  46.8 0.1 shard_map.150
  46.9 0.5 collective-permute-start.19
  47.3 2.6 %collective-permute-start.12 = (bf16[192,128]{1,0:T(8,128)(2,1)S(1)}, bf16[192,128]{1,0:T(8,128)(2,1)S(1)}, u32[]{:S(2)}, u32[]{:S(2)}) collective-permute-start(bf16[192,128]{1,0:T(8,128)(2,1)S(1)} %get-tuple-element.84), channel_id=1, source_target_pairs={{0,12},{4,0},{8,4},{12,8},{1,13},{5,1},{9,5},{13,9},{2,14},{6,2},{... | collective-permute-start | bytes 147464 | tf_op jit(solution)/shard_map/ppermute | solution.py:404
  50.0 0.2 collective-permute-start.13
  50.2 0.3 collective-permute-start.14
  50.5 3.9 %collective-permute-done.19.refs_1_ = bf16[864,128]{1,0:T(8,128)(2,1)S(1)} collective-permute-done((bf16[864,128]{1,0:T(8,128)(2,1)S(1)}, bf16[864,128]{1,0:T(8,128)(2,1)S(1)}, u32[]{:S(2)}, u32[]{:S(2)}) %collective-permute-start.19) | collective-permute-done | bytes 221216 | tf_op jit(solution)/shard_map/ppermute | solution.py:411
  54.4 0.1 shard_map.152.refs_11_.refs_0_
  54.5 1.3 %collective-permute-start.25 = (bf16[864,128]{1,0:T(8,128)(2,1)S(1)}, bf16[864,128]{1,0:T(8,128)(2,1)S(1)}, u32[]{:S(2)}, u32[]{:S(2)}) collective-permute-start(bf16[864,128]{1,0:T(8,128)(2,1)S(1)} %shard_map.152.refs_11_.refs_0_), channel_id=1, source_target_pairs={{0,4},{4,0},{8,12},{12,8},{1,5},{5,1},{9,13},{13,9},{2,6},{6,2},{1... | collective-permute-start | bytes 663560 | tf_op jit(solution)/shard_map/ppermute | solution.py:411
  55.8 0.3 collective-permute-done.14.refs_3_
  56.1 0.4 shard_map.151
  56.5 0.1 collective-permute-start.16
  56.5 1.6 %collective-permute-start.17 = (bf16[192,128]{1,0:T(8,128)(2,1)S(1)}, bf16[192,128]{1,0:T(8,128)(2,1)S(1)}, u32[]{:S(2)}, u32[]{:S(2)}) collective-permute-start(bf16[192,128]{1,0:T(8,128)(2,1)S(1)} %get-tuple-element.93), channel_id=1, source_target_pairs={{0,2},{1,3},{2,0},{3,1},{4,6},{5,7},{6,4},{7,5},{8,10},{9,11},{10,... | collective-permute-start | bytes 147464 | tf_op jit(solution)/shard_map/ppermute | solution.py:404
  58.2 1.4 %collective-permute-start.18 = (bf16[192,128]{1,0:T(8,128)(2,1)S(1)}, bf16[192,128]{1,0:T(8,128)(2,1)S(1)}, u32[]{:S(2)}, u32[]{:S(2)}) collective-permute-start(bf16[192,128]{1,0:T(8,128)(2,1)S(1)} %get-tuple-element.94), channel_id=1, source_target_pairs={{0,3},{1,0},{2,1},{3,2},{4,7},{5,4},{6,5},{7,6},{8,11},{9,8},{10,9... | collective-permute-start | bytes 147464 | tf_op jit(solution)/shard_map/ppermute | solution.py:404
  59.5 0.5 collective-permute-done.16.refs_1_
  60.0 0.7 collective-permute-done.17.refs_2_
  60.7 0.6 collective-permute-done.18.refs_3_
  61.3 6.0 %shard_map.153 = (bf16[192,128]{1,0:T(8,128)(2,1)S(1)}, bf16[192,128]{1,0:T(8,128)(2,1)S(1)}, bf16[192,128]{1,0:T(8,128)(2,1)S(1)}, bf16[192,128]{1,0:T(8,128)(2...) custom-call(bf16[192,128]{1,0:T(8,128)(2,1)S(1)} %get-tuple-element.91.refs_0_, ...), custom_call_target="tpu_custom_call" | custom-call | tf_op jit(solution)/shard_map/pallas_call | solution.py:387
  67.3 0.7 collective-permute-start.23
  67.9 1.0 %collective-permute-done.23.refs_1_ = bf16[576,128]{1,0:T(8,128)(2,1)S(1)} collective-permute-done((bf16[576,128]{1,0:T(8,128)(2,1)S(1)}, bf16[576,128]{1,0:T(8,128)(2,1)S(1)}, u32[]{:S(2)}, u32[]{:S(2)}) %collective-permute-start.23) | collective-permute-done | bytes 147488 | tf_op jit(solution)/shard_map/ppermute | solution.py:411
  69.0 0.1 shard_map.155.refs_2_.refs_0_
  69.0 1.4 %collective-permute-start.28 = (bf16[864,128]{1,0:T(8,128)(2,1)S(1)}, bf16[864,128]{1,0:T(8,128)(2,1)S(1)}, u32[]{:S(2)}, u32[]{:S(2)}) collective-permute-start(bf16[864,128]{1,0:T(8,128)(2,1)S(1)} %shard_map.155.refs_2_.refs_0_), channel_id=1, source_target_pairs={{0,8},{4,12},{8,0},{12,4},{1,9},{5,13},{9,1},{13,5},{2,10},{6,14},... | collective-permute-start | bytes 663560 | tf_op jit(solution)/shard_map/ppermute | solution.py:411
  70.4 0.9 collective-permute-start.24
  71.3 3.5 %collective-permute-done.24.refs_1_ = bf16[288,128]{1,0:T(8,128)(2,1)S(1)} collective-permute-done((bf16[288,128]{1,0:T(8,128)(2,1)S(1)}, bf16[288,128]{1,0:T(8,128)(2,1)S(1)}, u32[]{:S(2)}, u32[]{:S(2)}) %collective-permute-start.24) | collective-permute-done | bytes 73760 | tf_op jit(solution)/shard_map/ppermute | solution.py:411
  74.8 0.7 collective-permute-start.26
  75.5 1.1 %collective-permute-start.21 = (bf16[192,128]{1,0:T(8,128)(2,1)S(1)}, bf16[192,128]{1,0:T(8,128)(2,1)S(1)}, u32[]{:S(2)}, u32[]{:S(2)}) collective-permute-start(bf16[192,128]{1,0:T(8,128)(2,1)S(1)} %get-tuple-element.103), channel_id=1, source_target_pairs={{0,2},{1,3},{2,0},{3,1},{4,6},{5,7},{6,4},{7,5},{8,10},{9,11},{10,... | collective-permute-start | bytes 147464 | tf_op jit(solution)/shard_map/ppermute | solution.py:404
  76.6 0.2 collective-permute-start.22
  76.8 0.4 collective-permute-done.20.refs_1_
  77.2 2.6 %collective-permute-done.21.refs_2_ = bf16[192,128]{1,0:T(8,128)(2,1)S(1)} collective-permute-done((bf16[192,128]{1,0:T(8,128)(2,1)S(1)}, bf16[192,128]{1,0:T(8,128)(2,1)S(1)}, u32[]{:S(2)}, u32[]{:S(2)}) %collective-permute-start.21) | collective-permute-done | bytes 49184 | tf_op jit(solution)/shard_map/ppermute | solution.py:404
  79.9 0.3 collective-permute-done.22.refs_3_
  80.2 1.1 %shard_map.157.refs_2_ = bf16[8,12288]{1,0:T(8,128)(2,1)} custom-call(bf16[192,128]{1,0:T(8,128)(2,1)S(1)} %get-tuple-element.101.refs_0_, bf16[192,128]{1,0:T(8,128)(2,1)S(1)} %collective-permute-done.20.refs_1_, bf16[192,128]{1,0:T(8,128)(2,1)S(1)} %collective-permute-done.21.refs_2_, bf16[192,128]{1,0:T(8,128)(2,1)S(1)} %collective-permute-done.22.refs_3_, ...), custom_call_target="tpu_custom_call" | custom-call | tf_op jit(solution)/shard_map/pallas_call | solution.py:387
  81.3 1.9 %collective-permute-done.26.refs_1_ = bf16[288,128]{1,0:T(8,128)(2,1)S(1)} collective-permute-done((bf16[288,128]{1,0:T(8,128)(2,1)S(1)}, bf16[288,128]{1,0:T(8,128)(2,1)S(1)}, u32[]{:S(2)}, u32[]{:S(2)}) %collective-permute-start.26) | collective-permute-done | bytes 73760 | tf_op jit(solution)/shard_map/ppermute | solution.py:411
  83.2 0.9 copy-done
  84.2 0.1 shard_map.159.refs_2_.refs_0_
  84.3 0.7 collective-permute-start.33
  85.0 0.1 collective-permute-start.27
  85.0 5.2 %collective-permute-done.33.refs_2_ = bf16[864,128]{1,0:T(8,128)(2,1)S(1)} collective-permute-done((bf16[864,128]{1,0:T(8,128)(2,1)S(1)}, bf16[864,128]{1,0:T(8,128)(2,1)S(1)}, u32[]{:S(2)}, u32[]{:S(2)}) %collective-permute-start.33) | collective-permute-done | bytes 221216 | tf_op jit(solution)/shard_map/ppermute | solution.py:411
  90.3 1.4 %collective-permute-start.30 = (bf16[288,128]{1,0:T(8,128)(2,1)S(1)}, bf16[288,128]{1,0:T(8,128)(2,1)S(1)}, u32[]{:S(2)}, u32[]{:S(2)}) collective-permute-start(bf16[288,128]{1,0:T(8,128)(2,1)S(1)} %shard_map.160.refs_0_), channel_id=1, source_target_pairs={{0,2},{1,3},{2,0},{3,1},{4,6},{5,7},{6,4},{7,5},{8,10},{9,11},{10,... | collective-permute-start | bytes 221192 | tf_op jit(solution)/shard_map/ppermute | solution.py:411
  91.7 3.3 %collective-permute-done.30.refs_2_ = bf16[288,128]{1,0:T(8,128)(2,1)S(1)} collective-permute-done((bf16[288,128]{1,0:T(8,128)(2,1)S(1)}, bf16[288,128]{1,0:T(8,128)(2,1)S(1)}, u32[]{:S(2)}, u32[]{:S(2)}) %collective-permute-start.30) | collective-permute-done | bytes 73760 | tf_op jit(solution)/shard_map/ppermute | solution.py:411
  95.0 1.3 %collective-permute-done.31.refs_3_ = bf16[288,128]{1,0:T(8,128)(2,1)S(1)} collective-permute-done((bf16[288,128]{1,0:T(8,128)(2,1)S(1)}, bf16[288,128]{1,0:T(8,128)(2,1)S(1)}, u32[]{:S(2)}, u32[]{:S(2)}) %collective-permute-start.31) | collective-permute-done | bytes 73760 | tf_op jit(solution)/shard_map/ppermute | solution.py:411
  96.3 0.9 shard_map.161
  97.2 1.4 %shard_map.162 = (f32[192,576]{1,0:T(8,128)}, f32[192,192]{1,0:T(8,128)}, f32[192,768]{1,0:T(8,128)}, f32[192,768]{1,0:T(8,128)}) custom-call(bf16[864,128]{1,0:T(8,128)(2,1)S(1)} %shard_map.159.refs_2_.refs_0_, bf16[864,128]{1,0:T(8,128)(2,1)S(1)} %collective-permute-done.32.refs_1_, bf16[864,128]{1,0:T(8,128)(2,1)S(1)} %collective-permute-done.33.refs_2_, ...), custom_call_target="tpu_custom_call" | custom-call | tf_op jit(solution)/shard_map/pallas_call | solution.py:387
  (29 shorter events, 0.2 us)
Async XLA Ops:
  0.6 29.1 %copy-start.1 = (s32[32]{0:T(128)S(1)}, s32[32]{0:T(128)}, u32[]{:S(2)}) copy-start(s32[32]{0:T(128)} %param.17) | copy-start | bytes 388
  2.1 6.6 %collective-permute-start = (bf16[192,128]{1,0:T(8,128)(2,1)S(1)}, bf16[192,128]{1,0:T(8,128)(2,1)S(1)}, u32[]{:S(2)}, u32[]{:S(2)}) collective-permute-start(bf16[192,128]{1,0:T(8,128)(2,1)S(1)} %get-tuple-element.62), channel_id=1, source_target_pairs={{0,1},{1,2},{2,3},{3,0},{4,5},{5,6},{6,7},{7,4},{8,9},{9,10},{10,1... | collective-permute-start | bytes 147464 | tf_op jit(solution)/shard_map/ppermute | solution.py:404
  2.6 6.1 %collective-permute-start.1 = (bf16[192,128]{1,0:T(8,128)(2,1)S(1)}, bf16[192,128]{1,0:T(8,128)(2,1)S(1)}, u32[]{:S(2)}, u32[]{:S(2)}) collective-permute-start(bf16[192,128]{1,0:T(8,128)(2,1)S(1)} %get-tuple-element.63), channel_id=1, source_target_pairs={{0,2},{1,3},{2,0},{3,1},{4,6},{5,7},{6,4},{7,5},{8,10},{9,11},{10,... | collective-permute-start | bytes 147464 | tf_op jit(solution)/shard_map/ppermute | solution.py:404
  5.2 3.5 %collective-permute-start.2 = (bf16[192,128]{1,0:T(8,128)(2,1)S(1)}, bf16[192,128]{1,0:T(8,128)(2,1)S(1)}, u32[]{:S(2)}, u32[]{:S(2)}) collective-permute-start(bf16[192,128]{1,0:T(8,128)(2,1)S(1)} %get-tuple-element.64), channel_id=1, source_target_pairs={{0,3},{1,0},{2,1},{3,2},{4,7},{5,4},{6,5},{7,6},{8,11},{9,8},{10,9... | collective-permute-start | bytes 147464 | tf_op jit(solution)/shard_map/ppermute | solution.py:404
  13.7 6.1 %collective-permute-start.3 = (bf16[192,128]{1,0:T(8,128)(2,1)S(1)}, bf16[192,128]{1,0:T(8,128)(2,1)S(1)}, u32[]{:S(2)}, u32[]{:S(2)}) collective-permute-start(bf16[192,128]{1,0:T(8,128)(2,1)S(1)} %get-tuple-element.68), channel_id=1, source_target_pairs={{0,3},{1,0},{2,1},{3,2},{4,7},{5,4},{6,5},{7,6},{8,11},{9,8},{10,9... | collective-permute-start | bytes 147464 | tf_op jit(solution)/shard_map/ppermute | solution.py:404
  15.1 6.1 %collective-permute-start.4 = (bf16[192,128]{1,0:T(8,128)(2,1)S(1)}, bf16[192,128]{1,0:T(8,128)(2,1)S(1)}, u32[]{:S(2)}, u32[]{:S(2)}) collective-permute-start(bf16[192,128]{1,0:T(8,128)(2,1)S(1)} %get-tuple-element.69), channel_id=1, source_target_pairs={{0,2},{1,3},{2,0},{3,1},{4,6},{5,7},{6,4},{7,5},{8,10},{9,11},{10,... | collective-permute-start | bytes 147464 | tf_op jit(solution)/shard_map/ppermute | solution.py:404
  15.4 5.8 %collective-permute-start.5 = (bf16[192,128]{1,0:T(8,128)(2,1)S(1)}, bf16[192,128]{1,0:T(8,128)(2,1)S(1)}, u32[]{:S(2)}, u32[]{:S(2)}) collective-permute-start(bf16[192,128]{1,0:T(8,128)(2,1)S(1)} %get-tuple-element.70), channel_id=1, source_target_pairs={{0,1},{1,2},{2,3},{3,0},{4,5},{5,6},{6,7},{7,4},{8,9},{9,10},{10,1... | collective-permute-start | bytes 147464 | tf_op jit(solution)/shard_map/ppermute | solution.py:404
  15.4 8.8 %collective-permute-start.9 = (bf16[192,128]{1,0:T(8,128)(2,1)S(1)}, bf16[192,128]{1,0:T(8,128)(2,1)S(1)}, u32[]{:S(2)}, u32[]{:S(2)}) collective-permute-start(bf16[192,128]{1,0:T(8,128)(2,1)S(1)} %get-tuple-element.76), channel_id=1, source_target_pairs={{0,4},{4,8},{8,12},{12,0},{1,5},{5,9},{9,13},{13,1},{2,6},{6,10},{... | collective-permute-start | bytes 147464 | tf_op jit(solution)/shard_map/ppermute | solution.py:404
  17.2 8.3 %collective-permute-start.10 = (bf16[192,128]{1,0:T(8,128)(2,1)S(1)}, bf16[192,128]{1,0:T(8,128)(2,1)S(1)}, u32[]{:S(2)}, u32[]{:S(2)}) collective-permute-start(bf16[192,128]{1,0:T(8,128)(2,1)S(1)} %get-tuple-element.77), channel_id=1, source_target_pairs={{0,8},{4,12},{8,0},{12,4},{1,9},{5,13},{9,1},{13,5},{2,10},{6,14},... | collective-permute-start | bytes 147464 | tf_op jit(solution)/shard_map/ppermute | solution.py:404
  19.8 5.7 %collective-permute-start.11 = (bf16[192,128]{1,0:T(8,128)(2,1)S(1)}, bf16[192,128]{1,0:T(8,128)(2,1)S(1)}, u32[]{:S(2)}, u32[]{:S(2)}) collective-permute-start(bf16[192,128]{1,0:T(8,128)(2,1)S(1)} %get-tuple-element.78), channel_id=1, source_target_pairs={{0,12},{4,0},{8,4},{12,8},{1,13},{5,1},{9,5},{13,9},{2,14},{6,2},{... | collective-permute-start | bytes 147464 | tf_op jit(solution)/shard_map/ppermute | solution.py:404
  21.5 6.6 %collective-permute-start.6 = (bf16[192,128]{1,0:T(8,128)(2,1)S(1)}, bf16[192,128]{1,0:T(8,128)(2,1)S(1)}, u32[]{:S(2)}, u32[]{:S(2)}) collective-permute-start(bf16[192,128]{1,0:T(8,128)(2,1)S(1)} %get-tuple-element.72), channel_id=1, source_target_pairs={{0,4},{4,8},{8,12},{12,0},{1,5},{5,9},{9,13},{13,1},{2,6},{6,10},{... | collective-permute-start | bytes 147464 | tf_op jit(solution)/shard_map/ppermute | solution.py:404
  22.2 7.5 %collective-permute-start.7 = (bf16[192,128]{1,0:T(8,128)(2,1)S(1)}, bf16[192,128]{1,0:T(8,128)(2,1)S(1)}, u32[]{:S(2)}, u32[]{:S(2)}) collective-permute-start(bf16[192,128]{1,0:T(8,128)(2,1)S(1)} %get-tuple-element.73), channel_id=1, source_target_pairs={{0,8},{4,12},{8,0},{12,4},{1,9},{5,13},{9,1},{13,5},{2,10},{6,14},... | collective-permute-start | bytes 147464 | tf_op jit(solution)/shard_map/ppermute | solution.py:404
  24.2 5.5 %collective-permute-start.8 = (bf16[192,128]{1,0:T(8,128)(2,1)S(1)}, bf16[192,128]{1,0:T(8,128)(2,1)S(1)}, u32[]{:S(2)}, u32[]{:S(2)}) collective-permute-start(bf16[192,128]{1,0:T(8,128)(2,1)S(1)} %get-tuple-element.74), channel_id=1, source_target_pairs={{0,12},{4,0},{8,4},{12,8},{1,13},{5,1},{9,5},{13,9},{2,14},{6,2},{... | collective-permute-start | bytes 147464 | tf_op jit(solution)/shard_map/ppermute | solution.py:404
  44.9 1.9 %collective-permute-start.15 = (bf16[1728,128]{1,0:T(8,128)(2,1)S(1)}, bf16[1728,128]{1,0:T(8,128)(2,1)S(1)}, u32[]{:S(2)}, u32[]{:S(2)}) collective-permute-start(bf16[1728,128]{1,0:T(8,128)(2,1)S(1)} %get-tuple-element.89), channel_id=1, source_target_pairs={{0,1},{1,0},{2,3},{3,2},{4,5},{5,4},{6,7},{7,6},{8,9},{9,8},{10,11... | collective-permute-start | bytes 1327112 | tf_op jit(solution)/shard_map/ppermute | solution.py:411
  46.9 7.5 %collective-permute-start.19 = (bf16[864,128]{1,0:T(8,128)(2,1)S(1)}, bf16[864,128]{1,0:T(8,128)(2,1)S(1)}, u32[]{:S(2)}, u32[]{:S(2)}) collective-permute-start(bf16[864,128]{1,0:T(8,128)(2,1)S(1)} %get-tuple-element.100), channel_id=1, source_target_pairs={{0,2},{1,3},{2,0},{3,1},{4,6},{5,7},{6,4},{7,5},{8,10},{9,11},{10,... | collective-permute-start | bytes 663560 | tf_op jit(solution)/shard_map/ppermute | solution.py:411
  47.3 8.4 %collective-permute-start.12 = (bf16[192,128]{1,0:T(8,128)(2,1)S(1)}, bf16[192,128]{1,0:T(8,128)(2,1)S(1)}, u32[]{:S(2)}, u32[]{:S(2)}) collective-permute-start(bf16[192,128]{1,0:T(8,128)(2,1)S(1)} %get-tuple-element.84), channel_id=1, source_target_pairs={{0,12},{4,0},{8,4},{12,8},{1,13},{5,1},{9,5},{13,9},{2,14},{6,2},{... | collective-permute-start | bytes 147464 | tf_op jit(solution)/shard_map/ppermute | solution.py:404
  50.0 5.8 %collective-permute-start.13 = (bf16[192,128]{1,0:T(8,128)(2,1)S(1)}, bf16[192,128]{1,0:T(8,128)(2,1)S(1)}, u32[]{:S(2)}, u32[]{:S(2)}) collective-permute-start(bf16[192,128]{1,0:T(8,128)(2,1)S(1)} %get-tuple-element.85), channel_id=1, source_target_pairs={{0,8},{4,12},{8,0},{12,4},{1,9},{5,13},{9,1},{13,5},{2,10},{6,14},... | collective-permute-start | bytes 147464 | tf_op jit(solution)/shard_map/ppermute | solution.py:404
  50.2 5.9 %collective-permute-start.14 = (bf16[192,128]{1,0:T(8,128)(2,1)S(1)}, bf16[192,128]{1,0:T(8,128)(2,1)S(1)}, u32[]{:S(2)}, u32[]{:S(2)}) collective-permute-start(bf16[192,128]{1,0:T(8,128)(2,1)S(1)} %get-tuple-element.86), channel_id=1, source_target_pairs={{0,4},{4,8},{8,12},{12,0},{1,5},{5,9},{9,13},{13,1},{2,6},{6,10},{... | collective-permute-start | bytes 147464 | tf_op jit(solution)/shard_map/ppermute | solution.py:404
  54.5 14.5 %collective-permute-start.25 = (bf16[864,128]{1,0:T(8,128)(2,1)S(1)}, bf16[864,128]{1,0:T(8,128)(2,1)S(1)}, u32[]{:S(2)}, u32[]{:S(2)}) collective-permute-start(bf16[864,128]{1,0:T(8,128)(2,1)S(1)} %shard_map.152.refs_11_.refs_0_), channel_id=1, source_target_pairs={{0,4},{4,0},{8,12},{12,8},{1,5},{5,1},{9,13},{13,9},{2,6},{6,2},{1... | collective-permute-start | bytes 663560 | tf_op jit(solution)/shard_map/ppermute | solution.py:411
  56.5 3.6 %collective-permute-start.16 = (bf16[192,128]{1,0:T(8,128)(2,1)S(1)}, bf16[192,128]{1,0:T(8,128)(2,1)S(1)}, u32[]{:S(2)}, u32[]{:S(2)}) collective-permute-start(bf16[192,128]{1,0:T(8,128)(2,1)S(1)} %get-tuple-element.92), channel_id=1, source_target_pairs={{0,1},{1,2},{2,3},{3,0},{4,5},{5,6},{6,7},{7,4},{8,9},{9,10},{10,1... | collective-permute-start | bytes 147464 | tf_op jit(solution)/shard_map/ppermute | solution.py:404
  56.5 4.2 %collective-permute-start.17 = (bf16[192,128]{1,0:T(8,128)(2,1)S(1)}, bf16[192,128]{1,0:T(8,128)(2,1)S(1)}, u32[]{:S(2)}, u32[]{:S(2)}) collective-permute-start(bf16[192,128]{1,0:T(8,128)(2,1)S(1)} %get-tuple-element.93), channel_id=1, source_target_pairs={{0,2},{1,3},{2,0},{3,1},{4,6},{5,7},{6,4},{7,5},{8,10},{9,11},{10,... | collective-permute-start | bytes 147464 | tf_op jit(solution)/shard_map/ppermute | solution.py:404
  58.2 3.1 %collective-permute-start.18 = (bf16[192,128]{1,0:T(8,128)(2,1)S(1)}, bf16[192,128]{1,0:T(8,128)(2,1)S(1)}, u32[]{:S(2)}, u32[]{:S(2)}) collective-permute-start(bf16[192,128]{1,0:T(8,128)(2,1)S(1)} %get-tuple-element.94), channel_id=1, source_target_pairs={{0,3},{1,0},{2,1},{3,2},{4,7},{5,4},{6,5},{7,6},{8,11},{9,8},{10,9... | collective-permute-start | bytes 147464 | tf_op jit(solution)/shard_map/ppermute | solution.py:404
  67.3 1.7 %collective-permute-start.23 = (bf16[576,128]{1,0:T(8,128)(2,1)S(1)}, bf16[576,128]{1,0:T(8,128)(2,1)S(1)}, u32[]{:S(2)}, u32[]{:S(2)}) collective-permute-start(bf16[576,128]{1,0:T(8,128)(2,1)S(1)} %get-tuple-element.106), channel_id=1, source_target_pairs={{0,1},{1,0},{2,3},{3,2},{4,5},{5,4},{6,7},{7,6},{8,9},{9,8},{10,11... | collective-permute-start | bytes 442376 | tf_op jit(solution)/shard_map/ppermute | solution.py:411
  69.0 15.1 %collective-permute-start.28 = (bf16[864,128]{1,0:T(8,128)(2,1)S(1)}, bf16[864,128]{1,0:T(8,128)(2,1)S(1)}, u32[]{:S(2)}, u32[]{:S(2)}) collective-permute-start(bf16[864,128]{1,0:T(8,128)(2,1)S(1)} %shard_map.155.refs_2_.refs_0_), channel_id=1, source_target_pairs={{0,8},{4,12},{8,0},{12,4},{1,9},{5,13},{9,1},{13,5},{2,10},{6,14},... | collective-permute-start | bytes 663560 | tf_op jit(solution)/shard_map/ppermute | solution.py:411
  70.4 4.4 %collective-permute-start.24 = (bf16[288,128]{1,0:T(8,128)(2,1)S(1)}, bf16[288,128]{1,0:T(8,128)(2,1)S(1)}, u32[]{:S(2)}, u32[]{:S(2)}) collective-permute-start(bf16[288,128]{1,0:T(8,128)(2,1)S(1)} %get-tuple-element.108), channel_id=1, source_target_pairs={{0,2},{1,3},{2,0},{3,1},{4,6},{5,7},{6,4},{7,5},{8,10},{9,11},{10,... | collective-permute-start | bytes 221192 | tf_op jit(solution)/shard_map/ppermute | solution.py:411
  74.8 8.5 %collective-permute-start.26 = (bf16[288,128]{1,0:T(8,128)(2,1)S(1)}, bf16[288,128]{1,0:T(8,128)(2,1)S(1)}, u32[]{:S(2)}, u32[]{:S(2)}) collective-permute-start(bf16[288,128]{1,0:T(8,128)(2,1)S(1)} %shard_map.156.refs_4_.refs_0_), channel_id=1, source_target_pairs={{0,4},{4,0},{8,12},{12,8},{1,5},{5,1},{9,13},{13,9},{2,6},{6,2},{1... | collective-permute-start | bytes 221192 | tf_op jit(solution)/shard_map/ppermute | solution.py:411
  75.5 1.8 %collective-permute-start.20 = (bf16[192,128]{1,0:T(8,128)(2,1)S(1)}, bf16[192,128]{1,0:T(8,128)(2,1)S(1)}, u32[]{:S(2)}, u32[]{:S(2)}) collective-permute-start(bf16[192,128]{1,0:T(8,128)(2,1)S(1)} %get-tuple-element.102), channel_id=1, source_target_pairs={{0,3},{1,0},{2,1},{3,2},{4,7},{5,4},{6,5},{7,6},{8,11},{9,8},{10,9... | collective-permute-start | bytes 147464 | tf_op jit(solution)/shard_map/ppermute | solution.py:404
  75.5 4.4 %collective-permute-start.21 = (bf16[192,128]{1,0:T(8,128)(2,1)S(1)}, bf16[192,128]{1,0:T(8,128)(2,1)S(1)}, u32[]{:S(2)}, u32[]{:S(2)}) collective-permute-start(bf16[192,128]{1,0:T(8,128)(2,1)S(1)} %get-tuple-element.103), channel_id=1, source_target_pairs={{0,2},{1,3},{2,0},{3,1},{4,6},{5,7},{6,4},{7,5},{8,10},{9,11},{10,... | collective-permute-start | bytes 147464 | tf_op jit(solution)/shard_map/ppermute | solution.py:404
  76.6 3.6 %collective-permute-start.22 = (bf16[192,128]{1,0:T(8,128)(2,1)S(1)}, bf16[192,128]{1,0:T(8,128)(2,1)S(1)}, u32[]{:S(2)}, u32[]{:S(2)}) collective-permute-start(bf16[192,128]{1,0:T(8,128)(2,1)S(1)} %get-tuple-element.104), channel_id=1, source_target_pairs={{0,1},{1,2},{2,3},{3,0},{4,5},{5,6},{6,7},{7,4},{8,9},{9,10},{10,1... | collective-permute-start | bytes 147464 | tf_op jit(solution)/shard_map/ppermute | solution.py:404
  83.2 0.9 copy-start
  84.3 6.0 %collective-permute-start.33 = (bf16[864,128]{1,0:T(8,128)(2,1)S(1)}, bf16[864,128]{1,0:T(8,128)(2,1)S(1)}, u32[]{:S(2)}, u32[]{:S(2)}) collective-permute-start(bf16[864,128]{1,0:T(8,128)(2,1)S(1)} %shard_map.159.refs_2_.refs_0_), channel_id=1, source_target_pairs={{0,2},{1,3},{2,0},{3,1},{4,6},{5,7},{6,4},{7,5},{8,10},{9,11},{10,... | collective-permute-start | bytes 663560 | tf_op jit(solution)/shard_map/ppermute | solution.py:411
  85.0 5.3 %collective-permute-start.27 = (bf16[288,128]{1,0:T(8,128)(2,1)S(1)}, bf16[288,128]{1,0:T(8,128)(2,1)S(1)}, u32[]{:S(2)}, u32[]{:S(2)}) collective-permute-start(bf16[288,128]{1,0:T(8,128)(2,1)S(1)} %shard_map.158.refs_2_.refs_0_), channel_id=1, source_target_pairs={{0,8},{4,12},{8,0},{12,4},{1,9},{5,13},{9,1},{13,5},{2,10},{6,14},... | collective-permute-start | bytes 221192 | tf_op jit(solution)/shard_map/ppermute | solution.py:411
  85.0 12.2 %collective-permute-start.32 = (bf16[864,128]{1,0:T(8,128)(2,1)S(1)}, bf16[864,128]{1,0:T(8,128)(2,1)S(1)}, u32[]{:S(2)}, u32[]{:S(2)}) collective-permute-start(bf16[864,128]{1,0:T(8,128)(2,1)S(1)} %shard_map.159.refs_2_.refs_0_), channel_id=1, source_target_pairs={{0,1},{1,0},{2,3},{3,2},{4,5},{5,4},{6,7},{7,6},{8,9},{9,8},{10,11... | collective-permute-start | bytes 663560 | tf_op jit(solution)/shard_map/ppermute | solution.py:411
  90.3 7.0 %collective-permute-start.34 = (bf16[864,128]{1,0:T(8,128)(2,1)S(1)}, bf16[864,128]{1,0:T(8,128)(2,1)S(1)}, u32[]{:S(2)}, u32[]{:S(2)}) collective-permute-start(bf16[864,128]{1,0:T(8,128)(2,1)S(1)} %collective-permute-done.33.refs_2_), channel_id=1, source_target_pairs={{0,1},{1,0},{2,3},{3,2},{4,5},{5,4},{6,7},{7,6},{8,9},{9,8},{10,11... | collective-permute-start | bytes 663560 | tf_op jit(solution)/shard_map/ppermute | solution.py:411
  90.3 4.7 %collective-permute-start.30 = (bf16[288,128]{1,0:T(8,128)(2,1)S(1)}, bf16[288,128]{1,0:T(8,128)(2,1)S(1)}, u32[]{:S(2)}, u32[]{:S(2)}) collective-permute-start(bf16[288,128]{1,0:T(8,128)(2,1)S(1)} %shard_map.160.refs_0_), channel_id=1, source_target_pairs={{0,2},{1,3},{2,0},{3,1},{4,6},{5,7},{6,4},{7,5},{8,10},{9,11},{10,... | collective-permute-start | bytes 221192 | tf_op jit(solution)/shard_map/ppermute | solution.py:411
  91.7 3.3 %collective-permute-start.29 = (bf16[288,128]{1,0:T(8,128)(2,1)S(1)}, bf16[288,128]{1,0:T(8,128)(2,1)S(1)}, u32[]{:S(2)}, u32[]{:S(2)}) collective-permute-start(bf16[288,128]{1,0:T(8,128)(2,1)S(1)} %shard_map.160.refs_0_), channel_id=1, source_target_pairs={{0,1},{1,0},{2,3},{3,2},{4,5},{5,4},{6,7},{7,6},{8,9},{9,8},{10,11... | collective-permute-start | bytes 221192 | tf_op jit(solution)/shard_map/ppermute | solution.py:411
  95.0 1.3 %collective-permute-start.31 = (bf16[288,128]{1,0:T(8,128)(2,1)S(1)}, bf16[288,128]{1,0:T(8,128)(2,1)S(1)}, u32[]{:S(2)}, u32[]{:S(2)}) collective-permute-start(bf16[288,128]{1,0:T(8,128)(2,1)S(1)} %collective-permute-done.30.refs_2_), channel_id=1, source_target_pairs={{0,1},{1,0},{2,3},{3,2},{4,5},{5,4},{6,7},{7,6},{8,9},{9,8},{10,11... | collective-permute-start | bytes 221192 | tf_op jit(solution)/shard_map/ppermute | solution.py:411

commit v2 on v1

--- a/solution.py
+++ b/solution.py
@@ -20,6 +20,7 @@
 EXP2 = math.log2(math.e) / math.sqrt(HEAD)
 SCALE = 1.0 / math.sqrt(HEAD)
 HALF_ROOT = math.sqrt(0.5)
+BELL_EXP2 = -0.5 * math.log2(math.e)
 BELL = 1.0 / math.sqrt(2.0 * math.pi)
 
 
@@ -179,43 +180,105 @@
     return ref[start : start + HEAD, cols]
 
 
-def attend(x_ref, normed_ref, proj_ref, probs_ref, mixed_ref, qkv_t, out_t, width, mask):
+def staged(count, *stages):
+    held = {}
+    for step in range(count + len(stages) - 1):
+        for lag, stage in enumerate(stages):
+            unit = step - lag
+            if 0 <= unit < count:
+                held[unit] = stage(unit, held.get(unit))
+                if lag == len(stages) - 1:
+                    del held[unit]
+
+
+def units_of(total, width):
+    step = min(2 * LANES, width)
+    return [
+        (place, head, start, step, start == 0, start + step == width)
+        for place in range(total // width)
+        for head in range(HEADS)
+        for start in range(0, width, step)
+    ]
+
+
+def attend(x_ref, normed_ref, proj_ref, probs_ref, mixed_ref, qkv_t, out_t, width, mask_ref):
+    total = x_ref.shape[1]
+    for cols in blocks_of(2 * LANES, total):
+        normed_ref[:, cols] = norm(x_ref[:, cols].astype(F32))[0].astype(BF)
+    for cols in blocks_of(2 * LANES, total):
+        proj_ref[:, cols] = nn(qkv_t[...], normed_ref[:, cols]).astype(BF)
+    units = units_of(total, width)
+
+    def score(unit, _):
+        place, head, start, step, _, _ = units[unit]
+        cols = slice(place * width + start, place * width + start + step)
+        keys = slice(place * width, (place + 1) * width)
+        return tn(heads_of(proj_ref, 1, head, keys), heads_of(proj_ref, 0, head, cols))
+
+    def weigh(unit, scores):
+        place, head, start, step, _, _ = units[unit]
+        if mask_ref is not None:
+            scores = scores + mask_ref[:, start : start + step]
+        expo = jnp.exp2((scores - jnp.max(scores, axis=0, keepdims=True)) * EXP2)
+        probs = (expo * (1.0 / jnp.sum(expo, axis=0, keepdims=True))).astype(BF)
+        probs_ref[place * HEADS + head, :, start : start + step] = probs
+        return probs
+
+    def mix(unit, probs):
+        place, head, start, step, _, _ = units[unit]
+        value = heads_of(proj_ref, 2, head, slice(place * width, (place + 1) * width))
+        cols = slice(place * width + start, place * width + start + step)
+        mixed_ref[head * HEAD : (head + 1) * HEAD, cols] = nn(value, probs).astype(BF)
+
+    staged(len(units), score, weigh, mix)
+    return [
+        x_ref[:, cols].astype(F32) + nn(out_t[...], mixed_ref[:, cols])
+        for cols in blocks_of(2 * LANES, total)
+    ]
+
+
+def attend_back(grad_ref, x_ref, proj_ref, probs_ref, grad_proj_ref, grad_mixed_ref, qkv, out, width):
+    total = x_ref.shape[1]
+    for cols in blocks_of(2 * LANES, total):
+        grad_mixed_ref[:, cols] = nn(out[...], grad_ref[:, cols]).astype(BF)
+    units = units_of(total, width)
+    sums = {}
+
+    def spans(unit):
+        place, head, start, step, _, _ = units[unit]
+        rows = slice(head * HEAD, (head + 1) * HEAD)
+        keys = slice(place * width, (place + 1) * width)
+        return rows, slice(place * width + start, place * width + start + step), keys
+
+    def probs_of(unit):
+        place, head, start, step, _, _ = units[unit]
+        return probs_ref[place * HEADS + head, :, start : start + step]
+
+    def to_probs(unit, _):
+        rows, cols, keys = spans(unit)
+        return tn(heads_of(proj_ref, 2, units[unit][1], keys), grad_mixed_ref[rows, cols])
+
+    def to_scores(unit, grad_probs):
+        wide = probs_of(unit).astype(F32)
+        moved = grad_probs * wide
+        return (moved - wide * jnp.sum(moved, axis=0, keepdims=True)).astype(BF)
+
+    def to_proj(unit, grad_scores):
+        _, head, _, _, first, last = units[unit]
+        rows, cols, keys = spans(unit)
+        query, key = heads_of(proj_ref, 0, head, cols), heads_of(proj_ref, 1, head, keys)
+        grad_proj_ref[rows, cols] = (nn(key, grad_scores) * SCALE).astype(BF)
+        both = nt(query, grad_scores), nt(grad_mixed_ref[rows, cols], probs_of(unit))
+        if not first:
+            both = both[0] + sums["key"], both[1] + sums["value"]
+        sums["key"], sums["value"] = both
+        if last:
+            grad_proj_ref[E + rows.start : E + rows.stop, keys] = (both[0] * SCALE).astype(BF)
+            grad_proj_ref[2 * E + rows.start : 2 * E + rows.stop, keys] = both[1].astype(BF)
+
+    staged(len(units), to_probs, to_scores, to_proj)
     results = []
-    for place, cols in enumerate(blocks_of(width, x_ref.shape[1])):
-        table = x_ref[:, cols].astype(F32)
-        normed_ref[:, cols] = norm(table)[0].astype(BF)
-        proj_ref[:, cols] = nn(qkv_t[...], normed_ref[:, cols]).astype(BF)
-        for head in range(HEADS):
-            query, key, value = (heads_of(proj_ref, part, head, cols) for part in range(3))
-            scores = tn(key, query)
-            if mask is not None:
-                scores = scores + mask
-            expo = jnp.exp2((scores - jnp.max(scores, axis=0, keepdims=True)) * EXP2)
-            probs = (expo * (1.0 / jnp.sum(expo, axis=0, keepdims=True))).astype(BF)
-            probs_ref[place * HEADS + head] = probs
-            mixed_ref[head * HEAD : (head + 1) * HEAD, cols] = nn(value, probs).astype(BF)
-        results.append(x_ref[:, cols].astype(F32) + nn(out_t[...], mixed_ref[:, cols]))
-    return results
-
-
-def attend_back(grad_ref, x_ref, proj_ref, probs_ref, grad_proj_ref, qkv, out, width):
-    results = []
-    for place, cols in enumerate(blocks_of(width, x_ref.shape[1])):
-        grad_mixed = nn(out[...], grad_ref[:, cols]).astype(BF)
-        for head in range(HEADS):
-            query, key, value = (heads_of(proj_ref, part, head, cols) for part in range(3))
-            grad_head = grad_mixed[head * HEAD : (head + 1) * HEAD]
-            probs = probs_ref[place * HEADS + head]
-            grad_probs = tn(value, grad_head).astype(BF).astype(F32)
-            wide = probs.astype(F32)
-            moved = grad_probs * wide
-            grad_scores = (moved - wide * jnp.sum(moved, axis=0, keepdims=True)) * SCALE
-            grad_scores = grad_scores.astype(BF)
-            for part, value_of in enumerate(
-                (nn(key, grad_scores), nt(query, grad_scores), nt(grad_head, probs))
-            ):
-                start = part * E + head * HEAD
-                grad_proj_ref[start : start + HEAD, cols] = value_of.astype(BF)
+    for cols in blocks_of(2 * LANES, total):
         grad_normed = nn(qkv[...], grad_proj_ref[:, cols]).astype(BF).astype(F32)
         normed, root = norm(x_ref[:, cols].astype(F32))
         results.append(norm_back(grad_normed, normed, root) + grad_ref[:, cols].astype(F32))
@@ -267,11 +330,11 @@
     tiles, refs = refs[: plan.ranks_attr], refs[plan.ranks_attr :]
     (qkv, out, x_ref, normed_ref, proj_ref, probs_ref, mixed_ref), refs = refs[:7], refs[7:]
     outs, refs = refs[: plan.ranks_attr], refs[plan.ranks_attr :]
-    keep_ref, send_ref, sums_ref, grad_ref, grad_proj_ref = refs
+    keep_ref, send_ref, sums_ref, grad_ref, grad_proj_ref, grad_mixed_ref = refs
     order = one_hot(plan.cells, plan.grouped_from_rows())
     grad_ref[...] = nn(side_by_side(tiles), order).astype(BF)
     wait()
-    grads = attend_back(grad_ref, x_ref, proj_ref, probs_ref, grad_proj_ref, qkv, out, plan.all_attr)
+    grads = attend_back(grad_ref, x_ref, proj_ref, probs_ref, grad_proj_ref, grad_mixed_ref, qkv, out, plan.all_attr)
     put_tiles(outs, nt(jnp.concatenate(grads, axis=1).astype(BF), order))
     put_attend_grads(sums_ref, normed_ref, grad_proj_ref, mixed_ref, grad_ref)
     put_halves(bits_of("attr")[0], sums_ref, keep_ref, send_ref)
@@ -283,7 +346,7 @@
     (train_ref, qkv, out, up, down, qkv_t, out_t, up_t), refs = refs[:8], refs[8:]
     outs, (sums_ref,), refs = refs[:count], refs[count : count + 1], refs[count + 1 :]
     x_ref, cot_ref, normed_ref, proj_ref, probs_ref, mixed_ref, second_ref = refs[:7]
-    pre_ref, hidden_ref, grad_pre_ref, grad_ref, grad_proj_ref = refs[7:]
+    pre_ref, hidden_ref, grad_pre_ref, grad_ref, grad_proj_ref, grad_mixed_ref, mask_ref = refs[7:]
     width = max(LANES, plan.all_rec)
     order = one_hot(plan.cells, plan.grouped_from_cols())
     x_ref[...] = nn(side_by_side(tiles), order).astype(BF)
@@ -296,10 +359,10 @@
     chosen = (record == lane_index(plan.all_rec)) & (train_ref[...] > 0)
     allowed = jnp.max(jnp.where(chosen, 1.0, 0.0), axis=1, keepdims=True) > 0.5
     asker = digits(lane_index(width), (width // plan.all_rec, plan.all_rec))[0]
-    mask = jnp.where(allowed & (sequence == asker), 0.0, -1e30)
-
-    second = attend(x_ref, normed_ref, proj_ref, probs_ref, mixed_ref, qkv_t, out_t, width, mask)
-    for cols, value in zip(blocks_of(width, plan.cells), second):
+    mask_ref[...] = jnp.where(allowed & (sequence == asker), 0.0, -1e30)
+
+    second = attend(x_ref, normed_ref, proj_ref, probs_ref, mixed_ref, qkv_t, out_t, width, mask_ref)
+    for cols, value in zip(blocks_of(2 * LANES, plan.cells), second):
         second_ref[:, cols] = value.astype(BF)
 
     table, root = norm(second_ref[...].astype(F32))
@@ -312,8 +375,8 @@
         pre = pre_ref[rows, :]
         gate = 0.5 + 0.5 * lax.erf(pre * HALF_ROOT)
         hidden_ref[rows, :] = (pre * gate).astype(BF)
-        slope = gate + pre * (jnp.exp(-0.5 * pre * pre) * BELL)
-        grad_pre_ref[rows, :] = grad_pre_ref[rows, :].astype(BF).astype(F32) * slope
+        slope = gate + pre * (jnp.exp2(pre * pre * BELL_EXP2) * BELL)
+        grad_pre_ref[rows, :] = grad_pre_ref[rows, :] * slope
     grad_pre = grad_pre_ref[...].astype(BF)
 
     for base, grad_weight in (
@@ -327,7 +390,7 @@
     grad_normed = nn(up[...], grad_pre).astype(BF).astype(F32)
     grad = norm_back(grad_normed, table, root) + cot_ref[...].astype(F32)
     grad_ref[...] = grad.astype(BF)
-    grads = attend_back(grad_ref, x_ref, proj_ref, probs_ref, grad_proj_ref, qkv, out, width)
+    grads = attend_back(grad_ref, x_ref, proj_ref, probs_ref, grad_proj_ref, grad_mixed_ref, qkv, out, width)
     put_tiles(outs, nt(jnp.concatenate(grads, axis=1).astype(BF), order))
     put_attend_grads(sums_ref, normed_ref, grad_proj_ref, mixed_ref, grad_ref)
 
@@ -518,7 +581,7 @@
         kernel(cols_kernel),
         col_tiles + [((cols_sums, LANES), BF)],
         [table, table, table, wide, probs(width), table, table]
-        + [((FF, count), F32), ((FF, count), BF), ((FF, count), F32), table, wide],
+        + [((FF, count), F32), ((FF, count), BF), ((FF, count), F32), table, wide, table, ((width, width), F32)],
         *cols,
         *cot,
         train_split.reshape(1, -1),
@@ -541,7 +604,7 @@
     got = call(
         kernel(rows_back_kernel),
         row_tiles + [((rows_sums // 2, LANES), BF)] * 2,
-        [((rows_sums, LANES), BF), table, wide],
+        [((rows_sums, LANES), BF), table, wide, table],
         *grads,
         Far(qkv_attr),
         Far(out_attr),

time: 98.9 us -> 86 us (0.87)
  Pallas kernels: 34.1 us -> 21.3 us
    pallas_call x19, Pallas kernels: 34.1 us -> 21.3 us  [call(): pl.pallas_call(kernel, out_shape=[(pltpu.VMEM if out[2:] else jax.ShapeDt...]
  transfers between devices with their start and end apart: 35 -> 35, of which waited for: 17 -> 17; matrix products, arithmetic and copies ran while one was open for 0% -> 0% of each run, Pallas kernels for 11% -> 10%
where the time goes in v2:
time: 86 us; the launch traced here: 85.8 us
  waiting for transfers between devices  31.6 us (37%)
  starting transfers between devices  31.1 us (36%)
  Pallas kernels  21.3 us (25%)
  local copies, waits for them, and re-layouts  0.93 us (1%)
    ppermute x21, starting transfers between devices, exchange(): lax.ppermute(tiles[k], axis, [(i, (i + sign * k) % size) for i in range(s...  23.5 us
    ppermute x14, waiting for transfers between devices, swap(): return lax.ppermute(part, axis, [(i, i ^ bit) for i in range(size)])  21.9 us
    pallas_call x19, Pallas kernels, call(): pl.pallas_call(kernel, out_shape=[(pltpu.VMEM if out[2:] else jax.ShapeDt...  21.3 us
    ppermute x21, waiting for transfers between devices, exchange(): lax.ppermute(tiles[k], axis, [(i, (i + sign * k) % size) for i in range(s...  9.69 us
    ppermute x14, starting transfers between devices, swap(): return lax.ppermute(part, axis, [(i, i ^ bit) for i in range(size)])  7.59 us
  transfers between devices with their start and end apart: 35, of which 17 were waited for; matrix products, arithmetic and copies ran while one was open for 0% of the time, Pallas kernels for 10%

profile of v2, /device:TPU:0, one launch (start us, length us, event | category | flops | bytes accessed | tf_op | source)
XLA Modules:
  0.0 85.8 jit_solution(3432800401099889952)
XLA Ops:
  0.6 1.5 %shard_map.144 = (bf16[192,128]{1,0:T(8,128)(2,1)S(1)}, bf16[192,128]{1,0:T(8,128)(2,1)S(1)}, bf16[192,128]{1,0:T(8,128)(2,1)S(1)}, bf16[192,128]{1,0:T(8,128)(2,1)S(1)}) custom-call(bf16[8,12288]{1,0:T(8,128)(2,1)} %refs_0_.2), custom_call_target="tpu_custom_call" | custom-call | tf_op jit(solution)/shard_map/pallas_call | solution.py:450
  2.1 0.5 collective-permute-start
  2.6 2.6 %collective-permute-start.1 = (bf16[192,128]{1,0:T(8,128)(2,1)S(1)}, bf16[192,128]{1,0:T(8,128)(2,1)S(1)}, u32[]{:S(2)}, u32[]{:S(2)}) collective-permute-start(bf16[192,128]{1,0:T(8,128)(2,1)S(1)} %get-tuple-element.63), channel_id=1, source_target_pairs={{0,2},{1,3},{2,0},{3,1},{4,6},{5,7},{6,4},{7,5},{8,10},{9,11},{10,... | collective-permute-start | bytes 147464 | tf_op jit(solution)/shard_map/ppermute | solution.py:467
  5.2 1.4 %collective-permute-start.2 = (bf16[192,128]{1,0:T(8,128)(2,1)S(1)}, bf16[192,128]{1,0:T(8,128)(2,1)S(1)}, u32[]{:S(2)}, u32[]{:S(2)}) collective-permute-start(bf16[192,128]{1,0:T(8,128)(2,1)S(1)} %get-tuple-element.64), channel_id=1, source_target_pairs={{0,3},{1,0},{2,1},{3,2},{4,7},{5,4},{6,5},{7,6},{8,11},{9,8},{10,9... | collective-permute-start | bytes 147464 | tf_op jit(solution)/shard_map/ppermute | solution.py:467
  6.6 2.1 %shard_map.145 = (bf16[192,128]{1,0:T(8,128)(2,1)S(1)}, bf16[192,128]{1,0:T(8,128)(2,1)S(1)}, bf16[192,128]{1,0:T(8,128)(2,1)S(1)}, bf16[192,128]{1,0:T(8,128)(2...) custom-call(bf16[8,12288]{1,0:T(8,128)(2,1)} %refs_0_.3, ...), custom_call_target="tpu_custom_call" | custom-call | tf_op jit(solution)/shard_map/pallas_call | solution.py:450
  8.7 0.0 collective-permute-done.1.refs_2_
  8.7 0.0 collective-permute-done.2.refs_3_
  8.7 2.6 %shard_map.146 = (bf16[192,128]{1,0:T(8,128)(2,1)S(1)}, bf16[192,128]{1,0:T(8,128)(2,1)S(1)}, bf16[192,128]{1,0:T(8,128)(2,1)S(1)}, bf16[192,128]{1,0:T(8,128)(2...) custom-call(bf16[192,128]{1,0:T(8,128)(2,1)S(1)} %get-tuple-element., ...), custom_call_target="tpu_custom_call" | custom-call | tf_op jit(solution)/shard_map/pallas_call | solution.py:450
  11.3 1.4 %collective-permute-start.3 = (bf16[192,128]{1,0:T(8,128)(2,1)S(1)}, bf16[192,128]{1,0:T(8,128)(2,1)S(1)}, u32[]{:S(2)}, u32[]{:S(2)}) collective-permute-start(bf16[192,128]{1,0:T(8,128)(2,1)S(1)} %get-tuple-element.68), channel_id=1, source_target_pairs={{0,3},{1,0},{2,1},{3,2},{4,7},{5,4},{6,5},{7,6},{8,11},{9,8},{10,9... | collective-permute-start | bytes 147464 | tf_op jit(solution)/shard_map/ppermute | solution.py:467
  12.7 0.3 collective-permute-start.4
  13.0 1.8 %collective-permute-start.9 = (bf16[192,128]{1,0:T(8,128)(2,1)S(1)}, bf16[192,128]{1,0:T(8,128)(2,1)S(1)}, u32[]{:S(2)}, u32[]{:S(2)}) collective-permute-start(bf16[192,128]{1,0:T(8,128)(2,1)S(1)} %get-tuple-element.76), channel_id=1, source_target_pairs={{0,4},{4,8},{8,12},{12,0},{1,5},{5,9},{9,13},{13,1},{2,6},{6,10},{... | collective-permute-start | bytes 147464 | tf_op jit(solution)/shard_map/ppermute | solution.py:467
  14.8 2.6 %collective-permute-start.10 = (bf16[192,128]{1,0:T(8,128)(2,1)S(1)}, bf16[192,128]{1,0:T(8,128)(2,1)S(1)}, u32[]{:S(2)}, u32[]{:S(2)}) collective-permute-start(bf16[192,128]{1,0:T(8,128)(2,1)S(1)} %get-tuple-element.77), channel_id=1, source_target_pairs={{0,8},{4,12},{8,0},{12,4},{1,9},{5,13},{9,1},{13,5},{2,10},{6,14},... | collective-permute-start | bytes 147464 | tf_op jit(solution)/shard_map/ppermute | solution.py:467
  17.4 1.3 %collective-permute-start.11 = (bf16[192,128]{1,0:T(8,128)(2,1)S(1)}, bf16[192,128]{1,0:T(8,128)(2,1)S(1)}, u32[]{:S(2)}, u32[]{:S(2)}) collective-permute-start(bf16[192,128]{1,0:T(8,128)(2,1)S(1)} %get-tuple-element.78), channel_id=1, source_target_pairs={{0,12},{4,0},{8,4},{12,8},{1,13},{5,1},{9,5},{13,9},{2,14},{6,2},{... | collective-permute-start | bytes 147464 | tf_op jit(solution)/shard_map/ppermute | solution.py:467
  18.8 0.3 shard_map.147
  19.1 0.7 collective-permute-start.6
  19.8 2.0 %collective-permute-start.7 = (bf16[192,128]{1,0:T(8,128)(2,1)S(1)}, bf16[192,128]{1,0:T(8,128)(2,1)S(1)}, u32[]{:S(2)}, u32[]{:S(2)}) collective-permute-start(bf16[192,128]{1,0:T(8,128)(2,1)S(1)} %get-tuple-element.73), channel_id=1, source_target_pairs={{0,8},{4,12},{8,0},{12,4},{1,9},{5,13},{9,1},{13,5},{2,10},{6,14},... | collective-permute-start | bytes 147464 | tf_op jit(solution)/shard_map/ppermute | solution.py:467
  21.8 1.3 %collective-permute-start.8 = (bf16[192,128]{1,0:T(8,128)(2,1)S(1)}, bf16[192,128]{1,0:T(8,128)(2,1)S(1)}, u32[]{:S(2)}, u32[]{:S(2)}) collective-permute-start(bf16[192,128]{1,0:T(8,128)(2,1)S(1)} %get-tuple-element.74), channel_id=1, source_target_pairs={{0,12},{4,0},{8,4},{12,8},{1,13},{5,1},{9,5},{13,9},{2,14},{6,2},{... | collective-permute-start | bytes 147464 | tf_op jit(solution)/shard_map/ppermute | solution.py:467
  23.2 2.5 %collective-permute-done.6.refs_1_ = bf16[192,128]{1,0:T(8,128)(2,1)S(1)} collective-permute-done((bf16[192,128]{1,0:T(8,128)(2,1)S(1)}, bf16[192,128]{1,0:T(8,128)(2,1)S(1)}, u32[]{:S(2)}, u32[]{:S(2)}) %collective-permute-start.6) | collective-permute-done | bytes 49184 | tf_op jit(solution)/shard_map/ppermute | solution.py:467
  25.7 1.7 %collective-permute-done.7.refs_2_ = bf16[192,128]{1,0:T(8,128)(2,1)S(1)} collective-permute-done((bf16[192,128]{1,0:T(8,128)(2,1)S(1)}, bf16[192,128]{1,0:T(8,128)(2,1)S(1)}, u32[]{:S(2)}, u32[]{:S(2)}) %collective-permute-start.7) | collective-permute-done | bytes 49184 | tf_op jit(solution)/shard_map/ppermute | solution.py:467
  27.4 6.8 %shard_map.148 = (bf16[192,128]{1,0:T(8,128)(2,1)S(1)}, bf16[192,128]{1,0:T(8,128)(2,1)S(1)}, bf16[192,128]{1,0:T(8,128)(2,1)S(1)}, bf16[192,128]{1,0:T(8,128)(2,1)S(1)}, bf16[3456,128]{1,0:T(8,128)(2,1)S(1)}) custom-call(bf16[192,128]{1,0:T(8,128)(2,1)S(1)} %get-tuple-element.71.refs_0_, bf16[192,128]{1,0:T(8,128)(2,1)S(1)} %collective-permute-done.6.refs_1_, ...), custom_call_target="tpu_custom_call" | custom-call | tf_op jit(solution)/shard_map/pallas_call | solution.py:450
  34.2 0.2 shard_map.149
  34.4 0.1 collective-permute-start.15
  34.5 1.8 %collective-permute-done.15.refs_1_ = bf16[1728,128]{1,0:T(8,128)(2,1)S(1)} collective-permute-done((bf16[1728,128]{1,0:T(8,128)(2,1)S(1)}, bf16[1728,128]{1,0:T(8,128)(2,1)S(1)}, u32[]{:S(2)}, u32[]{:S(2)}) %collective-permute-start.15) | collective-permute-done | bytes 442400 | tf_op jit(solution)/shard_map/ppermute | solution.py:474
  36.2 0.1 shard_map.150
  36.3 0.5 collective-permute-start.19
  36.8 2.6 %collective-permute-start.12 = (bf16[192,128]{1,0:T(8,128)(2,1)S(1)}, bf16[192,128]{1,0:T(8,128)(2,1)S(1)}, u32[]{:S(2)}, u32[]{:S(2)}) collective-permute-start(bf16[192,128]{1,0:T(8,128)(2,1)S(1)} %get-tuple-element.84), channel_id=1, source_target_pairs={{0,12},{4,0},{8,4},{12,8},{1,13},{5,1},{9,5},{13,9},{2,14},{6,2},{... | collective-permute-start | bytes 147464 | tf_op jit(solution)/shard_map/ppermute | solution.py:467
  39.4 0.2 collective-permute-start.13
  39.6 0.3 collective-permute-start.14
  40.0 3.9 %collective-permute-done.19.refs_1_ = bf16[864,128]{1,0:T(8,128)(2,1)S(1)} collective-permute-done((bf16[864,128]{1,0:T(8,128)(2,1)S(1)}, bf16[864,128]{1,0:T(8,128)(2,1)S(1)}, u32[]{:S(2)}, u32[]{:S(2)}) %collective-permute-start.19) | collective-permute-done | bytes 221216 | tf_op jit(solution)/shard_map/ppermute | solution.py:474
  43.9 0.1 shard_map.152.refs_11_.refs_0_
  43.9 1.3 %collective-permute-start.25 = (bf16[864,128]{1,0:T(8,128)(2,1)S(1)}, bf16[864,128]{1,0:T(8,128)(2,1)S(1)}, u32[]{:S(2)}, u32[]{:S(2)}) collective-permute-start(bf16[864,128]{1,0:T(8,128)(2,1)S(1)} %shard_map.152.refs_11_.refs_0_), channel_id=1, source_target_pairs={{0,4},{4,0},{8,12},{12,8},{1,5},{5,1},{9,13},{13,9},{2,6},{6,2},{1... | collective-permute-start | bytes 663560 | tf_op jit(solution)/shard_map/ppermute | solution.py:474
  45.2 0.3 collective-permute-done.14.refs_3_
  45.5 0.4 shard_map.151
  45.9 0.1 collective-permute-start.16
  46.0 1.6 %collective-permute-start.17 = (bf16[192,128]{1,0:T(8,128)(2,1)S(1)}, bf16[192,128]{1,0:T(8,128)(2,1)S(1)}, u32[]{:S(2)}, u32[]{:S(2)}) collective-permute-start(bf16[192,128]{1,0:T(8,128)(2,1)S(1)} %get-tuple-element.93), channel_id=1, source_target_pairs={{0,2},{1,3},{2,0},{3,1},{4,6},{5,7},{6,4},{7,5},{8,10},{9,11},{10,... | collective-permute-start | bytes 147464 | tf_op jit(solution)/shard_map/ppermute | solution.py:467
  47.6 1.4 %collective-permute-start.18 = (bf16[192,128]{1,0:T(8,128)(2,1)S(1)}, bf16[192,128]{1,0:T(8,128)(2,1)S(1)}, u32[]{:S(2)}, u32[]{:S(2)}) collective-permute-start(bf16[192,128]{1,0:T(8,128)(2,1)S(1)} %get-tuple-element.94), channel_id=1, source_target_pairs={{0,3},{1,0},{2,1},{3,2},{4,7},{5,4},{6,5},{7,6},{8,11},{9,8},{10,9... | collective-permute-start | bytes 147464 | tf_op jit(solution)/shard_map/ppermute | solution.py:467
  49.0 0.5 collective-permute-done.16.refs_1_
  49.5 0.7 collective-permute-done.17.refs_2_
  50.1 0.6 collective-permute-done.18.refs_3_
  50.7 3.6 %shard_map.153 = (bf16[192,128]{1,0:T(8,128)(2,1)S(1)}, bf16[192,128]{1,0:T(8,128)(2,1)S(1)}, bf16[192,128]{1,0:T(8,128)(2,1)S(1)}, bf16[192,128]{1,0:T(8,128)(2...) custom-call(bf16[192,128]{1,0:T(8,128)(2,1)S(1)} %get-tuple-element.91.refs_0_, ...), custom_call_target="tpu_custom_call" | custom-call | tf_op jit(solution)/shard_map/pallas_call | solution.py:450
  54.4 0.7 collective-permute-start.23
  55.1 1.0 %collective-permute-done.23.refs_1_ = bf16[576,128]{1,0:T(8,128)(2,1)S(1)} collective-permute-done((bf16[576,128]{1,0:T(8,128)(2,1)S(1)}, bf16[576,128]{1,0:T(8,128)(2,1)S(1)}, u32[]{:S(2)}, u32[]{:S(2)}) %collective-permute-start.23) | collective-permute-done | bytes 147488 | tf_op jit(solution)/shard_map/ppermute | solution.py:474
  56.1 0.1 shard_map.155.refs_2_.refs_0_
  56.2 1.4 %collective-permute-start.28 = (bf16[864,128]{1,0:T(8,128)(2,1)S(1)}, bf16[864,128]{1,0:T(8,128)(2,1)S(1)}, u32[]{:S(2)}, u32[]{:S(2)}) collective-permute-start(bf16[864,128]{1,0:T(8,128)(2,1)S(1)} %shard_map.155.refs_2_.refs_0_), channel_id=1, source_target_pairs={{0,8},{4,12},{8,0},{12,4},{1,9},{5,13},{9,1},{13,5},{2,10},{6,14},... | collective-permute-start | bytes 663560 | tf_op jit(solution)/shard_map/ppermute | solution.py:474
  57.5 0.9 %collective-permute-start.24 = (bf16[288,128]{1,0:T(8,128)(2,1)S(1)}, bf16[288,128]{1,0:T(8,128)(2,1)S(1)}, u32[]{:S(2)}, u32[]{:S(2)}) collective-permute-start(bf16[288,128]{1,0:T(8,128)(2,1)S(1)} %get-tuple-element.108), channel_id=1, source_target_pairs={{0,2},{1,3},{2,0},{3,1},{4,6},{5,7},{6,4},{7,5},{8,10},{9,11},{10,... | collective-permute-start | bytes 221192 | tf_op jit(solution)/shard_map/ppermute | solution.py:474
  58.4 3.5 %collective-permute-done.24.refs_1_ = bf16[288,128]{1,0:T(8,128)(2,1)S(1)} collective-permute-done((bf16[288,128]{1,0:T(8,128)(2,1)S(1)}, bf16[288,128]{1,0:T(8,128)(2,1)S(1)}, u32[]{:S(2)}, u32[]{:S(2)}) %collective-permute-start.24) | collective-permute-done | bytes 73760 | tf_op jit(solution)/shard_map/ppermute | solution.py:474
  61.9 0.7 collective-permute-start.26
  62.6 1.1 %collective-permute-start.21 = (bf16[192,128]{1,0:T(8,128)(2,1)S(1)}, bf16[192,128]{1,0:T(8,128)(2,1)S(1)}, u32[]{:S(2)}, u32[]{:S(2)}) collective-permute-start(bf16[192,128]{1,0:T(8,128)(2,1)S(1)} %get-tuple-element.103), channel_id=1, source_target_pairs={{0,2},{1,3},{2,0},{3,1},{4,6},{5,7},{6,4},{7,5},{8,10},{9,11},{10,... | collective-permute-start | bytes 147464 | tf_op jit(solution)/shard_map/ppermute | solution.py:467
  63.7 0.2 collective-permute-start.22
  63.9 0.5 collective-permute-done.20.refs_1_
  64.4 2.6 %collective-permute-done.21.refs_2_ = bf16[192,128]{1,0:T(8,128)(2,1)S(1)} collective-permute-done((bf16[192,128]{1,0:T(8,128)(2,1)S(1)}, bf16[192,128]{1,0:T(8,128)(2,1)S(1)}, u32[]{:S(2)}, u32[]{:S(2)}) %collective-permute-start.21) | collective-permute-done | bytes 49184 | tf_op jit(solution)/shard_map/ppermute | solution.py:467
  67.0 0.3 collective-permute-done.22.refs_3_
  67.3 1.1 %shard_map.157.refs_2_ = bf16[8,12288]{1,0:T(8,128)(2,1)} custom-call(bf16[192,128]{1,0:T(8,128)(2,1)S(1)} %get-tuple-element.101.refs_0_, bf16[192,128]{1,0:T(8,128)(2,1)S(1)} %collective-permute-done.20.refs_1_, bf16[192,128]{1,0:T(8,128)(2,1)S(1)} %collective-permute-done.21.refs_2_, bf16[192,128]{1,0:T(8,128)(2,1)S(1)} %collective-permute-done.22.refs_3_, ...), custom_call_target="tpu_custom_call" | custom-call | tf_op jit(solution)/shard_map/pallas_call | solution.py:450
  68.4 1.9 %collective-permute-done.26.refs_1_ = bf16[288,128]{1,0:T(8,128)(2,1)S(1)} collective-permute-done((bf16[288,128]{1,0:T(8,128)(2,1)S(1)}, bf16[288,128]{1,0:T(8,128)(2,1)S(1)}, u32[]{:S(2)}, u32[]{:S(2)}) %collective-permute-start.26) | collective-permute-done | bytes 73760 | tf_op jit(solution)/shard_map/ppermute | solution.py:474
  70.4 0.9 %copy-done = bf16[8,12288]{1,0:T(8,128)(2,1)S(1)} copy-done((bf16[8,12288]{1,0:T(8,128)(2,1)S(1)}, bf16[8,12288]{1,0:T(8,128)(2,1)}, u32[]{:S(2)}) %copy-start) | copy-done | bytes 196632
  71.3 0.1 shard_map.159.refs_2_.refs_0_
  71.4 0.7 collective-permute-start.33
  72.1 0.1 collective-permute-start.27
  72.2 5.2 %collective-permute-done.33.refs_2_ = bf16[864,128]{1,0:T(8,128)(2,1)S(1)} collective-permute-done((bf16[864,128]{1,0:T(8,128)(2,1)S(1)}, bf16[864,128]{1,0:T(8,128)(2,1)S(1)}, u32[]{:S(2)}, u32[]{:S(2)}) %collective-permute-start.33) | collective-permute-done | bytes 221216 | tf_op jit(solution)/shard_map/ppermute | solution.py:474
  77.4 1.4 %collective-permute-start.30 = (bf16[288,128]{1,0:T(8,128)(2,1)S(1)}, bf16[288,128]{1,0:T(8,128)(2,1)S(1)}, u32[]{:S(2)}, u32[]{:S(2)}) collective-permute-start(bf16[288,128]{1,0:T(8,128)(2,1)S(1)} %shard_map.160.refs_0_), channel_id=1, source_target_pairs={{0,2},{1,3},{2,0},{3,1},{4,6},{5,7},{6,4},{7,5},{8,10},{9,11},{10,... | collective-permute-start | bytes 221192 | tf_op jit(solution)/shard_map/ppermute | solution.py:474
  78.8 3.3 %collective-permute-done.30.refs_2_ = bf16[288,128]{1,0:T(8,128)(2,1)S(1)} collective-permute-done((bf16[288,128]{1,0:T(8,128)(2,1)S(1)}, bf16[288,128]{1,0:T(8,128)(2,1)S(1)}, u32[]{:S(2)}, u32[]{:S(2)}) %collective-permute-start.30) | collective-permute-done | bytes 73760 | tf_op jit(solution)/shard_map/ppermute | solution.py:474
  82.2 1.3 %collective-permute-done.31.refs_3_ = bf16[288,128]{1,0:T(8,128)(2,1)S(1)} collective-permute-done((bf16[288,128]{1,0:T(8,128)(2,1)S(1)}, bf16[288,128]{1,0:T(8,128)(2,1)S(1)}, u32[]{:S(2)}, u32[]{:S(2)}) %collective-permute-start.31) | collective-permute-done | bytes 73760 | tf_op jit(solution)/shard_map/ppermute | solution.py:474
  83.4 0.9 %shard_map.161 = (f32[192,576]{1,0:T(8,128)}, f32[192,192]{1,0:T(8,128)}) custom-call(bf16[288,128]{1,0:T(8,128)(2,1)S(1)} %shard_map.160.refs_0_, bf16[288,128]{1,0:T(8,128)(2,1)S(1)} %collective-permute-done.29.refs_1_, bf16[288,128]{1,0:T(8,128)(2,1)S(1)} %collective-permute-done.30.refs_2_, bf16[288,128]{1,0:T(8,128)(2,1)S(1)} %collective-permute-done.31.refs_3_), custom_call_target="tpu_custom_call" | custom-call | tf_op jit(solution)/shard_map/pallas_call | solution.py:450
  84.4 1.4 %shard_map.162 = (f32[192,576]{1,0:T(8,128)}, f32[192,192]{1,0:T(8,128)}, f32[192,768]{1,0:T(8,128)}, f32[192,768]{1,0:T(8,128)}) custom-call(bf16[864,128]{1,0:T(8,128)(2,1)S(1)} %shard_map.159.refs_2_.refs_0_, bf16[864,128]{1,0:T(8,128)(2,1)S(1)} %collective-permute-done.32.refs_1_, bf16[864,128]{1,0:T(8,128)(2,1)S(1)} %collective-permute-done.33.refs_2_, ...), custom_call_target="tpu_custom_call" | custom-call | tf_op jit(solution)/shard_map/pallas_call | solution.py:450
  (29 shorter events, 0.2 us)
Async XLA Ops:
  0.6 26.7 %copy-start.1 = (s32[32]{0:T(128)S(1)}, s32[32]{0:T(128)}, u32[]{:S(2)}) copy-start(s32[32]{0:T(128)} %param.17) | copy-start | bytes 388
  2.1 6.6 %collective-permute-start = (bf16[192,128]{1,0:T(8,128)(2,1)S(1)}, bf16[192,128]{1,0:T(8,128)(2,1)S(1)}, u32[]{:S(2)}, u32[]{:S(2)}) collective-permute-start(bf16[192,128]{1,0:T(8,128)(2,1)S(1)} %get-tuple-element.62), channel_id=1, source_target_pairs={{0,1},{1,2},{2,3},{3,0},{4,5},{5,6},{6,7},{7,4},{8,9},{9,10},{10,1... | collective-permute-start | bytes 147464 | tf_op jit(solution)/shard_map/ppermute | solution.py:467
  2.6 6.1 %collective-permute-start.1 = (bf16[192,128]{1,0:T(8,128)(2,1)S(1)}, bf16[192,128]{1,0:T(8,128)(2,1)S(1)}, u32[]{:S(2)}, u32[]{:S(2)}) collective-permute-start(bf16[192,128]{1,0:T(8,128)(2,1)S(1)} %get-tuple-element.63), channel_id=1, source_target_pairs={{0,2},{1,3},{2,0},{3,1},{4,6},{5,7},{6,4},{7,5},{8,10},{9,11},{10,... | collective-permute-start | bytes 147464 | tf_op jit(solution)/shard_map/ppermute | solution.py:467
  5.2 3.5 %collective-permute-start.2 = (bf16[192,128]{1,0:T(8,128)(2,1)S(1)}, bf16[192,128]{1,0:T(8,128)(2,1)S(1)}, u32[]{:S(2)}, u32[]{:S(2)}) collective-permute-start(bf16[192,128]{1,0:T(8,128)(2,1)S(1)} %get-tuple-element.64), channel_id=1, source_target_pairs={{0,3},{1,0},{2,1},{3,2},{4,7},{5,4},{6,5},{7,6},{8,11},{9,8},{10,9... | collective-permute-start | bytes 147464 | tf_op jit(solution)/shard_map/ppermute | solution.py:467
  11.3 6.1 %collective-permute-start.3 = (bf16[192,128]{1,0:T(8,128)(2,1)S(1)}, bf16[192,128]{1,0:T(8,128)(2,1)S(1)}, u32[]{:S(2)}, u32[]{:S(2)}) collective-permute-start(bf16[192,128]{1,0:T(8,128)(2,1)S(1)} %get-tuple-element.68), channel_id=1, source_target_pairs={{0,3},{1,0},{2,1},{3,2},{4,7},{5,4},{6,5},{7,6},{8,11},{9,8},{10,9... | collective-permute-start | bytes 147464 | tf_op jit(solution)/shard_map/ppermute | solution.py:467
  12.7 6.1 %collective-permute-start.4 = (bf16[192,128]{1,0:T(8,128)(2,1)S(1)}, bf16[192,128]{1,0:T(8,128)(2,1)S(1)}, u32[]{:S(2)}, u32[]{:S(2)}) collective-permute-start(bf16[192,128]{1,0:T(8,128)(2,1)S(1)} %get-tuple-element.69), channel_id=1, source_target_pairs={{0,2},{1,3},{2,0},{3,1},{4,6},{5,7},{6,4},{7,5},{8,10},{9,11},{10,... | collective-permute-start | bytes 147464 | tf_op jit(solution)/shard_map/ppermute | solution.py:467
  13.0 5.8 %collective-permute-start.5 = (bf16[192,128]{1,0:T(8,128)(2,1)S(1)}, bf16[192,128]{1,0:T(8,128)(2,1)S(1)}, u32[]{:S(2)}, u32[]{:S(2)}) collective-permute-start(bf16[192,128]{1,0:T(8,128)(2,1)S(1)} %get-tuple-element.70), channel_id=1, source_target_pairs={{0,1},{1,2},{2,3},{3,0},{4,5},{5,6},{6,7},{7,4},{8,9},{9,10},{10,1... | collective-permute-start | bytes 147464 | tf_op jit(solution)/shard_map/ppermute | solution.py:467
  13.0 8.8 %collective-permute-start.9 = (bf16[192,128]{1,0:T(8,128)(2,1)S(1)}, bf16[192,128]{1,0:T(8,128)(2,1)S(1)}, u32[]{:S(2)}, u32[]{:S(2)}) collective-permute-start(bf16[192,128]{1,0:T(8,128)(2,1)S(1)} %get-tuple-element.76), channel_id=1, source_target_pairs={{0,4},{4,8},{8,12},{12,0},{1,5},{5,9},{9,13},{13,1},{2,6},{6,10},{... | collective-permute-start | bytes 147464 | tf_op jit(solution)/shard_map/ppermute | solution.py:467
  14.8 8.3 %collective-permute-start.10 = (bf16[192,128]{1,0:T(8,128)(2,1)S(1)}, bf16[192,128]{1,0:T(8,128)(2,1)S(1)}, u32[]{:S(2)}, u32[]{:S(2)}) collective-permute-start(bf16[192,128]{1,0:T(8,128)(2,1)S(1)} %get-tuple-element.77), channel_id=1, source_target_pairs={{0,8},{4,12},{8,0},{12,4},{1,9},{5,13},{9,1},{13,5},{2,10},{6,14},... | collective-permute-start | bytes 147464 | tf_op jit(solution)/shard_map/ppermute | solution.py:467
  17.4 5.7 %collective-permute-start.11 = (bf16[192,128]{1,0:T(8,128)(2,1)S(1)}, bf16[192,128]{1,0:T(8,128)(2,1)S(1)}, u32[]{:S(2)}, u32[]{:S(2)}) collective-permute-start(bf16[192,128]{1,0:T(8,128)(2,1)S(1)} %get-tuple-element.78), channel_id=1, source_target_pairs={{0,12},{4,0},{8,4},{12,8},{1,13},{5,1},{9,5},{13,9},{2,14},{6,2},{... | collective-permute-start | bytes 147464 | tf_op jit(solution)/shard_map/ppermute | solution.py:467
  19.1 6.6 %collective-permute-start.6 = (bf16[192,128]{1,0:T(8,128)(2,1)S(1)}, bf16[192,128]{1,0:T(8,128)(2,1)S(1)}, u32[]{:S(2)}, u32[]{:S(2)}) collective-permute-start(bf16[192,128]{1,0:T(8,128)(2,1)S(1)} %get-tuple-element.72), channel_id=1, source_target_pairs={{0,4},{4,8},{8,12},{12,0},{1,5},{5,9},{9,13},{13,1},{2,6},{6,10},{... | collective-permute-start | bytes 147464 | tf_op jit(solution)/shard_map/ppermute | solution.py:467
  19.8 7.6 %collective-permute-start.7 = (bf16[192,128]{1,0:T(8,128)(2,1)S(1)}, bf16[192,128]{1,0:T(8,128)(2,1)S(1)}, u32[]{:S(2)}, u32[]{:S(2)}) collective-permute-start(bf16[192,128]{1,0:T(8,128)(2,1)S(1)} %get-tuple-element.73), channel_id=1, source_target_pairs={{0,8},{4,12},{8,0},{12,4},{1,9},{5,13},{9,1},{13,5},{2,10},{6,14},... | collective-permute-start | bytes 147464 | tf_op jit(solution)/shard_map/ppermute | solution.py:467
  21.8 5.5 %collective-permute-start.8 = (bf16[192,128]{1,0:T(8,128)(2,1)S(1)}, bf16[192,128]{1,0:T(8,128)(2,1)S(1)}, u32[]{:S(2)}, u32[]{:S(2)}) collective-permute-start(bf16[192,128]{1,0:T(8,128)(2,1)S(1)} %get-tuple-element.74), channel_id=1, source_target_pairs={{0,12},{4,0},{8,4},{12,8},{1,13},{5,1},{9,5},{13,9},{2,14},{6,2},{... | collective-permute-start | bytes 147464 | tf_op jit(solution)/shard_map/ppermute | solution.py:467
  34.4 1.9 %collective-permute-start.15 = (bf16[1728,128]{1,0:T(8,128)(2,1)S(1)}, bf16[1728,128]{1,0:T(8,128)(2,1)S(1)}, u32[]{:S(2)}, u32[]{:S(2)}) collective-permute-start(bf16[1728,128]{1,0:T(8,128)(2,1)S(1)} %get-tuple-element.89), channel_id=1, source_target_pairs={{0,1},{1,0},{2,3},{3,2},{4,5},{5,4},{6,7},{7,6},{8,9},{9,8},{10,11... | collective-permute-start | bytes 1327112 | tf_op jit(solution)/shard_map/ppermute | solution.py:474
  36.3 7.5 %collective-permute-start.19 = (bf16[864,128]{1,0:T(8,128)(2,1)S(1)}, bf16[864,128]{1,0:T(8,128)(2,1)S(1)}, u32[]{:S(2)}, u32[]{:S(2)}) collective-permute-start(bf16[864,128]{1,0:T(8,128)(2,1)S(1)} %get-tuple-element.100), channel_id=1, source_target_pairs={{0,2},{1,3},{2,0},{3,1},{4,6},{5,7},{6,4},{7,5},{8,10},{9,11},{10,... | collective-permute-start | bytes 663560 | tf_op jit(solution)/shard_map/ppermute | solution.py:474
  36.8 8.4 %collective-permute-start.12 = (bf16[192,128]{1,0:T(8,128)(2,1)S(1)}, bf16[192,128]{1,0:T(8,128)(2,1)S(1)}, u32[]{:S(2)}, u32[]{:S(2)}) collective-permute-start(bf16[192,128]{1,0:T(8,128)(2,1)S(1)} %get-tuple-element.84), channel_id=1, source_target_pairs={{0,12},{4,0},{8,4},{12,8},{1,13},{5,1},{9,5},{13,9},{2,14},{6,2},{... | collective-permute-start | bytes 147464 | tf_op jit(solution)/shard_map/ppermute | solution.py:467
  39.4 5.8 %collective-permute-start.13 = (bf16[192,128]{1,0:T(8,128)(2,1)S(1)}, bf16[192,128]{1,0:T(8,128)(2,1)S(1)}, u32[]{:S(2)}, u32[]{:S(2)}) collective-permute-start(bf16[192,128]{1,0:T(8,128)(2,1)S(1)} %get-tuple-element.85), channel_id=1, source_target_pairs={{0,8},{4,12},{8,0},{12,4},{1,9},{5,13},{9,1},{13,5},{2,10},{6,14},... | collective-permute-start | bytes 147464 | tf_op jit(solution)/shard_map/ppermute | solution.py:467
  39.6 5.9 %collective-permute-start.14 = (bf16[192,128]{1,0:T(8,128)(2,1)S(1)}, bf16[192,128]{1,0:T(8,128)(2,1)S(1)}, u32[]{:S(2)}, u32[]{:S(2)}) collective-permute-start(bf16[192,128]{1,0:T(8,128)(2,1)S(1)} %get-tuple-element.86), channel_id=1, source_target_pairs={{0,4},{4,8},{8,12},{12,0},{1,5},{5,9},{9,13},{13,1},{2,6},{6,10},{... | collective-permute-start | bytes 147464 | tf_op jit(solution)/shard_map/ppermute | solution.py:467
  43.9 12.2 %collective-permute-start.25 = (bf16[864,128]{1,0:T(8,128)(2,1)S(1)}, bf16[864,128]{1,0:T(8,128)(2,1)S(1)}, u32[]{:S(2)}, u32[]{:S(2)}) collective-permute-start(bf16[864,128]{1,0:T(8,128)(2,1)S(1)} %shard_map.152.refs_11_.refs_0_), channel_id=1, source_target_pairs={{0,4},{4,0},{8,12},{12,8},{1,5},{5,1},{9,13},{13,9},{2,6},{6,2},{1... | collective-permute-start | bytes 663560 | tf_op jit(solution)/shard_map/ppermute | solution.py:474
  45.9 3.6 %collective-permute-start.16 = (bf16[192,128]{1,0:T(8,128)(2,1)S(1)}, bf16[192,128]{1,0:T(8,128)(2,1)S(1)}, u32[]{:S(2)}, u32[]{:S(2)}) collective-permute-start(bf16[192,128]{1,0:T(8,128)(2,1)S(1)} %get-tuple-element.92), channel_id=1, source_target_pairs={{0,1},{1,2},{2,3},{3,0},{4,5},{5,6},{6,7},{7,4},{8,9},{9,10},{10,1... | collective-permute-start | bytes 147464 | tf_op jit(solution)/shard_map/ppermute | solution.py:467
  46.0 4.2 %collective-permute-start.17 = (bf16[192,128]{1,0:T(8,128)(2,1)S(1)}, bf16[192,128]{1,0:T(8,128)(2,1)S(1)}, u32[]{:S(2)}, u32[]{:S(2)}) collective-permute-start(bf16[192,128]{1,0:T(8,128)(2,1)S(1)} %get-tuple-element.93), channel_id=1, source_target_pairs={{0,2},{1,3},{2,0},{3,1},{4,6},{5,7},{6,4},{7,5},{8,10},{9,11},{10,... | collective-permute-start | bytes 147464 | tf_op jit(solution)/shard_map/ppermute | solution.py:467
  47.6 3.1 %collective-permute-start.18 = (bf16[192,128]{1,0:T(8,128)(2,1)S(1)}, bf16[192,128]{1,0:T(8,128)(2,1)S(1)}, u32[]{:S(2)}, u32[]{:S(2)}) collective-permute-start(bf16[192,128]{1,0:T(8,128)(2,1)S(1)} %get-tuple-element.94), channel_id=1, source_target_pairs={{0,3},{1,0},{2,1},{3,2},{4,7},{5,4},{6,5},{7,6},{8,11},{9,8},{10,9... | collective-permute-start | bytes 147464 | tf_op jit(solution)/shard_map/ppermute | solution.py:467
  54.4 1.7 %collective-permute-start.23 = (bf16[576,128]{1,0:T(8,128)(2,1)S(1)}, bf16[576,128]{1,0:T(8,128)(2,1)S(1)}, u32[]{:S(2)}, u32[]{:S(2)}) collective-permute-start(bf16[576,128]{1,0:T(8,128)(2,1)S(1)} %get-tuple-element.106), channel_id=1, source_target_pairs={{0,1},{1,0},{2,3},{3,2},{4,5},{5,4},{6,7},{7,6},{8,9},{9,8},{10,11... | collective-permute-start | bytes 442376 | tf_op jit(solution)/shard_map/ppermute | solution.py:474
  56.2 15.1 %collective-permute-start.28 = (bf16[864,128]{1,0:T(8,128)(2,1)S(1)}, bf16[864,128]{1,0:T(8,128)(2,1)S(1)}, u32[]{:S(2)}, u32[]{:S(2)}) collective-permute-start(bf16[864,128]{1,0:T(8,128)(2,1)S(1)} %shard_map.155.refs_2_.refs_0_), channel_id=1, source_target_pairs={{0,8},{4,12},{8,0},{12,4},{1,9},{5,13},{9,1},{13,5},{2,10},{6,14},... | collective-permute-start | bytes 663560 | tf_op jit(solution)/shard_map/ppermute | solution.py:474
  57.5 4.4 %collective-permute-start.24 = (bf16[288,128]{1,0:T(8,128)(2,1)S(1)}, bf16[288,128]{1,0:T(8,128)(2,1)S(1)}, u32[]{:S(2)}, u32[]{:S(2)}) collective-permute-start(bf16[288,128]{1,0:T(8,128)(2,1)S(1)} %get-tuple-element.108), channel_id=1, source_target_pairs={{0,2},{1,3},{2,0},{3,1},{4,6},{5,7},{6,4},{7,5},{8,10},{9,11},{10,... | collective-permute-start | bytes 221192 | tf_op jit(solution)/shard_map/ppermute | solution.py:474
  61.9 8.5 %collective-permute-start.26 = (bf16[288,128]{1,0:T(8,128)(2,1)S(1)}, bf16[288,128]{1,0:T(8,128)(2,1)S(1)}, u32[]{:S(2)}, u32[]{:S(2)}) collective-permute-start(bf16[288,128]{1,0:T(8,128)(2,1)S(1)} %shard_map.156.refs_4_.refs_0_), channel_id=1, source_target_pairs={{0,4},{4,0},{8,12},{12,8},{1,5},{5,1},{9,13},{13,9},{2,6},{6,2},{1... | collective-permute-start | bytes 221192 | tf_op jit(solution)/shard_map/ppermute | solution.py:474
  62.6 1.8 %collective-permute-start.20 = (bf16[192,128]{1,0:T(8,128)(2,1)S(1)}, bf16[192,128]{1,0:T(8,128)(2,1)S(1)}, u32[]{:S(2)}, u32[]{:S(2)}) collective-permute-start(bf16[192,128]{1,0:T(8,128)(2,1)S(1)} %get-tuple-element.102), channel_id=1, source_target_pairs={{0,3},{1,0},{2,1},{3,2},{4,7},{5,4},{6,5},{7,6},{8,11},{9,8},{10,9... | collective-permute-start | bytes 147464 | tf_op jit(solution)/shard_map/ppermute | solution.py:467
  62.6 4.4 %collective-permute-start.21 = (bf16[192,128]{1,0:T(8,128)(2,1)S(1)}, bf16[192,128]{1,0:T(8,128)(2,1)S(1)}, u32[]{:S(2)}, u32[]{:S(2)}) collective-permute-start(bf16[192,128]{1,0:T(8,128)(2,1)S(1)} %get-tuple-element.103), channel_id=1, source_target_pairs={{0,2},{1,3},{2,0},{3,1},{4,6},{5,7},{6,4},{7,5},{8,10},{9,11},{10,... | collective-permute-start | bytes 147464 | tf_op jit(solution)/shard_map/ppermute | solution.py:467
  63.7 3.6 %collective-permute-start.22 = (bf16[192,128]{1,0:T(8,128)(2,1)S(1)}, bf16[192,128]{1,0:T(8,128)(2,1)S(1)}, u32[]{:S(2)}, u32[]{:S(2)}) collective-permute-start(bf16[192,128]{1,0:T(8,128)(2,1)S(1)} %get-tuple-element.104), channel_id=1, source_target_pairs={{0,1},{1,2},{2,3},{3,0},{4,5},{5,6},{6,7},{7,4},{8,9},{9,10},{10,1... | collective-permute-start | bytes 147464 | tf_op jit(solution)/shard_map/ppermute | solution.py:467
  70.4 0.9 %copy-start = (bf16[8,12288]{1,0:T(8,128)(2,1)S(1)}, bf16[8,12288]{1,0:T(8,128)(2,1)}, u32[]{:S(2)}) copy-start(bf16[8,12288]{1,0:T(8,128)(2,1)} %shard_map.157.refs_2_) | copy-start | bytes 589828
  71.4 6.0 %collective-permute-start.33 = (bf16[864,128]{1,0:T(8,128)(2,1)S(1)}, bf16[864,128]{1,0:T(8,128)(2,1)S(1)}, u32[]{:S(2)}, u32[]{:S(2)}) collective-permute-start(bf16[864,128]{1,0:T(8,128)(2,1)S(1)} %shard_map.159.refs_2_.refs_0_), channel_id=1, source_target_pairs={{0,2},{1,3},{2,0},{3,1},{4,6},{5,7},{6,4},{7,5},{8,10},{9,11},{10,... | collective-permute-start | bytes 663560 | tf_op jit(solution)/shard_map/ppermute | solution.py:474
  72.1 5.3 %collective-permute-start.27 = (bf16[288,128]{1,0:T(8,128)(2,1)S(1)}, bf16[288,128]{1,0:T(8,128)(2,1)S(1)}, u32[]{:S(2)}, u32[]{:S(2)}) collective-permute-start(bf16[288,128]{1,0:T(8,128)(2,1)S(1)} %shard_map.158.refs_2_.refs_0_), channel_id=1, source_target_pairs={{0,8},{4,12},{8,0},{12,4},{1,9},{5,13},{9,1},{13,5},{2,10},{6,14},... | collective-permute-start | bytes 221192 | tf_op jit(solution)/shard_map/ppermute | solution.py:474
  72.2 12.2 %collective-permute-start.32 = (bf16[864,128]{1,0:T(8,128)(2,1)S(1)}, bf16[864,128]{1,0:T(8,128)(2,1)S(1)}, u32[]{:S(2)}, u32[]{:S(2)}) collective-permute-start(bf16[864,128]{1,0:T(8,128)(2,1)S(1)} %shard_map.159.refs_2_.refs_0_), channel_id=1, source_target_pairs={{0,1},{1,0},{2,3},{3,2},{4,5},{5,4},{6,7},{7,6},{8,9},{9,8},{10,11... | collective-permute-start | bytes 663560 | tf_op jit(solution)/shard_map/ppermute | solution.py:474
  77.4 7.0 %collective-permute-start.34 = (bf16[864,128]{1,0:T(8,128)(2,1)S(1)}, bf16[864,128]{1,0:T(8,128)(2,1)S(1)}, u32[]{:S(2)}, u32[]{:S(2)}) collective-permute-start(bf16[864,128]{1,0:T(8,128)(2,1)S(1)} %collective-permute-done.33.refs_2_), channel_id=1, source_target_pairs={{0,1},{1,0},{2,3},{3,2},{4,5},{5,4},{6,7},{7,6},{8,9},{9,8},{10,11... | collective-permute-start | bytes 663560 | tf_op jit(solution)/shard_map/ppermute | solution.py:474
  77.4 4.7 %collective-permute-start.30 = (bf16[288,128]{1,0:T(8,128)(2,1)S(1)}, bf16[288,128]{1,0:T(8,128)(2,1)S(1)}, u32[]{:S(2)}, u32[]{:S(2)}) collective-permute-start(bf16[288,128]{1,0:T(8,128)(2,1)S(1)} %shard_map.160.refs_0_), channel_id=1, source_target_pairs={{0,2},{1,3},{2,0},{3,1},{4,6},{5,7},{6,4},{7,5},{8,10},{9,11},{10,... | collective-permute-start | bytes 221192 | tf_op jit(solution)/shard_map/ppermute | solution.py:474
  78.8 3.3 %collective-permute-start.29 = (bf16[288,128]{1,0:T(8,128)(2,1)S(1)}, bf16[288,128]{1,0:T(8,128)(2,1)S(1)}, u32[]{:S(2)}, u32[]{:S(2)}) collective-permute-start(bf16[288,128]{1,0:T(8,128)(2,1)S(1)} %shard_map.160.refs_0_), channel_id=1, source_target_pairs={{0,1},{1,0},{2,3},{3,2},{4,5},{5,4},{6,7},{7,6},{8,9},{9,8},{10,11... | collective-permute-start | bytes 221192 | tf_op jit(solution)/shard_map/ppermute | solution.py:474
  82.2 1.3 %collective-permute-start.31 = (bf16[288,128]{1,0:T(8,128)(2,1)S(1)}, bf16[288,128]{1,0:T(8,128)(2,1)S(1)}, u32[]{:S(2)}, u32[]{:S(2)}) collective-permute-start(bf16[288,128]{1,0:T(8,128)(2,1)S(1)} %collective-permute-done.30.refs_2_), channel_id=1, source_target_pairs={{0,1},{1,0},{2,3},{3,2},{4,5},{5,4},{6,7},{7,6},{8,9},{9,8},{10,11... | collective-permute-start | bytes 221192 | tf_op jit(solution)/shard_map/ppermute | solution.py:474

commit v3 on v2

--- a/solution.py
+++ b/solution.py
@@ -237,8 +237,8 @@
     ]
 
 
-def attend_back(grad_ref, x_ref, proj_ref, probs_ref, grad_proj_ref, grad_mixed_ref, qkv, out, width):
-    total = x_ref.shape[1]
+def attend_back(grad_ref, proj_ref, probs_ref, grad_proj_ref, grad_mixed_ref, out, width):
+    total = grad_ref.shape[1]
     for cols in blocks_of(2 * LANES, total):
         grad_mixed_ref[:, cols] = nn(out[...], grad_ref[:, cols]).astype(BF)
     units = units_of(total, width)
@@ -277,8 +277,11 @@
             grad_proj_ref[2 * E + rows.start : 2 * E + rows.stop, keys] = both[1].astype(BF)
 
     staged(len(units), to_probs, to_scores, to_proj)
+
+
+def project_back(grad_ref, x_ref, grad_proj_ref, qkv):
     results = []
-    for cols in blocks_of(2 * LANES, total):
+    for cols in blocks_of(2 * LANES, x_ref.shape[1]):
         grad_normed = nn(qkv[...], grad_proj_ref[:, cols]).astype(BF).astype(F32)
         normed, root = norm(x_ref[:, cols].astype(F32))
         results.append(norm_back(grad_normed, normed, root) + grad_ref[:, cols].astype(F32))
@@ -319,7 +322,8 @@
 def rows_forward_kernel(plan, wait, *refs):
     tiles, refs = refs[: plan.ranks_attr], refs[plan.ranks_attr :]
     (qkv_t, out_t), refs = refs[:2], refs[2:]
-    outs, (x_ref, normed_ref, proj_ref, probs_ref, mixed_ref) = refs[: plan.ranks_attr], refs[plan.ranks_attr :]
+    outs, refs = refs[: plan.ranks_attr], refs[plan.ranks_attr :]
+    x_ref, normed_ref, proj_ref, probs_ref, mixed_ref = refs
     order = one_hot(plan.cells, plan.grouped_from_rows())
     x_ref[...] = nn(side_by_side(tiles), order).astype(BF)
     first = attend(x_ref, normed_ref, proj_ref, probs_ref, mixed_ref, qkv_t, out_t, plan.all_attr, None)
@@ -328,30 +332,33 @@
 
 def rows_back_kernel(plan, wait, *refs):
     tiles, refs = refs[: plan.ranks_attr], refs[plan.ranks_attr :]
-    (qkv, out, x_ref, normed_ref, proj_ref, probs_ref, mixed_ref), refs = refs[:7], refs[7:]
-    outs, refs = refs[: plan.ranks_attr], refs[plan.ranks_attr :]
-    keep_ref, send_ref, sums_ref, grad_ref, grad_proj_ref, grad_mixed_ref = refs
+    (out, normed_ref, proj_ref, probs_ref, mixed_ref), refs = refs[:5], refs[5:]
+    keep_ref, send_ref, grad_ref, grad_proj_ref, sums_ref, grad_mixed_ref = refs
     order = one_hot(plan.cells, plan.grouped_from_rows())
     grad_ref[...] = nn(side_by_side(tiles), order).astype(BF)
     wait()
-    grads = attend_back(grad_ref, x_ref, proj_ref, probs_ref, grad_proj_ref, grad_mixed_ref, qkv, out, plan.all_attr)
-    put_tiles(outs, nt(jnp.concatenate(grads, axis=1).astype(BF), order))
+    attend_back(grad_ref, proj_ref, probs_ref, grad_proj_ref, grad_mixed_ref, out, plan.all_attr)
     put_attend_grads(sums_ref, normed_ref, grad_proj_ref, mixed_ref, grad_ref)
     put_halves(bits_of("attr")[0], sums_ref, keep_ref, send_ref)
+
+
+def rows_end_kernel(plan, wait, qkv, x_ref, grad_ref, grad_proj_ref, *outs):
+    order = one_hot(plan.cells, plan.grouped_from_rows())
+    wait()
+    grads = project_back(grad_ref, x_ref, grad_proj_ref, qkv)
+    put_tiles(outs, nt(jnp.concatenate(grads, axis=1).astype(BF), order))
 
 
 def cols_kernel(plan, wait, *refs):
     count = plan.ranks_rec
     tiles, cot_tiles, refs = refs[:count], refs[count : 2 * count], refs[2 * count :]
     (train_ref, qkv, out, up, down, qkv_t, out_t, up_t), refs = refs[:8], refs[8:]
-    outs, (sums_ref,), refs = refs[:count], refs[count : count + 1], refs[count + 1 :]
-    x_ref, cot_ref, normed_ref, proj_ref, probs_ref, mixed_ref, second_ref = refs[:7]
-    pre_ref, hidden_ref, grad_pre_ref, grad_ref, grad_proj_ref, grad_mixed_ref, mask_ref = refs[7:]
+    outs, refs = refs[:count], refs[count:]
+    normed_ref, mixed_ref, normed_second_ref, hidden_ref, cot_ref, grad_pre_ref, grad_ref, grad_proj_ref = refs[:8]
+    x_ref, proj_ref, probs_ref, second_ref, slope_ref, wide_ref, mask_ref, grad_mixed_ref = refs[8:]
     width = max(LANES, plan.all_rec)
     order = one_hot(plan.cells, plan.grouped_from_cols())
     x_ref[...] = nn(side_by_side(tiles), order).astype(BF)
-    wait()
-    cot_ref[...] = nn(side_by_side(cot_tiles), order).astype(BF)
 
     row = lax.broadcasted_iota(jnp.int32, (width, 1), 0)
     sequence, far, near, own = digits(row, (width // plan.all_rec, plan.ranks_rec, plan.ranks_attr, plan.own_rec))
@@ -364,35 +371,44 @@
     second = attend(x_ref, normed_ref, proj_ref, probs_ref, mixed_ref, qkv_t, out_t, width, mask_ref)
     for cols, value in zip(blocks_of(2 * LANES, plan.cells), second):
         second_ref[:, cols] = value.astype(BF)
-
-    table, root = norm(second_ref[...].astype(F32))
-    normed_second = table.astype(BF)
-    pre_ref[...] = nn(up_t[...], normed_second)
-    grad_pre_ref[...] = nn(down[...], cot_ref[...])
+        normed_second_ref[:, cols] = norm(second_ref[:, cols].astype(F32))[0].astype(BF)
+    wide_ref[...] = nn(up_t[...], normed_second_ref[...])
     step = 32
     for start in range(0, FF, step):
         rows = slice(start, start + step)
-        pre = pre_ref[rows, :]
+        pre = wide_ref[rows, :]
         gate = 0.5 + 0.5 * lax.erf(pre * HALF_ROOT)
         hidden_ref[rows, :] = (pre * gate).astype(BF)
-        slope = gate + pre * (jnp.exp2(pre * pre * BELL_EXP2) * BELL)
-        grad_pre_ref[rows, :] = grad_pre_ref[rows, :] * slope
-    grad_pre = grad_pre_ref[...].astype(BF)
-
+        slope_ref[rows, :] = gate + pre * (jnp.exp2(pre * pre * BELL_EXP2) * BELL)
+
+    cot_ref[...] = nn(side_by_side(cot_tiles), order).astype(BF)
+    wait()
+    wide_ref[...] = nn(down[...], cot_ref[...])
+    step = 64
+    for start in range(0, FF, step):
+        rows = slice(start, start + step)
+        grad_pre_ref[rows, :] = (wide_ref[rows, :] * slope_ref[rows, :]).astype(BF)
+    for cols in blocks_of(2 * LANES, plan.cells):
+        grad_normed = nn(up[...], grad_pre_ref[:, cols]).astype(BF).astype(F32)
+        table, root = norm(second_ref[:, cols].astype(F32))
+        grad_ref[:, cols] = (norm_back(grad_normed, table, root) + cot_ref[:, cols].astype(F32)).astype(BF)
+    attend_back(grad_ref, proj_ref, probs_ref, grad_proj_ref, grad_mixed_ref, out, width)
+    grads = project_back(grad_ref, x_ref, grad_proj_ref, qkv)
+    put_tiles(outs, nt(jnp.concatenate(grads, axis=1).astype(BF), order))
+
+
+def cols_sums_kernel(wait, *refs):
+    normed_ref, mixed_ref, normed_second_ref, hidden_ref, cot_ref, grad_pre_ref, grad_ref, grad_proj_ref = refs[:8]
+    keep_ref, send_ref, sums_ref = refs[8:]
     for base, grad_weight in (
-        (6 * E, nt(normed_second, grad_pre)),
+        (6 * E, nt(normed_second_ref[...], grad_pre_ref[...])),
         (12 * E, nt(cot_ref[...], hidden_ref[...])),
     ):
         for tile in range(FF // LANES):
             rows = slice(base + tile * E, base + (tile + 1) * E)
             sums_ref[rows, :] = grad_weight[:, tile * LANES : (tile + 1) * LANES].astype(BF)
-
-    grad_normed = nn(up[...], grad_pre).astype(BF).astype(F32)
-    grad = norm_back(grad_normed, table, root) + cot_ref[...].astype(F32)
-    grad_ref[...] = grad.astype(BF)
-    grads = attend_back(grad_ref, x_ref, proj_ref, probs_ref, grad_proj_ref, grad_mixed_ref, qkv, out, width)
-    put_tiles(outs, nt(jnp.concatenate(grads, axis=1).astype(BF), order))
     put_attend_grads(sums_ref, normed_ref, grad_proj_ref, mixed_ref, grad_ref)
+    put_halves(bits_of("attr")[0], sums_ref, keep_ref, send_ref)
 
 
 def finish_cols_kernel(factor, bits, wait, *refs):
@@ -417,6 +433,10 @@
 
 class Near(NamedTuple):
     array: jax.Array
+
+
+def in_hbm(array):
+    return pltpu.with_memory_space_constraint(array, pltpu.HBM)
 
 
 def call(body, outs, scratch, *args, after=()):
@@ -458,7 +478,7 @@
         + held
         + ([pltpu.SemaphoreType.DMA((n_far,))] if far else []),
         compiler_params=pltpu.CompilerParams(vmem_limit_bytes=VMEM),
-    )(*arrays, *after)
+    )(*arrays, *[in_hbm(arg.array) if isinstance(arg, Far) else arg for arg in after])
 
 
 def exchange(tiles, axis, sign):
@@ -478,9 +498,9 @@
     return digits(lax.axis_index(axis) // bit, (2,))[0]
 
 
-def halve_kernel(bit, wait, *refs):
+def halve_kernel(axis, bit, wait, *refs):
     parts, (keep, send) = refs[:-2], refs[-2:]
-    rows, mine = keep.shape[0], has_bit("attr", bit)
+    rows, mine = keep.shape[0], has_bit(axis, bit)
     for ref, half in ((keep, mine), (send, 1 - mine)):
         place = pl.ds(pl.multiple_of(half * rows, rows), rows)
         ref[...] = sum(part[place, :].astype(F32) for part in parts).astype(BF)
@@ -488,6 +508,13 @@
 
 def add_kernel(wait, *refs):
     refs[-1][...] = sum(part[...].astype(F32) for part in refs[:-1]).astype(BF)
+
+
+def lay_out_kernel(axis, bit, wait, own_ref, other_ref, out_ref):
+    rows = own_ref.shape[0]
+    mine = has_bit(axis, bit)
+    for ref, half in ((own_ref, mine), (other_ref, 1 - mine)):
+        out_ref[pl.ds(pl.multiple_of(half * rows, rows), rows), :] = ref[...]
 
 
 def lay_out(bits, parts, rows_ref):
@@ -508,28 +535,42 @@
     def __init__(self, *parts):
         self.parts, self.rows = list(parts), parts[0].shape[0]
 
-    def halve(self, bit, after=()):
+    def halve(self, axis, bit, after=()):
         self.rows //= 2
         keep, send = call(
-            functools.partial(halve_kernel, bit), [((self.rows, LANES), BF)] * 2, [], *self.parts, after=after
+            functools.partial(halve_kernel, axis, bit), [((self.rows, LANES), BF)] * 2, [], *self.parts, after=after
         )
-        self.parts = [keep, swap(send, "attr", bit)]
+        self.parts = [keep, swap(send, axis, bit)]
         return [keep]
+
+    def back(self, axis, bit, after=()):
+        self.rows *= 2
+        body = functools.partial(lay_out_kernel, axis, bit)
+        (part,) = call(body, [((self.rows, LANES), BF)], [], *self.parts, after=after)
+        self.parts = [part]
+        return [part]
 
     def add(self, bit=0, after=()):
         (part,) = call(add_kernel, [((self.rows, LANES), BF)], [], *self.parts, after=after)
         self.parts = [part] + ([swap(part, "rec", bit)] if bit else [])
         return [part]
 
-    def spread(self, bits):
+    def spread_after(self, bits, middle):
         done = {0: self.parts[0]}
-        for order, bit in reversed(list(enumerate(bits))):
+        for order, bit in reversed(list(enumerate(bits[1:], 1))):
             done.update({number | 1 << order: swap(part, "attr", bit) for number, part in sorted(done.items())})
-        return [done[number] for number in sorted(done)]
+        near = {1: swap(done[0], "attr", bits[0])}
+        results, after = middle()
+        for number, part in sorted(done.items()):
+            if number:
+                (part,) = call(add_kernel, [(part.shape, BF)], [], part, after=after)
+                near[number | 1] = swap(part, "attr", bits[0])
+        done.update(near)
+        return results, [done[number] for number in sorted(done)]
 
 
 def padded(rows):
-    devices = lax.axis_size("attr")
+    devices = 2 * lax.axis_size("attr")
     return -(-rows // (16 * devices)) * 16 * devices
 
 
@@ -571,17 +612,17 @@
         *rows,
         *turned[:2],
     )
-    first, saved = got[:ranks_attr], [Near(array) for array in got[ranks_attr:]]
+    first, (x, normed, proj, weights, mixed) = got[:ranks_attr], [Near(array) for array in got[ranks_attr:]]
     first = exchange(first, "attr", -1)
     cols = exchange(call(kernel(to_cols_kernel), col_tiles, [], *first), "rec", 1)
 
     width = max(LANES, plan.all_rec)
     rows_sums, cols_sums = padded(6 * E), padded(18 * E)
+    hidden, hidden_wide = ((FF, count), BF), ((FF, count), F32)
     got = call(
         kernel(cols_kernel),
-        col_tiles + [((cols_sums, LANES), BF)],
-        [table, table, table, wide, probs(width), table, table]
-        + [((FF, count), F32), ((FF, count), BF), ((FF, count), F32), table, wide, table, ((width, width), F32)],
+        col_tiles + [out + ("near",) for out in (table, table, table, hidden, table, hidden, table, wide)],
+        [table, wide, probs(width), table, hidden_wide, hidden_wide, ((width, width), F32), table],
         *cols,
         *cot,
         train_split.reshape(1, -1),
@@ -593,46 +634,65 @@
         turned[3],
         turned[4],
     )
+    grads, saved = exchange(got[:ranks_rec], "rec", -1), [Near(array) for array in got[ranks_rec:]]
     near, far = bits_of("attr"), bits_of("rec")
-    grads, sums = exchange(got[:ranks_rec], "rec", -1), Total(got[ranks_rec])
-    mark = sums.halve(near[0])
+    keep, send = call(
+        cols_sums_kernel, [((cols_sums // 2, LANES), BF)] * 2, [((cols_sums, LANES), BF)], *saved
+    )
+    sums = Total(keep, swap(send, "attr", near[0]))
+    rows_grads = call(kernel(to_rows_kernel), row_tiles, [], *grads, after=[keep])
+    grads = exchange(rows_grads, "attr", 1)
     for bit in near[1:]:
-        mark = sums.halve(bit, after=mark)
-    grads = exchange(call(kernel(to_rows_kernel), row_tiles, [], *grads, after=mark), "attr", 1)
+        sums.halve("attr", bit)
     mark = sums.add(far[0])
 
-    got = call(
+    keep, send, grad, grad_proj = call(
         kernel(rows_back_kernel),
-        row_tiles + [((rows_sums // 2, LANES), BF)] * 2,
-        [((rows_sums, LANES), BF), table, wide, table],
+        [((rows_sums // 2, LANES), BF)] * 2 + [table + ("near",), wide + ("near",)],
+        [((rows_sums, LANES), BF), table],
         *grads,
-        Far(qkv_attr),
         Far(out_attr),
-        *saved,
+        normed,
+        proj,
+        weights,
+        mixed,
         after=mark,
     )
-    grads, row_sums = exchange(got[:ranks_attr], "attr", -1), Total(*got[ranks_attr:])
-    row_sums.parts[1] = swap(row_sums.parts[1], "attr", near[0])
+    row_sums = Total(keep, swap(send, "attr", near[0]))
     mark = []
     for bit in near[1:]:
-        mark = row_sums.halve(bit, after=mark)
+        mark = row_sums.halve("attr", bit, after=mark)
     for bit in far[1:]:
         mark = sums.add(bit, after=mark)
-    mark = row_sums.add(far[0], after=mark)
-    (grad_cells,) = call(kernel(join_kernel), [(cells.shape, BF)], [((count, E), F32)], *grads, after=mark)
-    mark = [grad_cells]
+    grads = call(
+        kernel(rows_end_kernel), row_tiles, [], Far(qkv_attr), x, Near(grad), Near(grad_proj), after=mark
+    )
+    row_sums.add(far[0], after=mark)
+    grads = exchange(grads, "attr", -1)
+    mark = grads[1:]
     for bit in far[1:]:
         mark = row_sums.add(bit, after=mark)
     mark = sums.add(after=mark)
-    parts = sums.spread(near)
-    row_sums.add(after=mark)
-    row_parts = row_sums.spread(near)
-    grad_qkv_samp, grad_out_samp, grad_up, grad_down = call(
-        functools.partial(finish_cols_kernel, factor, near),
-        [((E, 3 * E), F32), ((E, E), F32), ((E, FF), F32), ((E, FF), F32)],
-        [((cols_sums, LANES), BF)],
-        *parts,
-    )
+
+    def last_sum():
+        last = row_sums.add(after=mark)
+        return last, last
+
+    last, parts = sums.spread_after(near, last_sum)
+
+    def middle():
+        (cells_out,) = call(kernel(join_kernel), [(cells.shape, BF)], [((count, E), F32)], *grads, after=last)
+        weights_out = call(
+            functools.partial(finish_cols_kernel, factor, near),
+            [((E, 3 * E), F32), ((E, E), F32), ((E, FF), F32), ((E, FF), F32)],
+            [((cols_sums, LANES), BF)],
+            *parts,
+        )
+        results = [cells_out, *weights_out]
+        return results, [Far(cells_out), Far(weights_out[0])]
+
+    results, row_parts = row_sums.spread_after(near, middle)
+    grad_cells, grad_qkv_samp, grad_out_samp, grad_up, grad_down = results
     grad_qkv_attr, grad_out_attr = call(
         functools.partial(finish_rows_kernel, factor, near),
         [((E, 3 * E), F32), ((E, E), F32)],

time: 86 us -> 84 us (0.977)
  waiting for transfers between devices: 31.6 us -> 28.6 us
  Pallas kernels: 21.3 us -> 22.6 us
  local copies, waits for them, and re-layouts: 0.93 us -> 0.01 us
    ppermute x14, waiting for transfers between devices: 21.9 us -> 18.9 us  [swap(): return lax.ppermute(part, axis, [(i, i ^ bit) for i in range(size)])]
    pallas_call x19 -> x22, Pallas kernels: 21.3 us -> 22.6 us  [call(): pl.pallas_call(kernel, out_shape=[(pltpu.VMEM if out[2:] else jax.ShapeDt...]
    unnamed x4 -> x2, local copies, waits for them, and re-layouts: 0.93 us -> 0.01 us
  transfers between devices with their start and end apart: 35 -> 35, of which waited for: 17 -> 17; matrix products, arithmetic and copies ran while one was open for 0% -> 0% of each run, Pallas kernels for 10% -> 12%
where the time goes in v3:
time: 84 us; the launch traced here: 83.7 us
  starting transfers between devices  31.7 us (38%)
  waiting for transfers between devices  28.6 us (34%)
  Pallas kernels  22.6 us (27%)
  between operations  0.88 us (1%)
    ppermute x21, starting transfers between devices, exchange(): lax.ppermute(tiles[k], axis, [(i, (i + sign * k) % size) for i in range(s...  23.6 us
    pallas_call x22, Pallas kernels, call(): pl.pallas_call(kernel, out_shape=[(pltpu.VMEM if out[2:] else jax.ShapeDt...  22.6 us
    ppermute x14, waiting for transfers between devices, swap(): return lax.ppermute(part, axis, [(i, i ^ bit) for i in range(size)])  18.9 us
    ppermute x21, waiting for transfers between devices, exchange(): lax.ppermute(tiles[k], axis, [(i, (i + sign * k) % size) for i in range(s...  9.68 us
    ppermute x14, starting transfers between devices, swap(): return lax.ppermute(part, axis, [(i, i ^ bit) for i in range(size)])  8.12 us
  transfers between devices with their start and end apart: 35, of which 17 were waited for; matrix products, arithmetic and copies ran while one was open for 0% of the time, Pallas kernels for 12%

profile of v3, /device:TPU:0, one launch (start us, length us, event | category | flops | bytes accessed | tf_op | source)
XLA Modules:
  0.0 83.7 jit_solution(10495281105003824556)
XLA Ops:
  0.6 1.5 %shard_map.144 = (bf16[192,128]{1,0:T(8,128)(2,1)S(1)}, bf16[192,128]{1,0:T(8,128)(2,1)S(1)}, bf16[192,128]{1,0:T(8,128)(2,1)S(1)}, bf16[192,128]{1,0:T(8,128)(2,1)S(1)}) custom-call(bf16[8,12288]{1,0:T(8,128)(2,1)} %refs_0_.3), custom_call_target="tpu_custom_call" | custom-call | tf_op jit(solution)/shard_map/pallas_call | solution.py:470
  2.1 0.5 collective-permute-start
  2.6 2.6 %collective-permute-start.1 = (bf16[192,128]{1,0:T(8,128)(2,1)S(1)}, bf16[192,128]{1,0:T(8,128)(2,1)S(1)}, u32[]{:S(2)}, u32[]{:S(2)}) collective-permute-start(bf16[192,128]{1,0:T(8,128)(2,1)S(1)} %get-tuple-element.72), channel_id=1, source_target_pairs={{0,2},{1,3},{2,0},{3,1},{4,6},{5,7},{6,4},{7,5},{8,10},{9,11},{10,... | collective-permute-start | bytes 147464 | tf_op jit(solution)/shard_map/ppermute | solution.py:487
  5.2 1.4 %collective-permute-start.2 = (bf16[192,128]{1,0:T(8,128)(2,1)S(1)}, bf16[192,128]{1,0:T(8,128)(2,1)S(1)}, u32[]{:S(2)}, u32[]{:S(2)}) collective-permute-start(bf16[192,128]{1,0:T(8,128)(2,1)S(1)} %get-tuple-element.73), channel_id=1, source_target_pairs={{0,3},{1,0},{2,1},{3,2},{4,7},{5,4},{6,5},{7,6},{8,11},{9,8},{10,9... | collective-permute-start | bytes 147464 | tf_op jit(solution)/shard_map/ppermute | solution.py:487
  6.6 2.1 %shard_map.145 = (bf16[192,128]{1,0:T(8,128)(2,1)S(1)}, bf16[192,128]{1,0:T(8,128)(2,1)S(1)}, bf16[192,128]{1,0:T(8,128)(2,1)S(1)}, bf16[192,128]{1,0:T(8,128)(2...) custom-call(bf16[8,12288]{1,0:T(8,128)(2,1)} %refs_0_.4, ...), custom_call_target="tpu_custom_call" | custom-call | tf_op jit(solution)/shard_map/pallas_call | solution.py:470
  8.7 2.6 %shard_map.146 = (bf16[192,128]{1,0:T(8,128)(2,1)S(1)}, bf16[192,128]{1,0:T(8,128)(2,1)S(1)}, bf16[192,128]{1,0:T(8,128)(2,1)S(1)}, bf16[192,128]{1,0:T(8,128)(2...) custom-call(bf16[192,128]{1,0:T(8,128)(2,1)S(1)} %get-tuple-element., ...), custom_call_target="tpu_custom_call" | custom-call | tf_op jit(solution)/shard_map/pallas_call | solution.py:470
  11.3 1.4 %collective-permute-start.3 = (bf16[192,128]{1,0:T(8,128)(2,1)S(1)}, bf16[192,128]{1,0:T(8,128)(2,1)S(1)}, u32[]{:S(2)}, u32[]{:S(2)}) collective-permute-start(bf16[192,128]{1,0:T(8,128)(2,1)S(1)} %get-tuple-element.78), channel_id=1, source_target_pairs={{0,3},{1,0},{2,1},{3,2},{4,7},{5,4},{6,5},{7,6},{8,11},{9,8},{10,9... | collective-permute-start | bytes 147464 | tf_op jit(solution)/shard_map/ppermute | solution.py:487
  12.7 0.3 collective-permute-start.4
  13.0 1.8 %collective-permute-start.9 = (bf16[192,128]{1,0:T(8,128)(2,1)S(1)}, bf16[192,128]{1,0:T(8,128)(2,1)S(1)}, u32[]{:S(2)}, u32[]{:S(2)}) collective-permute-start(bf16[192,128]{1,0:T(8,128)(2,1)S(1)} %get-tuple-element.86), channel_id=1, source_target_pairs={{0,4},{4,8},{8,12},{12,0},{1,5},{5,9},{9,13},{13,1},{2,6},{6,10},{... | collective-permute-start | bytes 147464 | tf_op jit(solution)/shard_map/ppermute | solution.py:487
  14.8 2.6 %collective-permute-start.10 = (bf16[192,128]{1,0:T(8,128)(2,1)S(1)}, bf16[192,128]{1,0:T(8,128)(2,1)S(1)}, u32[]{:S(2)}, u32[]{:S(2)}) collective-permute-start(bf16[192,128]{1,0:T(8,128)(2,1)S(1)} %get-tuple-element.87), channel_id=1, source_target_pairs={{0,8},{4,12},{8,0},{12,4},{1,9},{5,13},{9,1},{13,5},{2,10},{6,14},... | collective-permute-start | bytes 147464 | tf_op jit(solution)/shard_map/ppermute | solution.py:487
  17.4 1.3 %collective-permute-start.11 = (bf16[192,128]{1,0:T(8,128)(2,1)S(1)}, bf16[192,128]{1,0:T(8,128)(2,1)S(1)}, u32[]{:S(2)}, u32[]{:S(2)}) collective-permute-start(bf16[192,128]{1,0:T(8,128)(2,1)S(1)} %get-tuple-element.88), channel_id=1, source_target_pairs={{0,12},{4,0},{8,4},{12,8},{1,13},{5,1},{9,5},{13,9},{2,14},{6,2},{... | collective-permute-start | bytes 147464 | tf_op jit(solution)/shard_map/ppermute | solution.py:487
  18.8 0.3 shard_map.147
  19.1 0.7 collective-permute-start.6
  19.8 2.0 %collective-permute-start.7 = (bf16[192,128]{1,0:T(8,128)(2,1)S(1)}, bf16[192,128]{1,0:T(8,128)(2,1)S(1)}, u32[]{:S(2)}, u32[]{:S(2)}) collective-permute-start(bf16[192,128]{1,0:T(8,128)(2,1)S(1)} %get-tuple-element.83), channel_id=1, source_target_pairs={{0,8},{4,12},{8,0},{12,4},{1,9},{5,13},{9,1},{13,5},{2,10},{6,14},... | collective-permute-start | bytes 147464 | tf_op jit(solution)/shard_map/ppermute | solution.py:487
  21.8 1.3 %collective-permute-start.8 = (bf16[192,128]{1,0:T(8,128)(2,1)S(1)}, bf16[192,128]{1,0:T(8,128)(2,1)S(1)}, u32[]{:S(2)}, u32[]{:S(2)}) collective-permute-start(bf16[192,128]{1,0:T(8,128)(2,1)S(1)} %get-tuple-element.84), channel_id=1, source_target_pairs={{0,12},{4,0},{8,4},{12,8},{1,13},{5,1},{9,5},{13,9},{2,14},{6,2},{... | collective-permute-start | bytes 147464 | tf_op jit(solution)/shard_map/ppermute | solution.py:487
  23.2 2.5 %collective-permute-done.6.refs_1_ = bf16[192,128]{1,0:T(8,128)(2,1)S(1)} collective-permute-done((bf16[192,128]{1,0:T(8,128)(2,1)S(1)}, bf16[192,128]{1,0:T(8,128)(2,1)S(1)}, u32[]{:S(2)}, u32[]{:S(2)}) %collective-permute-start.6) | collective-permute-done | bytes 49184 | tf_op jit(solution)/shard_map/ppermute | solution.py:487
  25.7 1.7 %collective-permute-done.7.refs_2_ = bf16[192,128]{1,0:T(8,128)(2,1)S(1)} collective-permute-done((bf16[192,128]{1,0:T(8,128)(2,1)S(1)}, bf16[192,128]{1,0:T(8,128)(2,1)S(1)}, u32[]{:S(2)}, u32[]{:S(2)}) %collective-permute-start.7) | collective-permute-done | bytes 49184 | tf_op jit(solution)/shard_map/ppermute | solution.py:487
  27.4 6.0 %shard_map.148 = (bf16[192,128]{1,0:T(8,128)(2,1)S(1)}, bf16[192,128]{1,0:T(8,128)(2,1)S(1)}, bf16[192,128]{1,0:T(8,128)(2,1)S(1)}, bf16[192,128]{1,0:T(8,128)(2...) custom-call(bf16[192,128]{1,0:T(8,128)(2,1)S(1)} %get-tuple-element., ...), custom_call_target="tpu_custom_call" | custom-call | tf_op jit(solution)/shard_map/pallas_call | solution.py:470
  33.4 1.1 %shard_map.149 = (bf16[1728,128]{1,0:T(8,128)(2,1)S(1)}, bf16[1728,128]{1,0:T(8,128)(2,1)S(1)}) custom-call(bf16[192,512]{1,0:T(8,128)(2,1)S(1)} %get-tuple-element.97.refs_0_, bf16[192,512]{1,0:T(8,128)(2,1)S(1)} %get-tuple-element.98.refs_1_, bf16[192,512]{1,0:T(8,128)(2,1)S(1)} %get-tuple-element.99.refs_2_, ...), custom_call_target="tpu_custom_call" | custom-call | tf_op jit(solution)/shard_map/pallas_call | solution.py:470
  34.5 0.1 collective-permute-start.18
  34.6 1.8 %collective-permute-done.18.refs_1_ = bf16[1728,128]{1,0:T(8,128)(2,1)S(1)} collective-permute-done((bf16[1728,128]{1,0:T(8,128)(2,1)S(1)}, bf16[1728,128]{1,0:T(8,128)(2,1)S(1)}, u32[]{:S(2)}, u32[]{:S(2)}) %collective-permute-start.18) | collective-permute-done | bytes 442400 | tf_op jit(solution)/shard_map/ppermute | solution.py:494
  36.4 0.1 shard_map.151
  36.5 0.5 collective-permute-start.19
  36.9 2.6 %collective-permute-start.12 = (bf16[192,128]{1,0:T(8,128)(2,1)S(1)}, bf16[192,128]{1,0:T(8,128)(2,1)S(1)}, u32[]{:S(2)}, u32[]{:S(2)}) collective-permute-start(bf16[192,128]{1,0:T(8,128)(2,1)S(1)} %get-tuple-element.94), channel_id=1, source_target_pairs={{0,12},{4,0},{8,4},{12,8},{1,13},{5,1},{9,5},{13,9},{2,14},{6,2},{... | collective-permute-start | bytes 147464 | tf_op jit(solution)/shard_map/ppermute | solution.py:487
  39.5 0.2 collective-permute-start.13
  39.8 0.3 collective-permute-start.14
  40.1 3.9 %collective-permute-done.19.refs_1_ = bf16[864,128]{1,0:T(8,128)(2,1)S(1)} collective-permute-done((bf16[864,128]{1,0:T(8,128)(2,1)S(1)}, bf16[864,128]{1,0:T(8,128)(2,1)S(1)}, u32[]{:S(2)}, u32[]{:S(2)}) %collective-permute-start.19) | collective-permute-done | bytes 221216 | tf_op jit(solution)/shard_map/ppermute | solution.py:494
  44.1 1.3 %collective-permute-start.20 = (bf16[864,128]{1,0:T(8,128)(2,1)S(1)}, bf16[864,128]{1,0:T(8,128)(2,1)S(1)}, u32[]{:S(2)}, u32[]{:S(2)}) collective-permute-start(bf16[864,128]{1,0:T(8,128)(2,1)S(1)} %shard_map.152.refs_9_.refs_0_), channel_id=1, source_target_pairs={{0,4},{4,0},{8,12},{12,8},{1,5},{5,1},{9,13},{13,9},{2,6},{6,2},{1... | collective-permute-start | bytes 663560 | tf_op jit(solution)/shard_map/ppermute | solution.py:494
  45.3 0.3 collective-permute-done.14.refs_3_
  45.7 0.4 shard_map.150
  46.0 0.1 collective-permute-start.15
  46.1 1.6 %collective-permute-start.16 = (bf16[192,128]{1,0:T(8,128)(2,1)S(1)}, bf16[192,128]{1,0:T(8,128)(2,1)S(1)}, u32[]{:S(2)}, u32[]{:S(2)}) collective-permute-start(bf16[192,128]{1,0:T(8,128)(2,1)S(1)} %get-tuple-element.108), channel_id=1, source_target_pairs={{0,2},{1,3},{2,0},{3,1},{4,6},{5,7},{6,4},{7,5},{8,10},{9,11},{10,... | collective-permute-start | bytes 147464 | tf_op jit(solution)/shard_map/ppermute | solution.py:487
  47.7 1.4 %collective-permute-start.17 = (bf16[192,128]{1,0:T(8,128)(2,1)S(1)}, bf16[192,128]{1,0:T(8,128)(2,1)S(1)}, u32[]{:S(2)}, u32[]{:S(2)}) collective-permute-start(bf16[192,128]{1,0:T(8,128)(2,1)S(1)} %get-tuple-element.109), channel_id=1, source_target_pairs={{0,3},{1,0},{2,1},{3,2},{4,7},{5,4},{6,5},{7,6},{8,11},{9,8},{10,9... | collective-permute-start | bytes 147464 | tf_op jit(solution)/shard_map/ppermute | solution.py:487
  49.1 0.5 collective-permute-done.15.refs_1_
  49.6 0.7 collective-permute-done.16.refs_2_
  50.3 0.6 collective-permute-done.17.refs_3_
  50.9 3.1 %shard_map.153 = (bf16[576,128]{1,0:T(8,128)(2,1)S(1)}, bf16[576,128]{1,0:T(8,128)(2,1)S(1)}, bf16[192,512]{1,0:T(8,128)(2,1)S(1)}, bf16[576,512]{1,0:T(8,128)(2,1)S(1)}) custom-call(bf16[192,128]{1,0:T(8,128)(2,1)S(1)} %get-tuple-element.106.refs_0_, bf16[192,128]{1,0:T(8,128)(2,1)S(1)} %collective-permute-done.15.refs_1_, ...), custom_call_target="tpu_custom_call" | custom-call | tf_op jit(solution)/shard_map/pallas_call | solution.py:470
  54.0 0.7 collective-permute-start.21
  54.7 1.0 %collective-permute-done.21.refs_1_ = bf16[576,128]{1,0:T(8,128)(2,1)S(1)} collective-permute-done((bf16[576,128]{1,0:T(8,128)(2,1)S(1)}, bf16[576,128]{1,0:T(8,128)(2,1)S(1)}, u32[]{:S(2)}, u32[]{:S(2)}) %collective-permute-start.21) | collective-permute-done | bytes 147488 | tf_op jit(solution)/shard_map/ppermute | solution.py:494
  55.7 0.1 shard_map.155.refs_4_.refs_2_.refs_0_
  55.8 1.4 %collective-permute-start.28 = (bf16[864,128]{1,0:T(8,128)(2,1)S(1)}, bf16[864,128]{1,0:T(8,128)(2,1)S(1)}, u32[]{:S(2)}, u32[]{:S(2)}) collective-permute-start(bf16[864,128]{1,0:T(8,128)(2,1)S(1)} %shard_map.155.refs_4_.refs_2_.refs_0_), channel_id=1, source_target_pairs={{0,8},{4,12},{8,0},{12,4},{1,9},{5,13},{9,1},{13,5},{2,10},{6,14},... | collective-permute-start | bytes 663560 | tf_op jit(solution)/shard_map/ppermute | solution.py:494
  57.2 0.9 %collective-permute-start.25 = (bf16[288,128]{1,0:T(8,128)(2,1)S(1)}, bf16[288,128]{1,0:T(8,128)(2,1)S(1)}, u32[]{:S(2)}, u32[]{:S(2)}) collective-permute-start(bf16[288,128]{1,0:T(8,128)(2,1)S(1)} %get-tuple-element.126), channel_id=1, source_target_pairs={{0,2},{1,3},{2,0},{3,1},{4,6},{5,7},{6,4},{7,5},{8,10},{9,11},{10,... | collective-permute-start | bytes 221192 | tf_op jit(solution)/shard_map/ppermute | solution.py:494
  58.1 3.5 %collective-permute-done.25.refs_1_ = bf16[288,128]{1,0:T(8,128)(2,1)S(1)} collective-permute-done((bf16[288,128]{1,0:T(8,128)(2,1)S(1)}, bf16[288,128]{1,0:T(8,128)(2,1)S(1)}, u32[]{:S(2)}, u32[]{:S(2)}) %collective-permute-start.25) | collective-permute-done | bytes 73760 | tf_op jit(solution)/shard_map/ppermute | solution.py:494
  61.5 0.7 collective-permute-start.26
  62.2 1.6 %shard_map.156 = (bf16[192,128]{1,0:T(8,128)(2,1)S(1)}, bf16[192,128]{1,0:T(8,128)(2,1)S(1)}, bf16[192,128]{1,0:T(8,128)(2,1)S(1)}, bf16[192,128]{1,0:T(8,128)(2,1)S(1)}) custom-call(bf16[192,576]{1,0:T(8,128)(2,1)} %refs_0_.5, bf16[192,512]{1,0:T(8,128)(2,1)S(1)} %get-tuple-element.76.refs_1_, bf16[192,512]{1,0:T(8,128)(2,1)S(1)} %get-tuple-element.117.refs_2_, ...), custom_call_target="tpu_custom_call" | custom-call | tf_op jit(solution)/shard_map/pallas_call | solution.py:470
  63.9 0.1 collective-permute-start.22
  63.9 1.1 %collective-permute-start.23 = (bf16[192,128]{1,0:T(8,128)(2,1)S(1)}, bf16[192,128]{1,0:T(8,128)(2,1)S(1)}, u32[]{:S(2)}, u32[]{:S(2)}) collective-permute-start(bf16[192,128]{1,0:T(8,128)(2,1)S(1)} %get-tuple-element.124), channel_id=1, source_target_pairs={{0,2},{1,3},{2,0},{3,1},{4,6},{5,7},{6,4},{7,5},{8,10},{9,11},{10,... | collective-permute-start | bytes 147464 | tf_op jit(solution)/shard_map/ppermute | solution.py:487
  65.1 0.2 collective-permute-start.24
  65.2 0.4 collective-permute-done.22.refs_2_.refs_1_
  65.7 2.6 %collective-permute-done.23.refs_3_.refs_2_ = bf16[192,128]{1,0:T(8,128)(2,1)S(1)} collective-permute-done((bf16[192,128]{1,0:T(8,128)(2,1)S(1)}, bf16[192,128]{1,0:T(8,128)(2,1)S(1)}, u32[]{:S(2)}, u32[]{:S(2)}) %collective-permute-start.23) | collective-permute-done | bytes 49184 | tf_op jit(solution)/shard_map/ppermute | solution.py:487
  68.2 0.4 collective-permute-done.24.refs_4_.refs_3_
  68.6 1.4 %collective-permute-done.26.refs_1_ = bf16[288,128]{1,0:T(8,128)(2,1)S(1)} collective-permute-done((bf16[288,128]{1,0:T(8,128)(2,1)S(1)}, bf16[288,128]{1,0:T(8,128)(2,1)S(1)}, u32[]{:S(2)}, u32[]{:S(2)}) %collective-permute-start.26) | collective-permute-done | bytes 73760 | tf_op jit(solution)/shard_map/ppermute | solution.py:494
  70.1 0.7 collective-permute-start.32
  70.8 0.6 collective-permute-start.27
  71.4 5.2 %collective-permute-done.27.refs_1_ = bf16[288,128]{1,0:T(8,128)(2,1)S(1)} collective-permute-done((bf16[288,128]{1,0:T(8,128)(2,1)S(1)}, bf16[288,128]{1,0:T(8,128)(2,1)S(1)}, u32[]{:S(2)}, u32[]{:S(2)}) %collective-permute-start.27) | collective-permute-done | bytes 73760 | tf_op jit(solution)/shard_map/ppermute | solution.py:494
  76.7 0.1 collective-permute-start.33
  76.8 1.1 %collective-permute-start.30 = (bf16[288,128]{1,0:T(8,128)(2,1)S(1)}, bf16[288,128]{1,0:T(8,128)(2,1)S(1)}, u32[]{:S(2)}, u32[]{:S(2)}) collective-permute-start(bf16[288,128]{1,0:T(8,128)(2,1)S(1)} %shard_map.160.refs_4_.refs_1_.refs_0_), channel_id=1, source_target_pairs={{0,2},{1,3},{2,0},{3,1},{4,6},{5,7},{6,4},{7,5},{8,10},{9,11},{10,... | collective-permute-start | bytes 221192 | tf_op jit(solution)/shard_map/ppermute | solution.py:494
  77.9 0.2 collective-permute-start.29
  78.1 1.1 %shard_map.161.refs_1_ = bf16[8,12288]{1,0:T(8,128)(2,1)} custom-call(bf16[192,128]{1,0:T(8,128)(2,1)S(1)} %get-tuple-element.122.refs_0_, bf16[192,128]{1,0:T(8,128)(2,1)S(1)} %collective-permute-done.22.refs_2_.refs_1_, bf16[192,128]{1,0:T(8,128)(2,1)S(1)} %collective-permute-done.23.refs_3_.refs_2_, ...), custom_call_target="tpu_custom_call" | custom-call | tf_op jit(solution)/shard_map/pallas_call | solution.py:470
  79.2 1.4 %shard_map.163 = (f32[192,576]{1,0:T(8,128)}, f32[192,192]{1,0:T(8,128)}, f32[192,768]{1,0:T(8,128)}, f32[192,768]{1,0:T(8,128)}) custom-call(bf16[864,128]{1,0:T(8,128)(2,1)S(1)} %shard_map.159.refs_2_.refs_0_, bf16[864,128]{1,0:T(8,128)(2,1)S(1)} %collective-permute-done.31.refs_1_, bf16[864,128]{1,0:T(8,128)(2,1)S(1)} %collective-permute-done.32.refs_0_.refs_2_, ...), custom_call_target="tpu_custom_call" | custom-call | tf_op jit(solution)/shard_map/pallas_call | solution.py:470
  80.6 0.9 %collective-permute-done.30.refs_0_.refs_2_ = bf16[288,128]{1,0:T(8,128)(2,1)S(1)} collective-permute-done((bf16[288,128]{1,0:T(8,128)(2,1)S(1)}, bf16[288,128]{1,0:T(8,128)(2,1)S(1)}, u32[]{:S(2)}, u32[]{:S(2)}) %collective-permute-start.30) | collective-permute-done | bytes 73760 | tf_op jit(solution)/shard_map/ppermute | solution.py:494
  81.5 0.1 collective-permute-start.34
  81.6 1.2 %collective-permute-done.34.refs_3_ = bf16[288,128]{1,0:T(8,128)(2,1)S(1)} collective-permute-done((bf16[288,128]{1,0:T(8,128)(2,1)S(1)}, bf16[288,128]{1,0:T(8,128)(2,1)S(1)}, u32[]{:S(2)}, u32[]{:S(2)}) %collective-permute-start.34) | collective-permute-done | bytes 73760 | tf_op jit(solution)/shard_map/ppermute | solution.py:494
  82.8 0.9 %shard_map.165 = (f32[192,576]{1,0:T(8,128)}, f32[192,192]{1,0:T(8,128)}) custom-call(bf16[288,128]{1,0:T(8,128)(2,1)S(1)} %shard_map.160.refs_4_.refs_1_.refs_0_, bf16[288,128]{1,0:T(8,128)(2,1)S(1)} %collective-permute-done.29.refs_1_, bf16[288,128]{1,0:T(8,128)(2,1)S(1)} %collective-permute-done.30.refs_0_.refs_2_, ...), custom_call_target="tpu_custom_call" | custom-call | tf_op jit(solution)/shard_map/pallas_call | solution.py:470
  (30 shorter events, 0.3 us)
Async XLA Ops:
  0.6 26.7 %copy-start = (s32[32]{0:T(128)S(1)}, s32[32]{0:T(128)}, u32[]{:S(2)}) copy-start(s32[32]{0:T(128)} %param.17) | copy-start | bytes 388
  2.1 6.6 %collective-permute-start = (bf16[192,128]{1,0:T(8,128)(2,1)S(1)}, bf16[192,128]{1,0:T(8,128)(2,1)S(1)}, u32[]{:S(2)}, u32[]{:S(2)}) collective-permute-start(bf16[192,128]{1,0:T(8,128)(2,1)S(1)} %get-tuple-element.71), channel_id=1, source_target_pairs={{0,1},{1,2},{2,3},{3,0},{4,5},{5,6},{6,7},{7,4},{8,9},{9,10},{10,1... | collective-permute-start | bytes 147464 | tf_op jit(solution)/shard_map/ppermute | solution.py:487
  2.6 6.1 %collective-permute-start.1 = (bf16[192,128]{1,0:T(8,128)(2,1)S(1)}, bf16[192,128]{1,0:T(8,128)(2,1)S(1)}, u32[]{:S(2)}, u32[]{:S(2)}) collective-permute-start(bf16[192,128]{1,0:T(8,128)(2,1)S(1)} %get-tuple-element.72), channel_id=1, source_target_pairs={{0,2},{1,3},{2,0},{3,1},{4,6},{5,7},{6,4},{7,5},{8,10},{9,11},{10,... | collective-permute-start | bytes 147464 | tf_op jit(solution)/shard_map/ppermute | solution.py:487
  5.2 3.5 %collective-permute-start.2 = (bf16[192,128]{1,0:T(8,128)(2,1)S(1)}, bf16[192,128]{1,0:T(8,128)(2,1)S(1)}, u32[]{:S(2)}, u32[]{:S(2)}) collective-permute-start(bf16[192,128]{1,0:T(8,128)(2,1)S(1)} %get-tuple-element.73), channel_id=1, source_target_pairs={{0,3},{1,0},{2,1},{3,2},{4,7},{5,4},{6,5},{7,6},{8,11},{9,8},{10,9... | collective-permute-start | bytes 147464 | tf_op jit(solution)/shard_map/ppermute | solution.py:487
  11.3 6.1 %collective-permute-start.3 = (bf16[192,128]{1,0:T(8,128)(2,1)S(1)}, bf16[192,128]{1,0:T(8,128)(2,1)S(1)}, u32[]{:S(2)}, u32[]{:S(2)}) collective-permute-start(bf16[192,128]{1,0:T(8,128)(2,1)S(1)} %get-tuple-element.78), channel_id=1, source_target_pairs={{0,3},{1,0},{2,1},{3,2},{4,7},{5,4},{6,5},{7,6},{8,11},{9,8},{10,9... | collective-permute-start | bytes 147464 | tf_op jit(solution)/shard_map/ppermute | solution.py:487
  12.7 6.1 %collective-permute-start.4 = (bf16[192,128]{1,0:T(8,128)(2,1)S(1)}, bf16[192,128]{1,0:T(8,128)(2,1)S(1)}, u32[]{:S(2)}, u32[]{:S(2)}) collective-permute-start(bf16[192,128]{1,0:T(8,128)(2,1)S(1)} %get-tuple-element.79), channel_id=1, source_target_pairs={{0,2},{1,3},{2,0},{3,1},{4,6},{5,7},{6,4},{7,5},{8,10},{9,11},{10,... | collective-permute-start | bytes 147464 | tf_op jit(solution)/shard_map/ppermute | solution.py:487
  13.0 5.8 %collective-permute-start.5 = (bf16[192,128]{1,0:T(8,128)(2,1)S(1)}, bf16[192,128]{1,0:T(8,128)(2,1)S(1)}, u32[]{:S(2)}, u32[]{:S(2)}) collective-permute-start(bf16[192,128]{1,0:T(8,128)(2,1)S(1)} %get-tuple-element.80), channel_id=1, source_target_pairs={{0,1},{1,2},{2,3},{3,0},{4,5},{5,6},{6,7},{7,4},{8,9},{9,10},{10,1... | collective-permute-start | bytes 147464 | tf_op jit(solution)/shard_map/ppermute | solution.py:487
  13.0 8.8 %collective-permute-start.9 = (bf16[192,128]{1,0:T(8,128)(2,1)S(1)}, bf16[192,128]{1,0:T(8,128)(2,1)S(1)}, u32[]{:S(2)}, u32[]{:S(2)}) collective-permute-start(bf16[192,128]{1,0:T(8,128)(2,1)S(1)} %get-tuple-element.86), channel_id=1, source_target_pairs={{0,4},{4,8},{8,12},{12,0},{1,5},{5,9},{9,13},{13,1},{2,6},{6,10},{... | collective-permute-start | bytes 147464 | tf_op jit(solution)/shard_map/ppermute | solution.py:487
  14.8 8.3 %collective-permute-start.10 = (bf16[192,128]{1,0:T(8,128)(2,1)S(1)}, bf16[192,128]{1,0:T(8,128)(2,1)S(1)}, u32[]{:S(2)}, u32[]{:S(2)}) collective-permute-start(bf16[192,128]{1,0:T(8,128)(2,1)S(1)} %get-tuple-element.87), channel_id=1, source_target_pairs={{0,8},{4,12},{8,0},{12,4},{1,9},{5,13},{9,1},{13,5},{2,10},{6,14},... | collective-permute-start | bytes 147464 | tf_op jit(solution)/shard_map/ppermute | solution.py:487
  17.4 5.7 %collective-permute-start.11 = (bf16[192,128]{1,0:T(8,128)(2,1)S(1)}, bf16[192,128]{1,0:T(8,128)(2,1)S(1)}, u32[]{:S(2)}, u32[]{:S(2)}) collective-permute-start(bf16[192,128]{1,0:T(8,128)(2,1)S(1)} %get-tuple-element.88), channel_id=1, source_target_pairs={{0,12},{4,0},{8,4},{12,8},{1,13},{5,1},{9,5},{13,9},{2,14},{6,2},{... | collective-permute-start | bytes 147464 | tf_op jit(solution)/shard_map/ppermute | solution.py:487
  19.1 6.6 %collective-permute-start.6 = (bf16[192,128]{1,0:T(8,128)(2,1)S(1)}, bf16[192,128]{1,0:T(8,128)(2,1)S(1)}, u32[]{:S(2)}, u32[]{:S(2)}) collective-permute-start(bf16[192,128]{1,0:T(8,128)(2,1)S(1)} %get-tuple-element.82), channel_id=1, source_target_pairs={{0,4},{4,8},{8,12},{12,0},{1,5},{5,9},{9,13},{13,1},{2,6},{6,10},{... | collective-permute-start | bytes 147464 | tf_op jit(solution)/shard_map/ppermute | solution.py:487
  19.8 7.6 %collective-permute-start.7 = (bf16[192,128]{1,0:T(8,128)(2,1)S(1)}, bf16[192,128]{1,0:T(8,128)(2,1)S(1)}, u32[]{:S(2)}, u32[]{:S(2)}) collective-permute-start(bf16[192,128]{1,0:T(8,128)(2,1)S(1)} %get-tuple-element.83), channel_id=1, source_target_pairs={{0,8},{4,12},{8,0},{12,4},{1,9},{5,13},{9,1},{13,5},{2,10},{6,14},... | collective-permute-start | bytes 147464 | tf_op jit(solution)/shard_map/ppermute | solution.py:487
  21.8 5.5 %collective-permute-start.8 = (bf16[192,128]{1,0:T(8,128)(2,1)S(1)}, bf16[192,128]{1,0:T(8,128)(2,1)S(1)}, u32[]{:S(2)}, u32[]{:S(2)}) collective-permute-start(bf16[192,128]{1,0:T(8,128)(2,1)S(1)} %get-tuple-element.84), channel_id=1, source_target_pairs={{0,12},{4,0},{8,4},{12,8},{1,13},{5,1},{9,5},{13,9},{2,14},{6,2},{... | collective-permute-start | bytes 147464 | tf_op jit(solution)/shard_map/ppermute | solution.py:487
  34.5 1.9 %collective-permute-start.18 = (bf16[1728,128]{1,0:T(8,128)(2,1)S(1)}, bf16[1728,128]{1,0:T(8,128)(2,1)S(1)}, u32[]{:S(2)}, u32[]{:S(2)}) collective-permute-start(bf16[1728,128]{1,0:T(8,128)(2,1)S(1)} %get-tuple-element.114), channel_id=1, source_target_pairs={{0,1},{1,0},{2,3},{3,2},{4,5},{5,4},{6,7},{7,6},{8,9},{9,8},{10,11... | collective-permute-start | bytes 1327112 | tf_op jit(solution)/shard_map/ppermute | solution.py:494
  36.5 7.5 %collective-permute-start.19 = (bf16[864,128]{1,0:T(8,128)(2,1)S(1)}, bf16[864,128]{1,0:T(8,128)(2,1)S(1)}, u32[]{:S(2)}, u32[]{:S(2)}) collective-permute-start(bf16[864,128]{1,0:T(8,128)(2,1)S(1)} %get-tuple-element.116), channel_id=1, source_target_pairs={{0,2},{1,3},{2,0},{3,1},{4,6},{5,7},{6,4},{7,5},{8,10},{9,11},{10,... | collective-permute-start | bytes 663560 | tf_op jit(solution)/shard_map/ppermute | solution.py:494
  36.9 8.4 %collective-permute-start.12 = (bf16[192,128]{1,0:T(8,128)(2,1)S(1)}, bf16[192,128]{1,0:T(8,128)(2,1)S(1)}, u32[]{:S(2)}, u32[]{:S(2)}) collective-permute-start(bf16[192,128]{1,0:T(8,128)(2,1)S(1)} %get-tuple-element.94), channel_id=1, source_target_pairs={{0,12},{4,0},{8,4},{12,8},{1,13},{5,1},{9,5},{13,9},{2,14},{6,2},{... | collective-permute-start | bytes 147464 | tf_op jit(solution)/shard_map/ppermute | solution.py:487
  39.5 5.8 %collective-permute-start.13 = (bf16[192,128]{1,0:T(8,128)(2,1)S(1)}, bf16[192,128]{1,0:T(8,128)(2,1)S(1)}, u32[]{:S(2)}, u32[]{:S(2)}) collective-permute-start(bf16[192,128]{1,0:T(8,128)(2,1)S(1)} %get-tuple-element.95), channel_id=1, source_target_pairs={{0,8},{4,12},{8,0},{12,4},{1,9},{5,13},{9,1},{13,5},{2,10},{6,14},... | collective-permute-start | bytes 147464 | tf_op jit(solution)/shard_map/ppermute | solution.py:487
  39.8 5.9 %collective-permute-start.14 = (bf16[192,128]{1,0:T(8,128)(2,1)S(1)}, bf16[192,128]{1,0:T(8,128)(2,1)S(1)}, u32[]{:S(2)}, u32[]{:S(2)}) collective-permute-start(bf16[192,128]{1,0:T(8,128)(2,1)S(1)} %get-tuple-element.96), channel_id=1, source_target_pairs={{0,4},{4,8},{8,12},{12,0},{1,5},{5,9},{9,13},{13,1},{2,6},{6,10},{... | collective-permute-start | bytes 147464 | tf_op jit(solution)/shard_map/ppermute | solution.py:487
  44.1 11.7 %collective-permute-start.20 = (bf16[864,128]{1,0:T(8,128)(2,1)S(1)}, bf16[864,128]{1,0:T(8,128)(2,1)S(1)}, u32[]{:S(2)}, u32[]{:S(2)}) collective-permute-start(bf16[864,128]{1,0:T(8,128)(2,1)S(1)} %shard_map.152.refs_9_.refs_0_), channel_id=1, source_target_pairs={{0,4},{4,0},{8,12},{12,8},{1,5},{5,1},{9,13},{13,9},{2,6},{6,2},{1... | collective-permute-start | bytes 663560 | tf_op jit(solution)/shard_map/ppermute | solution.py:494
  46.0 3.6 %collective-permute-start.15 = (bf16[192,128]{1,0:T(8,128)(2,1)S(1)}, bf16[192,128]{1,0:T(8,128)(2,1)S(1)}, u32[]{:S(2)}, u32[]{:S(2)}) collective-permute-start(bf16[192,128]{1,0:T(8,128)(2,1)S(1)} %get-tuple-element.107), channel_id=1, source_target_pairs={{0,1},{1,2},{2,3},{3,0},{4,5},{5,6},{6,7},{7,4},{8,9},{9,10},{10,1... | collective-permute-start | bytes 147464 | tf_op jit(solution)/shard_map/ppermute | solution.py:487
  46.1 4.2 %collective-permute-start.16 = (bf16[192,128]{1,0:T(8,128)(2,1)S(1)}, bf16[192,128]{1,0:T(8,128)(2,1)S(1)}, u32[]{:S(2)}, u32[]{:S(2)}) collective-permute-start(bf16[192,128]{1,0:T(8,128)(2,1)S(1)} %get-tuple-element.108), channel_id=1, source_target_pairs={{0,2},{1,3},{2,0},{3,1},{4,6},{5,7},{6,4},{7,5},{8,10},{9,11},{10,... | collective-permute-start | bytes 147464 | tf_op jit(solution)/shard_map/ppermute | solution.py:487
  47.7 3.1 %collective-permute-start.17 = (bf16[192,128]{1,0:T(8,128)(2,1)S(1)}, bf16[192,128]{1,0:T(8,128)(2,1)S(1)}, u32[]{:S(2)}, u32[]{:S(2)}) collective-permute-start(bf16[192,128]{1,0:T(8,128)(2,1)S(1)} %get-tuple-element.109), channel_id=1, source_target_pairs={{0,3},{1,0},{2,1},{3,2},{4,7},{5,4},{6,5},{7,6},{8,11},{9,8},{10,9... | collective-permute-start | bytes 147464 | tf_op jit(solution)/shard_map/ppermute | solution.py:487
  54.0 1.7 %collective-permute-start.21 = (bf16[576,128]{1,0:T(8,128)(2,1)S(1)}, bf16[576,128]{1,0:T(8,128)(2,1)S(1)}, u32[]{:S(2)}, u32[]{:S(2)}) collective-permute-start(bf16[576,128]{1,0:T(8,128)(2,1)S(1)} %get-tuple-element.120), channel_id=1, source_target_pairs={{0,1},{1,0},{2,3},{3,2},{4,5},{5,4},{6,7},{7,6},{8,9},{9,8},{10,11... | collective-permute-start | bytes 442376 | tf_op jit(solution)/shard_map/ppermute | solution.py:494
  55.8 14.2 %collective-permute-start.28 = (bf16[864,128]{1,0:T(8,128)(2,1)S(1)}, bf16[864,128]{1,0:T(8,128)(2,1)S(1)}, u32[]{:S(2)}, u32[]{:S(2)}) collective-permute-start(bf16[864,128]{1,0:T(8,128)(2,1)S(1)} %shard_map.155.refs_4_.refs_2_.refs_0_), channel_id=1, source_target_pairs={{0,8},{4,12},{8,0},{12,4},{1,9},{5,13},{9,1},{13,5},{2,10},{6,14},... | collective-permute-start | bytes 663560 | tf_op jit(solution)/shard_map/ppermute | solution.py:494
  57.2 4.4 %collective-permute-start.25 = (bf16[288,128]{1,0:T(8,128)(2,1)S(1)}, bf16[288,128]{1,0:T(8,128)(2,1)S(1)}, u32[]{:S(2)}, u32[]{:S(2)}) collective-permute-start(bf16[288,128]{1,0:T(8,128)(2,1)S(1)} %get-tuple-element.126), channel_id=1, source_target_pairs={{0,2},{1,3},{2,0},{3,1},{4,6},{5,7},{6,4},{7,5},{8,10},{9,11},{10,... | collective-permute-start | bytes 221192 | tf_op jit(solution)/shard_map/ppermute | solution.py:494
  61.5 8.5 %collective-permute-start.26 = (bf16[288,128]{1,0:T(8,128)(2,1)S(1)}, bf16[288,128]{1,0:T(8,128)(2,1)S(1)}, u32[]{:S(2)}, u32[]{:S(2)}) collective-permute-start(bf16[288,128]{1,0:T(8,128)(2,1)S(1)} %shard_map.157.refs_0_), channel_id=1, source_target_pairs={{0,4},{4,0},{8,12},{12,8},{1,5},{5,1},{9,13},{13,9},{2,6},{6,2},{1... | collective-permute-start | bytes 221192 | tf_op jit(solution)/shard_map/ppermute | solution.py:494
  63.9 1.8 %collective-permute-start.22 = (bf16[192,128]{1,0:T(8,128)(2,1)S(1)}, bf16[192,128]{1,0:T(8,128)(2,1)S(1)}, u32[]{:S(2)}, u32[]{:S(2)}) collective-permute-start(bf16[192,128]{1,0:T(8,128)(2,1)S(1)} %get-tuple-element.123), channel_id=1, source_target_pairs={{0,3},{1,0},{2,1},{3,2},{4,7},{5,4},{6,5},{7,6},{8,11},{9,8},{10,9... | collective-permute-start | bytes 147464 | tf_op jit(solution)/shard_map/ppermute | solution.py:487
  63.9 4.3 %collective-permute-start.23 = (bf16[192,128]{1,0:T(8,128)(2,1)S(1)}, bf16[192,128]{1,0:T(8,128)(2,1)S(1)}, u32[]{:S(2)}, u32[]{:S(2)}) collective-permute-start(bf16[192,128]{1,0:T(8,128)(2,1)S(1)} %get-tuple-element.124), channel_id=1, source_target_pairs={{0,2},{1,3},{2,0},{3,1},{4,6},{5,7},{6,4},{7,5},{8,10},{9,11},{10,... | collective-permute-start | bytes 147464 | tf_op jit(solution)/shard_map/ppermute | solution.py:487
  65.1 3.6 %collective-permute-start.24 = (bf16[192,128]{1,0:T(8,128)(2,1)S(1)}, bf16[192,128]{1,0:T(8,128)(2,1)S(1)}, u32[]{:S(2)}, u32[]{:S(2)}) collective-permute-start(bf16[192,128]{1,0:T(8,128)(2,1)S(1)} %get-tuple-element.125), channel_id=1, source_target_pairs={{0,1},{1,2},{2,3},{3,0},{4,5},{5,6},{6,7},{7,4},{8,9},{9,10},{10,1... | collective-permute-start | bytes 147464 | tf_op jit(solution)/shard_map/ppermute | solution.py:487
  70.1 6.6 %collective-permute-start.32 = (bf16[864,128]{1,0:T(8,128)(2,1)S(1)}, bf16[864,128]{1,0:T(8,128)(2,1)S(1)}, u32[]{:S(2)}, u32[]{:S(2)}) collective-permute-start(bf16[864,128]{1,0:T(8,128)(2,1)S(1)} %shard_map.159.refs_2_.refs_0_), channel_id=1, source_target_pairs={{0,2},{1,3},{2,0},{3,1},{4,6},{5,7},{6,4},{7,5},{8,10},{9,11},{10,... | collective-permute-start | bytes 663560 | tf_op jit(solution)/shard_map/ppermute | solution.py:494
  70.8 5.9 %collective-permute-start.27 = (bf16[288,128]{1,0:T(8,128)(2,1)S(1)}, bf16[288,128]{1,0:T(8,128)(2,1)S(1)}, u32[]{:S(2)}, u32[]{:S(2)}) collective-permute-start(bf16[288,128]{1,0:T(8,128)(2,1)S(1)} %shard_map.158.refs_2_.refs_0_), channel_id=1, source_target_pairs={{0,8},{4,12},{8,0},{12,4},{1,9},{5,13},{9,1},{13,5},{2,10},{6,14},... | collective-permute-start | bytes 221192 | tf_op jit(solution)/shard_map/ppermute | solution.py:494
  71.4 7.8 %collective-permute-start.31 = (bf16[864,128]{1,0:T(8,128)(2,1)S(1)}, bf16[864,128]{1,0:T(8,128)(2,1)S(1)}, u32[]{:S(2)}, u32[]{:S(2)}) collective-permute-start(bf16[864,128]{1,0:T(8,128)(2,1)S(1)} %shard_map.159.refs_2_.refs_0_), channel_id=1, source_target_pairs={{0,1},{1,0},{2,3},{3,2},{4,5},{5,4},{6,7},{7,6},{8,9},{9,8},{10,11... | collective-permute-start | bytes 663560 | tf_op jit(solution)/shard_map/ppermute | solution.py:494
  76.7 2.5 %collective-permute-start.33 = (bf16[864,128]{1,0:T(8,128)(2,1)S(1)}, bf16[864,128]{1,0:T(8,128)(2,1)S(1)}, u32[]{:S(2)}, u32[]{:S(2)}) collective-permute-start(bf16[864,128]{1,0:T(8,128)(2,1)S(1)} %shard_map.162), channel_id=1, source_target_pairs={{0,1},{1,0},{2,3},{3,2},{4,5},{5,4},{6,7},{7,6},{8,9},{9,8},{10,11... | collective-permute-start | bytes 663560 | tf_op jit(solution)/shard_map/ppermute | solution.py:494
  76.8 4.7 %collective-permute-start.30 = (bf16[288,128]{1,0:T(8,128)(2,1)S(1)}, bf16[288,128]{1,0:T(8,128)(2,1)S(1)}, u32[]{:S(2)}, u32[]{:S(2)}) collective-permute-start(bf16[288,128]{1,0:T(8,128)(2,1)S(1)} %shard_map.160.refs_4_.refs_1_.refs_0_), channel_id=1, source_target_pairs={{0,2},{1,3},{2,0},{3,1},{4,6},{5,7},{6,4},{7,5},{8,10},{9,11},{10,... | collective-permute-start | bytes 221192 | tf_op jit(solution)/shard_map/ppermute | solution.py:494
  77.9 3.7 %collective-permute-start.29 = (bf16[288,128]{1,0:T(8,128)(2,1)S(1)}, bf16[288,128]{1,0:T(8,128)(2,1)S(1)}, u32[]{:S(2)}, u32[]{:S(2)}) collective-permute-start(bf16[288,128]{1,0:T(8,128)(2,1)S(1)} %shard_map.160.refs_4_.refs_1_.refs_0_), channel_id=1, source_target_pairs={{0,1},{1,0},{2,3},{3,2},{4,5},{5,4},{6,7},{7,6},{8,9},{9,8},{10,11... | collective-permute-start | bytes 221192 | tf_op jit(solution)/shard_map/ppermute | solution.py:494
  81.5 1.3 %collective-permute-start.34 = (bf16[288,128]{1,0:T(8,128)(2,1)S(1)}, bf16[288,128]{1,0:T(8,128)(2,1)S(1)}, u32[]{:S(2)}, u32[]{:S(2)}) collective-permute-start(bf16[288,128]{1,0:T(8,128)(2,1)S(1)} %shard_map.164), channel_id=1, source_target_pairs={{0,1},{1,0},{2,3},{3,2},{4,5},{5,4},{6,7},{7,6},{8,9},{9,8},{10,11... | collective-permute-start | bytes 221192 | tf_op jit(solution)/shard_map/ppermute | solution.py:494

commit v4 on v3

--- a/solution.py
+++ b/solution.py
@@ -14,6 +14,10 @@
 FF = 768
 HEAD = E // HEADS
 LANES = 128
+FORWARD_GROUP = 1
+BACK_GROUP = 3
+WIDE_FORWARD_GROUP = 3
+WIDE_BACK_GROUP = 2
 VMEM = 24 * 1024 * 1024
 BF = jnp.bfloat16
 F32 = jnp.float32
@@ -152,11 +156,21 @@
     put_tiles(outs, nt(side_by_side(tiles), one_hot(plan.cells, plan.cols_from_rows())))
 
 
-def split_turn_kernel(plan, count, wait, table_ref, *refs):
-    weights, refs = refs[:count], refs[count:]
-    split_kernel(plan, False, wait, table_ref, *refs[: plan.ranks_rec], refs[-1])
-    for source, target in zip(weights, refs[plan.ranks_rec : -1]):
+def turn_kernel(wait, weights, turned, kept):
+    for source, target in zip(weights, turned):
         target[...] = source[...].astype(F32).T.astype(BF)
+    for source, target in zip(weights, kept):
+        target[...] = source[...]
+
+
+def split_turn_kernel(plan, wait, table_ref, *refs):
+    split_kernel(plan, False, wait, table_ref, *refs[2 : 2 + plan.ranks_rec], refs[-1])
+    turn_kernel(wait, refs[:2], refs[2 + plan.ranks_rec : 4 + plan.ranks_rec], refs[4 + plan.ranks_rec : -1])
+
+
+def turn_more_kernel(wait, *refs):
+    wait()
+    turn_kernel(wait, refs[:4], refs[4:8], refs[8:])
 
 
 def norm(table):
@@ -180,15 +194,14 @@
     return ref[start : start + HEAD, cols]
 
 
-def staged(count, *stages):
+def staged(count, group, *stages):
     held = {}
-    for step in range(count + len(stages) - 1):
+    groups = [range(start, min(start + group, count)) for start in range(0, count, group)]
+    for step in range(len(groups) + len(stages) - 1):
         for lag, stage in enumerate(stages):
-            unit = step - lag
-            if 0 <= unit < count:
-                held[unit] = stage(unit, held.get(unit))
-                if lag == len(stages) - 1:
-                    del held[unit]
+            if 0 <= step - lag < len(groups):
+                for unit in groups[step - lag]:
+                    held[unit] = stage(unit, held.get(unit))
 
 
 def units_of(total, width):
@@ -230,7 +243,7 @@
         cols = slice(place * width + start, place * width + start + step)
         mixed_ref[head * HEAD : (head + 1) * HEAD, cols] = nn(value, probs).astype(BF)
 
-    staged(len(units), score, weigh, mix)
+    staged(len(units), FORWARD_GROUP if width <= LANES else WIDE_FORWARD_GROUP, score, weigh, mix)
     return [
         x_ref[:, cols].astype(F32) + nn(out_t[...], mixed_ref[:, cols])
         for cols in blocks_of(2 * LANES, total)
@@ -276,7 +289,7 @@
             grad_proj_ref[E + rows.start : E + rows.stop, keys] = (both[0] * SCALE).astype(BF)
             grad_proj_ref[2 * E + rows.start : 2 * E + rows.stop, keys] = both[1].astype(BF)
 
-    staged(len(units), to_probs, to_scores, to_proj)
+    staged(len(units), BACK_GROUP if width <= LANES else WIDE_BACK_GROUP, to_probs, to_scores, to_proj)
 
 
 def project_back(grad_ref, x_ref, grad_proj_ref, qkv):
@@ -342,8 +355,8 @@
     put_halves(bits_of("attr")[0], sums_ref, keep_ref, send_ref)
 
 
-def rows_end_kernel(plan, wait, qkv, x_ref, grad_ref, grad_proj_ref, *outs):
-    order = one_hot(plan.cells, plan.grouped_from_rows())
+def end_kernel(plan, by_rows, wait, qkv, x_ref, grad_ref, grad_proj_ref, *outs):
+    order = one_hot(plan.cells, plan.grouped_from_rows() if by_rows else plan.grouped_from_cols())
     wait()
     grads = project_back(grad_ref, x_ref, grad_proj_ref, qkv)
     put_tiles(outs, nt(jnp.concatenate(grads, axis=1).astype(BF), order))
@@ -352,8 +365,7 @@
 def cols_kernel(plan, wait, *refs):
     count = plan.ranks_rec
     tiles, cot_tiles, refs = refs[:count], refs[count : 2 * count], refs[2 * count :]
-    (train_ref, qkv, out, up, down, qkv_t, out_t, up_t), refs = refs[:8], refs[8:]
-    outs, refs = refs[:count], refs[count:]
+    (train_ref, out, up, down, qkv_t, out_t, up_t), refs = refs[:7], refs[7:]
     normed_ref, mixed_ref, normed_second_ref, hidden_ref, cot_ref, grad_pre_ref, grad_ref, grad_proj_ref = refs[:8]
     x_ref, proj_ref, probs_ref, second_ref, slope_ref, wide_ref, mask_ref, grad_mixed_ref = refs[8:]
     width = max(LANES, plan.all_rec)
@@ -393,8 +405,6 @@
         table, root = norm(second_ref[:, cols].astype(F32))
         grad_ref[:, cols] = (norm_back(grad_normed, table, root) + cot_ref[:, cols].astype(F32)).astype(BF)
     attend_back(grad_ref, proj_ref, probs_ref, grad_proj_ref, grad_mixed_ref, out, width)
-    grads = project_back(grad_ref, x_ref, grad_proj_ref, qkv)
-    put_tiles(outs, nt(jnp.concatenate(grads, axis=1).astype(BF), order))
 
 
 def cols_sums_kernel(wait, *refs):
@@ -498,6 +508,14 @@
     return digits(lax.axis_index(axis) // bit, (2,))[0]
 
 
+def pass_kernel(wait, source, target):
+    target[...] = source[...]
+
+
+def row_tiles_of(arrays):
+    return [(array.shape, array.dtype) for array in arrays]
+
+
 def halve_kernel(axis, bit, wait, *refs):
     parts, (keep, send) = refs[:-2], refs[-2:]
     rows, mine = keep.shape[0], has_bit(axis, bit)
@@ -593,17 +611,17 @@
 
     rows = call(kernel(split_kernel, True), row_tiles, [((count, E), F32)], Far(cells))
     rows = exchange(rows, "attr", 1)
-    weights = (qkv_attr, out_attr, qkv_samp, out_samp, up_weight, down_weight.T)
+    weights = (qkv_attr, out_attr)
     got = call(
-        kernel(split_turn_kernel, len(weights)),
-        col_tiles + [(w.shape[::-1], BF, "near") for w in weights],
+        kernel(split_turn_kernel),
+        col_tiles + [(w.shape[::-1], BF, "near") for w in weights] + [(w.shape, BF, "near") for w in weights],
         [((count, E), F32)],
         Far(cotangent),
         *[Far(w) for w in weights],
         after=[rows[0]],
     )
     cot = exchange(got[:ranks_rec], "rec", 1)
-    turned = [Near(w) for w in got[ranks_rec:]]
+    turned, kept = ([Near(w) for w in part] for part in (got[ranks_rec:-2], got[-2:]))
 
     got = call(
         kernel(rows_forward_kernel),
@@ -615,43 +633,56 @@
     first, (x, normed, proj, weights, mixed) = got[:ranks_attr], [Near(array) for array in got[ranks_attr:]]
     first = exchange(first, "attr", -1)
     cols = exchange(call(kernel(to_cols_kernel), col_tiles, [], *first), "rec", 1)
+    weights_more = (qkv_samp, out_samp, up_weight, down_weight.T)
+    got = call(
+        turn_more_kernel,
+        [(w.shape[::-1], BF, "near") for w in weights_more] + [(w.shape, BF, "near") for w in weights_more[:3]],
+        [],
+        *[Far(w) for w in weights_more],
+        after=cols[:1],
+    )
+    turned, kept = turned + [Near(w) for w in got[:4]], kept + [Near(w) for w in got[4:]]
 
     width = max(LANES, plan.all_rec)
     rows_sums, cols_sums = padded(6 * E), padded(18 * E)
     hidden, hidden_wide = ((FF, count), BF), ((FF, count), F32)
     got = call(
         kernel(cols_kernel),
-        col_tiles + [out + ("near",) for out in (table, table, table, hidden, table, hidden, table, wide)],
-        [table, wide, probs(width), table, hidden_wide, hidden_wide, ((width, width), F32), table],
+        [out + ("near",) for out in (table, table, table, hidden, table, hidden, table, wide, table)],
+        [wide, probs(width), table, hidden_wide, hidden_wide, ((width, width), F32), table],
         *cols,
         *cot,
         train_split.reshape(1, -1),
-        Far(qkv_samp),
-        Far(out_samp),
-        Far(up_weight),
+        kept[3],
+        kept[4],
         turned[5],
         turned[2],
         turned[3],
         turned[4],
     )
-    grads, saved = exchange(got[:ranks_rec], "rec", -1), [Near(array) for array in got[ranks_rec:]]
+    saved = [Near(array) for array in got]
     near, far = bits_of("attr"), bits_of("rec")
     keep, send = call(
-        cols_sums_kernel, [((cols_sums // 2, LANES), BF)] * 2, [((cols_sums, LANES), BF)], *saved
+        cols_sums_kernel, [((cols_sums // 2, LANES), BF)] * 2, [((cols_sums, LANES), BF)], *saved[:8]
     )
+    grads = call(kernel(end_kernel, False), col_tiles, [], kept[2], saved[8], *saved[6:8], after=[keep])
     sums = Total(keep, swap(send, "attr", near[0]))
-    rows_grads = call(kernel(to_rows_kernel), row_tiles, [], *grads, after=[keep])
+    mark = grads[:1]
+    for bit in near[1:]:
+        mark = sums.halve("attr", bit, after=mark)
+    (last,) = call(pass_kernel, row_tiles_of(grads[-1:]), [], grads[-1], after=mark)
+    grads = exchange([*grads[:-1], last], "rec", -1)
+    arrived = grads[1:]
+    rows_grads = call(kernel(to_rows_kernel), row_tiles, [], *grads, after=mark)
     grads = exchange(rows_grads, "attr", 1)
-    for bit in near[1:]:
-        sums.halve("attr", bit)
-    mark = sums.add(far[0])
+    mark = sums.add(far[0], after=arrived)
 
     keep, send, grad, grad_proj = call(
         kernel(rows_back_kernel),
         [((rows_sums // 2, LANES), BF)] * 2 + [table + ("near",), wide + ("near",)],
         [((rows_sums, LANES), BF), table],
         *grads,
-        Far(out_attr),
+        kept[1],
         normed,
         proj,
         weights,
@@ -659,13 +690,13 @@
         after=mark,
     )
     row_sums = Total(keep, swap(send, "attr", near[0]))
-    mark = []
+    mark = [keep]
+    for bit in far[1:]:
+        mark = sums.add(bit, after=mark)
     for bit in near[1:]:
         mark = row_sums.halve("attr", bit, after=mark)
-    for bit in far[1:]:
-        mark = sums.add(bit, after=mark)
     grads = call(
-        kernel(rows_end_kernel), row_tiles, [], Far(qkv_attr), x, Near(grad), Near(grad_proj), after=mark
+        kernel(end_kernel, True), row_tiles, [], kept[0], x, Near(grad), Near(grad_proj), after=mark
     )
     row_sums.add(far[0], after=mark)
     grads = exchange(grads, "attr", -1)

time: 84 us -> 80.4 us (0.957)
  waiting for transfers between devices: 28.6 us -> 24.1 us
  starting transfers between devices: 31.7 us -> 34.3 us
  Pallas kernels: 22.6 us -> 20.9 us
    ppermute x14, waiting for transfers between devices: 18.9 us -> 10.9 us  [swap(): return lax.ppermute(part, axis, [(i, i ^ bit) for i in range(size)])]
    ppermute x21, waiting for transfers between devices: 9.68 us -> 13.2 us  [exchange(): lax.ppermute(tiles[k], axis, [(i, (i + sign * k) % size) for i in range(s...]
    ppermute x14, starting transfers between devices: 8.12 us -> 9.93 us  [swap(): return lax.ppermute(part, axis, [(i, i ^ bit) for i in range(size)])]
    pallas_call x22 -> x25, Pallas kernels: 22.6 us -> 20.9 us  [call(): pl.pallas_call(kernel, out_shape=[(pltpu.VMEM if out[2:] else jax.ShapeDt...]
  transfers between devices with their start and end apart: 35 -> 35, of which waited for: 17 -> 17; matrix products, arithmetic and copies ran while one was open for 0% -> 0% of each run, Pallas kernels for 12% -> 13%
where the time goes in v4:
time: 80.4 us; the launch traced here: 80.2 us
  starting transfers between devices  34.3 us (43%)
  waiting for transfers between devices  24.1 us (30%)
  Pallas kernels  20.9 us (26%)
  between operations  0.88 us (1%)
    ppermute x21, starting transfers between devices, exchange(): lax.ppermute(tiles[k], axis, [(i, (i + sign * k) % size) for i in range(s...  24.3 us
    pallas_call x25, Pallas kernels, call(): pl.pallas_call(kernel, out_shape=[(pltpu.VMEM if out[2:] else jax.ShapeDt...  20.9 us
    ppermute x21, waiting for transfers between devices, exchange(): lax.ppermute(tiles[k], axis, [(i, (i + sign * k) % size) for i in range(s...  13.2 us
    ppermute x14, waiting for transfers between devices, swap(): return lax.ppermute(part, axis, [(i, i ^ bit) for i in range(size)])  10.9 us
    ppermute x14, starting transfers between devices, swap(): return lax.ppermute(part, axis, [(i, i ^ bit) for i in range(size)])  9.93 us
  transfers between devices with their start and end apart: 35, of which 17 were waited for; matrix products, arithmetic and copies ran while one was open for 0% of the time, Pallas kernels for 13%

profile of v4, /device:TPU:0, one launch (start us, length us, event | category | flops | bytes accessed | tf_op | source)
XLA Modules:
  0.0 80.2 jit_solution(6282530461619950375)
XLA Ops:
  0.6 1.5 %shard_map.144 = (bf16[192,128]{1,0:T(8,128)(2,1)S(1)}, bf16[192,128]{1,0:T(8,128)(2,1)S(1)}, bf16[192,128]{1,0:T(8,128)(2,1)S(1)}, bf16[192,128]{1,0:T(8,128)(2,1)S(1)}) custom-call(bf16[8,12288]{1,0:T(8,128)(2,1)} %refs_0_.3), custom_call_target="tpu_custom_call" | custom-call | tf_op jit(solution)/shard_map/pallas_call | solution.py:480
  2.1 0.5 collective-permute-start
  2.6 2.6 %collective-permute-start.1 = (bf16[192,128]{1,0:T(8,128)(2,1)S(1)}, bf16[192,128]{1,0:T(8,128)(2,1)S(1)}, u32[]{:S(2)}, u32[]{:S(2)}) collective-permute-start(bf16[192,128]{1,0:T(8,128)(2,1)S(1)} %get-tuple-element.79), channel_id=1, source_target_pairs={{0,2},{1,3},{2,0},{3,1},{4,6},{5,7},{6,4},{7,5},{8,10},{9,11},{10,... | collective-permute-start | bytes 147464 | tf_op jit(solution)/shard_map/ppermute | solution.py:497
  5.2 1.4 %collective-permute-start.2 = (bf16[192,128]{1,0:T(8,128)(2,1)S(1)}, bf16[192,128]{1,0:T(8,128)(2,1)S(1)}, u32[]{:S(2)}, u32[]{:S(2)}) collective-permute-start(bf16[192,128]{1,0:T(8,128)(2,1)S(1)} %get-tuple-element.80), channel_id=1, source_target_pairs={{0,3},{1,0},{2,1},{3,2},{4,7},{5,4},{6,5},{7,6},{8,11},{9,8},{10,9... | collective-permute-start | bytes 147464 | tf_op jit(solution)/shard_map/ppermute | solution.py:497
  6.6 1.7 %shard_map.145 = (bf16[192,128]{1,0:T(8,128)(2,1)S(1)}, bf16[192,128]{1,0:T(8,128)(2,1)S(1)}, bf16[192,128]{1,0:T(8,128)(2,1)S(1)}, bf16[192,128]{1,0:T(8,128)(2...) custom-call(bf16[8,12288]{1,0:T(8,128)(2,1)} %refs_0_.4, ...), custom_call_target="tpu_custom_call" | custom-call | tf_op jit(solution)/shard_map/pallas_call | solution.py:480
  8.3 2.2 %shard_map.146 = (bf16[192,128]{1,0:T(8,128)(2,1)S(1)}, bf16[192,128]{1,0:T(8,128)(2,1)S(1)}, bf16[192,128]{1,0:T(8,128)(2,1)S(1)}, bf16[192,128]{1,0:T(8,128)(2...) custom-call(bf16[192,128]{1,0:T(8,128)(2,1)S(1)} %get-tuple-element., ...), custom_call_target="tpu_custom_call" | custom-call | tf_op jit(solution)/shard_map/pallas_call | solution.py:480
  10.6 1.8 %collective-permute-start.3 = (bf16[192,128]{1,0:T(8,128)(2,1)S(1)}, bf16[192,128]{1,0:T(8,128)(2,1)S(1)}, u32[]{:S(2)}, u32[]{:S(2)}) collective-permute-start(bf16[192,128]{1,0:T(8,128)(2,1)S(1)} %get-tuple-element.85), channel_id=1, source_target_pairs={{0,3},{1,0},{2,1},{3,2},{4,7},{5,4},{6,5},{7,6},{8,11},{9,8},{10,9... | collective-permute-start | bytes 147464 | tf_op jit(solution)/shard_map/ppermute | solution.py:497
  12.4 0.3 collective-permute-start.4
  12.7 1.8 %collective-permute-start.9 = (bf16[192,128]{1,0:T(8,128)(2,1)S(1)}, bf16[192,128]{1,0:T(8,128)(2,1)S(1)}, u32[]{:S(2)}, u32[]{:S(2)}) collective-permute-start(bf16[192,128]{1,0:T(8,128)(2,1)S(1)} %get-tuple-element.94), channel_id=1, source_target_pairs={{0,4},{4,8},{8,12},{12,0},{1,5},{5,9},{9,13},{13,1},{2,6},{6,10},{... | collective-permute-start | bytes 147464 | tf_op jit(solution)/shard_map/ppermute | solution.py:497
  14.5 2.6 %collective-permute-start.10 = (bf16[192,128]{1,0:T(8,128)(2,1)S(1)}, bf16[192,128]{1,0:T(8,128)(2,1)S(1)}, u32[]{:S(2)}, u32[]{:S(2)}) collective-permute-start(bf16[192,128]{1,0:T(8,128)(2,1)S(1)} %get-tuple-element.95), channel_id=1, source_target_pairs={{0,8},{4,12},{8,0},{12,4},{1,9},{5,13},{9,1},{13,5},{2,10},{6,14},... | collective-permute-start | bytes 147464 | tf_op jit(solution)/shard_map/ppermute | solution.py:497
  17.1 1.3 %collective-permute-start.11 = (bf16[192,128]{1,0:T(8,128)(2,1)S(1)}, bf16[192,128]{1,0:T(8,128)(2,1)S(1)}, u32[]{:S(2)}, u32[]{:S(2)}) collective-permute-start(bf16[192,128]{1,0:T(8,128)(2,1)S(1)} %get-tuple-element.96), channel_id=1, source_target_pairs={{0,12},{4,0},{8,4},{12,8},{1,13},{5,1},{9,5},{13,9},{2,14},{6,2},{... | collective-permute-start | bytes 147464 | tf_op jit(solution)/shard_map/ppermute | solution.py:497
  18.5 0.3 shard_map.147
  18.8 0.7 collective-permute-start.6
  19.5 2.0 %collective-permute-start.7 = (bf16[192,128]{1,0:T(8,128)(2,1)S(1)}, bf16[192,128]{1,0:T(8,128)(2,1)S(1)}, u32[]{:S(2)}, u32[]{:S(2)}) collective-permute-start(bf16[192,128]{1,0:T(8,128)(2,1)S(1)} %get-tuple-element.91), channel_id=1, source_target_pairs={{0,8},{4,12},{8,0},{12,4},{1,9},{5,13},{9,1},{13,5},{2,10},{6,14},... | collective-permute-start | bytes 147464 | tf_op jit(solution)/shard_map/ppermute | solution.py:497
  21.5 1.3 %collective-permute-start.8 = (bf16[192,128]{1,0:T(8,128)(2,1)S(1)}, bf16[192,128]{1,0:T(8,128)(2,1)S(1)}, u32[]{:S(2)}, u32[]{:S(2)}) collective-permute-start(bf16[192,128]{1,0:T(8,128)(2,1)S(1)} %get-tuple-element.92), channel_id=1, source_target_pairs={{0,12},{4,0},{8,4},{12,8},{1,13},{5,1},{9,5},{13,9},{2,14},{6,2},{... | collective-permute-start | bytes 147464 | tf_op jit(solution)/shard_map/ppermute | solution.py:497
  22.8 1.7 %shard_map.148 = (bf16[576,192]{1,0:T(8,128)(2,1)S(1)}, bf16[192,192]{1,0:T(8,128)(2,1)S(1)}, bf16[768,192]{1,0:T(8,128)(2,1)S(1)}, bf16[768,192]{1,0:T(8,128)(2...) custom-call(bf16[192,576]{1,0:T(8,128)(2,1)} %refs_0_.5, ...), custom_call_target="tpu_custom_call" | custom-call | tf_op jit(solution)/shard_map/pallas_call | solution.py:480
  24.6 0.8 collective-permute-done.6.refs_1_
  25.3 1.7 %collective-permute-done.7.refs_2_ = bf16[192,128]{1,0:T(8,128)(2,1)S(1)} collective-permute-done((bf16[192,128]{1,0:T(8,128)(2,1)S(1)}, bf16[192,128]{1,0:T(8,128)(2,1)S(1)}, u32[]{:S(2)}, u32[]{:S(2)}) %collective-permute-start.7) | collective-permute-done | bytes 49184 | tf_op jit(solution)/shard_map/ppermute | solution.py:497
  27.0 4.3 %shard_map.149 = (bf16[192,512]{1,0:T(8,128)(2,1)S(1)}, bf16[192,512]{1,0:T(8,128)(2,1)S(1)}, bf16[192,512]{1,0:T(8,128)(2,1)S(1)}, bf16[768,512]{1,0:T(8,128)(2...) custom-call(bf16[192,128]{1,0:T(8,128)(2,1)S(1)} %get-tuple-element., ...), custom_call_target="tpu_custom_call" | custom-call | tf_op jit(solution)/shard_map/pallas_call | solution.py:480
  31.4 1.1 %shard_map.150 = (bf16[1728,128]{1,0:T(8,128)(2,1)S(1)}, bf16[1728,128]{1,0:T(8,128)(2,1)S(1)}) custom-call(bf16[192,512]{1,0:T(8,128)(2,1)S(1)} %get-tuple-element.106.refs_0_, bf16[192,512]{1,0:T(8,128)(2,1)S(1)} %get-tuple-element.107.refs_1_, bf16[192,512]{1,0:T(8,128)(2,1)S(1)} %get-tuple-element.108.refs_2_, ...), custom_call_target="tpu_custom_call" | custom-call | tf_op jit(solution)/shard_map/pallas_call | solution.py:480
  32.5 0.1 collective-permute-start.14
  32.6 0.7 shard_map.151
  33.2 1.1 %collective-permute-done.14.refs_1_ = bf16[1728,128]{1,0:T(8,128)(2,1)S(1)} collective-permute-done((bf16[1728,128]{1,0:T(8,128)(2,1)S(1)}, bf16[1728,128]{1,0:T(8,128)(2,1)S(1)}, u32[]{:S(2)}, u32[]{:S(2)}) %collective-permute-start.14) | collective-permute-done | bytes 442400 | tf_op jit(solution)/shard_map/ppermute | solution.py:504
  34.4 0.1 shard_map.152
  34.5 0.5 collective-permute-start.19
  34.9 2.6 %collective-permute-start.12 = (bf16[192,128]{1,0:T(8,128)(2,1)S(1)}, bf16[192,128]{1,0:T(8,128)(2,1)S(1)}, u32[]{:S(2)}, u32[]{:S(2)}) collective-permute-start(bf16[192,128]{1,0:T(8,128)(2,1)S(1)} %get-tuple-element.114), channel_id=1, source_target_pairs={{0,12},{4,0},{8,4},{12,8},{1,13},{5,1},{9,5},{13,9},{2,14},{6,2},{... | collective-permute-start | bytes 147464 | tf_op jit(solution)/shard_map/ppermute | solution.py:497
  37.5 0.2 collective-permute-start.13
  37.8 0.3 collective-permute-start.15
  38.1 1.5 %collective-permute-done.12.refs_1_.refs_2_ = bf16[192,128]{1,0:T(8,128)(2,1)S(1)} collective-permute-done((bf16[192,128]{1,0:T(8,128)(2,1)S(1)}, bf16[192,128]{1,0:T(8,128)(2,1)S(1)}, u32[]{:S(2)}, u32[]{:S(2)}) %collective-permute-start.12) | collective-permute-done | bytes 49184 | tf_op jit(solution)/shard_map/ppermute | solution.py:497
  39.6 3.1 %collective-permute-done.13.refs_2_.refs_3_ = bf16[192,128]{1,0:T(8,128)(2,1)S(1)} collective-permute-done((bf16[192,128]{1,0:T(8,128)(2,1)S(1)}, bf16[192,128]{1,0:T(8,128)(2,1)S(1)}, u32[]{:S(2)}, u32[]{:S(2)}) %collective-permute-start.13) | collective-permute-done | bytes 49184 | tf_op jit(solution)/shard_map/ppermute | solution.py:497
  42.7 0.9 %collective-permute-done.15.refs_3_.refs_4_ = bf16[192,128]{1,0:T(8,128)(2,1)S(1)} collective-permute-done((bf16[192,128]{1,0:T(8,128)(2,1)S(1)}, bf16[192,128]{1,0:T(8,128)(2,1)S(1)}, u32[]{:S(2)}, u32[]{:S(2)}) %collective-permute-start.15) | collective-permute-done | bytes 49184 | tf_op jit(solution)/shard_map/ppermute | solution.py:497
  43.7 0.1 collective-permute-start.21
  43.8 0.4 shard_map.154
  44.2 1.5 %collective-permute-start.17 = (bf16[192,128]{1,0:T(8,128)(2,1)S(1)}, bf16[192,128]{1,0:T(8,128)(2,1)S(1)}, u32[]{:S(2)}, u32[]{:S(2)}) collective-permute-start(bf16[192,128]{1,0:T(8,128)(2,1)S(1)} %get-tuple-element.121), channel_id=1, source_target_pairs={{0,2},{1,3},{2,0},{3,1},{4,6},{5,7},{6,4},{7,5},{8,10},{9,11},{10,... | collective-permute-start | bytes 147464 | tf_op jit(solution)/shard_map/ppermute | solution.py:497
  45.8 1.4 %collective-permute-start.18 = (bf16[192,128]{1,0:T(8,128)(2,1)S(1)}, bf16[192,128]{1,0:T(8,128)(2,1)S(1)}, u32[]{:S(2)}, u32[]{:S(2)}) collective-permute-start(bf16[192,128]{1,0:T(8,128)(2,1)S(1)} %get-tuple-element.122), channel_id=1, source_target_pairs={{0,3},{1,0},{2,1},{3,2},{4,7},{5,4},{6,5},{7,6},{8,11},{9,8},{10,9... | collective-permute-start | bytes 147464 | tf_op jit(solution)/shard_map/ppermute | solution.py:497
  47.2 0.6 collective-permute-done.16.refs_1_
  47.7 0.7 collective-permute-done.17.refs_2_
  48.4 0.5 collective-permute-done.18.refs_3_
  48.9 2.5 %shard_map.156 = (bf16[576,128]{1,0:T(8,128)(2,1)S(1)}, bf16[576,128]{1,0:T(8,128)(2,1)S(1)}, bf16[192,512]{1,0:T(8,128)(2,1)S(1)}, bf16[576,512]{1,0:T(8,128)(2,1)S(1)}) custom-call(bf16[192,128]{1,0:T(8,128)(2,1)S(1)} %get-tuple-element.119.refs_0_, bf16[192,128]{1,0:T(8,128)(2,1)S(1)} %collective-permute-done.16.refs_1_, ...), custom_call_target="tpu_custom_call" | custom-call | tf_op jit(solution)/shard_map/pallas_call | solution.py:480
  51.5 1.0 %collective-permute-start.20 = (bf16[576,128]{1,0:T(8,128)(2,1)S(1)}, bf16[576,128]{1,0:T(8,128)(2,1)S(1)}, u32[]{:S(2)}, u32[]{:S(2)}) collective-permute-start(bf16[576,128]{1,0:T(8,128)(2,1)S(1)} %get-tuple-element.132), channel_id=1, source_target_pairs={{0,1},{1,0},{2,3},{3,2},{4,5},{5,4},{6,7},{7,6},{8,9},{9,8},{10,11... | collective-permute-start | bytes 442376 | tf_op jit(solution)/shard_map/ppermute | solution.py:504
  52.6 1.6 %collective-permute-start.28 = (bf16[864,128]{1,0:T(8,128)(2,1)S(1)}, bf16[864,128]{1,0:T(8,128)(2,1)S(1)}, u32[]{:S(2)}, u32[]{:S(2)}) collective-permute-start(bf16[864,128]{1,0:T(8,128)(2,1)S(1)} %shard_map.157.refs_2_.refs_0_), channel_id=1, source_target_pairs={{0,8},{4,12},{8,0},{12,4},{1,9},{5,13},{9,1},{13,5},{2,10},{6,14},... | collective-permute-start | bytes 663560 | tf_op jit(solution)/shard_map/ppermute | solution.py:504
  54.2 1.3 %collective-permute-start.25 = (bf16[288,128]{1,0:T(8,128)(2,1)S(1)}, bf16[288,128]{1,0:T(8,128)(2,1)S(1)}, u32[]{:S(2)}, u32[]{:S(2)}) collective-permute-start(bf16[288,128]{1,0:T(8,128)(2,1)S(1)} %get-tuple-element.138), channel_id=1, source_target_pairs={{0,2},{1,3},{2,0},{3,1},{4,6},{5,7},{6,4},{7,5},{8,10},{9,11},{10,... | collective-permute-start | bytes 221192 | tf_op jit(solution)/shard_map/ppermute | solution.py:504
  55.5 3.1 %collective-permute-done.25.refs_1_ = bf16[288,128]{1,0:T(8,128)(2,1)S(1)} collective-permute-done((bf16[288,128]{1,0:T(8,128)(2,1)S(1)}, bf16[288,128]{1,0:T(8,128)(2,1)S(1)}, u32[]{:S(2)}, u32[]{:S(2)}) %collective-permute-start.25) | collective-permute-done | bytes 73760 | tf_op jit(solution)/shard_map/ppermute | solution.py:504
  58.7 1.3 %collective-permute-start.26 = (bf16[288,128]{1,0:T(8,128)(2,1)S(1)}, bf16[288,128]{1,0:T(8,128)(2,1)S(1)}, u32[]{:S(2)}, u32[]{:S(2)}) collective-permute-start(bf16[288,128]{1,0:T(8,128)(2,1)S(1)} %shard_map.160.refs_0_), channel_id=1, source_target_pairs={{0,4},{4,0},{8,12},{12,8},{1,5},{5,1},{9,13},{13,9},{2,6},{6,2},{1... | collective-permute-start | bytes 221192 | tf_op jit(solution)/shard_map/ppermute | solution.py:504
  60.0 0.7 shard_map.159
  60.6 0.4 collective-permute-start.22
  61.0 1.2 %collective-permute-start.23 = (bf16[192,128]{1,0:T(8,128)(2,1)S(1)}, bf16[192,128]{1,0:T(8,128)(2,1)S(1)}, u32[]{:S(2)}, u32[]{:S(2)}) collective-permute-start(bf16[192,128]{1,0:T(8,128)(2,1)S(1)} %get-tuple-element.136), channel_id=1, source_target_pairs={{0,2},{1,3},{2,0},{3,1},{4,6},{5,7},{6,4},{7,5},{8,10},{9,11},{10,... | collective-permute-start | bytes 147464 | tf_op jit(solution)/shard_map/ppermute | solution.py:497
  62.2 0.2 collective-permute-start.24
  62.4 0.4 collective-permute-done.22.refs_2_.refs_1_
  62.8 2.5 %collective-permute-done.23.refs_3_.refs_2_ = bf16[192,128]{1,0:T(8,128)(2,1)S(1)} collective-permute-done((bf16[192,128]{1,0:T(8,128)(2,1)S(1)}, bf16[192,128]{1,0:T(8,128)(2,1)S(1)}, u32[]{:S(2)}, u32[]{:S(2)}) %collective-permute-start.23) | collective-permute-done | bytes 49184 | tf_op jit(solution)/shard_map/ppermute | solution.py:497
  65.3 0.5 collective-permute-done.24.refs_4_.refs_3_
  65.8 0.2 collective-permute-done.26.refs_1_
  66.2 1.3 %collective-permute-start.32 = (bf16[864,128]{1,0:T(8,128)(2,1)S(1)}, bf16[864,128]{1,0:T(8,128)(2,1)S(1)}, u32[]{:S(2)}, u32[]{:S(2)}) collective-permute-start(bf16[864,128]{1,0:T(8,128)(2,1)S(1)} %shard_map.162.refs_2_.refs_0_), channel_id=1, source_target_pairs={{0,2},{1,3},{2,0},{3,1},{4,6},{5,7},{6,4},{7,5},{8,10},{9,11},{10,... | collective-permute-start | bytes 663560 | tf_op jit(solution)/shard_map/ppermute | solution.py:504
  67.5 1.4 %collective-permute-start.27 = (bf16[288,128]{1,0:T(8,128)(2,1)S(1)}, bf16[288,128]{1,0:T(8,128)(2,1)S(1)}, u32[]{:S(2)}, u32[]{:S(2)}) collective-permute-start(bf16[288,128]{1,0:T(8,128)(2,1)S(1)} %shard_map.161.refs_2_.refs_0_), channel_id=1, source_target_pairs={{0,8},{4,12},{8,0},{12,4},{1,9},{5,13},{9,1},{13,5},{2,10},{6,14},... | collective-permute-start | bytes 221192 | tf_op jit(solution)/shard_map/ppermute | solution.py:504
  68.9 4.2 %collective-permute-done.27.refs_1_ = bf16[288,128]{1,0:T(8,128)(2,1)S(1)} collective-permute-done((bf16[288,128]{1,0:T(8,128)(2,1)S(1)}, bf16[288,128]{1,0:T(8,128)(2,1)S(1)}, u32[]{:S(2)}, u32[]{:S(2)}) %collective-permute-start.27) | collective-permute-done | bytes 73760 | tf_op jit(solution)/shard_map/ppermute | solution.py:504
  73.1 0.1 collective-permute-start.33
  73.2 1.0 %collective-permute-start.30 = (bf16[288,128]{1,0:T(8,128)(2,1)S(1)}, bf16[288,128]{1,0:T(8,128)(2,1)S(1)}, u32[]{:S(2)}, u32[]{:S(2)}) collective-permute-start(bf16[288,128]{1,0:T(8,128)(2,1)S(1)} %shard_map.163.refs_4_.refs_1_.refs_0_), channel_id=1, source_target_pairs={{0,2},{1,3},{2,0},{3,1},{4,6},{5,7},{6,4},{7,5},{8,10},{9,11},{10,... | collective-permute-start | bytes 221192 | tf_op jit(solution)/shard_map/ppermute | solution.py:504
  74.3 0.2 collective-permute-start.29
  74.4 1.1 %shard_map.164.refs_1_ = bf16[8,12288]{1,0:T(8,128)(2,1)} custom-call(bf16[192,128]{1,0:T(8,128)(2,1)S(1)} %get-tuple-element.134.refs_0_, bf16[192,128]{1,0:T(8,128)(2,1)S(1)} %collective-permute-done.22.refs_2_.refs_1_, bf16[192,128]{1,0:T(8,128)(2,1)S(1)} %collective-permute-done.23.refs_3_.refs_2_, ...), custom_call_target="tpu_custom_call" | custom-call | tf_op jit(solution)/shard_map/pallas_call | solution.py:480
  75.5 1.4 %shard_map.166 = (f32[192,576]{1,0:T(8,128)}, f32[192,192]{1,0:T(8,128)}, f32[192,768]{1,0:T(8,128)}, f32[192,768]{1,0:T(8,128)}) custom-call(bf16[864,128]{1,0:T(8,128)(2,1)S(1)} %shard_map.162.refs_2_.refs_0_, bf16[864,128]{1,0:T(8,128)(2,1)S(1)} %collective-permute-done.31.refs_1_, bf16[864,128]{1,0:T(8,128)(2,1)S(1)} %collective-permute-done.32.refs_0_.refs_2_, ...), custom_call_target="tpu_custom_call" | custom-call | tf_op jit(solution)/shard_map/pallas_call | solution.py:480
  76.9 1.0 %collective-permute-done.30.refs_0_.refs_2_ = bf16[288,128]{1,0:T(8,128)(2,1)S(1)} collective-permute-done((bf16[288,128]{1,0:T(8,128)(2,1)S(1)}, bf16[288,128]{1,0:T(8,128)(2,1)S(1)}, u32[]{:S(2)}, u32[]{:S(2)}) %collective-permute-start.30) | collective-permute-done | bytes 73760 | tf_op jit(solution)/shard_map/ppermute | solution.py:504
  77.9 0.1 collective-permute-start.34
  78.0 1.2 %collective-permute-done.34.refs_3_ = bf16[288,128]{1,0:T(8,128)(2,1)S(1)} collective-permute-done((bf16[288,128]{1,0:T(8,128)(2,1)S(1)}, bf16[288,128]{1,0:T(8,128)(2,1)S(1)}, u32[]{:S(2)}, u32[]{:S(2)}) %collective-permute-start.34) | collective-permute-done | bytes 73760 | tf_op jit(solution)/shard_map/ppermute | solution.py:504
  79.3 0.9 %shard_map.168 = (f32[192,576]{1,0:T(8,128)}, f32[192,192]{1,0:T(8,128)}) custom-call(bf16[288,128]{1,0:T(8,128)(2,1)S(1)} %shard_map.163.refs_4_.refs_1_.refs_0_, bf16[288,128]{1,0:T(8,128)(2,1)S(1)} %collective-permute-done.29.refs_1_, bf16[288,128]{1,0:T(8,128)(2,1)S(1)} %collective-permute-done.30.refs_0_.refs_2_, ...), custom_call_target="tpu_custom_call" | custom-call | tf_op jit(solution)/shard_map/pallas_call | solution.py:480
  (33 shorter events, 0.4 us)
Async XLA Ops:
  0.6 26.4 %copy-start = (s32[32]{0:T(128)S(1)}, s32[32]{0:T(128)}, u32[]{:S(2)}) copy-start(s32[32]{0:T(128)} %param.17) | copy-start | bytes 388
  2.1 6.2 %collective-permute-start = (bf16[192,128]{1,0:T(8,128)(2,1)S(1)}, bf16[192,128]{1,0:T(8,128)(2,1)S(1)}, u32[]{:S(2)}, u32[]{:S(2)}) collective-permute-start(bf16[192,128]{1,0:T(8,128)(2,1)S(1)} %get-tuple-element.78), channel_id=1, source_target_pairs={{0,1},{1,2},{2,3},{3,0},{4,5},{5,6},{6,7},{7,4},{8,9},{9,10},{10,1... | collective-permute-start | bytes 147464 | tf_op jit(solution)/shard_map/ppermute | solution.py:497
  2.6 5.7 %collective-permute-start.1 = (bf16[192,128]{1,0:T(8,128)(2,1)S(1)}, bf16[192,128]{1,0:T(8,128)(2,1)S(1)}, u32[]{:S(2)}, u32[]{:S(2)}) collective-permute-start(bf16[192,128]{1,0:T(8,128)(2,1)S(1)} %get-tuple-element.79), channel_id=1, source_target_pairs={{0,2},{1,3},{2,0},{3,1},{4,6},{5,7},{6,4},{7,5},{8,10},{9,11},{10,... | collective-permute-start | bytes 147464 | tf_op jit(solution)/shard_map/ppermute | solution.py:497
  5.2 3.1 %collective-permute-start.2 = (bf16[192,128]{1,0:T(8,128)(2,1)S(1)}, bf16[192,128]{1,0:T(8,128)(2,1)S(1)}, u32[]{:S(2)}, u32[]{:S(2)}) collective-permute-start(bf16[192,128]{1,0:T(8,128)(2,1)S(1)} %get-tuple-element.80), channel_id=1, source_target_pairs={{0,3},{1,0},{2,1},{3,2},{4,7},{5,4},{6,5},{7,6},{8,11},{9,8},{10,9... | collective-permute-start | bytes 147464 | tf_op jit(solution)/shard_map/ppermute | solution.py:497
  10.6 6.5 %collective-permute-start.3 = (bf16[192,128]{1,0:T(8,128)(2,1)S(1)}, bf16[192,128]{1,0:T(8,128)(2,1)S(1)}, u32[]{:S(2)}, u32[]{:S(2)}) collective-permute-start(bf16[192,128]{1,0:T(8,128)(2,1)S(1)} %get-tuple-element.85), channel_id=1, source_target_pairs={{0,3},{1,0},{2,1},{3,2},{4,7},{5,4},{6,5},{7,6},{8,11},{9,8},{10,9... | collective-permute-start | bytes 147464 | tf_op jit(solution)/shard_map/ppermute | solution.py:497
  12.4 6.1 %collective-permute-start.4 = (bf16[192,128]{1,0:T(8,128)(2,1)S(1)}, bf16[192,128]{1,0:T(8,128)(2,1)S(1)}, u32[]{:S(2)}, u32[]{:S(2)}) collective-permute-start(bf16[192,128]{1,0:T(8,128)(2,1)S(1)} %get-tuple-element.86), channel_id=1, source_target_pairs={{0,2},{1,3},{2,0},{3,1},{4,6},{5,7},{6,4},{7,5},{8,10},{9,11},{10,... | collective-permute-start | bytes 147464 | tf_op jit(solution)/shard_map/ppermute | solution.py:497
  12.7 5.8 %collective-permute-start.5 = (bf16[192,128]{1,0:T(8,128)(2,1)S(1)}, bf16[192,128]{1,0:T(8,128)(2,1)S(1)}, u32[]{:S(2)}, u32[]{:S(2)}) collective-permute-start(bf16[192,128]{1,0:T(8,128)(2,1)S(1)} %get-tuple-element.87), channel_id=1, source_target_pairs={{0,1},{1,2},{2,3},{3,0},{4,5},{5,6},{6,7},{7,4},{8,9},{9,10},{10,1... | collective-permute-start | bytes 147464 | tf_op jit(solution)/shard_map/ppermute | solution.py:497
  12.7 8.8 %collective-permute-start.9 = (bf16[192,128]{1,0:T(8,128)(2,1)S(1)}, bf16[192,128]{1,0:T(8,128)(2,1)S(1)}, u32[]{:S(2)}, u32[]{:S(2)}) collective-permute-start(bf16[192,128]{1,0:T(8,128)(2,1)S(1)} %get-tuple-element.94), channel_id=1, source_target_pairs={{0,4},{4,8},{8,12},{12,0},{1,5},{5,9},{9,13},{13,1},{2,6},{6,10},{... | collective-permute-start | bytes 147464 | tf_op jit(solution)/shard_map/ppermute | solution.py:497
  14.5 10.0 %collective-permute-start.10 = (bf16[192,128]{1,0:T(8,128)(2,1)S(1)}, bf16[192,128]{1,0:T(8,128)(2,1)S(1)}, u32[]{:S(2)}, u32[]{:S(2)}) collective-permute-start(bf16[192,128]{1,0:T(8,128)(2,1)S(1)} %get-tuple-element.95), channel_id=1, source_target_pairs={{0,8},{4,12},{8,0},{12,4},{1,9},{5,13},{9,1},{13,5},{2,10},{6,14},... | collective-permute-start | bytes 147464 | tf_op jit(solution)/shard_map/ppermute | solution.py:497
  17.1 7.4 %collective-permute-start.11 = (bf16[192,128]{1,0:T(8,128)(2,1)S(1)}, bf16[192,128]{1,0:T(8,128)(2,1)S(1)}, u32[]{:S(2)}, u32[]{:S(2)}) collective-permute-start(bf16[192,128]{1,0:T(8,128)(2,1)S(1)} %get-tuple-element.96), channel_id=1, source_target_pairs={{0,12},{4,0},{8,4},{12,8},{1,13},{5,1},{9,5},{13,9},{2,14},{6,2},{... | collective-permute-start | bytes 147464 | tf_op jit(solution)/shard_map/ppermute | solution.py:497
  18.8 6.6 %collective-permute-start.6 = (bf16[192,128]{1,0:T(8,128)(2,1)S(1)}, bf16[192,128]{1,0:T(8,128)(2,1)S(1)}, u32[]{:S(2)}, u32[]{:S(2)}) collective-permute-start(bf16[192,128]{1,0:T(8,128)(2,1)S(1)} %get-tuple-element.90), channel_id=1, source_target_pairs={{0,4},{4,8},{8,12},{12,0},{1,5},{5,9},{9,13},{13,1},{2,6},{6,10},{... | collective-permute-start | bytes 147464 | tf_op jit(solution)/shard_map/ppermute | solution.py:497
  19.5 7.5 %collective-permute-start.7 = (bf16[192,128]{1,0:T(8,128)(2,1)S(1)}, bf16[192,128]{1,0:T(8,128)(2,1)S(1)}, u32[]{:S(2)}, u32[]{:S(2)}) collective-permute-start(bf16[192,128]{1,0:T(8,128)(2,1)S(1)} %get-tuple-element.91), channel_id=1, source_target_pairs={{0,8},{4,12},{8,0},{12,4},{1,9},{5,13},{9,1},{13,5},{2,10},{6,14},... | collective-permute-start | bytes 147464 | tf_op jit(solution)/shard_map/ppermute | solution.py:497
  21.5 5.5 %collective-permute-start.8 = (bf16[192,128]{1,0:T(8,128)(2,1)S(1)}, bf16[192,128]{1,0:T(8,128)(2,1)S(1)}, u32[]{:S(2)}, u32[]{:S(2)}) collective-permute-start(bf16[192,128]{1,0:T(8,128)(2,1)S(1)} %get-tuple-element.92), channel_id=1, source_target_pairs={{0,12},{4,0},{8,4},{12,8},{1,13},{5,1},{9,5},{13,9},{2,14},{6,2},{... | collective-permute-start | bytes 147464 | tf_op jit(solution)/shard_map/ppermute | solution.py:497
  32.5 1.9 %collective-permute-start.14 = (bf16[1728,128]{1,0:T(8,128)(2,1)S(1)}, bf16[1728,128]{1,0:T(8,128)(2,1)S(1)}, u32[]{:S(2)}, u32[]{:S(2)}) collective-permute-start(bf16[1728,128]{1,0:T(8,128)(2,1)S(1)} %get-tuple-element.117), channel_id=1, source_target_pairs={{0,1},{1,0},{2,3},{3,2},{4,5},{5,4},{6,7},{7,6},{8,9},{9,8},{10,11... | collective-permute-start | bytes 1327112 | tf_op jit(solution)/shard_map/ppermute | solution.py:504
  34.5 9.2 %collective-permute-start.19 = (bf16[864,128]{1,0:T(8,128)(2,1)S(1)}, bf16[864,128]{1,0:T(8,128)(2,1)S(1)}, u32[]{:S(2)}, u32[]{:S(2)}) collective-permute-start(bf16[864,128]{1,0:T(8,128)(2,1)S(1)} %get-tuple-element.128), channel_id=1, source_target_pairs={{0,2},{1,3},{2,0},{3,1},{4,6},{5,7},{6,4},{7,5},{8,10},{9,11},{10,... | collective-permute-start | bytes 663560 | tf_op jit(solution)/shard_map/ppermute | solution.py:504
  34.9 4.7 %collective-permute-start.12 = (bf16[192,128]{1,0:T(8,128)(2,1)S(1)}, bf16[192,128]{1,0:T(8,128)(2,1)S(1)}, u32[]{:S(2)}, u32[]{:S(2)}) collective-permute-start(bf16[192,128]{1,0:T(8,128)(2,1)S(1)} %get-tuple-element.114), channel_id=1, source_target_pairs={{0,12},{4,0},{8,4},{12,8},{1,13},{5,1},{9,5},{13,9},{2,14},{6,2},{... | collective-permute-start | bytes 147464 | tf_op jit(solution)/shard_map/ppermute | solution.py:497
  37.5 5.2 %collective-permute-start.13 = (bf16[192,128]{1,0:T(8,128)(2,1)S(1)}, bf16[192,128]{1,0:T(8,128)(2,1)S(1)}, u32[]{:S(2)}, u32[]{:S(2)}) collective-permute-start(bf16[192,128]{1,0:T(8,128)(2,1)S(1)} %get-tuple-element.115), channel_id=1, source_target_pairs={{0,8},{4,12},{8,0},{12,4},{1,9},{5,13},{9,1},{13,5},{2,10},{6,14},... | collective-permute-start | bytes 147464 | tf_op jit(solution)/shard_map/ppermute | solution.py:497
  37.8 5.9 %collective-permute-start.15 = (bf16[192,128]{1,0:T(8,128)(2,1)S(1)}, bf16[192,128]{1,0:T(8,128)(2,1)S(1)}, u32[]{:S(2)}, u32[]{:S(2)}) collective-permute-start(bf16[192,128]{1,0:T(8,128)(2,1)S(1)} %shard_map.153), channel_id=1, source_target_pairs={{0,4},{4,8},{8,12},{12,0},{1,5},{5,9},{9,13},{13,1},{2,6},{6,10},{... | collective-permute-start | bytes 147464 | tf_op jit(solution)/shard_map/ppermute | solution.py:497
  43.7 8.8 %collective-permute-start.21 = (bf16[864,128]{1,0:T(8,128)(2,1)S(1)}, bf16[864,128]{1,0:T(8,128)(2,1)S(1)}, u32[]{:S(2)}, u32[]{:S(2)}) collective-permute-start(bf16[864,128]{1,0:T(8,128)(2,1)S(1)} %shard_map.155.refs_9_.refs_0_), channel_id=1, source_target_pairs={{0,4},{4,0},{8,12},{12,8},{1,5},{5,1},{9,13},{13,9},{2,6},{6,2},{1... | collective-permute-start | bytes 663560 | tf_op jit(solution)/shard_map/ppermute | solution.py:504
  44.2 3.6 %collective-permute-start.16 = (bf16[192,128]{1,0:T(8,128)(2,1)S(1)}, bf16[192,128]{1,0:T(8,128)(2,1)S(1)}, u32[]{:S(2)}, u32[]{:S(2)}) collective-permute-start(bf16[192,128]{1,0:T(8,128)(2,1)S(1)} %get-tuple-element.120), channel_id=1, source_target_pairs={{0,1},{1,2},{2,3},{3,0},{4,5},{5,6},{6,7},{7,4},{8,9},{9,10},{10,1... | collective-permute-start | bytes 147464 | tf_op jit(solution)/shard_map/ppermute | solution.py:497
  44.2 4.2 %collective-permute-start.17 = (bf16[192,128]{1,0:T(8,128)(2,1)S(1)}, bf16[192,128]{1,0:T(8,128)(2,1)S(1)}, u32[]{:S(2)}, u32[]{:S(2)}) collective-permute-start(bf16[192,128]{1,0:T(8,128)(2,1)S(1)} %get-tuple-element.121), channel_id=1, source_target_pairs={{0,2},{1,3},{2,0},{3,1},{4,6},{5,7},{6,4},{7,5},{8,10},{9,11},{10,... | collective-permute-start | bytes 147464 | tf_op jit(solution)/shard_map/ppermute | solution.py:497
  45.8 3.1 %collective-permute-start.18 = (bf16[192,128]{1,0:T(8,128)(2,1)S(1)}, bf16[192,128]{1,0:T(8,128)(2,1)S(1)}, u32[]{:S(2)}, u32[]{:S(2)}) collective-permute-start(bf16[192,128]{1,0:T(8,128)(2,1)S(1)} %get-tuple-element.122), channel_id=1, source_target_pairs={{0,3},{1,0},{2,1},{3,2},{4,7},{5,4},{6,5},{7,6},{8,11},{9,8},{10,9... | collective-permute-start | bytes 147464 | tf_op jit(solution)/shard_map/ppermute | solution.py:497
  51.5 2.7 %collective-permute-start.20 = (bf16[576,128]{1,0:T(8,128)(2,1)S(1)}, bf16[576,128]{1,0:T(8,128)(2,1)S(1)}, u32[]{:S(2)}, u32[]{:S(2)}) collective-permute-start(bf16[576,128]{1,0:T(8,128)(2,1)S(1)} %get-tuple-element.132), channel_id=1, source_target_pairs={{0,1},{1,0},{2,3},{3,2},{4,5},{5,4},{6,7},{7,6},{8,9},{9,8},{10,11... | collective-permute-start | bytes 442376 | tf_op jit(solution)/shard_map/ppermute | solution.py:504
  52.6 13.5 %collective-permute-start.28 = (bf16[864,128]{1,0:T(8,128)(2,1)S(1)}, bf16[864,128]{1,0:T(8,128)(2,1)S(1)}, u32[]{:S(2)}, u32[]{:S(2)}) collective-permute-start(bf16[864,128]{1,0:T(8,128)(2,1)S(1)} %shard_map.157.refs_2_.refs_0_), channel_id=1, source_target_pairs={{0,8},{4,12},{8,0},{12,4},{1,9},{5,13},{9,1},{13,5},{2,10},{6,14},... | collective-permute-start | bytes 663560 | tf_op jit(solution)/shard_map/ppermute | solution.py:504
  54.2 4.4 %collective-permute-start.25 = (bf16[288,128]{1,0:T(8,128)(2,1)S(1)}, bf16[288,128]{1,0:T(8,128)(2,1)S(1)}, u32[]{:S(2)}, u32[]{:S(2)}) collective-permute-start(bf16[288,128]{1,0:T(8,128)(2,1)S(1)} %get-tuple-element.138), channel_id=1, source_target_pairs={{0,2},{1,3},{2,0},{3,1},{4,6},{5,7},{6,4},{7,5},{8,10},{9,11},{10,... | collective-permute-start | bytes 221192 | tf_op jit(solution)/shard_map/ppermute | solution.py:504
  58.7 7.4 %collective-permute-start.26 = (bf16[288,128]{1,0:T(8,128)(2,1)S(1)}, bf16[288,128]{1,0:T(8,128)(2,1)S(1)}, u32[]{:S(2)}, u32[]{:S(2)}) collective-permute-start(bf16[288,128]{1,0:T(8,128)(2,1)S(1)} %shard_map.160.refs_0_), channel_id=1, source_target_pairs={{0,4},{4,0},{8,12},{12,8},{1,5},{5,1},{9,13},{13,9},{2,6},{6,2},{1... | collective-permute-start | bytes 221192 | tf_op jit(solution)/shard_map/ppermute | solution.py:504
  60.6 2.2 %collective-permute-start.22 = (bf16[192,128]{1,0:T(8,128)(2,1)S(1)}, bf16[192,128]{1,0:T(8,128)(2,1)S(1)}, u32[]{:S(2)}, u32[]{:S(2)}) collective-permute-start(bf16[192,128]{1,0:T(8,128)(2,1)S(1)} %get-tuple-element.135), channel_id=1, source_target_pairs={{0,3},{1,0},{2,1},{3,2},{4,7},{5,4},{6,5},{7,6},{8,11},{9,8},{10,9... | collective-permute-start | bytes 147464 | tf_op jit(solution)/shard_map/ppermute | solution.py:497
  61.0 4.3 %collective-permute-start.23 = (bf16[192,128]{1,0:T(8,128)(2,1)S(1)}, bf16[192,128]{1,0:T(8,128)(2,1)S(1)}, u32[]{:S(2)}, u32[]{:S(2)}) collective-permute-start(bf16[192,128]{1,0:T(8,128)(2,1)S(1)} %get-tuple-element.136), channel_id=1, source_target_pairs={{0,2},{1,3},{2,0},{3,1},{4,6},{5,7},{6,4},{7,5},{8,10},{9,11},{10,... | collective-permute-start | bytes 147464 | tf_op jit(solution)/shard_map/ppermute | solution.py:497
  62.2 3.6 %collective-permute-start.24 = (bf16[192,128]{1,0:T(8,128)(2,1)S(1)}, bf16[192,128]{1,0:T(8,128)(2,1)S(1)}, u32[]{:S(2)}, u32[]{:S(2)}) collective-permute-start(bf16[192,128]{1,0:T(8,128)(2,1)S(1)} %get-tuple-element.137), channel_id=1, source_target_pairs={{0,1},{1,2},{2,3},{3,0},{4,5},{5,6},{6,7},{7,4},{8,9},{9,10},{10,1... | collective-permute-start | bytes 147464 | tf_op jit(solution)/shard_map/ppermute | solution.py:497
  66.2 6.9 %collective-permute-start.32 = (bf16[864,128]{1,0:T(8,128)(2,1)S(1)}, bf16[864,128]{1,0:T(8,128)(2,1)S(1)}, u32[]{:S(2)}, u32[]{:S(2)}) collective-permute-start(bf16[864,128]{1,0:T(8,128)(2,1)S(1)} %shard_map.162.refs_2_.refs_0_), channel_id=1, source_target_pairs={{0,2},{1,3},{2,0},{3,1},{4,6},{5,7},{6,4},{7,5},{8,10},{9,11},{10,... | collective-permute-start | bytes 663560 | tf_op jit(solution)/shard_map/ppermute | solution.py:504
  67.5 5.6 %collective-permute-start.27 = (bf16[288,128]{1,0:T(8,128)(2,1)S(1)}, bf16[288,128]{1,0:T(8,128)(2,1)S(1)}, u32[]{:S(2)}, u32[]{:S(2)}) collective-permute-start(bf16[288,128]{1,0:T(8,128)(2,1)S(1)} %shard_map.161.refs_2_.refs_0_), channel_id=1, source_target_pairs={{0,8},{4,12},{8,0},{12,4},{1,9},{5,13},{9,1},{13,5},{2,10},{6,14},... | collective-permute-start | bytes 221192 | tf_op jit(solution)/shard_map/ppermute | solution.py:504
  68.9 6.6 %collective-permute-start.31 = (bf16[864,128]{1,0:T(8,128)(2,1)S(1)}, bf16[864,128]{1,0:T(8,128)(2,1)S(1)}, u32[]{:S(2)}, u32[]{:S(2)}) collective-permute-start(bf16[864,128]{1,0:T(8,128)(2,1)S(1)} %shard_map.162.refs_2_.refs_0_), channel_id=1, source_target_pairs={{0,1},{1,0},{2,3},{3,2},{4,5},{5,4},{6,7},{7,6},{8,9},{9,8},{10,11... | collective-permute-start | bytes 663560 | tf_op jit(solution)/shard_map/ppermute | solution.py:504
  73.1 2.4 %collective-permute-start.33 = (bf16[864,128]{1,0:T(8,128)(2,1)S(1)}, bf16[864,128]{1,0:T(8,128)(2,1)S(1)}, u32[]{:S(2)}, u32[]{:S(2)}) collective-permute-start(bf16[864,128]{1,0:T(8,128)(2,1)S(1)} %shard_map.165), channel_id=1, source_target_pairs={{0,1},{1,0},{2,3},{3,2},{4,5},{5,4},{6,7},{7,6},{8,9},{9,8},{10,11... | collective-permute-start | bytes 663560 | tf_op jit(solution)/shard_map/ppermute | solution.py:504
  73.2 4.7 %collective-permute-start.30 = (bf16[288,128]{1,0:T(8,128)(2,1)S(1)}, bf16[288,128]{1,0:T(8,128)(2,1)S(1)}, u32[]{:S(2)}, u32[]{:S(2)}) collective-permute-start(bf16[288,128]{1,0:T(8,128)(2,1)S(1)} %shard_map.163.refs_4_.refs_1_.refs_0_), channel_id=1, source_target_pairs={{0,2},{1,3},{2,0},{3,1},{4,6},{5,7},{6,4},{7,5},{8,10},{9,11},{10,... | collective-permute-start | bytes 221192 | tf_op jit(solution)/shard_map/ppermute | solution.py:504
  74.3 3.8 %collective-permute-start.29 = (bf16[288,128]{1,0:T(8,128)(2,1)S(1)}, bf16[288,128]{1,0:T(8,128)(2,1)S(1)}, u32[]{:S(2)}, u32[]{:S(2)}) collective-permute-start(bf16[288,128]{1,0:T(8,128)(2,1)S(1)} %shard_map.163.refs_4_.refs_1_.refs_0_), channel_id=1, source_target_pairs={{0,1},{1,0},{2,3},{3,2},{4,5},{5,4},{6,7},{7,6},{8,9},{9,8},{10,11... | collective-permute-start | bytes 221192 | tf_op jit(solution)/shard_map/ppermute | solution.py:504
  77.9 1.3 %collective-permute-start.34 = (bf16[288,128]{1,0:T(8,128)(2,1)S(1)}, bf16[288,128]{1,0:T(8,128)(2,1)S(1)}, u32[]{:S(2)}, u32[]{:S(2)}) collective-permute-start(bf16[288,128]{1,0:T(8,128)(2,1)S(1)} %shard_map.167), channel_id=1, source_target_pairs={{0,1},{1,0},{2,3},{3,2},{4,5},{5,4},{6,7},{7,6},{8,9},{9,8},{10,11... | collective-permute-start | bytes 221192 | tf_op jit(solution)/shard_map/ppermute | solution.py:504

commit v5 on v4

--- a/solution.py
+++ b/solution.py
@@ -152,8 +152,8 @@
 
 
 def to_rows_kernel(plan, wait, *refs):
-    tiles, outs = refs[: plan.ranks_rec], refs[plan.ranks_rec :]
-    put_tiles(outs, nt(side_by_side(tiles), one_hot(plan.cells, plan.cols_from_rows())))
+    tiles, across, outs = refs[: plan.ranks_rec], refs[plan.ranks_rec], refs[plan.ranks_rec + 1 :]
+    put_tiles(outs, nt(side_by_side(tiles), across[...]))
 
 
 def turn_kernel(wait, weights, turned, kept):
@@ -168,9 +168,21 @@
     turn_kernel(wait, refs[:2], refs[2 + plan.ranks_rec : 4 + plan.ranks_rec], refs[4 + plan.ranks_rec : -1])
 
 
-def turn_more_kernel(wait, *refs):
+def prepare_kernel(plan, wait, train_ref, *refs):
+    weights, turned, kept, (by_cols, by_rows, across, mask_ref) = refs[:4], refs[4:8], refs[8:11], refs[11:]
+    by_cols[...] = one_hot(plan.cells, plan.grouped_from_cols())
+    by_rows[...] = one_hot(plan.cells, plan.grouped_from_rows())
+    across[...] = one_hot(plan.cells, plan.cols_from_rows())
+    width = max(LANES, plan.all_rec)
+    row = lax.broadcasted_iota(jnp.int32, (width, 1), 0)
+    sequence, far, near, own = digits(row, (width // plan.all_rec, plan.ranks_rec, plan.ranks_attr, plan.own_rec))
+    record = plan.rec * wrap(lax.axis_index("rec") - far, plan.ranks_rec) + plan.record_of(near, own)
+    chosen = (record == lane_index(plan.all_rec)) & (train_ref[...] > 0)
+    allowed = jnp.max(jnp.where(chosen, 1.0, 0.0), axis=1, keepdims=True) > 0.5
+    asker = digits(lane_index(width), (width // plan.all_rec, plan.all_rec))[0]
+    mask_ref[...] = jnp.where(allowed & (sequence == asker), 0.0, -1e30)
     wait()
-    turn_kernel(wait, refs[:4], refs[4:8], refs[8:])
+    turn_kernel(wait, weights, turned, kept)
 
 
 def norm(table):
@@ -276,20 +288,33 @@
         moved = grad_probs * wide
         return (moved - wide * jnp.sum(moved, axis=0, keepdims=True)).astype(BF)
 
-    def to_proj(unit, grad_scores):
+    def to_query(unit, grad_scores):
+        rows, cols, keys = spans(unit)
+        key = heads_of(proj_ref, 1, units[unit][1], keys)
+        grad_proj_ref[rows, cols] = (nn(key, grad_scores) * SCALE).astype(BF)
+        return grad_scores
+
+    def to_key(unit, grad_scores):
         _, head, _, _, first, last = units[unit]
         rows, cols, keys = spans(unit)
-        query, key = heads_of(proj_ref, 0, head, cols), heads_of(proj_ref, 1, head, keys)
-        grad_proj_ref[rows, cols] = (nn(key, grad_scores) * SCALE).astype(BF)
-        both = nt(query, grad_scores), nt(grad_mixed_ref[rows, cols], probs_of(unit))
+        grad_key = nt(heads_of(proj_ref, 0, head, cols), grad_scores)
         if not first:
-            both = both[0] + sums["key"], both[1] + sums["value"]
-        sums["key"], sums["value"] = both
+            grad_key = grad_key + sums["key"]
+        sums["key"] = grad_key
         if last:
-            grad_proj_ref[E + rows.start : E + rows.stop, keys] = (both[0] * SCALE).astype(BF)
-            grad_proj_ref[2 * E + rows.start : 2 * E + rows.stop, keys] = both[1].astype(BF)
-
-    staged(len(units), BACK_GROUP if width <= LANES else WIDE_BACK_GROUP, to_probs, to_scores, to_proj)
+            grad_proj_ref[E + rows.start : E + rows.stop, keys] = (grad_key * SCALE).astype(BF)
+
+    def to_value(unit, _):
+        _, head, _, _, first, last = units[unit]
+        rows, cols, keys = spans(unit)
+        grad_value = nt(grad_mixed_ref[rows, cols], probs_of(unit))
+        if not first:
+            grad_value = grad_value + sums["value"]
+        sums["value"] = grad_value
+        if last:
+            grad_proj_ref[2 * E + rows.start : 2 * E + rows.stop, keys] = grad_value.astype(BF)
+
+    staged(len(units), BACK_GROUP if width <= LANES else WIDE_BACK_GROUP, to_value, to_probs, to_scores, to_query, to_key)
 
 
 def project_back(grad_ref, x_ref, grad_proj_ref, qkv):
@@ -345,41 +370,27 @@
 
 def rows_back_kernel(plan, wait, *refs):
     tiles, refs = refs[: plan.ranks_attr], refs[plan.ranks_attr :]
-    (out, normed_ref, proj_ref, probs_ref, mixed_ref), refs = refs[:5], refs[5:]
+    (order, out, normed_ref, proj_ref, probs_ref, mixed_ref), refs = refs[:6], refs[6:]
     keep_ref, send_ref, grad_ref, grad_proj_ref, sums_ref, grad_mixed_ref = refs
-    order = one_hot(plan.cells, plan.grouped_from_rows())
-    grad_ref[...] = nn(side_by_side(tiles), order).astype(BF)
-    wait()
+    grad_ref[...] = nn(side_by_side(tiles), order[...]).astype(BF)
     attend_back(grad_ref, proj_ref, probs_ref, grad_proj_ref, grad_mixed_ref, out, plan.all_attr)
     put_attend_grads(sums_ref, normed_ref, grad_proj_ref, mixed_ref, grad_ref)
     put_halves(bits_of("attr")[0], sums_ref, keep_ref, send_ref)
 
 
-def end_kernel(plan, by_rows, wait, qkv, x_ref, grad_ref, grad_proj_ref, *outs):
-    order = one_hot(plan.cells, plan.grouped_from_rows() if by_rows else plan.grouped_from_cols())
-    wait()
+def end_kernel(wait, order, qkv, x_ref, grad_ref, grad_proj_ref, *outs):
     grads = project_back(grad_ref, x_ref, grad_proj_ref, qkv)
-    put_tiles(outs, nt(jnp.concatenate(grads, axis=1).astype(BF), order))
+    put_tiles(outs, nt(jnp.concatenate(grads, axis=1).astype(BF), order[...]))
 
 
 def cols_kernel(plan, wait, *refs):
     count = plan.ranks_rec
     tiles, cot_tiles, refs = refs[:count], refs[count : 2 * count], refs[2 * count :]
-    (train_ref, out, up, down, qkv_t, out_t, up_t), refs = refs[:7], refs[7:]
+    (order, mask_ref, out, up, down, qkv_t, out_t, up_t), refs = refs[:8], refs[8:]
     normed_ref, mixed_ref, normed_second_ref, hidden_ref, cot_ref, grad_pre_ref, grad_ref, grad_proj_ref = refs[:8]
-    x_ref, proj_ref, probs_ref, second_ref, slope_ref, wide_ref, mask_ref, grad_mixed_ref = refs[8:]
+    x_ref, proj_ref, probs_ref, second_ref, slope_ref, wide_ref, grad_mixed_ref = refs[8:]
     width = max(LANES, plan.all_rec)
-    order = one_hot(plan.cells, plan.grouped_from_cols())
-    x_ref[...] = nn(side_by_side(tiles), order).astype(BF)
-
-    row = lax.broadcasted_iota(jnp.int32, (width, 1), 0)
-    sequence, far, near, own = digits(row, (width // plan.all_rec, plan.ranks_rec, plan.ranks_attr, plan.own_rec))
-    record = plan.rec * wrap(lax.axis_index("rec") - far, plan.ranks_rec) + plan.record_of(near, own)
-    chosen = (record == lane_index(plan.all_rec)) & (train_ref[...] > 0)
-    allowed = jnp.max(jnp.where(chosen, 1.0, 0.0), axis=1, keepdims=True) > 0.5
-    asker = digits(lane_index(width), (width // plan.all_rec, plan.all_rec))[0]
-    mask_ref[...] = jnp.where(allowed & (sequence == asker), 0.0, -1e30)
-
+    x_ref[...] = nn(side_by_side(tiles), order[...]).astype(BF)
     second = attend(x_ref, normed_ref, proj_ref, probs_ref, mixed_ref, qkv_t, out_t, width, mask_ref)
     for cols, value in zip(blocks_of(2 * LANES, plan.cells), second):
         second_ref[:, cols] = value.astype(BF)
@@ -393,8 +404,7 @@
         hidden_ref[rows, :] = (pre * gate).astype(BF)
         slope_ref[rows, :] = gate + pre * (jnp.exp2(pre * pre * BELL_EXP2) * BELL)
 
-    cot_ref[...] = nn(side_by_side(cot_tiles), order).astype(BF)
-    wait()
+    cot_ref[...] = nn(side_by_side(cot_tiles), order[...]).astype(BF)
     wide_ref[...] = nn(down[...], cot_ref[...])
     step = 64
     for start in range(0, FF, step):
@@ -634,25 +644,32 @@
     first = exchange(first, "attr", -1)
     cols = exchange(call(kernel(to_cols_kernel), col_tiles, [], *first), "rec", 1)
     weights_more = (qkv_samp, out_samp, up_weight, down_weight.T)
+    width = max(LANES, plan.all_rec)
+    order = ((count, count), BF, "near")
     got = call(
-        turn_more_kernel,
-        [(w.shape[::-1], BF, "near") for w in weights_more] + [(w.shape, BF, "near") for w in weights_more[:3]],
+        kernel(prepare_kernel),
+        [(w.shape[::-1], BF, "near") for w in weights_more]
+        + [(w.shape, BF, "near") for w in weights_more[:3]]
+        + [order] * 3
+        + [((width, width), F32, "near")],
         [],
+        train_split.reshape(1, -1),
         *[Far(w) for w in weights_more],
         after=cols[:1],
     )
-    turned, kept = turned + [Near(w) for w in got[:4]], kept + [Near(w) for w in got[4:]]
-
-    width = max(LANES, plan.all_rec)
+    got = [Near(array) for array in got]
+    turned, kept, (by_cols, by_rows, across, mask) = turned + got[:4], kept + got[4:7], got[7:]
+
     rows_sums, cols_sums = padded(6 * E), padded(18 * E)
     hidden, hidden_wide = ((FF, count), BF), ((FF, count), F32)
     got = call(
         kernel(cols_kernel),
         [out + ("near",) for out in (table, table, table, hidden, table, hidden, table, wide, table)],
-        [wide, probs(width), table, hidden_wide, hidden_wide, ((width, width), F32), table],
+        [wide, probs(width), table, hidden_wide, hidden_wide, table],
         *cols,
         *cot,
-        train_split.reshape(1, -1),
+        by_cols,
+        mask,
         kept[3],
         kept[4],
         turned[5],
@@ -665,7 +682,7 @@
     keep, send = call(
         cols_sums_kernel, [((cols_sums // 2, LANES), BF)] * 2, [((cols_sums, LANES), BF)], *saved[:8]
     )
-    grads = call(kernel(end_kernel, False), col_tiles, [], kept[2], saved[8], *saved[6:8], after=[keep])
+    grads = call(end_kernel, col_tiles, [], by_cols, kept[2], saved[8], *saved[6:8], after=[keep])
     sums = Total(keep, swap(send, "attr", near[0]))
     mark = grads[:1]
     for bit in near[1:]:
@@ -673,7 +690,7 @@
     (last,) = call(pass_kernel, row_tiles_of(grads[-1:]), [], grads[-1], after=mark)
     grads = exchange([*grads[:-1], last], "rec", -1)
     arrived = grads[1:]
-    rows_grads = call(kernel(to_rows_kernel), row_tiles, [], *grads, after=mark)
+    rows_grads = call(kernel(to_rows_kernel), row_tiles, [], *grads, across, after=mark)
     grads = exchange(rows_grads, "attr", 1)
     mark = sums.add(far[0], after=arrived)
 
@@ -682,6 +699,7 @@
         [((rows_sums // 2, LANES), BF)] * 2 + [table + ("near",), wide + ("near",)],
         [((rows_sums, LANES), BF), table],
         *grads,
+        by_rows,
         kept[1],
         normed,
         proj,
@@ -696,7 +714,7 @@
     for bit in near[1:]:
         mark = row_sums.halve("attr", bit, after=mark)
     grads = call(
-        kernel(end_kernel, True), row_tiles, [], kept[0], x, Near(grad), Near(grad_proj), after=mark
+        end_kernel, row_tiles, [], by_rows, kept[0], x, Near(grad), Near(grad_proj), after=mark
     )
     row_sums.add(far[0], after=mark)
     grads = exchange(grads, "attr", -1)

time: 80.4 us -> 79.9 us (level)
  no operation moved by 1% of the time
where the time goes in v5:
time: 79.9 us; the launch traced here: 79.7 us
  starting transfers between devices  34.2 us (43%)
  waiting for transfers between devices  24.2 us (30%)
  Pallas kernels  20.4 us (26%)
  between operations  0.87 us (1%)
    ppermute x21, starting transfers between devices, exchange(): lax.ppermute(tiles[k], axis, [(i, (i + sign * k) % size) for i in range(s...  24.3 us
    pallas_call x25, Pallas kernels, call(): pl.pallas_call(kernel, out_shape=[(pltpu.VMEM if out[2:] else jax.ShapeDt...  20.4 us
    ppermute x21, waiting for transfers between devices, exchange(): lax.ppermute(tiles[k], axis, [(i, (i + sign * k) % size) for i in range(s...  13.2 us
    ppermute x14, waiting for transfers between devices, swap(): return lax.ppermute(part, axis, [(i, i ^ bit) for i in range(size)])  11 us
    ppermute x14, starting transfers between devices, swap(): return lax.ppermute(part, axis, [(i, i ^ bit) for i in range(size)])  9.84 us
  transfers between devices with their start and end apart: 35, of which 17 were waited for; matrix products, arithmetic and copies ran while one was open for 0% of the time, Pallas kernels for 13%

profile of v5, /device:TPU:0, one launch (start us, length us, event | category | flops | bytes accessed | tf_op | source)
XLA Modules:
  0.0 79.7 jit_solution(6146353780916165752)
XLA Ops:
  0.6 1.5 %shard_map.144 = (bf16[192,128]{1,0:T(8,128)(2,1)S(1)}, bf16[192,128]{1,0:T(8,128)(2,1)S(1)}, bf16[192,128]{1,0:T(8,128)(2,1)S(1)}, bf16[192,128]{1,0:T(8,128)(2,1)S(1)}) custom-call(bf16[8,12288]{1,0:T(8,128)(2,1)} %refs_0_.2), custom_call_target="tpu_custom_call" | custom-call | tf_op jit(solution)/shard_map/pallas_call | solution.py:490
  2.1 0.5 collective-permute-start
  2.6 2.6 %collective-permute-start.1 = (bf16[192,128]{1,0:T(8,128)(2,1)S(1)}, bf16[192,128]{1,0:T(8,128)(2,1)S(1)}, u32[]{:S(2)}, u32[]{:S(2)}) collective-permute-start(bf16[192,128]{1,0:T(8,128)(2,1)S(1)} %get-tuple-element.82), channel_id=1, source_target_pairs={{0,2},{1,3},{2,0},{3,1},{4,6},{5,7},{6,4},{7,5},{8,10},{9,11},{10,... | collective-permute-start | bytes 147464 | tf_op jit(solution)/shard_map/ppermute | solution.py:507
  5.2 1.4 %collective-permute-start.2 = (bf16[192,128]{1,0:T(8,128)(2,1)S(1)}, bf16[192,128]{1,0:T(8,128)(2,1)S(1)}, u32[]{:S(2)}, u32[]{:S(2)}) collective-permute-start(bf16[192,128]{1,0:T(8,128)(2,1)S(1)} %get-tuple-element.83), channel_id=1, source_target_pairs={{0,3},{1,0},{2,1},{3,2},{4,7},{5,4},{6,5},{7,6},{8,11},{9,8},{10,9... | collective-permute-start | bytes 147464 | tf_op jit(solution)/shard_map/ppermute | solution.py:507
  6.6 1.7 %shard_map.145 = (bf16[192,128]{1,0:T(8,128)(2,1)S(1)}, bf16[192,128]{1,0:T(8,128)(2,1)S(1)}, bf16[192,128]{1,0:T(8,128)(2,1)S(1)}, bf16[192,128]{1,0:T(8,128)(2...) custom-call(bf16[8,12288]{1,0:T(8,128)(2,1)} %refs_0_.3, ...), custom_call_target="tpu_custom_call" | custom-call | tf_op jit(solution)/shard_map/pallas_call | solution.py:490
  8.3 2.2 %shard_map.146 = (bf16[192,128]{1,0:T(8,128)(2,1)S(1)}, bf16[192,128]{1,0:T(8,128)(2,1)S(1)}, bf16[192,128]{1,0:T(8,128)(2,1)S(1)}, bf16[192,128]{1,0:T(8,128)(2...) custom-call(bf16[192,128]{1,0:T(8,128)(2,1)S(1)} %get-tuple-element., ...), custom_call_target="tpu_custom_call" | custom-call | tf_op jit(solution)/shard_map/pallas_call | solution.py:490
  10.6 1.8 %collective-permute-start.3 = (bf16[192,128]{1,0:T(8,128)(2,1)S(1)}, bf16[192,128]{1,0:T(8,128)(2,1)S(1)}, u32[]{:S(2)}, u32[]{:S(2)}) collective-permute-start(bf16[192,128]{1,0:T(8,128)(2,1)S(1)} %get-tuple-element.87), channel_id=1, source_target_pairs={{0,3},{1,0},{2,1},{3,2},{4,7},{5,4},{6,5},{7,6},{8,11},{9,8},{10,9... | collective-permute-start | bytes 147464 | tf_op jit(solution)/shard_map/ppermute | solution.py:507
  12.4 0.3 collective-permute-start.4
  12.7 1.8 %collective-permute-start.9 = (bf16[192,128]{1,0:T(8,128)(2,1)S(1)}, bf16[192,128]{1,0:T(8,128)(2,1)S(1)}, u32[]{:S(2)}, u32[]{:S(2)}) collective-permute-start(bf16[192,128]{1,0:T(8,128)(2,1)S(1)} %get-tuple-element.100), channel_id=1, source_target_pairs={{0,4},{4,8},{8,12},{12,0},{1,5},{5,9},{9,13},{13,1},{2,6},{6,10},{... | collective-permute-start | bytes 147464 | tf_op jit(solution)/shard_map/ppermute | solution.py:507
  14.5 2.6 %collective-permute-start.10 = (bf16[192,128]{1,0:T(8,128)(2,1)S(1)}, bf16[192,128]{1,0:T(8,128)(2,1)S(1)}, u32[]{:S(2)}, u32[]{:S(2)}) collective-permute-start(bf16[192,128]{1,0:T(8,128)(2,1)S(1)} %get-tuple-element.101), channel_id=1, source_target_pairs={{0,8},{4,12},{8,0},{12,4},{1,9},{5,13},{9,1},{13,5},{2,10},{6,14},... | collective-permute-start | bytes 147464 | tf_op jit(solution)/shard_map/ppermute | solution.py:507
  17.1 1.3 %collective-permute-start.11 = (bf16[192,128]{1,0:T(8,128)(2,1)S(1)}, bf16[192,128]{1,0:T(8,128)(2,1)S(1)}, u32[]{:S(2)}, u32[]{:S(2)}) collective-permute-start(bf16[192,128]{1,0:T(8,128)(2,1)S(1)} %get-tuple-element.102), channel_id=1, source_target_pairs={{0,12},{4,0},{8,4},{12,8},{1,13},{5,1},{9,5},{13,9},{2,14},{6,2},{... | collective-permute-start | bytes 147464 | tf_op jit(solution)/shard_map/ppermute | solution.py:507
  18.4 0.3 shard_map.147
  18.7 0.7 collective-permute-start.6
  19.5 2.0 %collective-permute-start.7 = (bf16[192,128]{1,0:T(8,128)(2,1)S(1)}, bf16[192,128]{1,0:T(8,128)(2,1)S(1)}, u32[]{:S(2)}, u32[]{:S(2)}) collective-permute-start(bf16[192,128]{1,0:T(8,128)(2,1)S(1)} %get-tuple-element.97), channel_id=1, source_target_pairs={{0,8},{4,12},{8,0},{12,4},{1,9},{5,13},{9,1},{13,5},{2,10},{6,14},... | collective-permute-start | bytes 147464 | tf_op jit(solution)/shard_map/ppermute | solution.py:507
  21.5 1.3 %collective-permute-start.8 = (bf16[192,128]{1,0:T(8,128)(2,1)S(1)}, bf16[192,128]{1,0:T(8,128)(2,1)S(1)}, u32[]{:S(2)}, u32[]{:S(2)}) collective-permute-start(bf16[192,128]{1,0:T(8,128)(2,1)S(1)} %get-tuple-element.98), channel_id=1, source_target_pairs={{0,12},{4,0},{8,4},{12,8},{1,13},{5,1},{9,5},{13,9},{2,14},{6,2},{... | collective-permute-start | bytes 147464 | tf_op jit(solution)/shard_map/ppermute | solution.py:507
  22.8 1.7 %shard_map.148 = (bf16[576,192]{1,0:T(8,128)(2,1)S(1)}, bf16[192,192]{1,0:T(8,128)(2,1)S(1)}, bf16[768,192]{1,0:T(8,128)(2,1)S(1)}, bf16[768,192]{1,0:T(8,128)(2...) custom-call(s32[1,32]{1,0:T(1,128)S(1)} %bitcast.3, ...), custom_call_target="tpu_custom_call" | custom-call | tf_op jit(solution)/shard_map/pallas_call | solution.py:490
  24.5 0.7 collective-permute-done.6.refs_1_
  25.3 1.7 %collective-permute-done.7.refs_2_ = bf16[192,128]{1,0:T(8,128)(2,1)S(1)} collective-permute-done((bf16[192,128]{1,0:T(8,128)(2,1)S(1)}, bf16[192,128]{1,0:T(8,128)(2,1)S(1)}, u32[]{:S(2)}, u32[]{:S(2)}) %collective-permute-start.7) | collective-permute-done | bytes 49184 | tf_op jit(solution)/shard_map/ppermute | solution.py:507
  27.0 4.2 %shard_map.149 = (bf16[192,512]{1,0:T(8,128)(2,1)S(1)}, bf16[192,512]{1,0:T(8,128)(2,1)S(1)}, bf16[192,512]{1,0:T(8,128)(2,1)S(1)}, bf16[768,512]{1,0:T(8,128)(2...) custom-call(bf16[192,128]{1,0:T(8,128)(2,1)S(1)} %get-tuple-element., ...), custom_call_target="tpu_custom_call" | custom-call | tf_op jit(solution)/shard_map/pallas_call | solution.py:490
  31.2 1.1 %shard_map.150 = (bf16[1728,128]{1,0:T(8,128)(2,1)S(1)}, bf16[1728,128]{1,0:T(8,128)(2,1)S(1)}) custom-call(bf16[192,512]{1,0:T(8,128)(2,1)S(1)} %get-tuple-element.113.refs_0_, bf16[192,512]{1,0:T(8,128)(2,1)S(1)} %get-tuple-element.114.refs_1_, bf16[192,512]{1,0:T(8,128)(2,1)S(1)} %get-tuple-element.115.refs_2_, ...), custom_call_target="tpu_custom_call" | custom-call | tf_op jit(solution)/shard_map/pallas_call | solution.py:490
  32.3 0.1 collective-permute-start.14
  32.4 0.6 shard_map.151
  33.0 1.1 %collective-permute-done.14.refs_1_ = bf16[1728,128]{1,0:T(8,128)(2,1)S(1)} collective-permute-done((bf16[1728,128]{1,0:T(8,128)(2,1)S(1)}, bf16[1728,128]{1,0:T(8,128)(2,1)S(1)}, u32[]{:S(2)}, u32[]{:S(2)}) %collective-permute-start.14) | collective-permute-done | bytes 442400 | tf_op jit(solution)/shard_map/ppermute | solution.py:514
  34.1 0.1 shard_map.152
  34.2 0.5 collective-permute-start.19
  34.7 2.6 %collective-permute-start.12 = (bf16[192,128]{1,0:T(8,128)(2,1)S(1)}, bf16[192,128]{1,0:T(8,128)(2,1)S(1)}, u32[]{:S(2)}, u32[]{:S(2)}) collective-permute-start(bf16[192,128]{1,0:T(8,128)(2,1)S(1)} %get-tuple-element.121), channel_id=1, source_target_pairs={{0,12},{4,0},{8,4},{12,8},{1,13},{5,1},{9,5},{13,9},{2,14},{6,2},{... | collective-permute-start | bytes 147464 | tf_op jit(solution)/shard_map/ppermute | solution.py:507
  37.3 0.2 collective-permute-start.13
  37.5 0.3 collective-permute-start.15
  37.9 1.5 %collective-permute-done.12.refs_1_.refs_2_ = bf16[192,128]{1,0:T(8,128)(2,1)S(1)} collective-permute-done((bf16[192,128]{1,0:T(8,128)(2,1)S(1)}, bf16[192,128]{1,0:T(8,128)(2,1)S(1)}, u32[]{:S(2)}, u32[]{:S(2)}) %collective-permute-start.12) | collective-permute-done | bytes 49184 | tf_op jit(solution)/shard_map/ppermute | solution.py:507
  39.4 3.1 %collective-permute-done.13.refs_2_.refs_3_ = bf16[192,128]{1,0:T(8,128)(2,1)S(1)} collective-permute-done((bf16[192,128]{1,0:T(8,128)(2,1)S(1)}, bf16[192,128]{1,0:T(8,128)(2,1)S(1)}, u32[]{:S(2)}, u32[]{:S(2)}) %collective-permute-start.13) | collective-permute-done | bytes 49184 | tf_op jit(solution)/shard_map/ppermute | solution.py:507
  42.5 0.9 %collective-permute-done.15.refs_3_.refs_4_ = bf16[192,128]{1,0:T(8,128)(2,1)S(1)} collective-permute-done((bf16[192,128]{1,0:T(8,128)(2,1)S(1)}, bf16[192,128]{1,0:T(8,128)(2,1)S(1)}, u32[]{:S(2)}, u32[]{:S(2)}) %collective-permute-start.15) | collective-permute-done | bytes 49184 | tf_op jit(solution)/shard_map/ppermute | solution.py:507
  43.5 0.1 collective-permute-start.21
  43.6 0.3 shard_map.154
  44.0 1.5 %collective-permute-start.17 = (bf16[192,128]{1,0:T(8,128)(2,1)S(1)}, bf16[192,128]{1,0:T(8,128)(2,1)S(1)}, u32[]{:S(2)}, u32[]{:S(2)}) collective-permute-start(bf16[192,128]{1,0:T(8,128)(2,1)S(1)} %get-tuple-element.129), channel_id=1, source_target_pairs={{0,2},{1,3},{2,0},{3,1},{4,6},{5,7},{6,4},{7,5},{8,10},{9,11},{10,... | collective-permute-start | bytes 147464 | tf_op jit(solution)/shard_map/ppermute | solution.py:507
  45.5 1.4 %collective-permute-start.18 = (bf16[192,128]{1,0:T(8,128)(2,1)S(1)}, bf16[192,128]{1,0:T(8,128)(2,1)S(1)}, u32[]{:S(2)}, u32[]{:S(2)}) collective-permute-start(bf16[192,128]{1,0:T(8,128)(2,1)S(1)} %get-tuple-element.130), channel_id=1, source_target_pairs={{0,3},{1,0},{2,1},{3,2},{4,7},{5,4},{6,5},{7,6},{8,11},{9,8},{10,9... | collective-permute-start | bytes 147464 | tf_op jit(solution)/shard_map/ppermute | solution.py:507
  46.9 0.6 collective-permute-done.16.refs_1_
  47.5 0.7 collective-permute-done.17.refs_2_
  48.1 0.5 collective-permute-done.18.refs_3_
  48.6 2.3 %shard_map.156 = (bf16[576,128]{1,0:T(8,128)(2,1)S(1)}, bf16[576,128]{1,0:T(8,128)(2,1)S(1)}, bf16[192,512]{1,0:T(8,128)(2,1)S(1)}, bf16[576,512]{1,0:T(8,128)(2,1)S(1)}) custom-call(bf16[192,128]{1,0:T(8,128)(2,1)S(1)} %get-tuple-element.127.refs_0_, bf16[192,128]{1,0:T(8,128)(2,1)S(1)} %collective-permute-done.16.refs_1_, ...), custom_call_target="tpu_custom_call" | custom-call | tf_op jit(solution)/shard_map/pallas_call | solution.py:490
  51.0 1.1 %collective-permute-start.20 = (bf16[576,128]{1,0:T(8,128)(2,1)S(1)}, bf16[576,128]{1,0:T(8,128)(2,1)S(1)}, u32[]{:S(2)}, u32[]{:S(2)}) collective-permute-start(bf16[576,128]{1,0:T(8,128)(2,1)S(1)} %get-tuple-element.140), channel_id=1, source_target_pairs={{0,1},{1,0},{2,3},{3,2},{4,5},{5,4},{6,7},{7,6},{8,9},{9,8},{10,11... | collective-permute-start | bytes 442376 | tf_op jit(solution)/shard_map/ppermute | solution.py:514
  52.1 1.7 %collective-permute-start.28 = (bf16[864,128]{1,0:T(8,128)(2,1)S(1)}, bf16[864,128]{1,0:T(8,128)(2,1)S(1)}, u32[]{:S(2)}, u32[]{:S(2)}) collective-permute-start(bf16[864,128]{1,0:T(8,128)(2,1)S(1)} %shard_map.157.refs_2_.refs_0_), channel_id=1, source_target_pairs={{0,8},{4,12},{8,0},{12,4},{1,9},{5,13},{9,1},{13,5},{2,10},{6,14},... | collective-permute-start | bytes 663560 | tf_op jit(solution)/shard_map/ppermute | solution.py:514
  53.8 1.3 %collective-permute-start.25 = (bf16[288,128]{1,0:T(8,128)(2,1)S(1)}, bf16[288,128]{1,0:T(8,128)(2,1)S(1)}, u32[]{:S(2)}, u32[]{:S(2)}) collective-permute-start(bf16[288,128]{1,0:T(8,128)(2,1)S(1)} %get-tuple-element.146), channel_id=1, source_target_pairs={{0,2},{1,3},{2,0},{3,1},{4,6},{5,7},{6,4},{7,5},{8,10},{9,11},{10,... | collective-permute-start | bytes 221192 | tf_op jit(solution)/shard_map/ppermute | solution.py:514
  55.1 3.1 %collective-permute-done.25.refs_1_ = bf16[288,128]{1,0:T(8,128)(2,1)S(1)} collective-permute-done((bf16[288,128]{1,0:T(8,128)(2,1)S(1)}, bf16[288,128]{1,0:T(8,128)(2,1)S(1)}, u32[]{:S(2)}, u32[]{:S(2)}) %collective-permute-start.25) | collective-permute-done | bytes 73760 | tf_op jit(solution)/shard_map/ppermute | solution.py:514
  58.2 1.2 %collective-permute-start.26 = (bf16[288,128]{1,0:T(8,128)(2,1)S(1)}, bf16[288,128]{1,0:T(8,128)(2,1)S(1)}, u32[]{:S(2)}, u32[]{:S(2)}) collective-permute-start(bf16[288,128]{1,0:T(8,128)(2,1)S(1)} %shard_map.160.refs_0_), channel_id=1, source_target_pairs={{0,4},{4,0},{8,12},{12,8},{1,5},{5,1},{9,13},{13,9},{2,6},{6,2},{1... | collective-permute-start | bytes 221192 | tf_op jit(solution)/shard_map/ppermute | solution.py:514
  59.5 0.6 shard_map.159
  60.1 0.4 collective-permute-start.22
  60.5 1.2 %collective-permute-start.23 = (bf16[192,128]{1,0:T(8,128)(2,1)S(1)}, bf16[192,128]{1,0:T(8,128)(2,1)S(1)}, u32[]{:S(2)}, u32[]{:S(2)}) collective-permute-start(bf16[192,128]{1,0:T(8,128)(2,1)S(1)} %get-tuple-element.144), channel_id=1, source_target_pairs={{0,2},{1,3},{2,0},{3,1},{4,6},{5,7},{6,4},{7,5},{8,10},{9,11},{10,... | collective-permute-start | bytes 147464 | tf_op jit(solution)/shard_map/ppermute | solution.py:507
  61.7 0.2 collective-permute-start.24
  61.9 0.4 collective-permute-done.22.refs_2_.refs_1_
  62.3 2.5 %collective-permute-done.23.refs_3_.refs_2_ = bf16[192,128]{1,0:T(8,128)(2,1)S(1)} collective-permute-done((bf16[192,128]{1,0:T(8,128)(2,1)S(1)}, bf16[192,128]{1,0:T(8,128)(2,1)S(1)}, u32[]{:S(2)}, u32[]{:S(2)}) %collective-permute-start.23) | collective-permute-done | bytes 49184 | tf_op jit(solution)/shard_map/ppermute | solution.py:507
  64.8 0.5 collective-permute-done.24.refs_4_.refs_3_
  65.3 0.4 collective-permute-done.26.refs_1_
  65.8 1.3 %collective-permute-start.32 = (bf16[864,128]{1,0:T(8,128)(2,1)S(1)}, bf16[864,128]{1,0:T(8,128)(2,1)S(1)}, u32[]{:S(2)}, u32[]{:S(2)}) collective-permute-start(bf16[864,128]{1,0:T(8,128)(2,1)S(1)} %shard_map.162.refs_2_.refs_0_), channel_id=1, source_target_pairs={{0,2},{1,3},{2,0},{3,1},{4,6},{5,7},{6,4},{7,5},{8,10},{9,11},{10,... | collective-permute-start | bytes 663560 | tf_op jit(solution)/shard_map/ppermute | solution.py:514
  67.1 1.3 %collective-permute-start.27 = (bf16[288,128]{1,0:T(8,128)(2,1)S(1)}, bf16[288,128]{1,0:T(8,128)(2,1)S(1)}, u32[]{:S(2)}, u32[]{:S(2)}) collective-permute-start(bf16[288,128]{1,0:T(8,128)(2,1)S(1)} %shard_map.161.refs_2_.refs_0_), channel_id=1, source_target_pairs={{0,8},{4,12},{8,0},{12,4},{1,9},{5,13},{9,1},{13,5},{2,10},{6,14},... | collective-permute-start | bytes 221192 | tf_op jit(solution)/shard_map/ppermute | solution.py:514
  68.4 4.2 %collective-permute-done.27.refs_1_ = bf16[288,128]{1,0:T(8,128)(2,1)S(1)} collective-permute-done((bf16[288,128]{1,0:T(8,128)(2,1)S(1)}, bf16[288,128]{1,0:T(8,128)(2,1)S(1)}, u32[]{:S(2)}, u32[]{:S(2)}) %collective-permute-start.27) | collective-permute-done | bytes 73760 | tf_op jit(solution)/shard_map/ppermute | solution.py:514
  72.7 0.1 collective-permute-start.33
  72.8 1.0 %collective-permute-start.30 = (bf16[288,128]{1,0:T(8,128)(2,1)S(1)}, bf16[288,128]{1,0:T(8,128)(2,1)S(1)}, u32[]{:S(2)}, u32[]{:S(2)}) collective-permute-start(bf16[288,128]{1,0:T(8,128)(2,1)S(1)} %shard_map.163.refs_4_.refs_1_.refs_0_), channel_id=1, source_target_pairs={{0,2},{1,3},{2,0},{3,1},{4,6},{5,7},{6,4},{7,5},{8,10},{9,11},{10,... | collective-permute-start | bytes 221192 | tf_op jit(solution)/shard_map/ppermute | solution.py:514
  73.8 0.2 collective-permute-start.29
  74.0 1.1 %shard_map.164.refs_1_ = bf16[8,12288]{1,0:T(8,128)(2,1)} custom-call(bf16[192,128]{1,0:T(8,128)(2,1)S(1)} %get-tuple-element.142.refs_0_, bf16[192,128]{1,0:T(8,128)(2,1)S(1)} %collective-permute-done.22.refs_2_.refs_1_, bf16[192,128]{1,0:T(8,128)(2,1)S(1)} %collective-permute-done.23.refs_3_.refs_2_, ...), custom_call_target="tpu_custom_call" | custom-call | tf_op jit(solution)/shard_map/pallas_call | solution.py:490
  75.1 1.4 %shard_map.166 = (f32[192,576]{1,0:T(8,128)}, f32[192,192]{1,0:T(8,128)}, f32[192,768]{1,0:T(8,128)}, f32[192,768]{1,0:T(8,128)}) custom-call(bf16[864,128]{1,0:T(8,128)(2,1)S(1)} %shard_map.162.refs_2_.refs_0_, bf16[864,128]{1,0:T(8,128)(2,1)S(1)} %collective-permute-done.31.refs_1_, bf16[864,128]{1,0:T(8,128)(2,1)S(1)} %collective-permute-done.32.refs_0_.refs_2_, ...), custom_call_target="tpu_custom_call" | custom-call | tf_op jit(solution)/shard_map/pallas_call | solution.py:490
  76.5 0.9 %collective-permute-done.30.refs_0_.refs_2_ = bf16[288,128]{1,0:T(8,128)(2,1)S(1)} collective-permute-done((bf16[288,128]{1,0:T(8,128)(2,1)S(1)}, bf16[288,128]{1,0:T(8,128)(2,1)S(1)}, u32[]{:S(2)}, u32[]{:S(2)}) %collective-permute-start.30) | collective-permute-done | bytes 73760 | tf_op jit(solution)/shard_map/ppermute | solution.py:514
  77.5 0.1 collective-permute-start.34
  77.6 1.2 %collective-permute-done.34.refs_3_ = bf16[288,128]{1,0:T(8,128)(2,1)S(1)} collective-permute-done((bf16[288,128]{1,0:T(8,128)(2,1)S(1)}, bf16[288,128]{1,0:T(8,128)(2,1)S(1)}, u32[]{:S(2)}, u32[]{:S(2)}) %collective-permute-start.34) | collective-permute-done | bytes 73760 | tf_op jit(solution)/shard_map/ppermute | solution.py:514
  78.8 0.9 %shard_map.168 = (f32[192,576]{1,0:T(8,128)}, f32[192,192]{1,0:T(8,128)}) custom-call(bf16[288,128]{1,0:T(8,128)(2,1)S(1)} %shard_map.163.refs_4_.refs_1_.refs_0_, bf16[288,128]{1,0:T(8,128)(2,1)S(1)} %collective-permute-done.29.refs_1_, bf16[288,128]{1,0:T(8,128)(2,1)S(1)} %collective-permute-done.30.refs_0_.refs_2_, ...), custom_call_target="tpu_custom_call" | custom-call | tf_op jit(solution)/shard_map/pallas_call | solution.py:490
  (33 shorter events, 0.4 us)
Async XLA Ops:
  0.6 22.2 %copy-start = (s32[32]{0:T(128)S(1)}, s32[32]{0:T(128)}, u32[]{:S(2)}) copy-start(s32[32]{0:T(128)} %param.17) | copy-start | bytes 388
  2.1 6.2 %collective-permute-start = (bf16[192,128]{1,0:T(8,128)(2,1)S(1)}, bf16[192,128]{1,0:T(8,128)(2,1)S(1)}, u32[]{:S(2)}, u32[]{:S(2)}) collective-permute-start(bf16[192,128]{1,0:T(8,128)(2,1)S(1)} %get-tuple-element.81), channel_id=1, source_target_pairs={{0,1},{1,2},{2,3},{3,0},{4,5},{5,6},{6,7},{7,4},{8,9},{9,10},{10,1... | collective-permute-start | bytes 147464 | tf_op jit(solution)/shard_map/ppermute | solution.py:507
  2.6 5.7 %collective-permute-start.1 = (bf16[192,128]{1,0:T(8,128)(2,1)S(1)}, bf16[192,128]{1,0:T(8,128)(2,1)S(1)}, u32[]{:S(2)}, u32[]{:S(2)}) collective-permute-start(bf16[192,128]{1,0:T(8,128)(2,1)S(1)} %get-tuple-element.82), channel_id=1, source_target_pairs={{0,2},{1,3},{2,0},{3,1},{4,6},{5,7},{6,4},{7,5},{8,10},{9,11},{10,... | collective-permute-start | bytes 147464 | tf_op jit(solution)/shard_map/ppermute | solution.py:507
  5.2 3.1 %collective-permute-start.2 = (bf16[192,128]{1,0:T(8,128)(2,1)S(1)}, bf16[192,128]{1,0:T(8,128)(2,1)S(1)}, u32[]{:S(2)}, u32[]{:S(2)}) collective-permute-start(bf16[192,128]{1,0:T(8,128)(2,1)S(1)} %get-tuple-element.83), channel_id=1, source_target_pairs={{0,3},{1,0},{2,1},{3,2},{4,7},{5,4},{6,5},{7,6},{8,11},{9,8},{10,9... | collective-permute-start | bytes 147464 | tf_op jit(solution)/shard_map/ppermute | solution.py:507
  10.6 6.5 %collective-permute-start.3 = (bf16[192,128]{1,0:T(8,128)(2,1)S(1)}, bf16[192,128]{1,0:T(8,128)(2,1)S(1)}, u32[]{:S(2)}, u32[]{:S(2)}) collective-permute-start(bf16[192,128]{1,0:T(8,128)(2,1)S(1)} %get-tuple-element.87), channel_id=1, source_target_pairs={{0,3},{1,0},{2,1},{3,2},{4,7},{5,4},{6,5},{7,6},{8,11},{9,8},{10,9... | collective-permute-start | bytes 147464 | tf_op jit(solution)/shard_map/ppermute | solution.py:507
  12.4 6.1 %collective-permute-start.4 = (bf16[192,128]{1,0:T(8,128)(2,1)S(1)}, bf16[192,128]{1,0:T(8,128)(2,1)S(1)}, u32[]{:S(2)}, u32[]{:S(2)}) collective-permute-start(bf16[192,128]{1,0:T(8,128)(2,1)S(1)} %get-tuple-element.88), channel_id=1, source_target_pairs={{0,2},{1,3},{2,0},{3,1},{4,6},{5,7},{6,4},{7,5},{8,10},{9,11},{10,... | collective-permute-start | bytes 147464 | tf_op jit(solution)/shard_map/ppermute | solution.py:507
  12.7 5.7 %collective-permute-start.5 = (bf16[192,128]{1,0:T(8,128)(2,1)S(1)}, bf16[192,128]{1,0:T(8,128)(2,1)S(1)}, u32[]{:S(2)}, u32[]{:S(2)}) collective-permute-start(bf16[192,128]{1,0:T(8,128)(2,1)S(1)} %get-tuple-element.89), channel_id=1, source_target_pairs={{0,1},{1,2},{2,3},{3,0},{4,5},{5,6},{6,7},{7,4},{8,9},{9,10},{10,1... | collective-permute-start | bytes 147464 | tf_op jit(solution)/shard_map/ppermute | solution.py:507
  12.7 8.8 %collective-permute-start.9 = (bf16[192,128]{1,0:T(8,128)(2,1)S(1)}, bf16[192,128]{1,0:T(8,128)(2,1)S(1)}, u32[]{:S(2)}, u32[]{:S(2)}) collective-permute-start(bf16[192,128]{1,0:T(8,128)(2,1)S(1)} %get-tuple-element.100), channel_id=1, source_target_pairs={{0,4},{4,8},{8,12},{12,0},{1,5},{5,9},{9,13},{13,1},{2,6},{6,10},{... | collective-permute-start | bytes 147464 | tf_op jit(solution)/shard_map/ppermute | solution.py:507
  14.5 10.0 %collective-permute-start.10 = (bf16[192,128]{1,0:T(8,128)(2,1)S(1)}, bf16[192,128]{1,0:T(8,128)(2,1)S(1)}, u32[]{:S(2)}, u32[]{:S(2)}) collective-permute-start(bf16[192,128]{1,0:T(8,128)(2,1)S(1)} %get-tuple-element.101), channel_id=1, source_target_pairs={{0,8},{4,12},{8,0},{12,4},{1,9},{5,13},{9,1},{13,5},{2,10},{6,14},... | collective-permute-start | bytes 147464 | tf_op jit(solution)/shard_map/ppermute | solution.py:507
  17.1 7.5 %collective-permute-start.11 = (bf16[192,128]{1,0:T(8,128)(2,1)S(1)}, bf16[192,128]{1,0:T(8,128)(2,1)S(1)}, u32[]{:S(2)}, u32[]{:S(2)}) collective-permute-start(bf16[192,128]{1,0:T(8,128)(2,1)S(1)} %get-tuple-element.102), channel_id=1, source_target_pairs={{0,12},{4,0},{8,4},{12,8},{1,13},{5,1},{9,5},{13,9},{2,14},{6,2},{... | collective-permute-start | bytes 147464 | tf_op jit(solution)/shard_map/ppermute | solution.py:507
  18.7 6.6 %collective-permute-start.6 = (bf16[192,128]{1,0:T(8,128)(2,1)S(1)}, bf16[192,128]{1,0:T(8,128)(2,1)S(1)}, u32[]{:S(2)}, u32[]{:S(2)}) collective-permute-start(bf16[192,128]{1,0:T(8,128)(2,1)S(1)} %get-tuple-element.96), channel_id=1, source_target_pairs={{0,4},{4,8},{8,12},{12,0},{1,5},{5,9},{9,13},{13,1},{2,6},{6,10},{... | collective-permute-start | bytes 147464 | tf_op jit(solution)/shard_map/ppermute | solution.py:507
  19.5 7.5 %collective-permute-start.7 = (bf16[192,128]{1,0:T(8,128)(2,1)S(1)}, bf16[192,128]{1,0:T(8,128)(2,1)S(1)}, u32[]{:S(2)}, u32[]{:S(2)}) collective-permute-start(bf16[192,128]{1,0:T(8,128)(2,1)S(1)} %get-tuple-element.97), channel_id=1, source_target_pairs={{0,8},{4,12},{8,0},{12,4},{1,9},{5,13},{9,1},{13,5},{2,10},{6,14},... | collective-permute-start | bytes 147464 | tf_op jit(solution)/shard_map/ppermute | solution.py:507
  21.5 5.5 %collective-permute-start.8 = (bf16[192,128]{1,0:T(8,128)(2,1)S(1)}, bf16[192,128]{1,0:T(8,128)(2,1)S(1)}, u32[]{:S(2)}, u32[]{:S(2)}) collective-permute-start(bf16[192,128]{1,0:T(8,128)(2,1)S(1)} %get-tuple-element.98), channel_id=1, source_target_pairs={{0,12},{4,0},{8,4},{12,8},{1,13},{5,1},{9,5},{13,9},{2,14},{6,2},{... | collective-permute-start | bytes 147464 | tf_op jit(solution)/shard_map/ppermute | solution.py:507
  32.3 1.9 %collective-permute-start.14 = (bf16[1728,128]{1,0:T(8,128)(2,1)S(1)}, bf16[1728,128]{1,0:T(8,128)(2,1)S(1)}, u32[]{:S(2)}, u32[]{:S(2)}) collective-permute-start(bf16[1728,128]{1,0:T(8,128)(2,1)S(1)} %get-tuple-element.124), channel_id=1, source_target_pairs={{0,1},{1,0},{2,3},{3,2},{4,5},{5,4},{6,7},{7,6},{8,9},{9,8},{10,11... | collective-permute-start | bytes 1327112 | tf_op jit(solution)/shard_map/ppermute | solution.py:514
  34.2 9.2 %collective-permute-start.19 = (bf16[864,128]{1,0:T(8,128)(2,1)S(1)}, bf16[864,128]{1,0:T(8,128)(2,1)S(1)}, u32[]{:S(2)}, u32[]{:S(2)}) collective-permute-start(bf16[864,128]{1,0:T(8,128)(2,1)S(1)} %get-tuple-element.136), channel_id=1, source_target_pairs={{0,2},{1,3},{2,0},{3,1},{4,6},{5,7},{6,4},{7,5},{8,10},{9,11},{10,... | collective-permute-start | bytes 663560 | tf_op jit(solution)/shard_map/ppermute | solution.py:514
  34.7 4.7 %collective-permute-start.12 = (bf16[192,128]{1,0:T(8,128)(2,1)S(1)}, bf16[192,128]{1,0:T(8,128)(2,1)S(1)}, u32[]{:S(2)}, u32[]{:S(2)}) collective-permute-start(bf16[192,128]{1,0:T(8,128)(2,1)S(1)} %get-tuple-element.121), channel_id=1, source_target_pairs={{0,12},{4,0},{8,4},{12,8},{1,13},{5,1},{9,5},{13,9},{2,14},{6,2},{... | collective-permute-start | bytes 147464 | tf_op jit(solution)/shard_map/ppermute | solution.py:507
  37.3 5.2 %collective-permute-start.13 = (bf16[192,128]{1,0:T(8,128)(2,1)S(1)}, bf16[192,128]{1,0:T(8,128)(2,1)S(1)}, u32[]{:S(2)}, u32[]{:S(2)}) collective-permute-start(bf16[192,128]{1,0:T(8,128)(2,1)S(1)} %get-tuple-element.122), channel_id=1, source_target_pairs={{0,8},{4,12},{8,0},{12,4},{1,9},{5,13},{9,1},{13,5},{2,10},{6,14},... | collective-permute-start | bytes 147464 | tf_op jit(solution)/shard_map/ppermute | solution.py:507
  37.5 5.9 %collective-permute-start.15 = (bf16[192,128]{1,0:T(8,128)(2,1)S(1)}, bf16[192,128]{1,0:T(8,128)(2,1)S(1)}, u32[]{:S(2)}, u32[]{:S(2)}) collective-permute-start(bf16[192,128]{1,0:T(8,128)(2,1)S(1)} %shard_map.153), channel_id=1, source_target_pairs={{0,4},{4,8},{8,12},{12,0},{1,5},{5,9},{9,13},{13,1},{2,6},{6,10},{... | collective-permute-start | bytes 147464 | tf_op jit(solution)/shard_map/ppermute | solution.py:507
  43.5 8.6 %collective-permute-start.21 = (bf16[864,128]{1,0:T(8,128)(2,1)S(1)}, bf16[864,128]{1,0:T(8,128)(2,1)S(1)}, u32[]{:S(2)}, u32[]{:S(2)}) collective-permute-start(bf16[864,128]{1,0:T(8,128)(2,1)S(1)} %shard_map.155.refs_10_.refs_0_), channel_id=1, source_target_pairs={{0,4},{4,0},{8,12},{12,8},{1,5},{5,1},{9,13},{13,9},{2,6},{6,2},{1... | collective-permute-start | bytes 663560 | tf_op jit(solution)/shard_map/ppermute | solution.py:514
  43.9 3.6 %collective-permute-start.16 = (bf16[192,128]{1,0:T(8,128)(2,1)S(1)}, bf16[192,128]{1,0:T(8,128)(2,1)S(1)}, u32[]{:S(2)}, u32[]{:S(2)}) collective-permute-start(bf16[192,128]{1,0:T(8,128)(2,1)S(1)} %get-tuple-element.128), channel_id=1, source_target_pairs={{0,1},{1,2},{2,3},{3,0},{4,5},{5,6},{6,7},{7,4},{8,9},{9,10},{10,1... | collective-permute-start | bytes 147464 | tf_op jit(solution)/shard_map/ppermute | solution.py:507
  44.0 4.2 %collective-permute-start.17 = (bf16[192,128]{1,0:T(8,128)(2,1)S(1)}, bf16[192,128]{1,0:T(8,128)(2,1)S(1)}, u32[]{:S(2)}, u32[]{:S(2)}) collective-permute-start(bf16[192,128]{1,0:T(8,128)(2,1)S(1)} %get-tuple-element.129), channel_id=1, source_target_pairs={{0,2},{1,3},{2,0},{3,1},{4,6},{5,7},{6,4},{7,5},{8,10},{9,11},{10,... | collective-permute-start | bytes 147464 | tf_op jit(solution)/shard_map/ppermute | solution.py:507
  45.5 3.1 %collective-permute-start.18 = (bf16[192,128]{1,0:T(8,128)(2,1)S(1)}, bf16[192,128]{1,0:T(8,128)(2,1)S(1)}, u32[]{:S(2)}, u32[]{:S(2)}) collective-permute-start(bf16[192,128]{1,0:T(8,128)(2,1)S(1)} %get-tuple-element.130), channel_id=1, source_target_pairs={{0,3},{1,0},{2,1},{3,2},{4,7},{5,4},{6,5},{7,6},{8,11},{9,8},{10,9... | collective-permute-start | bytes 147464 | tf_op jit(solution)/shard_map/ppermute | solution.py:507
  51.0 2.8 %collective-permute-start.20 = (bf16[576,128]{1,0:T(8,128)(2,1)S(1)}, bf16[576,128]{1,0:T(8,128)(2,1)S(1)}, u32[]{:S(2)}, u32[]{:S(2)}) collective-permute-start(bf16[576,128]{1,0:T(8,128)(2,1)S(1)} %get-tuple-element.140), channel_id=1, source_target_pairs={{0,1},{1,0},{2,3},{3,2},{4,5},{5,4},{6,7},{7,6},{8,9},{9,8},{10,11... | collective-permute-start | bytes 442376 | tf_op jit(solution)/shard_map/ppermute | solution.py:514
  52.1 13.6 %collective-permute-start.28 = (bf16[864,128]{1,0:T(8,128)(2,1)S(1)}, bf16[864,128]{1,0:T(8,128)(2,1)S(1)}, u32[]{:S(2)}, u32[]{:S(2)}) collective-permute-start(bf16[864,128]{1,0:T(8,128)(2,1)S(1)} %shard_map.157.refs_2_.refs_0_), channel_id=1, source_target_pairs={{0,8},{4,12},{8,0},{12,4},{1,9},{5,13},{9,1},{13,5},{2,10},{6,14},... | collective-permute-start | bytes 663560 | tf_op jit(solution)/shard_map/ppermute | solution.py:514
  53.8 4.4 %collective-permute-start.25 = (bf16[288,128]{1,0:T(8,128)(2,1)S(1)}, bf16[288,128]{1,0:T(8,128)(2,1)S(1)}, u32[]{:S(2)}, u32[]{:S(2)}) collective-permute-start(bf16[288,128]{1,0:T(8,128)(2,1)S(1)} %get-tuple-element.146), channel_id=1, source_target_pairs={{0,2},{1,3},{2,0},{3,1},{4,6},{5,7},{6,4},{7,5},{8,10},{9,11},{10,... | collective-permute-start | bytes 221192 | tf_op jit(solution)/shard_map/ppermute | solution.py:514
  58.2 7.4 %collective-permute-start.26 = (bf16[288,128]{1,0:T(8,128)(2,1)S(1)}, bf16[288,128]{1,0:T(8,128)(2,1)S(1)}, u32[]{:S(2)}, u32[]{:S(2)}) collective-permute-start(bf16[288,128]{1,0:T(8,128)(2,1)S(1)} %shard_map.160.refs_0_), channel_id=1, source_target_pairs={{0,4},{4,0},{8,12},{12,8},{1,5},{5,1},{9,13},{13,9},{2,6},{6,2},{1... | collective-permute-start | bytes 221192 | tf_op jit(solution)/shard_map/ppermute | solution.py:514
  60.1 2.1 %collective-permute-start.22 = (bf16[192,128]{1,0:T(8,128)(2,1)S(1)}, bf16[192,128]{1,0:T(8,128)(2,1)S(1)}, u32[]{:S(2)}, u32[]{:S(2)}) collective-permute-start(bf16[192,128]{1,0:T(8,128)(2,1)S(1)} %get-tuple-element.143), channel_id=1, source_target_pairs={{0,3},{1,0},{2,1},{3,2},{4,7},{5,4},{6,5},{7,6},{8,11},{9,8},{10,9... | collective-permute-start | bytes 147464 | tf_op jit(solution)/shard_map/ppermute | solution.py:507
  60.5 4.3 %collective-permute-start.23 = (bf16[192,128]{1,0:T(8,128)(2,1)S(1)}, bf16[192,128]{1,0:T(8,128)(2,1)S(1)}, u32[]{:S(2)}, u32[]{:S(2)}) collective-permute-start(bf16[192,128]{1,0:T(8,128)(2,1)S(1)} %get-tuple-element.144), channel_id=1, source_target_pairs={{0,2},{1,3},{2,0},{3,1},{4,6},{5,7},{6,4},{7,5},{8,10},{9,11},{10,... | collective-permute-start | bytes 147464 | tf_op jit(solution)/shard_map/ppermute | solution.py:507
  61.7 3.6 %collective-permute-start.24 = (bf16[192,128]{1,0:T(8,128)(2,1)S(1)}, bf16[192,128]{1,0:T(8,128)(2,1)S(1)}, u32[]{:S(2)}, u32[]{:S(2)}) collective-permute-start(bf16[192,128]{1,0:T(8,128)(2,1)S(1)} %get-tuple-element.145), channel_id=1, source_target_pairs={{0,1},{1,2},{2,3},{3,0},{4,5},{5,6},{6,7},{7,4},{8,9},{9,10},{10,1... | collective-permute-start | bytes 147464 | tf_op jit(solution)/shard_map/ppermute | solution.py:507
  65.8 6.9 %collective-permute-start.32 = (bf16[864,128]{1,0:T(8,128)(2,1)S(1)}, bf16[864,128]{1,0:T(8,128)(2,1)S(1)}, u32[]{:S(2)}, u32[]{:S(2)}) collective-permute-start(bf16[864,128]{1,0:T(8,128)(2,1)S(1)} %shard_map.162.refs_2_.refs_0_), channel_id=1, source_target_pairs={{0,2},{1,3},{2,0},{3,1},{4,6},{5,7},{6,4},{7,5},{8,10},{9,11},{10,... | collective-permute-start | bytes 663560 | tf_op jit(solution)/shard_map/ppermute | solution.py:514
  67.1 5.5 %collective-permute-start.27 = (bf16[288,128]{1,0:T(8,128)(2,1)S(1)}, bf16[288,128]{1,0:T(8,128)(2,1)S(1)}, u32[]{:S(2)}, u32[]{:S(2)}) collective-permute-start(bf16[288,128]{1,0:T(8,128)(2,1)S(1)} %shard_map.161.refs_2_.refs_0_), channel_id=1, source_target_pairs={{0,8},{4,12},{8,0},{12,4},{1,9},{5,13},{9,1},{13,5},{2,10},{6,14},... | collective-permute-start | bytes 221192 | tf_op jit(solution)/shard_map/ppermute | solution.py:514
  68.4 6.7 %collective-permute-start.31 = (bf16[864,128]{1,0:T(8,128)(2,1)S(1)}, bf16[864,128]{1,0:T(8,128)(2,1)S(1)}, u32[]{:S(2)}, u32[]{:S(2)}) collective-permute-start(bf16[864,128]{1,0:T(8,128)(2,1)S(1)} %shard_map.162.refs_2_.refs_0_), channel_id=1, source_target_pairs={{0,1},{1,0},{2,3},{3,2},{4,5},{5,4},{6,7},{7,6},{8,9},{9,8},{10,11... | collective-permute-start | bytes 663560 | tf_op jit(solution)/shard_map/ppermute | solution.py:514
  72.7 2.4 %collective-permute-start.33 = (bf16[864,128]{1,0:T(8,128)(2,1)S(1)}, bf16[864,128]{1,0:T(8,128)(2,1)S(1)}, u32[]{:S(2)}, u32[]{:S(2)}) collective-permute-start(bf16[864,128]{1,0:T(8,128)(2,1)S(1)} %shard_map.165), channel_id=1, source_target_pairs={{0,1},{1,0},{2,3},{3,2},{4,5},{5,4},{6,7},{7,6},{8,9},{9,8},{10,11... | collective-permute-start | bytes 663560 | tf_op jit(solution)/shard_map/ppermute | solution.py:514
  72.8 4.7 %collective-permute-start.30 = (bf16[288,128]{1,0:T(8,128)(2,1)S(1)}, bf16[288,128]{1,0:T(8,128)(2,1)S(1)}, u32[]{:S(2)}, u32[]{:S(2)}) collective-permute-start(bf16[288,128]{1,0:T(8,128)(2,1)S(1)} %shard_map.163.refs_4_.refs_1_.refs_0_), channel_id=1, source_target_pairs={{0,2},{1,3},{2,0},{3,1},{4,6},{5,7},{6,4},{7,5},{8,10},{9,11},{10,... | collective-permute-start | bytes 221192 | tf_op jit(solution)/shard_map/ppermute | solution.py:514
  73.8 3.7 %collective-permute-start.29 = (bf16[288,128]{1,0:T(8,128)(2,1)S(1)}, bf16[288,128]{1,0:T(8,128)(2,1)S(1)}, u32[]{:S(2)}, u32[]{:S(2)}) collective-permute-start(bf16[288,128]{1,0:T(8,128)(2,1)S(1)} %shard_map.163.refs_4_.refs_1_.refs_0_), channel_id=1, source_target_pairs={{0,1},{1,0},{2,3},{3,2},{4,5},{5,4},{6,7},{7,6},{8,9},{9,8},{10,11... | collective-permute-start | bytes 221192 | tf_op jit(solution)/shard_map/ppermute | solution.py:514
  77.5 1.3 %collective-permute-start.34 = (bf16[288,128]{1,0:T(8,128)(2,1)S(1)}, bf16[288,128]{1,0:T(8,128)(2,1)S(1)}, u32[]{:S(2)}, u32[]{:S(2)}) collective-permute-start(bf16[288,128]{1,0:T(8,128)(2,1)S(1)} %shard_map.167), channel_id=1, source_target_pairs={{0,1},{1,0},{2,3},{3,2},{4,5},{5,4},{6,7},{7,6},{8,9},{9,8},{10,11... | collective-permute-start | bytes 221192 | tf_op jit(solution)/shard_map/ppermute | solution.py:514

commit v6 on v5

--- a/solution.py
+++ b/solution.py
@@ -692,7 +692,7 @@
     arrived = grads[1:]
     rows_grads = call(kernel(to_rows_kernel), row_tiles, [], *grads, across, after=mark)
     grads = exchange(rows_grads, "attr", 1)
-    mark = sums.add(far[0], after=arrived)
+    mark = sums.add(far[-1], after=arrived)
 
     keep, send, grad, grad_proj = call(
         kernel(rows_back_kernel),
@@ -708,17 +708,14 @@
         after=mark,
     )
     row_sums = Total(keep, swap(send, "attr", near[0]))
-    mark = [keep]
-    for bit in far[1:]:
-        mark = sums.add(bit, after=mark)
+    grads = call(end_kernel, row_tiles, [], by_rows, kept[0], x, Near(grad), Near(grad_proj), after=[keep])
+    mark = grads[:1]
     for bit in near[1:]:
         mark = row_sums.halve("attr", bit, after=mark)
-    grads = call(
-        end_kernel, row_tiles, [], by_rows, kept[0], x, Near(grad), Near(grad_proj), after=mark
-    )
-    row_sums.add(far[0], after=mark)
+    for bit in far[-2::-1]:
+        mark = sums.add(bit, after=mark)
     grads = exchange(grads, "attr", -1)
-    mark = grads[1:]
+    mark = row_sums.add(far[0], after=mark + grads[1:])
     for bit in far[1:]:
         mark = row_sums.add(bit, after=mark)
     mark = sums.add(after=mark)

time: 79.9 us -> 79.6 us (level)
    ppermute x14, waiting for transfers between devices: 11 us -> 10.2 us  [swap(): return lax.ppermute(part, axis, [(i, i ^ bit) for i in range(size)])]
where the time goes in v6:
time: 79.6 us; the launch traced here: 79.4 us
  starting transfers between devices  33.9 us (43%)
  waiting for transfers between devices  24.2 us (30%)
  Pallas kernels  20.4 us (26%)
  between operations  0.88 us (1%)
    ppermute x21, starting transfers between devices, exchange(): lax.ppermute(tiles[k], axis, [(i, (i + sign * k) % size) for i in range(s...  23.7 us
    pallas_call x25, Pallas kernels, call(): pl.pallas_call(kernel, out_shape=[(pltpu.VMEM if out[2:] else jax.ShapeDt...  20.4 us
    ppermute x21, waiting for transfers between devices, exchange(): lax.ppermute(tiles[k], axis, [(i, (i + sign * k) % size) for i in range(s...  13.9 us
    ppermute x14, starting transfers between devices, swap(): return lax.ppermute(part, axis, [(i, i ^ bit) for i in range(size)])  10.3 us
    ppermute x14, waiting for transfers between devices, swap(): return lax.ppermute(part, axis, [(i, i ^ bit) for i in range(size)])  10.2 us
  transfers between devices with their start and end apart: 35, of which 17 were waited for; matrix products, arithmetic and copies ran while one was open for 0% of the time, Pallas kernels for 13%

profile of v6, /device:TPU:0, one launch (start us, length us, event | category | flops | bytes accessed | tf_op | source)
XLA Modules:
  0.0 79.4 jit_solution(13172892167005789008)
XLA Ops:
  0.6 1.5 %shard_map.144 = (bf16[192,128]{1,0:T(8,128)(2,1)S(1)}, bf16[192,128]{1,0:T(8,128)(2,1)S(1)}, bf16[192,128]{1,0:T(8,128)(2,1)S(1)}, bf16[192,128]{1,0:T(8,128)(2,1)S(1)}) custom-call(bf16[8,12288]{1,0:T(8,128)(2,1)} %refs_0_.2), custom_call_target="tpu_custom_call" | custom-call | tf_op jit(solution)/shard_map/pallas_call | solution.py:490
  2.1 0.5 collective-permute-start
  2.6 2.6 %collective-permute-start.1 = (bf16[192,128]{1,0:T(8,128)(2,1)S(1)}, bf16[192,128]{1,0:T(8,128)(2,1)S(1)}, u32[]{:S(2)}, u32[]{:S(2)}) collective-permute-start(bf16[192,128]{1,0:T(8,128)(2,1)S(1)} %get-tuple-element.82), channel_id=1, source_target_pairs={{0,2},{1,3},{2,0},{3,1},{4,6},{5,7},{6,4},{7,5},{8,10},{9,11},{10,... | collective-permute-start | bytes 147464 | tf_op jit(solution)/shard_map/ppermute | solution.py:507
  5.2 1.4 %collective-permute-start.2 = (bf16[192,128]{1,0:T(8,128)(2,1)S(1)}, bf16[192,128]{1,0:T(8,128)(2,1)S(1)}, u32[]{:S(2)}, u32[]{:S(2)}) collective-permute-start(bf16[192,128]{1,0:T(8,128)(2,1)S(1)} %get-tuple-element.83), channel_id=1, source_target_pairs={{0,3},{1,0},{2,1},{3,2},{4,7},{5,4},{6,5},{7,6},{8,11},{9,8},{10,9... | collective-permute-start | bytes 147464 | tf_op jit(solution)/shard_map/ppermute | solution.py:507
  6.6 1.7 %shard_map.145 = (bf16[192,128]{1,0:T(8,128)(2,1)S(1)}, bf16[192,128]{1,0:T(8,128)(2,1)S(1)}, bf16[192,128]{1,0:T(8,128)(2,1)S(1)}, bf16[192,128]{1,0:T(8,128)(2...) custom-call(bf16[8,12288]{1,0:T(8,128)(2,1)} %refs_0_.3, ...), custom_call_target="tpu_custom_call" | custom-call | tf_op jit(solution)/shard_map/pallas_call | solution.py:490
  8.3 2.2 %shard_map.146 = (bf16[192,128]{1,0:T(8,128)(2,1)S(1)}, bf16[192,128]{1,0:T(8,128)(2,1)S(1)}, bf16[192,128]{1,0:T(8,128)(2,1)S(1)}, bf16[192,128]{1,0:T(8,128)(2...) custom-call(bf16[192,128]{1,0:T(8,128)(2,1)S(1)} %get-tuple-element., ...), custom_call_target="tpu_custom_call" | custom-call | tf_op jit(solution)/shard_map/pallas_call | solution.py:490
  10.6 1.8 %collective-permute-start.3 = (bf16[192,128]{1,0:T(8,128)(2,1)S(1)}, bf16[192,128]{1,0:T(8,128)(2,1)S(1)}, u32[]{:S(2)}, u32[]{:S(2)}) collective-permute-start(bf16[192,128]{1,0:T(8,128)(2,1)S(1)} %get-tuple-element.87), channel_id=1, source_target_pairs={{0,3},{1,0},{2,1},{3,2},{4,7},{5,4},{6,5},{7,6},{8,11},{9,8},{10,9... | collective-permute-start | bytes 147464 | tf_op jit(solution)/shard_map/ppermute | solution.py:507
  12.4 0.3 collective-permute-start.4
  12.7 1.8 %collective-permute-start.9 = (bf16[192,128]{1,0:T(8,128)(2,1)S(1)}, bf16[192,128]{1,0:T(8,128)(2,1)S(1)}, u32[]{:S(2)}, u32[]{:S(2)}) collective-permute-start(bf16[192,128]{1,0:T(8,128)(2,1)S(1)} %get-tuple-element.100), channel_id=1, source_target_pairs={{0,4},{4,8},{8,12},{12,0},{1,5},{5,9},{9,13},{13,1},{2,6},{6,10},{... | collective-permute-start | bytes 147464 | tf_op jit(solution)/shard_map/ppermute | solution.py:507
  14.5 2.6 %collective-permute-start.10 = (bf16[192,128]{1,0:T(8,128)(2,1)S(1)}, bf16[192,128]{1,0:T(8,128)(2,1)S(1)}, u32[]{:S(2)}, u32[]{:S(2)}) collective-permute-start(bf16[192,128]{1,0:T(8,128)(2,1)S(1)} %get-tuple-element.101), channel_id=1, source_target_pairs={{0,8},{4,12},{8,0},{12,4},{1,9},{5,13},{9,1},{13,5},{2,10},{6,14},... | collective-permute-start | bytes 147464 | tf_op jit(solution)/shard_map/ppermute | solution.py:507
  17.1 1.3 %collective-permute-start.11 = (bf16[192,128]{1,0:T(8,128)(2,1)S(1)}, bf16[192,128]{1,0:T(8,128)(2,1)S(1)}, u32[]{:S(2)}, u32[]{:S(2)}) collective-permute-start(bf16[192,128]{1,0:T(8,128)(2,1)S(1)} %get-tuple-element.102), channel_id=1, source_target_pairs={{0,12},{4,0},{8,4},{12,8},{1,13},{5,1},{9,5},{13,9},{2,14},{6,2},{... | collective-permute-start | bytes 147464 | tf_op jit(solution)/shard_map/ppermute | solution.py:507
  18.4 0.3 shard_map.147
  18.7 0.7 collective-permute-start.6
  19.5 2.0 %collective-permute-start.7 = (bf16[192,128]{1,0:T(8,128)(2,1)S(1)}, bf16[192,128]{1,0:T(8,128)(2,1)S(1)}, u32[]{:S(2)}, u32[]{:S(2)}) collective-permute-start(bf16[192,128]{1,0:T(8,128)(2,1)S(1)} %get-tuple-element.97), channel_id=1, source_target_pairs={{0,8},{4,12},{8,0},{12,4},{1,9},{5,13},{9,1},{13,5},{2,10},{6,14},... | collective-permute-start | bytes 147464 | tf_op jit(solution)/shard_map/ppermute | solution.py:507
  21.5 1.3 %collective-permute-start.8 = (bf16[192,128]{1,0:T(8,128)(2,1)S(1)}, bf16[192,128]{1,0:T(8,128)(2,1)S(1)}, u32[]{:S(2)}, u32[]{:S(2)}) collective-permute-start(bf16[192,128]{1,0:T(8,128)(2,1)S(1)} %get-tuple-element.98), channel_id=1, source_target_pairs={{0,12},{4,0},{8,4},{12,8},{1,13},{5,1},{9,5},{13,9},{2,14},{6,2},{... | collective-permute-start | bytes 147464 | tf_op jit(solution)/shard_map/ppermute | solution.py:507
  22.8 1.7 %shard_map.148 = (bf16[576,192]{1,0:T(8,128)(2,1)S(1)}, bf16[192,192]{1,0:T(8,128)(2,1)S(1)}, bf16[768,192]{1,0:T(8,128)(2,1)S(1)}, bf16[768,192]{1,0:T(8,128)(2...) custom-call(s32[1,32]{1,0:T(1,128)S(1)} %bitcast.3, ...), custom_call_target="tpu_custom_call" | custom-call | tf_op jit(solution)/shard_map/pallas_call | solution.py:490
  24.5 0.7 collective-permute-done.6.refs_1_
  25.3 1.7 %collective-permute-done.7.refs_2_ = bf16[192,128]{1,0:T(8,128)(2,1)S(1)} collective-permute-done((bf16[192,128]{1,0:T(8,128)(2,1)S(1)}, bf16[192,128]{1,0:T(8,128)(2,1)S(1)}, u32[]{:S(2)}, u32[]{:S(2)}) %collective-permute-start.7) | collective-permute-done | bytes 49184 | tf_op jit(solution)/shard_map/ppermute | solution.py:507
  27.0 4.2 %shard_map.149 = (bf16[192,512]{1,0:T(8,128)(2,1)S(1)}, bf16[192,512]{1,0:T(8,128)(2,1)S(1)}, bf16[192,512]{1,0:T(8,128)(2,1)S(1)}, bf16[768,512]{1,0:T(8,128)(2...) custom-call(bf16[192,128]{1,0:T(8,128)(2,1)S(1)} %get-tuple-element., ...), custom_call_target="tpu_custom_call" | custom-call | tf_op jit(solution)/shard_map/pallas_call | solution.py:490
  31.2 1.1 %shard_map.150 = (bf16[1728,128]{1,0:T(8,128)(2,1)S(1)}, bf16[1728,128]{1,0:T(8,128)(2,1)S(1)}) custom-call(bf16[192,512]{1,0:T(8,128)(2,1)S(1)} %get-tuple-element.113.refs_0_, bf16[192,512]{1,0:T(8,128)(2,1)S(1)} %get-tuple-element.114.refs_1_, bf16[192,512]{1,0:T(8,128)(2,1)S(1)} %get-tuple-element.115.refs_2_, ...), custom_call_target="tpu_custom_call" | custom-call | tf_op jit(solution)/shard_map/pallas_call | solution.py:490
  32.3 0.1 collective-permute-start.14
  32.4 0.6 shard_map.151
  33.0 1.1 %collective-permute-done.14.refs_1_ = bf16[1728,128]{1,0:T(8,128)(2,1)S(1)} collective-permute-done((bf16[1728,128]{1,0:T(8,128)(2,1)S(1)}, bf16[1728,128]{1,0:T(8,128)(2,1)S(1)}, u32[]{:S(2)}, u32[]{:S(2)}) %collective-permute-start.14) | collective-permute-done | bytes 442400 | tf_op jit(solution)/shard_map/ppermute | solution.py:514
  34.1 0.1 shard_map.152
  34.2 0.5 collective-permute-start.19
  34.7 2.6 %collective-permute-start.12 = (bf16[192,128]{1,0:T(8,128)(2,1)S(1)}, bf16[192,128]{1,0:T(8,128)(2,1)S(1)}, u32[]{:S(2)}, u32[]{:S(2)}) collective-permute-start(bf16[192,128]{1,0:T(8,128)(2,1)S(1)} %get-tuple-element.121), channel_id=1, source_target_pairs={{0,12},{4,0},{8,4},{12,8},{1,13},{5,1},{9,5},{13,9},{2,14},{6,2},{... | collective-permute-start | bytes 147464 | tf_op jit(solution)/shard_map/ppermute | solution.py:507
  37.3 0.2 collective-permute-start.13
  37.5 0.3 collective-permute-start.15
  37.9 1.5 %collective-permute-done.12.refs_1_.refs_2_ = bf16[192,128]{1,0:T(8,128)(2,1)S(1)} collective-permute-done((bf16[192,128]{1,0:T(8,128)(2,1)S(1)}, bf16[192,128]{1,0:T(8,128)(2,1)S(1)}, u32[]{:S(2)}, u32[]{:S(2)}) %collective-permute-start.12) | collective-permute-done | bytes 49184 | tf_op jit(solution)/shard_map/ppermute | solution.py:507
  39.4 3.1 %collective-permute-done.13.refs_2_.refs_3_ = bf16[192,128]{1,0:T(8,128)(2,1)S(1)} collective-permute-done((bf16[192,128]{1,0:T(8,128)(2,1)S(1)}, bf16[192,128]{1,0:T(8,128)(2,1)S(1)}, u32[]{:S(2)}, u32[]{:S(2)}) %collective-permute-start.13) | collective-permute-done | bytes 49184 | tf_op jit(solution)/shard_map/ppermute | solution.py:507
  42.5 0.9 %collective-permute-done.15.refs_3_.refs_4_ = bf16[192,128]{1,0:T(8,128)(2,1)S(1)} collective-permute-done((bf16[192,128]{1,0:T(8,128)(2,1)S(1)}, bf16[192,128]{1,0:T(8,128)(2,1)S(1)}, u32[]{:S(2)}, u32[]{:S(2)}) %collective-permute-start.15) | collective-permute-done | bytes 49184 | tf_op jit(solution)/shard_map/ppermute | solution.py:507
  43.5 1.0 %collective-permute-start.25 = (bf16[864,128]{1,0:T(8,128)(2,1)S(1)}, bf16[864,128]{1,0:T(8,128)(2,1)S(1)}, u32[]{:S(2)}, u32[]{:S(2)}) collective-permute-start(bf16[864,128]{1,0:T(8,128)(2,1)S(1)} %shard_map.155.refs_10_.refs_0_), channel_id=1, source_target_pairs={{0,8},{4,12},{8,0},{12,4},{1,9},{5,13},{9,1},{13,5},{2,10},{6,14},... | collective-permute-start | bytes 663560 | tf_op jit(solution)/shard_map/ppermute | solution.py:514
  44.5 0.3 shard_map.154
  44.8 0.1 collective-permute-start.16
  44.9 1.3 %collective-permute-start.17 = (bf16[192,128]{1,0:T(8,128)(2,1)S(1)}, bf16[192,128]{1,0:T(8,128)(2,1)S(1)}, u32[]{:S(2)}, u32[]{:S(2)}) collective-permute-start(bf16[192,128]{1,0:T(8,128)(2,1)S(1)} %get-tuple-element.129), channel_id=1, source_target_pairs={{0,2},{1,3},{2,0},{3,1},{4,6},{5,7},{6,4},{7,5},{8,10},{9,11},{10,... | collective-permute-start | bytes 147464 | tf_op jit(solution)/shard_map/ppermute | solution.py:507
  46.2 1.4 %collective-permute-start.18 = (bf16[192,128]{1,0:T(8,128)(2,1)S(1)}, bf16[192,128]{1,0:T(8,128)(2,1)S(1)}, u32[]{:S(2)}, u32[]{:S(2)}) collective-permute-start(bf16[192,128]{1,0:T(8,128)(2,1)S(1)} %get-tuple-element.130), channel_id=1, source_target_pairs={{0,3},{1,0},{2,1},{3,2},{4,7},{5,4},{6,5},{7,6},{8,11},{9,8},{10,9... | collective-permute-start | bytes 147464 | tf_op jit(solution)/shard_map/ppermute | solution.py:507
  47.5 0.8 %collective-permute-done.16.refs_1_ = bf16[192,128]{1,0:T(8,128)(2,1)S(1)} collective-permute-done((bf16[192,128]{1,0:T(8,128)(2,1)S(1)}, bf16[192,128]{1,0:T(8,128)(2,1)S(1)}, u32[]{:S(2)}, u32[]{:S(2)}) %collective-permute-start.16) | collective-permute-done | bytes 49184 | tf_op jit(solution)/shard_map/ppermute | solution.py:507
  48.4 0.9 %collective-permute-done.17.refs_2_ = bf16[192,128]{1,0:T(8,128)(2,1)S(1)} collective-permute-done((bf16[192,128]{1,0:T(8,128)(2,1)S(1)}, bf16[192,128]{1,0:T(8,128)(2,1)S(1)}, u32[]{:S(2)}, u32[]{:S(2)}) %collective-permute-start.17) | collective-permute-done | bytes 49184 | tf_op jit(solution)/shard_map/ppermute | solution.py:507
  49.2 0.1 collective-permute-done.18.refs_3_
  49.3 2.3 %shard_map.156 = (bf16[576,128]{1,0:T(8,128)(2,1)S(1)}, bf16[576,128]{1,0:T(8,128)(2,1)S(1)}, bf16[192,512]{1,0:T(8,128)(2,1)S(1)}, bf16[576,512]{1,0:T(8,128)(2,1)S(1)}) custom-call(bf16[192,128]{1,0:T(8,128)(2,1)S(1)} %get-tuple-element.127.refs_0_, bf16[192,128]{1,0:T(8,128)(2,1)S(1)} %collective-permute-done.16.refs_1_, ...), custom_call_target="tpu_custom_call" | custom-call | tf_op jit(solution)/shard_map/pallas_call | solution.py:490
  51.6 1.3 %collective-permute-start.23 = (bf16[576,128]{1,0:T(8,128)(2,1)S(1)}, bf16[576,128]{1,0:T(8,128)(2,1)S(1)}, u32[]{:S(2)}, u32[]{:S(2)}) collective-permute-start(bf16[576,128]{1,0:T(8,128)(2,1)S(1)} %get-tuple-element.144), channel_id=1, source_target_pairs={{0,1},{1,0},{2,3},{3,2},{4,5},{5,4},{6,7},{7,6},{8,9},{9,8},{10,11... | collective-permute-start | bytes 442376 | tf_op jit(solution)/shard_map/ppermute | solution.py:514
  52.9 0.6 shard_map.157
  53.6 0.4 collective-permute-done.23.refs_1_
  54.0 0.8 %collective-permute-done.25.refs_1_ = bf16[864,128]{1,0:T(8,128)(2,1)S(1)} collective-permute-done((bf16[864,128]{1,0:T(8,128)(2,1)S(1)}, bf16[864,128]{1,0:T(8,128)(2,1)S(1)}, u32[]{:S(2)}, u32[]{:S(2)}) %collective-permute-start.25) | collective-permute-done | bytes 221216 | tf_op jit(solution)/shard_map/ppermute | solution.py:514
  54.9 0.1 collective-permute-start.28
  55.0 1.0 %collective-permute-start.24 = (bf16[288,128]{1,0:T(8,128)(2,1)S(1)}, bf16[288,128]{1,0:T(8,128)(2,1)S(1)}, u32[]{:S(2)}, u32[]{:S(2)}) collective-permute-start(bf16[288,128]{1,0:T(8,128)(2,1)S(1)} %get-tuple-element.146), channel_id=1, source_target_pairs={{0,2},{1,3},{2,0},{3,1},{4,6},{5,7},{6,4},{7,5},{8,10},{9,11},{10,... | collective-permute-start | bytes 221192 | tf_op jit(solution)/shard_map/ppermute | solution.py:514
  56.0 0.4 collective-permute-start.20
  56.4 1.0 %collective-permute-start.21 = (bf16[192,128]{1,0:T(8,128)(2,1)S(1)}, bf16[192,128]{1,0:T(8,128)(2,1)S(1)}, u32[]{:S(2)}, u32[]{:S(2)}) collective-permute-start(bf16[192,128]{1,0:T(8,128)(2,1)S(1)} %get-tuple-element.142), channel_id=1, source_target_pairs={{0,2},{1,3},{2,0},{3,1},{4,6},{5,7},{6,4},{7,5},{8,10},{9,11},{10,... | collective-permute-start | bytes 147464 | tf_op jit(solution)/shard_map/ppermute | solution.py:507
  57.4 1.6 %collective-permute-done.20.refs_3_.refs_1_ = bf16[192,128]{1,0:T(8,128)(2,1)S(1)} collective-permute-done((bf16[192,128]{1,0:T(8,128)(2,1)S(1)}, bf16[192,128]{1,0:T(8,128)(2,1)S(1)}, u32[]{:S(2)}, u32[]{:S(2)}) %collective-permute-start.20) | collective-permute-done | bytes 49184 | tf_op jit(solution)/shard_map/ppermute | solution.py:507
  58.9 2.6 %collective-permute-done.21.refs_4_.refs_2_ = bf16[192,128]{1,0:T(8,128)(2,1)S(1)} collective-permute-done((bf16[192,128]{1,0:T(8,128)(2,1)S(1)}, bf16[192,128]{1,0:T(8,128)(2,1)S(1)}, u32[]{:S(2)}, u32[]{:S(2)}) %collective-permute-start.21) | collective-permute-done | bytes 49184 | tf_op jit(solution)/shard_map/ppermute | solution.py:507
  61.5 2.0 %collective-permute-start.26 = (bf16[288,128]{1,0:T(8,128)(2,1)S(1)}, bf16[288,128]{1,0:T(8,128)(2,1)S(1)}, u32[]{:S(2)}, u32[]{:S(2)}) collective-permute-start(bf16[288,128]{1,0:T(8,128)(2,1)S(1)} %shard_map.160.refs_0_.refs_2_), channel_id=1, source_target_pairs={{0,4},{4,0},{8,12},{12,8},{1,5},{5,1},{9,13},{13,9},{2,6},{6,2},{1... | collective-permute-start | bytes 221192 | tf_op jit(solution)/shard_map/ppermute | solution.py:514
  63.5 2.4 %collective-permute-done.26.refs_1_ = bf16[288,128]{1,0:T(8,128)(2,1)S(1)} collective-permute-done((bf16[288,128]{1,0:T(8,128)(2,1)S(1)}, bf16[288,128]{1,0:T(8,128)(2,1)S(1)}, u32[]{:S(2)}, u32[]{:S(2)}) %collective-permute-start.26) | collective-permute-done | bytes 73760 | tf_op jit(solution)/shard_map/ppermute | solution.py:514
  66.0 1.0 %collective-permute-start.32 = (bf16[864,128]{1,0:T(8,128)(2,1)S(1)}, bf16[864,128]{1,0:T(8,128)(2,1)S(1)}, u32[]{:S(2)}, u32[]{:S(2)}) collective-permute-start(bf16[864,128]{1,0:T(8,128)(2,1)S(1)} %shard_map.162.refs_2_.refs_0_), channel_id=1, source_target_pairs={{0,2},{1,3},{2,0},{3,1},{4,6},{5,7},{6,4},{7,5},{8,10},{9,11},{10,... | collective-permute-start | bytes 663560 | tf_op jit(solution)/shard_map/ppermute | solution.py:514
  67.0 1.9 %collective-permute-start.27 = (bf16[288,128]{1,0:T(8,128)(2,1)S(1)}, bf16[288,128]{1,0:T(8,128)(2,1)S(1)}, u32[]{:S(2)}, u32[]{:S(2)}) collective-permute-start(bf16[288,128]{1,0:T(8,128)(2,1)S(1)} %shard_map.161.refs_2_.refs_0_), channel_id=1, source_target_pairs={{0,8},{4,12},{8,0},{12,4},{1,9},{5,13},{9,1},{13,5},{2,10},{6,14},... | collective-permute-start | bytes 221192 | tf_op jit(solution)/shard_map/ppermute | solution.py:514
  68.9 3.4 %collective-permute-done.27.refs_1_ = bf16[288,128]{1,0:T(8,128)(2,1)S(1)} collective-permute-done((bf16[288,128]{1,0:T(8,128)(2,1)S(1)}, bf16[288,128]{1,0:T(8,128)(2,1)S(1)}, u32[]{:S(2)}, u32[]{:S(2)}) %collective-permute-start.27) | collective-permute-done | bytes 73760 | tf_op jit(solution)/shard_map/ppermute | solution.py:514
  72.4 0.1 collective-permute-start.33
  72.5 1.1 %collective-permute-start.30 = (bf16[288,128]{1,0:T(8,128)(2,1)S(1)}, bf16[288,128]{1,0:T(8,128)(2,1)S(1)}, u32[]{:S(2)}, u32[]{:S(2)}) collective-permute-start(bf16[288,128]{1,0:T(8,128)(2,1)S(1)} %shard_map.163.refs_4_.refs_1_.refs_0_), channel_id=1, source_target_pairs={{0,2},{1,3},{2,0},{3,1},{4,6},{5,7},{6,4},{7,5},{8,10},{9,11},{10,... | collective-permute-start | bytes 221192 | tf_op jit(solution)/shard_map/ppermute | solution.py:514
  73.6 0.2 collective-permute-start.29
  73.8 1.1 %shard_map.164.refs_1_ = bf16[8,12288]{1,0:T(8,128)(2,1)} custom-call(bf16[192,128]{1,0:T(8,128)(2,1)S(1)} %get-tuple-element.140.refs_2_.refs_0_, bf16[192,128]{1,0:T(8,128)(2,1)S(1)} %collective-permute-done.20.refs_3_.refs_1_, bf16[192,128]{1,0:T(8,128)(2,1)S(1)} %collective-permute-done.21.refs_4_.refs_2_, ...), custom_call_target="tpu_custom_call" | custom-call | tf_op jit(solution)/shard_map/pallas_call | solution.py:490
  74.9 1.4 %shard_map.166 = (f32[192,576]{1,0:T(8,128)}, f32[192,192]{1,0:T(8,128)}, f32[192,768]{1,0:T(8,128)}, f32[192,768]{1,0:T(8,128)}) custom-call(bf16[864,128]{1,0:T(8,128)(2,1)S(1)} %shard_map.162.refs_2_.refs_0_, bf16[864,128]{1,0:T(8,128)(2,1)S(1)} %collective-permute-done.31.refs_1_, bf16[864,128]{1,0:T(8,128)(2,1)S(1)} %collective-permute-done.32.refs_0_.refs_2_, ...), custom_call_target="tpu_custom_call" | custom-call | tf_op jit(solution)/shard_map/pallas_call | solution.py:490
  76.3 0.9 %collective-permute-done.30.refs_0_.refs_2_ = bf16[288,128]{1,0:T(8,128)(2,1)S(1)} collective-permute-done((bf16[288,128]{1,0:T(8,128)(2,1)S(1)}, bf16[288,128]{1,0:T(8,128)(2,1)S(1)}, u32[]{:S(2)}, u32[]{:S(2)}) %collective-permute-start.30) | collective-permute-done | bytes 73760 | tf_op jit(solution)/shard_map/ppermute | solution.py:514
  77.2 0.1 collective-permute-start.34
  77.3 1.2 %collective-permute-done.34.refs_3_ = bf16[288,128]{1,0:T(8,128)(2,1)S(1)} collective-permute-done((bf16[288,128]{1,0:T(8,128)(2,1)S(1)}, bf16[288,128]{1,0:T(8,128)(2,1)S(1)}, u32[]{:S(2)}, u32[]{:S(2)}) %collective-permute-start.34) | collective-permute-done | bytes 73760 | tf_op jit(solution)/shard_map/ppermute | solution.py:514
  78.5 0.9 %shard_map.168 = (f32[192,576]{1,0:T(8,128)}, f32[192,192]{1,0:T(8,128)}) custom-call(bf16[288,128]{1,0:T(8,128)(2,1)S(1)} %shard_map.163.refs_4_.refs_1_.refs_0_, bf16[288,128]{1,0:T(8,128)(2,1)S(1)} %collective-permute-done.29.refs_1_, bf16[288,128]{1,0:T(8,128)(2,1)S(1)} %collective-permute-done.30.refs_0_.refs_2_, ...), custom_call_target="tpu_custom_call" | custom-call | tf_op jit(solution)/shard_map/pallas_call | solution.py:490
  (33 shorter events, 0.4 us)
Async XLA Ops:
  0.6 22.2 %copy-start = (s32[32]{0:T(128)S(1)}, s32[32]{0:T(128)}, u32[]{:S(2)}) copy-start(s32[32]{0:T(128)} %param.17) | copy-start | bytes 388
  2.1 6.2 %collective-permute-start = (bf16[192,128]{1,0:T(8,128)(2,1)S(1)}, bf16[192,128]{1,0:T(8,128)(2,1)S(1)}, u32[]{:S(2)}, u32[]{:S(2)}) collective-permute-start(bf16[192,128]{1,0:T(8,128)(2,1)S(1)} %get-tuple-element.81), channel_id=1, source_target_pairs={{0,1},{1,2},{2,3},{3,0},{4,5},{5,6},{6,7},{7,4},{8,9},{9,10},{10,1... | collective-permute-start | bytes 147464 | tf_op jit(solution)/shard_map/ppermute | solution.py:507
  2.6 5.7 %collective-permute-start.1 = (bf16[192,128]{1,0:T(8,128)(2,1)S(1)}, bf16[192,128]{1,0:T(8,128)(2,1)S(1)}, u32[]{:S(2)}, u32[]{:S(2)}) collective-permute-start(bf16[192,128]{1,0:T(8,128)(2,1)S(1)} %get-tuple-element.82), channel_id=1, source_target_pairs={{0,2},{1,3},{2,0},{3,1},{4,6},{5,7},{6,4},{7,5},{8,10},{9,11},{10,... | collective-permute-start | bytes 147464 | tf_op jit(solution)/shard_map/ppermute | solution.py:507
  5.2 3.1 %collective-permute-start.2 = (bf16[192,128]{1,0:T(8,128)(2,1)S(1)}, bf16[192,128]{1,0:T(8,128)(2,1)S(1)}, u32[]{:S(2)}, u32[]{:S(2)}) collective-permute-start(bf16[192,128]{1,0:T(8,128)(2,1)S(1)} %get-tuple-element.83), channel_id=1, source_target_pairs={{0,3},{1,0},{2,1},{3,2},{4,7},{5,4},{6,5},{7,6},{8,11},{9,8},{10,9... | collective-permute-start | bytes 147464 | tf_op jit(solution)/shard_map/ppermute | solution.py:507
  10.6 6.5 %collective-permute-start.3 = (bf16[192,128]{1,0:T(8,128)(2,1)S(1)}, bf16[192,128]{1,0:T(8,128)(2,1)S(1)}, u32[]{:S(2)}, u32[]{:S(2)}) collective-permute-start(bf16[192,128]{1,0:T(8,128)(2,1)S(1)} %get-tuple-element.87), channel_id=1, source_target_pairs={{0,3},{1,0},{2,1},{3,2},{4,7},{5,4},{6,5},{7,6},{8,11},{9,8},{10,9... | collective-permute-start | bytes 147464 | tf_op jit(solution)/shard_map/ppermute | solution.py:507
  12.4 6.1 %collective-permute-start.4 = (bf16[192,128]{1,0:T(8,128)(2,1)S(1)}, bf16[192,128]{1,0:T(8,128)(2,1)S(1)}, u32[]{:S(2)}, u32[]{:S(2)}) collective-permute-start(bf16[192,128]{1,0:T(8,128)(2,1)S(1)} %get-tuple-element.88), channel_id=1, source_target_pairs={{0,2},{1,3},{2,0},{3,1},{4,6},{5,7},{6,4},{7,5},{8,10},{9,11},{10,... | collective-permute-start | bytes 147464 | tf_op jit(solution)/shard_map/ppermute | solution.py:507
  12.7 5.7 %collective-permute-start.5 = (bf16[192,128]{1,0:T(8,128)(2,1)S(1)}, bf16[192,128]{1,0:T(8,128)(2,1)S(1)}, u32[]{:S(2)}, u32[]{:S(2)}) collective-permute-start(bf16[192,128]{1,0:T(8,128)(2,1)S(1)} %get-tuple-element.89), channel_id=1, source_target_pairs={{0,1},{1,2},{2,3},{3,0},{4,5},{5,6},{6,7},{7,4},{8,9},{9,10},{10,1... | collective-permute-start | bytes 147464 | tf_op jit(solution)/shard_map/ppermute | solution.py:507
  12.7 8.8 %collective-permute-start.9 = (bf16[192,128]{1,0:T(8,128)(2,1)S(1)}, bf16[192,128]{1,0:T(8,128)(2,1)S(1)}, u32[]{:S(2)}, u32[]{:S(2)}) collective-permute-start(bf16[192,128]{1,0:T(8,128)(2,1)S(1)} %get-tuple-element.100), channel_id=1, source_target_pairs={{0,4},{4,8},{8,12},{12,0},{1,5},{5,9},{9,13},{13,1},{2,6},{6,10},{... | collective-permute-start | bytes 147464 | tf_op jit(solution)/shard_map/ppermute | solution.py:507
  14.5 10.0 %collective-permute-start.10 = (bf16[192,128]{1,0:T(8,128)(2,1)S(1)}, bf16[192,128]{1,0:T(8,128)(2,1)S(1)}, u32[]{:S(2)}, u32[]{:S(2)}) collective-permute-start(bf16[192,128]{1,0:T(8,128)(2,1)S(1)} %get-tuple-element.101), channel_id=1, source_target_pairs={{0,8},{4,12},{8,0},{12,4},{1,9},{5,13},{9,1},{13,5},{2,10},{6,14},... | collective-permute-start | bytes 147464 | tf_op jit(solution)/shard_map/ppermute | solution.py:507
  17.1 7.5 %collective-permute-start.11 = (bf16[192,128]{1,0:T(8,128)(2,1)S(1)}, bf16[192,128]{1,0:T(8,128)(2,1)S(1)}, u32[]{:S(2)}, u32[]{:S(2)}) collective-permute-start(bf16[192,128]{1,0:T(8,128)(2,1)S(1)} %get-tuple-element.102), channel_id=1, source_target_pairs={{0,12},{4,0},{8,4},{12,8},{1,13},{5,1},{9,5},{13,9},{2,14},{6,2},{... | collective-permute-start | bytes 147464 | tf_op jit(solution)/shard_map/ppermute | solution.py:507
  18.7 6.6 %collective-permute-start.6 = (bf16[192,128]{1,0:T(8,128)(2,1)S(1)}, bf16[192,128]{1,0:T(8,128)(2,1)S(1)}, u32[]{:S(2)}, u32[]{:S(2)}) collective-permute-start(bf16[192,128]{1,0:T(8,128)(2,1)S(1)} %get-tuple-element.96), channel_id=1, source_target_pairs={{0,4},{4,8},{8,12},{12,0},{1,5},{5,9},{9,13},{13,1},{2,6},{6,10},{... | collective-permute-start | bytes 147464 | tf_op jit(solution)/shard_map/ppermute | solution.py:507
  19.5 7.5 %collective-permute-start.7 = (bf16[192,128]{1,0:T(8,128)(2,1)S(1)}, bf16[192,128]{1,0:T(8,128)(2,1)S(1)}, u32[]{:S(2)}, u32[]{:S(2)}) collective-permute-start(bf16[192,128]{1,0:T(8,128)(2,1)S(1)} %get-tuple-element.97), channel_id=1, source_target_pairs={{0,8},{4,12},{8,0},{12,4},{1,9},{5,13},{9,1},{13,5},{2,10},{6,14},... | collective-permute-start | bytes 147464 | tf_op jit(solution)/shard_map/ppermute | solution.py:507
  21.5 5.5 %collective-permute-start.8 = (bf16[192,128]{1,0:T(8,128)(2,1)S(1)}, bf16[192,128]{1,0:T(8,128)(2,1)S(1)}, u32[]{:S(2)}, u32[]{:S(2)}) collective-permute-start(bf16[192,128]{1,0:T(8,128)(2,1)S(1)} %get-tuple-element.98), channel_id=1, source_target_pairs={{0,12},{4,0},{8,4},{12,8},{1,13},{5,1},{9,5},{13,9},{2,14},{6,2},{... | collective-permute-start | bytes 147464 | tf_op jit(solution)/shard_map/ppermute | solution.py:507
  32.3 1.9 %collective-permute-start.14 = (bf16[1728,128]{1,0:T(8,128)(2,1)S(1)}, bf16[1728,128]{1,0:T(8,128)(2,1)S(1)}, u32[]{:S(2)}, u32[]{:S(2)}) collective-permute-start(bf16[1728,128]{1,0:T(8,128)(2,1)S(1)} %get-tuple-element.124), channel_id=1, source_target_pairs={{0,1},{1,0},{2,3},{3,2},{4,5},{5,4},{6,7},{7,6},{8,9},{9,8},{10,11... | collective-permute-start | bytes 1327112 | tf_op jit(solution)/shard_map/ppermute | solution.py:514
  34.2 9.2 %collective-permute-start.19 = (bf16[864,128]{1,0:T(8,128)(2,1)S(1)}, bf16[864,128]{1,0:T(8,128)(2,1)S(1)}, u32[]{:S(2)}, u32[]{:S(2)}) collective-permute-start(bf16[864,128]{1,0:T(8,128)(2,1)S(1)} %get-tuple-element.136), channel_id=1, source_target_pairs={{0,2},{1,3},{2,0},{3,1},{4,6},{5,7},{6,4},{7,5},{8,10},{9,11},{10,... | collective-permute-start | bytes 663560 | tf_op jit(solution)/shard_map/ppermute | solution.py:514
  34.7 4.7 %collective-permute-start.12 = (bf16[192,128]{1,0:T(8,128)(2,1)S(1)}, bf16[192,128]{1,0:T(8,128)(2,1)S(1)}, u32[]{:S(2)}, u32[]{:S(2)}) collective-permute-start(bf16[192,128]{1,0:T(8,128)(2,1)S(1)} %get-tuple-element.121), channel_id=1, source_target_pairs={{0,12},{4,0},{8,4},{12,8},{1,13},{5,1},{9,5},{13,9},{2,14},{6,2},{... | collective-permute-start | bytes 147464 | tf_op jit(solution)/shard_map/ppermute | solution.py:507
  37.3 5.2 %collective-permute-start.13 = (bf16[192,128]{1,0:T(8,128)(2,1)S(1)}, bf16[192,128]{1,0:T(8,128)(2,1)S(1)}, u32[]{:S(2)}, u32[]{:S(2)}) collective-permute-start(bf16[192,128]{1,0:T(8,128)(2,1)S(1)} %get-tuple-element.122), channel_id=1, source_target_pairs={{0,8},{4,12},{8,0},{12,4},{1,9},{5,13},{9,1},{13,5},{2,10},{6,14},... | collective-permute-start | bytes 147464 | tf_op jit(solution)/shard_map/ppermute | solution.py:507
  37.5 5.9 %collective-permute-start.15 = (bf16[192,128]{1,0:T(8,128)(2,1)S(1)}, bf16[192,128]{1,0:T(8,128)(2,1)S(1)}, u32[]{:S(2)}, u32[]{:S(2)}) collective-permute-start(bf16[192,128]{1,0:T(8,128)(2,1)S(1)} %shard_map.153), channel_id=1, source_target_pairs={{0,4},{4,8},{8,12},{12,0},{1,5},{5,9},{9,13},{13,1},{2,6},{6,10},{... | collective-permute-start | bytes 147464 | tf_op jit(solution)/shard_map/ppermute | solution.py:507
  43.5 11.3 %collective-permute-start.25 = (bf16[864,128]{1,0:T(8,128)(2,1)S(1)}, bf16[864,128]{1,0:T(8,128)(2,1)S(1)}, u32[]{:S(2)}, u32[]{:S(2)}) collective-permute-start(bf16[864,128]{1,0:T(8,128)(2,1)S(1)} %shard_map.155.refs_10_.refs_0_), channel_id=1, source_target_pairs={{0,8},{4,12},{8,0},{12,4},{1,9},{5,13},{9,1},{13,5},{2,10},{6,14},... | collective-permute-start | bytes 663560 | tf_op jit(solution)/shard_map/ppermute | solution.py:514
  44.8 3.6 %collective-permute-start.16 = (bf16[192,128]{1,0:T(8,128)(2,1)S(1)}, bf16[192,128]{1,0:T(8,128)(2,1)S(1)}, u32[]{:S(2)}, u32[]{:S(2)}) collective-permute-start(bf16[192,128]{1,0:T(8,128)(2,1)S(1)} %get-tuple-element.128), channel_id=1, source_target_pairs={{0,1},{1,2},{2,3},{3,0},{4,5},{5,6},{6,7},{7,4},{8,9},{9,10},{10,1... | collective-permute-start | bytes 147464 | tf_op jit(solution)/shard_map/ppermute | solution.py:507
  44.9 4.4 %collective-permute-start.17 = (bf16[192,128]{1,0:T(8,128)(2,1)S(1)}, bf16[192,128]{1,0:T(8,128)(2,1)S(1)}, u32[]{:S(2)}, u32[]{:S(2)}) collective-permute-start(bf16[192,128]{1,0:T(8,128)(2,1)S(1)} %get-tuple-element.129), channel_id=1, source_target_pairs={{0,2},{1,3},{2,0},{3,1},{4,6},{5,7},{6,4},{7,5},{8,10},{9,11},{10,... | collective-permute-start | bytes 147464 | tf_op jit(solution)/shard_map/ppermute | solution.py:507
  46.2 3.1 %collective-permute-start.18 = (bf16[192,128]{1,0:T(8,128)(2,1)S(1)}, bf16[192,128]{1,0:T(8,128)(2,1)S(1)}, u32[]{:S(2)}, u32[]{:S(2)}) collective-permute-start(bf16[192,128]{1,0:T(8,128)(2,1)S(1)} %get-tuple-element.130), channel_id=1, source_target_pairs={{0,3},{1,0},{2,1},{3,2},{4,7},{5,4},{6,5},{7,6},{8,11},{9,8},{10,9... | collective-permute-start | bytes 147464 | tf_op jit(solution)/shard_map/ppermute | solution.py:507
  51.6 2.3 %collective-permute-start.23 = (bf16[576,128]{1,0:T(8,128)(2,1)S(1)}, bf16[576,128]{1,0:T(8,128)(2,1)S(1)}, u32[]{:S(2)}, u32[]{:S(2)}) collective-permute-start(bf16[576,128]{1,0:T(8,128)(2,1)S(1)} %get-tuple-element.144), channel_id=1, source_target_pairs={{0,1},{1,0},{2,3},{3,2},{4,5},{5,4},{6,7},{7,6},{8,9},{9,8},{10,11... | collective-permute-start | bytes 442376 | tf_op jit(solution)/shard_map/ppermute | solution.py:514
  54.9 11.1 %collective-permute-start.28 = (bf16[864,128]{1,0:T(8,128)(2,1)S(1)}, bf16[864,128]{1,0:T(8,128)(2,1)S(1)}, u32[]{:S(2)}, u32[]{:S(2)}) collective-permute-start(bf16[864,128]{1,0:T(8,128)(2,1)S(1)} %shard_map.159.refs_2_.refs_0_), channel_id=1, source_target_pairs={{0,4},{4,0},{8,12},{12,8},{1,5},{5,1},{9,13},{13,9},{2,6},{6,2},{1... | collective-permute-start | bytes 663560 | tf_op jit(solution)/shard_map/ppermute | solution.py:514
  55.0 6.5 %collective-permute-start.24 = (bf16[288,128]{1,0:T(8,128)(2,1)S(1)}, bf16[288,128]{1,0:T(8,128)(2,1)S(1)}, u32[]{:S(2)}, u32[]{:S(2)}) collective-permute-start(bf16[288,128]{1,0:T(8,128)(2,1)S(1)} %get-tuple-element.146), channel_id=1, source_target_pairs={{0,2},{1,3},{2,0},{3,1},{4,6},{5,7},{6,4},{7,5},{8,10},{9,11},{10,... | collective-permute-start | bytes 221192 | tf_op jit(solution)/shard_map/ppermute | solution.py:514
  56.0 2.9 %collective-permute-start.20 = (bf16[192,128]{1,0:T(8,128)(2,1)S(1)}, bf16[192,128]{1,0:T(8,128)(2,1)S(1)}, u32[]{:S(2)}, u32[]{:S(2)}) collective-permute-start(bf16[192,128]{1,0:T(8,128)(2,1)S(1)} %get-tuple-element.141), channel_id=1, source_target_pairs={{0,3},{1,0},{2,1},{3,2},{4,7},{5,4},{6,5},{7,6},{8,11},{9,8},{10,9... | collective-permute-start | bytes 147464 | tf_op jit(solution)/shard_map/ppermute | solution.py:507
  56.4 5.1 %collective-permute-start.21 = (bf16[192,128]{1,0:T(8,128)(2,1)S(1)}, bf16[192,128]{1,0:T(8,128)(2,1)S(1)}, u32[]{:S(2)}, u32[]{:S(2)}) collective-permute-start(bf16[192,128]{1,0:T(8,128)(2,1)S(1)} %get-tuple-element.142), channel_id=1, source_target_pairs={{0,2},{1,3},{2,0},{3,1},{4,6},{5,7},{6,4},{7,5},{8,10},{9,11},{10,... | collective-permute-start | bytes 147464 | tf_op jit(solution)/shard_map/ppermute | solution.py:507
  57.3 4.1 %collective-permute-start.22 = (bf16[192,128]{1,0:T(8,128)(2,1)S(1)}, bf16[192,128]{1,0:T(8,128)(2,1)S(1)}, u32[]{:S(2)}, u32[]{:S(2)}) collective-permute-start(bf16[192,128]{1,0:T(8,128)(2,1)S(1)} %get-tuple-element.143), channel_id=1, source_target_pairs={{0,1},{1,2},{2,3},{3,0},{4,5},{5,6},{6,7},{7,4},{8,9},{9,10},{10,1... | collective-permute-start | bytes 147464 | tf_op jit(solution)/shard_map/ppermute | solution.py:507
  61.5 4.4 %collective-permute-start.26 = (bf16[288,128]{1,0:T(8,128)(2,1)S(1)}, bf16[288,128]{1,0:T(8,128)(2,1)S(1)}, u32[]{:S(2)}, u32[]{:S(2)}) collective-permute-start(bf16[288,128]{1,0:T(8,128)(2,1)S(1)} %shard_map.160.refs_0_.refs_2_), channel_id=1, source_target_pairs={{0,4},{4,0},{8,12},{12,8},{1,5},{5,1},{9,13},{13,9},{2,6},{6,2},{1... | collective-permute-start | bytes 221192 | tf_op jit(solution)/shard_map/ppermute | solution.py:514
  66.0 6.3 %collective-permute-start.32 = (bf16[864,128]{1,0:T(8,128)(2,1)S(1)}, bf16[864,128]{1,0:T(8,128)(2,1)S(1)}, u32[]{:S(2)}, u32[]{:S(2)}) collective-permute-start(bf16[864,128]{1,0:T(8,128)(2,1)S(1)} %shard_map.162.refs_2_.refs_0_), channel_id=1, source_target_pairs={{0,2},{1,3},{2,0},{3,1},{4,6},{5,7},{6,4},{7,5},{8,10},{9,11},{10,... | collective-permute-start | bytes 663560 | tf_op jit(solution)/shard_map/ppermute | solution.py:514
  67.0 5.3 %collective-permute-start.27 = (bf16[288,128]{1,0:T(8,128)(2,1)S(1)}, bf16[288,128]{1,0:T(8,128)(2,1)S(1)}, u32[]{:S(2)}, u32[]{:S(2)}) collective-permute-start(bf16[288,128]{1,0:T(8,128)(2,1)S(1)} %shard_map.161.refs_2_.refs_0_), channel_id=1, source_target_pairs={{0,8},{4,12},{8,0},{12,4},{1,9},{5,13},{9,1},{13,5},{2,10},{6,14},... | collective-permute-start | bytes 221192 | tf_op jit(solution)/shard_map/ppermute | solution.py:514
  68.9 6.0 %collective-permute-start.31 = (bf16[864,128]{1,0:T(8,128)(2,1)S(1)}, bf16[864,128]{1,0:T(8,128)(2,1)S(1)}, u32[]{:S(2)}, u32[]{:S(2)}) collective-permute-start(bf16[864,128]{1,0:T(8,128)(2,1)S(1)} %shard_map.162.refs_2_.refs_0_), channel_id=1, source_target_pairs={{0,1},{1,0},{2,3},{3,2},{4,5},{5,4},{6,7},{7,6},{8,9},{9,8},{10,11... | collective-permute-start | bytes 663560 | tf_op jit(solution)/shard_map/ppermute | solution.py:514
  72.4 2.5 %collective-permute-start.33 = (bf16[864,128]{1,0:T(8,128)(2,1)S(1)}, bf16[864,128]{1,0:T(8,128)(2,1)S(1)}, u32[]{:S(2)}, u32[]{:S(2)}) collective-permute-start(bf16[864,128]{1,0:T(8,128)(2,1)S(1)} %shard_map.165), channel_id=1, source_target_pairs={{0,1},{1,0},{2,3},{3,2},{4,5},{5,4},{6,7},{7,6},{8,9},{9,8},{10,11... | collective-permute-start | bytes 663560 | tf_op jit(solution)/shard_map/ppermute | solution.py:514
  72.5 4.7 %collective-permute-start.30 = (bf16[288,128]{1,0:T(8,128)(2,1)S(1)}, bf16[288,128]{1,0:T(8,128)(2,1)S(1)}, u32[]{:S(2)}, u32[]{:S(2)}) collective-permute-start(bf16[288,128]{1,0:T(8,128)(2,1)S(1)} %shard_map.163.refs_4_.refs_1_.refs_0_), channel_id=1, source_target_pairs={{0,2},{1,3},{2,0},{3,1},{4,6},{5,7},{6,4},{7,5},{8,10},{9,11},{10,... | collective-permute-start | bytes 221192 | tf_op jit(solution)/shard_map/ppermute | solution.py:514
  73.6 3.6 %collective-permute-start.29 = (bf16[288,128]{1,0:T(8,128)(2,1)S(1)}, bf16[288,128]{1,0:T(8,128)(2,1)S(1)}, u32[]{:S(2)}, u32[]{:S(2)}) collective-permute-start(bf16[288,128]{1,0:T(8,128)(2,1)S(1)} %shard_map.163.refs_4_.refs_1_.refs_0_), channel_id=1, source_target_pairs={{0,1},{1,0},{2,3},{3,2},{4,5},{5,4},{6,7},{7,6},{8,9},{9,8},{10,11... | collective-permute-start | bytes 221192 | tf_op jit(solution)/shard_map/ppermute | solution.py:514
  77.2 1.3 %collective-permute-start.34 = (bf16[288,128]{1,0:T(8,128)(2,1)S(1)}, bf16[288,128]{1,0:T(8,128)(2,1)S(1)}, u32[]{:S(2)}, u32[]{:S(2)}) collective-permute-start(bf16[288,128]{1,0:T(8,128)(2,1)S(1)} %shard_map.167), channel_id=1, source_target_pairs={{0,1},{1,0},{2,3},{3,2},{4,5},{5,4},{6,7},{7,6},{8,9},{9,8},{10,11... | collective-permute-start | bytes 221192 | tf_op jit(solution)/shard_map/ppermute | solution.py:514
